TPU v7x, 32 devices: a whole 2x2x4 slice. The times are simulated.
32 devices in a mesh: sector: 8 (over z, core), slab: 4 (over y, x).
Axes of the slice: x: 2, y: 2, z: 4, core: 2. Of those that a mesh axis runs over, the one named last changes fastest.
Arguments:
- volume_rhs: float32 [128, 64, 8, 256], P('sector', 'slab'), may hold values from -80 to 80
- surface_rhs: float32 [64, 64, 256], P('sector', 'slab'), may hold values from -6 to 6
- volume_guess: float32 [128, 64, 8, 256], P('sector', 'slab'), may hold values from -6 to 6
- surface_guess: float32 [64, 64, 256], P('sector', 'slab'), may hold values from -6 to 6
- bem_matrix: bfloat16 [2, 4096, 4096], P(None, 'sector', 'slab'), may hold values from -0.0625 to 0.0625
- stiffness: float32 [3, 8, 8], replicated, may hold values from -1.05 to 3, as said below
- mass_shift: float32 [128, 64, 8], P('sector', 'slab'), may hold values from -3 to 0
Outputs:
- volume_solution: float32 [128, 64, 8, 256], P('sector', 'slab')
- surface_solution: float32 [64, 64, 256], P('sector', 'slab')
Inputs may be any that keep to these rules, and one draw needn't show every extreme that they name: stiffness[d] is symmetric, its diagonal entries between 1.5 and 3.
All inputs are finite; a program needn't handle non-finite values.
Results may differ from a plain program's by a relative error of at most 0.0003.
Values may be sent and summed in bfloat16 or wider, within the bound.
No kernel may reach another device: no remote copies, remote signals or barrier semaphores. Data moves between devices by JAX's collectives and lax.ppermute only.
A program may use at most 128 MiB of HBM per device.

v0:
```python
import functools
import math

import jax
import jax.numpy as jnp
from jax import lax
from jax.experimental import pallas as pl
from jax.experimental.pallas import tpu as pltpu
from jax.sharding import PartitionSpec as P

PENALTY = 1.0
EPSILON = 1e-06
F32 = jnp.float32
BF16 = jnp.bfloat16
WIRE = jnp.float16
LANES = 256
HALF = 128
VMEM_LIMIT = 48 * 1024 * 1024
WHOLE = pl.BlockSpec(memory_space=pltpu.VMEM)
SCALARS = pl.BlockSpec(memory_space=pltpu.SMEM)


def call(kernel, out_shape, n_scalars, n_arrays, scratch=(), flops=0, bytes_accessed=0, name=None):
    return pl.pallas_call(
        kernel,
        out_shape=out_shape,
        in_specs=[SCALARS] * n_scalars + [WHOLE] * n_arrays,
        out_specs=jax.tree.map(lambda _: WHOLE, out_shape),
        scratch_shapes=list(scratch),
        compiler_params=pltpu.CompilerParams(vmem_limit_bytes=VMEM_LIMIT),
        cost_estimate=pl.CostEstimate(
            flops=flops, bytes_accessed=bytes_accessed, transcendentals=0
        ),
        name=name,
    )


def shape(*dims):
    return jax.ShapeDtypeStruct(dims, F32)


def split_bf16(values):
    upper = values.astype(BF16)
    lower = (values - upper.astype(F32)).astype(BF16)
    return upper, lower


def one_hot(rows, columns, pick):
    row = lax.broadcasted_iota(jnp.int32, (rows, columns), 0)
    column = lax.broadcasted_iota(jnp.int32, (rows, columns), 1)
    return (pick(row) == column).astype(F32)


def line_matrix(stiffness, order, nodes, rows, fast):
    select = one_hot(rows, order, lambda row: (row // fast) % order)
    spread = jnp.dot(select, stiffness, precision=lax.Precision.HIGHEST)
    full = lax.dot_general(
        spread, select, (((1,), (1,)), ((), ())), precision=lax.Precision.HIGHEST
    )
    row = lax.broadcasted_iota(jnp.int32, (rows, rows), 0)
    column = lax.broadcasted_iota(jnp.int32, (rows, rows), 1)
    row_node, column_node = row // fast, column // fast
    same_fast = row % fast == column % fast
    same_element = (row_node // order == column_node // order) & same_fast
    block = jnp.where(same_element, full, 0.0)
    edge = (row_node % order == 0) | (row_node % order == order - 1)
    block = block + jnp.where((row == column) & edge, PENALTY, 0.0)
    back = (row_node % order == 0) & (column_node == row_node - 1) & same_fast
    ahead = (row_node % order == order - 1) & (column_node == row_node + 1) & same_fast
    return block - jnp.where(back | ahead, PENALTY, 0.0)


def matrices_kernel(nodes, radial, stiffness_ref, wide_ref, narrow_ref):
    order = stiffness_ref.shape[1]
    rows = nodes * radial
    theta = line_matrix(stiffness_ref[0], order, nodes, rows, radial)
    axial = line_matrix(stiffness_ref[1], order, nodes, rows, radial)
    select = one_hot(rows, order, lambda row: row % radial)
    spread = jnp.dot(select, stiffness_ref[2], precision=lax.Precision.HIGHEST)
    full = lax.dot_general(
        spread, select, (((1,), (1,)), ((), ())), precision=lax.Precision.HIGHEST
    )
    row = lax.broadcasted_iota(jnp.int32, (rows, rows), 0)
    column = lax.broadcasted_iota(jnp.int32, (rows, rows), 1)
    axial = axial + jnp.where(row // radial == column // radial, full, 0.0)
    edge = (row % radial == 0) | (row % radial == radial - 1)
    axial = axial + jnp.where((row == column) & edge, PENALTY, 0.0)
    for index, matrix in enumerate((theta, axial)):
        upper, lower = split_bf16(matrix)
        wide_ref[index, :, :rows] = upper
        wide_ref[index, :, rows:] = upper
        narrow_ref[index] = lower


def volume_matrices(stiffness, nodes, radial):
    rows = nodes * radial
    return call(
        functools.partial(matrices_kernel, nodes, radial),
        (
            jax.ShapeDtypeStruct((2, rows, 2 * rows), BF16),
            jax.ShapeDtypeStruct((2, rows, rows), BF16),
        ),
        0,
        1,
        name="volume_matrices",
    )(stiffness)


def bulk_kernel(x_ref, mass_ref, wide_ref, narrow_ref, y_ref):
    n_theta, n_axial, radial, lanes = x_ref.shape

    def product(index, values):
        upper, lower = split_bf16(values)
        both = jnp.concatenate([upper, lower], axis=0)
        return jnp.dot(wide_ref[index], both, preferred_element_type=F32) + jnp.dot(
            narrow_ref[index], upper, preferred_element_type=F32
        )

    def along_theta(z, carry):
        values = x_ref[:, z].reshape(n_theta * radial, lanes)
        y_ref[:, z] = product(0, values).reshape(n_theta, radial, lanes)
        return carry

    def along_axial(a, carry):
        values = x_ref[a].reshape(n_axial * radial, lanes)
        total = product(1, values).reshape(n_axial, radial, lanes)
        mass = mass_ref[a]
        old = y_ref[a] + total
        x = x_ref[a]
        y_ref[a, :, :, :HALF] = old[:, :, :HALF] + mass * x[:, :, :HALF]
        y_ref[a, :, :, HALF:] = old[:, :, HALF:] + mass * x[:, :, HALF:]
        return carry

    lax.fori_loop(0, n_axial, along_theta, 0, unroll=2)
    lax.fori_loop(0, n_theta, along_axial, 0, unroll=2)


def volume_bulk(x, mass, wide, narrow):
    rows = x.shape[1] * x.shape[2]
    return call(
        bulk_kernel,
        shape(*x.shape),
        0,
        4,
        flops=2 * 2 * 3 * x.size * rows,
        bytes_accessed=16 * x.size,
        name="volume_bulk",
    )(x, mass, wide, narrow)


def pair_sums(left, right):
    left_real, left_imag = left[..., :HALF], left[..., HALF:]
    right_real, right_imag = right[..., :HALF], right[..., HALF:]
    return (
        jnp.sum(left_real * right_real + left_imag * right_imag, axis=0),
        jnp.sum(left_real * right_imag - left_imag * right_real, axis=0),
    )


def square_sums(values):
    squares = values * values
    return jnp.sum(squares[..., :HALF] + squares[..., HALF:], axis=0)


def finish_row(a, bulk, s_ref, before_ref, beyond_ref, axial_before_ref, axial_beyond_ref, n_theta):
    n_axial, radial, lanes = bulk.shape
    if isinstance(a, int) and a == 0:
        bulk = bulk - before_ref[...]
    if isinstance(a, int) and a == n_theta - 1:
        bulk = bulk - beyond_ref[...]
    outer = lax.broadcasted_iota(jnp.int32, (radial, lanes), 0) == radial - 1
    tiles = []
    for z in range(n_axial):
        tile = bulk[z]
        if z == 0:
            tile = tile - axial_before_ref[a]
        if z == n_axial - 1:
            tile = tile - axial_beyond_ref[a]
        face = jnp.broadcast_to(s_ref[a // 2, z : z + 1, :], (radial, lanes))
        tiles.append(tile + jnp.where(outer, face, 0.0))
    return jnp.stack(tiles)


def over_rows(n_theta, body):
    body(0)
    lax.fori_loop(1, n_theta - 1, lambda a, carry: (body(a), carry)[1], 0)
    body(n_theta - 1)


def put_faces(u_ref, face_ref):
    radial = u_ref.shape[2]
    for pair in range(face_ref.shape[0]):
        face_ref[pair] = 0.5 * (
            u_ref[2 * pair, :, radial - 1, :] + u_ref[2 * pair + 1, :, radial - 1, :]
        )


def finish_first_kernel(
    bulk_ref, s_ref, before_ref, beyond_ref, ax_before_ref, ax_beyond_ref, rhs_ref,
    u_ref, face_ref, sums_ref,
):
    n_theta = bulk_ref.shape[0]
    sums_ref[...] = jnp.zeros_like(sums_ref)

    def body(a):
        image = finish_row(
            a, bulk_ref[a], s_ref, before_ref, beyond_ref, ax_before_ref, ax_beyond_ref, n_theta
        )
        u = rhs_ref[a] - image
        u_ref[a] = u
        sums_ref[0] += square_sums(u)

    over_rows(n_theta, body)
    put_faces(u_ref, face_ref)


def finish_second_kernel(
    bulk_ref, s_ref, before_ref, beyond_ref, ax_before_ref, ax_beyond_ref, u0_ref,
    u_ref, face_ref, sums_ref,
):
    n_theta = bulk_ref.shape[0]
    sums_ref[...] = jnp.zeros_like(sums_ref)

    def body(a):
        u = finish_row(
            a, bulk_ref[a], s_ref, before_ref, beyond_ref, ax_before_ref, ax_beyond_ref, n_theta
        )
        u_ref[a] = u
        real, imag = pair_sums(u0_ref[a], u)
        sums_ref[0] += real
        sums_ref[1] += imag
        sums_ref[2] += square_sums(u)

    over_rows(n_theta, body)
    put_faces(u_ref, face_ref)


def finish_third_kernel(
    bulk_ref, s_ref, before_ref, beyond_ref, ax_before_ref, ax_beyond_ref, u0_ref, u1_ref, sums_ref
):
    n_theta = bulk_ref.shape[0]
    sums_ref[...] = jnp.zeros_like(sums_ref)

    def body(a):
        u = finish_row(
            a, bulk_ref[a], s_ref, before_ref, beyond_ref, ax_before_ref, ax_beyond_ref, n_theta
        )
        real, imag = pair_sums(u0_ref[a], u)
        sums_ref[0] += real
        sums_ref[1] += imag
        real, imag = pair_sums(u1_ref[a], u)
        sums_ref[2] += real
        sums_ref[3] += imag
        sums_ref[4] += square_sums(u)

    over_rows(n_theta, body)


def finish(kernel, n_sums, with_result, bulk, s, halos, *others):
    n_theta, n_axial, radial, lanes = bulk.shape
    outs = (shape(n_sums, radial, HALF),)
    if with_result:
        outs = (shape(*bulk.shape), shape(n_theta // 2, n_axial, lanes)) + outs
    return call(
        kernel,
        outs,
        0,
        6 + len(others),
        flops=20 * bulk.size,
        bytes_accessed=4 * bulk.size * (2 + len(others)),
        name=kernel.__name__,
    )(bulk, s, *halos, *others)


def bem_kernel(sign, chunk, place_ref, m_ref, s_ref, add_ref, out_ref, upper_ref, lower_ref, p_ref):
    pairs, n_axial, lanes = add_ref.shape
    slabs = out_ref.shape[0]
    axial_all = p_ref.shape[1]
    columns = s_ref.shape[0]
    rows = m_ref.shape[1]
    for piece in range(columns // chunk):
        values = s_ref[piece * chunk : (piece + 1) * chunk, :]
        upper, lower = split_bf16(values)
        at = pl.ds(pl.multiple_of(place_ref[1 + piece], chunk), chunk)
        upper_ref[at, :] = upper
        lower_ref[at, :] = lower

    step = 2 * axial_all if axial_all < 128 else axial_all

    def block(index, carry):
        at = pl.ds(pl.multiple_of(index * step, step), step)
        real = m_ref[0, at, :]
        imag = m_ref[1, at, :]
        by_real = jnp.dot(real, upper_ref[...], preferred_element_type=F32) + jnp.dot(
            real, lower_ref[...], preferred_element_type=F32
        )
        by_imag = jnp.dot(imag, upper_ref[...], preferred_element_type=F32) + jnp.dot(
            imag, lower_ref[...], preferred_element_type=F32
        )
        here = pl.ds(index * (step // axial_all), step // axial_all)
        three = (step // axial_all, axial_all, HALF)
        p_ref[here, :, :HALF] = sign * (by_real[:, :HALF] - by_imag[:, HALF:]).reshape(three)
        p_ref[here, :, HALF:] = sign * (by_real[:, HALF:] + by_imag[:, :HALF]).reshape(three)
        return carry

    lax.fori_loop(0, rows // step, block, 0)
    slab = place_ref[0]
    own = pl.ds(pl.multiple_of(slab * n_axial, n_axial), n_axial)
    p_ref[:, own, :] += add_ref[...]
    for shift in range(slabs):
        target = lax.rem(slab + shift, slabs)
        for turn in range(pairs // slabs):
            out_ref[shift, turn * axial_all : (turn + 1) * axial_all, :] = p_ref[
                target + turn * slabs
            ]
        there = pl.ds(pl.multiple_of(target * n_axial, n_axial), n_axial)
        out_ref[shift, chunk:, :] = p_ref[:, there, :].reshape(pairs * n_axial, lanes)


def bem_partial(sign, place, matrix, gathered, add, slabs):
    pairs, n_axial, lanes = add.shape
    axial_all = n_axial * slabs
    chunk = pairs // slabs * axial_all
    rows, columns = matrix.shape[1:]
    return call(
        functools.partial(bem_kernel, sign, chunk),
        shape(slabs, 2 * chunk, lanes),
        1,
        3,
        scratch=[
            pltpu.VMEM((columns, lanes), BF16),
            pltpu.VMEM((columns, lanes), BF16),
            pltpu.VMEM((pairs, axial_all, lanes), F32),
        ],
        flops=2 * 4 * rows * columns * lanes,
        bytes_accessed=4 * rows * columns + 4 * columns * lanes + 8 * chunk * slabs * lanes,
        name="bem_partial",
    )(place, matrix, gathered, add)


def surface_sums(u0, u1, u2):
    sums = (square_sums(u0),) + pair_sums(u0, u1) + (square_sums(u1),)
    return sums + pair_sums(u0, u2) + pair_sums(u1, u2) + (square_sums(u2),)


def gram_kernel(first_ref, second_ref, third_ref, s0_ref, s1_ref, s2_ref, out_ref):
    volume = (
        [first_ref[0]]
        + [second_ref[row] for row in range(3)]
        + [third_ref[row] for row in range(5)]
    )
    surface = surface_sums(s0_ref[...], s1_ref[...], s2_ref[...])
    for row, (one, two) in enumerate(zip(volume, surface)):
        out_ref[row : row + 1, :] = jnp.sum(one, axis=0, keepdims=True) + jnp.sum(
            two, axis=0, keepdims=True
        )


def local_gram(first, second, third, s0, s1, s2):
    tiles = [values.reshape(-1, 8, LANES) for values in (s0, s1, s2)]
    return call(gram_kernel, shape(9, HALF), 0, 6, name="local_gram")(
        first, second, third, *tiles
    )


def times(left, right):
    return (
        left[0] * right[0] - left[1] * right[1],
        left[0] * right[1] + left[1] * right[0],
    )


def conj_times(left, right):
    return (
        left[0] * right[0] + left[1] * right[1],
        left[0] * right[1] - left[1] * right[0],
    )


def square(value):
    return value[0] * value[0] + value[1] * value[1]


def coefficients(rows):
    g00, g11, g22 = rows[0], rows[3], rows[8]
    g01, g02, g12 = (rows[1], rows[2]), (rows[4], rows[5]), (rows[6], rows[7])
    beta_sq = g00 + EPSILON
    beta = jnp.sqrt(beta_sq)
    h00 = (g01[0] / beta_sq, g01[1] / beta_sq)
    h00_sq = square(h00)
    cross = conj_times(h00, g01)[0]
    rest = jnp.maximum(g11 - 2.0 * cross + h00_sq * g00, 0.0) / beta_sq
    h10_sq = rest + EPSILON
    h10 = jnp.sqrt(h10_sq)
    over_first = 1.0 / (beta_sq * h10)
    over_second = 1.0 / (beta_sq * h10_sq)
    h00_g01 = times(h00, g01)
    h01 = tuple((g02[k] - h00_g01[k]) * over_first for k in (0, 1))
    conj_g02 = conj_times(h00, g02)
    h11 = tuple(
        (g12[k] - h00[k] * g11 - conj_g02[k] + h00_sq * g01[k]) * over_second for k in (0, 1)
    )
    image_sq = (g22 - 2.0 * conj_times(h00, g12)[0] + h00_sq * g11) * over_second
    first_sq, second_sq = g00 / beta_sq, rest / h10_sq
    overlap = (h00[0] * EPSILON * over_first, h00[1] * EPSILON * over_first)
    mixed = conj_times(h01, times(h11, overlap))[0]
    bottom_sq = (
        jnp.maximum(
            image_sq
            - (2.0 - first_sq) * square(h01)
            - (2.0 - second_sq) * square(h11)
            + 2.0 * mixed,
            0.0,
        )
        + EPSILON
    )
    rho = jnp.sqrt(h00_sq + h10_sq)
    cos = (h00[0] / rho, h00[1] / rho)
    sine = h10 / rho
    top = conj_times(cos, h01)
    top = tuple(top[k] + sine * h11[k] for k in (0, 1))
    turn = times(cos, h11)
    turn = tuple(turn[k] - sine * h01[k] for k in (0, 1))
    lower = -sine * beta / (square(turn) + bottom_sq)
    one = (turn[0] * lower, -turn[1] * lower)
    top_one = times(top, one)
    zero = ((cos[0] * beta - top_one[0]) / rho, (-cos[1] * beta - top_one[1]) / rho)
    of_second = (one[0] / (beta * h10), one[1] / (beta * h10))
    back = times(of_second, h00)
    of_first = (zero[0] / beta - back[0], zero[1] / beta - back[1])
    return of_first, of_second


def combine(first, second, guess, u0, u1):
    u0_real, u0_imag = u0[..., :HALF], u0[..., HALF:]
    u1_real, u1_imag = u1[..., :HALF], u1[..., HALF:]
    real = guess[..., :HALF] + (first[0] * u0_real - first[1] * u0_imag)
    imag = guess[..., HALF:] + (first[0] * u0_imag + first[1] * u0_real)
    real = real + (second[0] * u1_real - second[1] * u1_imag)
    imag = imag + (second[0] * u1_imag + second[1] * u1_real)
    return real, imag


def solution_kernel(
    gram_ref, x_ref, u0_ref, u1_ref, s_ref, s0_ref, s1_ref, volume_ref, surface_ref
):
    rows = [jnp.sum(gram_ref[row], axis=0, keepdims=True) for row in range(9)]
    first, second = coefficients(rows)
    real, imag = combine(first, second, s_ref[...], s0_ref[...], s1_ref[...])
    surface_ref[..., :HALF] = real
    surface_ref[..., HALF:] = imag

    def body(a, carry):
        real, imag = combine(first, second, x_ref[a], u0_ref[a], u1_ref[a])
        volume_ref[a, :, :, :HALF] = real
        volume_ref[a, :, :, HALF:] = imag
        return carry

    lax.fori_loop(0, x_ref.shape[0], body, 0)


def final_solution(gram_all, x, u0, u1, s, s0, s1):
    return call(
        solution_kernel,
        (shape(*x.shape), shape(*s.shape)),
        0,
        7,
        flops=10 * x.size,
        bytes_accessed=16 * x.size,
        name="final_solution",
    )(gram_all, x, u0, u1, s, s0, s1)


def power_scale(bound):
    return 2.0 ** math.floor(math.log2(60000.0 / bound))


def to_wire(values, scale):
    return (values * scale).astype(WIRE)


def from_wire(values, scale):
    return values.astype(F32) * (1.0 / scale)


def shift_perm(peers, shift):
    return [(i, (i + shift) % peers) for i in range(peers)]


def slab_exchange(messages):
    slabs = lax.axis_size("slab")
    return [
        lax.ppermute(messages[shift], "slab", shift_perm(slabs, shift))
        for shift in range(1, slabs)
    ]


def axial_halos(received_first, received_last, scale, tail):
    slab, slabs = lax.axis_index("slab"), lax.axis_size("slab")
    before = from_wire(received_first[-tail:], scale) * (slab > 0).astype(F32)
    beyond = from_wire(received_last[-tail:], scale) * (slab < slabs - 1).astype(F32)
    return before, beyond


def sector_gather(values, scale, layers, layer_scale):
    sectors = lax.axis_size("sector")
    chips = sectors // 2
    core = lax.rem(lax.axis_index("sector"), 2)
    chunk = values.shape[0]
    tail = layers[0].shape[0]
    own = to_wire(values, scale)
    first, last = (to_wire(layer, layer_scale) for layer in layers)
    sibling = [(i, i ^ 1) for i in range(sectors)]

    def up_down(shift):
        pairs = []
        for i in range(sectors):
            chip, c = i // 2, i % 2
            pairs.append((i, (chip + (shift if c == 0 else -shift)) % chips * 2 + c))
        return pairs

    half = [(i, (i + sectors // 2) % sectors) for i in range(sectors)]
    from_half = lax.ppermute(own, "sector", half)
    beside = lax.ppermute(jnp.concatenate([own, first, last]), "sector", sibling)
    beside_first, beside_last = beside[chunk : chunk + tail], beside[chunk + tail :]
    far = jnp.where(core == 0, beside_last, beside_first)
    near = jnp.where(core == 0, beside_first, beside_last)
    both = jnp.concatenate([own, beside[:chunk]])
    arrived = []
    for shift in range(1, chips // 2):
        message = jnp.concatenate([both, far]) if shift == 1 else both
        arrived.append(lax.ppermute(message, "sector", up_down(shift)))
    far_halo = arrived[0][2 * chunk :]
    arrived = [message[: 2 * chunk] for message in arrived]
    here = jnp.concatenate(arrived + [from_half])
    there = lax.ppermute(here, "sector", sibling)
    gathered = from_wire(jnp.concatenate([both, here, there]), scale)
    before = from_wire(jnp.where(core == 0, far_halo, near), layer_scale)
    beyond = from_wire(jnp.where(core == 0, near, far_halo), layer_scale)
    return gathered, (before, beyond)


def gather_places(chunk):
    sectors = lax.axis_size("sector")
    chips = sectors // 2
    sector = lax.axis_index("sector")
    chip, core = sector // 2, lax.rem(sector, 2)

    def place(chip_shift, other):
        source = lax.rem(chip + chip_shift + 2 * chips, chips)
        return (2 * source + jnp.where(other, 1 - core, core)) * chunk

    up = jnp.where(core == 0, -1, 1)
    places = [lax.axis_index("slab"), place(0, False), place(0, True)]
    for mirrored in (False, True):
        sign = -1 if mirrored else 1
        for shift in range(1, chips // 2):
            places.append(place(sign * up * shift, mirrored))
            places.append(place(sign * up * shift, not mirrored))
        places.append(place(chips // 2, mirrored))
    return jnp.stack([jnp.asarray(value, jnp.int32) for value in places])


def edge_rows(volume):
    lanes = volume.shape[-1]
    theta = (volume[0].reshape(-1, lanes), volume[-1].reshape(-1, lanes))
    axial = (volume[:, 0].reshape(-1, lanes), volume[:, -1].reshape(-1, lanes))
    return theta, axial


def scatter_sum(parts, scale, axial, layer_scale):
    slabs = parts.shape[0]
    rows = parts.shape[1]
    messages = [None]
    for shift in range(1, slabs):
        message = to_wire(parts[shift], scale)
        if axial is not None and shift == 1:
            message = jnp.concatenate([message, to_wire(axial[1], layer_scale)])
        if axial is not None and shift == slabs - 1:
            message = jnp.concatenate([message, to_wire(axial[0], layer_scale)])
        messages.append(message)
    received = slab_exchange(messages)
    total = parts[0]
    for message in received:
        total = total + from_wire(message[:rows], scale)
    halos = None
    if axial is not None:
        halos = axial_halos(received[0], received[-1], layer_scale, axial[0].shape[0])
    return total, halos


def per_device(
    volume_rhs, surface_rhs, volume_guess, surface_guess, bem_matrix, stiffness, mass_shift
):
    slabs, sectors = lax.axis_size("slab"), lax.axis_size("sector")
    slab = lax.axis_index("slab")
    n_theta, n_axial, radial, lanes = volume_guess.shape
    pairs = surface_guess.shape[0]
    axial_all = n_axial * slabs
    turns = pairs // slabs
    chunk = turns * axial_all
    unknowns = sectors * pairs * axial_all

    gain = 8.0 * math.sqrt(unknowns)
    stiff = 3 * (3.0 + 7 * 1.05) + 6 + 3.0
    surface_0 = 6.0
    volume_0 = 6.0
    surface_1 = gain * surface_0 + 12.0
    volume_1 = 80.0 + stiff * volume_0 + surface_0
    surface_2 = gain * surface_1 + volume_1
    volume_2 = stiff * volume_1 + surface_1
    scale_s = [power_scale(bound) for bound in (surface_0, surface_1, surface_2)]
    scale_v = [power_scale(bound) for bound in (volume_0, volume_1, volume_2)]
    scale_p = [
        power_scale(gain / slabs * surface_0 + 12.0),
        power_scale(gain / slabs * surface_1 + volume_1),
        power_scale(gain / slabs * surface_2 + volume_2),
    ]

    place = gather_places(chunk)
    wide, narrow = volume_matrices(stiffness, n_theta, radial)
    mass = jnp.broadcast_to(mass_shift[..., None], mass_shift.shape + (HALF,))

    def layers(rows, count):
        return rows.reshape(count, radial, lanes)

    def shaped(theta, axial):
        return (
            layers(theta[0], n_axial),
            layers(theta[1], n_axial),
            layers(axial[0], n_theta),
            layers(axial[1], n_theta),
        )

    theta_edges, axial_edges = edge_rows(volume_guess)
    by_owner = surface_guess.reshape(turns, slabs, n_axial, lanes)
    messages = [None]
    for shift in range(1, slabs):
        share = lax.dynamic_index_in_dim(
            by_owner, lax.rem(slab + shift, slabs), axis=1, keepdims=False
        ).reshape(turns * n_axial, lanes)
        message = to_wire(share, scale_s[0])
        if shift == 1:
            message = jnp.concatenate([message, to_wire(axial_edges[1], scale_v[0])])
        if shift == slabs - 1:
            message = jnp.concatenate([message, to_wire(axial_edges[0], scale_v[0])])
        messages.append(message)
    received = slab_exchange(messages)
    axial = axial_halos(received[0], received[-1], scale_v[0], n_theta * radial)
    share = lax.dynamic_index_in_dim(by_owner, slab, axis=1, keepdims=False)
    parts = [share] + [
        from_wire(message[: turns * n_axial], scale_s[0]).reshape(turns, n_axial, lanes)
        for message in received
    ]
    columns = jnp.concatenate(
        [
            lax.dynamic_index_in_dim(
                jnp.stack(parts), lax.rem(slab - owner + slabs, slabs), axis=0, keepdims=False
            )
            for owner in range(slabs)
        ],
        axis=1,
    ).reshape(chunk, lanes)

    bulk = volume_bulk(volume_guess, mass, wide, narrow)
    gathered, theta = sector_gather(columns, scale_s[0], theta_edges, scale_v[0])
    outer = volume_guess[:, :, radial - 1, :].reshape(pairs, 2, n_axial, lanes)
    add = surface_rhs + 0.5 * (outer[:, 0] + outer[:, 1])
    u0, face0, first = finish(
        finish_first_kernel, 1, True, bulk, surface_guess, shaped(theta, axial), volume_rhs
    )
    theta_edges, axial_edges = edge_rows(u0)
    partial = bem_partial(-1.0, place, bem_matrix, gathered, add, slabs)
    total, axial = scatter_sum(partial, scale_p[0], axial_edges, scale_v[1])
    s0_owner, s0 = total[:chunk], total[chunk:].reshape(pairs, n_axial, lanes)

    bulk = volume_bulk(u0, mass, wide, narrow)
    gathered, theta = sector_gather(s0_owner, scale_s[1], theta_edges, scale_v[1])
    u1, face1, second = finish(
        finish_second_kernel, 3, True, bulk, s0, shaped(theta, axial), u0
    )
    theta_edges, axial_edges = edge_rows(u1)
    partial = bem_partial(1.0, place, bem_matrix, gathered, -face0, slabs)
    total, axial = scatter_sum(partial, scale_p[1], axial_edges, scale_v[2])
    s1_owner, s1 = total[:chunk], total[chunk:].reshape(pairs, n_axial, lanes)

    bulk = volume_bulk(u1, mass, wide, narrow)
    gathered, theta = sector_gather(s1_owner, scale_s[2], theta_edges, scale_v[2])
    (third,) = finish(
        finish_third_kernel, 5, False, bulk, s1, shaped(theta, axial), u0, u1
    )
    partial = bem_partial(1.0, place, bem_matrix, gathered, -face1, slabs)
    total, _ = scatter_sum(partial[:, :chunk], scale_p[2], None, 1.0)

    gram = local_gram(first, second, third, s0_owner, s1_owner, total)
    devices = sectors * slabs
    copies = jnp.broadcast_to(gram.reshape(1, 1, -1), (devices, 1, gram.size))
    gram_all = lax.all_to_all(copies, ("sector", "slab"), split_axis=0, concat_axis=0, tiled=True)
    gram_all = jnp.swapaxes(gram_all.reshape(devices, 9, HALF), 0, 1)
    return final_solution(gram_all, volume_guess, u0, u1, surface_guess, s0, s1)


def solution(mesh):
    return jax.shard_map(
        per_device,
        mesh=mesh,
        in_specs=(
            P("sector", "slab", None, None),
            P("sector", "slab", None),
            P("sector", "slab", None, None),
            P("sector", "slab", None),
            P(None, "sector", "slab"),
            P(),
            P("sector", "slab", None),
        ),
        out_specs=(P("sector", "slab", None, None), P("sector", "slab", None)),
        check_vma=False,
    )
```

profile of v0, /device:TPU:0, one launch (start us, length us, event | category | flops | bytes accessed | tf_op | source)
XLA Modules:
  0.0 129.1 jit_solution(395631571339515531)
XLA Ops:
  0.7 1.1 fusion.36
  1.8 1.4 %dynamic-slice_bitcast_fusion.4 = (f32[1,2,16,256]{3,2,1,0:T(8,128)}, f16[2,1,16,256]{3,2,1,0:T(8,128)(2,1)S(1)}, f16[2,1,16,256]{3,2,1,0:T(8,128)(2,1)S(1)}, f16[2,1,16,256]{3,2,1,0:T(8,128)(2,1)S(1)}) fusion(f32[2,4,16,256]{3,2,1,0:T(8,128)} %bitcast.154, s32[]{:T(128)S(6)} %select_n.91, s32[]{:T(128)S(6)} %select_n.94, s32[]{:T(128)S(6)} %select_n.93, ...), kind=kLoop, calls=%fused_computation.145 | loop fusion | flops 49152 | bytes 213008 | tf_op jit(solution)/shard_map/stack | solution.py:658
  3.9 3.9 %collective-permute-start.2 = (f16[160,256]{1,0:T(8,128)(2,1)}, f16[160,256]{1,0:T(8,128)(2,1)}, u32[]{:S(2)}, u32[]{:S(2)}) collective-permute-start(f16[160,256]{1,0:T(8,128)(2,1)} %pad_maximum_fusion.15), channel_id=1, source_target_pairs={{0,3},{1,0},{2,1},{3,2},{4,7},{5,4},{6,5},{7,6},{8,11},{9,8},{10,9... | collective-permute-start | bytes 245768 | tf_op jit(solution)/shard_map/ppermute | solution.py:493
  9.6 1.6 %fusion.38 = (f16[128,256]{1,0:T(8,128)(2,1)}, f16[128,256]{1,0:T(8,128)(2,1)}) fusion(f32[16,16,8,256]{3,2,1,0:T(8,128)} %x_ref.3), kind=kLoop, calls=%fused_computation.101 | loop fusion | flops 131072 | bytes 393216 | tf_op jit(solution)/shard_map/convert_element_type | solution.py:479
  11.2 1.9 %slice.192 = f32[16,16,1,256]{3,2,1,0:T(1,128)S(1)} slice(f32[16,16,8,256]{3,2,1,0:T(8,128)} %x_ref.3), slice={[0:16], [0:16], [7:8], [0:256]} | slice | bytes 524288 | tf_op jit(solution)/shard_map/slice | solution.py:667
  13.1 1.6 %copy.15 = f32[16,16,8]{2,1,0:T(8,128)} copy(f32[16,16,8]{1,2,0:T(8,128)} %param.13) | data formatting | bytes 16384 | tf_op args[6]
  14.7 1.1 volume_matrices.1
  16.5 1.2 broadcast_in_dim.6.mass_ref
  17.8 3.5 %volume_bulk.3.bulk_ref = f32[16,16,8,256]{3,2,1,0:T(8,128)S(1)} custom-call(f32[16,16,8,256]{3,2,1,0:T(8,128)S(1)} %copy-done.4, f32[16,16,8,128]{3,2,1,0:T(8,128)S(1)} %broadcast_in_dim.6.mass_ref, bf16[2,128,256]{2,1,0:T(8,128)(2,1)S(1)} %get-tuple-element.10.wide_ref, bf16[2,128,128]{2,1,0:T(8,128)(2,1)S(1)} %get-tuple-element.11.narrow_ref), custom_call_target="tpu_custom_call" | custom-call | flops 805306368 | bytes 8388608 | tf_op jit(solution)/shard_map/volume_bulk/pallas_call | solution.py:140
  21.4 1.3 %copy-done.6 = f32[16,16,8,256]{3,2,1,0:T(8,128)} copy-done((f32[16,16,8,256]{3,2,1,0:T(8,128)}, f32[16,16,8,256]{3,2,1,0:T(8,128)S(1)}, u32[]{:S(2)}) %copy-start.6) | copy-done | bytes 2097176
  22.8 0.9 convert_multiply_fusion.3
  25.2 2.7 %collective-permute-start.5 = (f16[128,256]{1,0:T(8,128)(2,1)S(1)}, f16[128,256]{1,0:T(8,128)(2,1)S(1)}, u32[]{:S(2)}, u32[]{:S(2)}) collective-permute-start(f16[128,256]{1,0:T(8,128)(2,1)S(1)} %bitcast.162), channel_id=1, source_target_pairs={{0,16},{4,20},{8,24},{12,28},{16,0},{20,4},{24,8},{28,12},{1,17},{... | collective-permute-start | bytes 196616 | tf_op jit(solution)/shard_map/ppermute | solution.py:523
  27.9 0.9 fusion.17
  28.9 0.9 multiply_bitcast_fusion.9.ax_before_ref
  30.4 1.6 %collective-permute-start.4 = (f16[384,256]{1,0:T(8,128)(2,1)S(1)}, f16[384,256]{1,0:T(8,128)(2,1)S(1)}, u32[]{:S(2)}, u32[]{:S(2)}) collective-permute-start(f16[384,256]{1,0:T(8,128)(2,1)S(1)} %fusion.16), channel_id=1, source_target_pairs={{0,8},{4,28},{8,16},{12,4},{16,24},{20,12},{24,0},{28,20},{1,9},{5... | collective-permute-start | bytes 589832 | tf_op jit(solution)/shard_map/ppermute | solution.py:532
  32.1 0.9 multiply_bitcast_fusion.8.ax_beyond_ref
  32.9 5.1 %collective-permute-done.4 = f16[384,256]{1,0:T(8,128)(2,1)S(1)} collective-permute-done((f16[384,256]{1,0:T(8,128)(2,1)S(1)}, f16[384,256]{1,0:T(8,128)(2,1)S(1)}, u32[]{:S(2)}, u32[]{:S(2)}) %collective-permute-start.4) | collective-permute-done | bytes 196640 | tf_op jit(solution)/shard_map/ppermute | solution.py:532
  38.3 2.2 %finish_first_kernel.1 = (f32[16,16,8,256]{3,2,1,0:T(8,128)S(1)}, f32[8,16,256]{2,1,0:T(8,128)S(1)}, f32[1,8,128]{2,1,0:T(8,128)S(1)}) custom-call(f32[16,16,8,256]{3,2,1,0:T(8,128)S(1)} %copy-done.7, f32[8,16,256]{2,1,0:T(8,128)S(1)} %copy-done.8, f32[16,8,256]{2,1,0:T(8,128)S(1)} %get-tuple-element.48.before_ref, ...), custom_call_target="tpu_custom_call" | custom-call | flops 10485760 | bytes 6291456 | tf_op jit(solution)/shard_map/finish_first_kernel/pallas_call | solution.py:264
  40.8 2.1 %copy-done.3 = bf16[2,512,1024]{2,1,0:T(8,128)(2,1)S(1)} copy-done((bf16[2,512,1024]{2,1,0:T(8,128)(2,1)S(1)}, bf16[2,512,1024]{2,1,0:T(8,128)(2,1)}, u32[]{:S(2)}) %copy-start.3) | copy-done | bytes 2097176
  42.9 2.6 %bem_partial.3 = f32[4,256,256]{2,1,0:T(8,128)S(1)} custom-call(s32[9]{0:T(128)S(1)} %stack.53.place_ref, bf16[2,512,1024]{2,1,0:T(8,128)(2,1)S(1)} %copy-done.3, f32[1024,256]{1,0:T(8,128)S(1)} %convert_multiply_fusion.2.s_ref, f32[8,16,256]{2,1,0:T(8,128)S(1)} %copy-done.11), custom_call_target="tpu_custom_call" | custom-call | flops 1073741824 | bytes 4194304 | tf_op jit(solution)/shard_map/bem_partial/pallas_call | solution.py:325
  45.6 1.0 collective-permute-start.8
  46.6 3.0 %collective-permute-start.9 = (f16[384,256]{1,0:T(8,128)(2,1)S(1)}, f16[384,256]{1,0:T(8,128)(2,1)S(1)}, u32[]{:S(2)}, u32[]{:S(2)}) collective-permute-start(f16[384,256]{1,0:T(8,128)(2,1)S(1)} %pad_maximum_fusion.8), channel_id=1, source_target_pairs={{0,3},{1,0},{2,1},{3,2},{4,7},{5,4},{6,5},{7,6},{8,11},{9,8},{10,9... | collective-permute-start | bytes 589832 | tf_op jit(solution)/shard_map/ppermute | solution.py:493
  49.8 3.5 %volume_bulk.4.bulk_ref = f32[16,16,8,256]{3,2,1,0:T(8,128)S(1)} custom-call(f32[16,16,8,256]{3,2,1,0:T(8,128)S(1)} %get-tuple-element.13.x_ref.u0_ref, f32[16,16,8,128]{3,2,1,0:T(8,128)S(1)} %broadcast_in_dim.6.mass_ref, bf16[2,128,256]{2,1,0:T(8,128)(2,1)S(1)} %get-tuple-element.10.wide_ref, bf16[2,128,128]{2,1,0:T(8,128)(2,1)S(1)} %get-tuple-element.11.narrow_ref), custom_call_target="tpu_custom_call" | custom-call | flops 805306368 | bytes 8388608 | tf_op jit(solution)/shard_map/volume_bulk/pallas_call | solution.py:140
  53.4 1.5 %collective-permute-done.9 = f16[384,256]{1,0:T(8,128)(2,1)S(1)} collective-permute-done((f16[384,256]{1,0:T(8,128)(2,1)S(1)}, f16[384,256]{1,0:T(8,128)(2,1)S(1)}, u32[]{:S(2)}, u32[]{:S(2)}) %collective-permute-start.9) | collective-permute-done | bytes 196640 | tf_op jit(solution)/shard_map/ppermute | solution.py:493
  54.9 4.2 %collective-permute-done.7 = f16[384,256]{1,0:T(8,128)(2,1)S(1)} collective-permute-done((f16[384,256]{1,0:T(8,128)(2,1)S(1)}, f16[384,256]{1,0:T(8,128)(2,1)S(1)}, u32[]{:S(2)}, u32[]{:S(2)}) %collective-permute-start.7) | collective-permute-done | bytes 196640 | tf_op jit(solution)/shard_map/ppermute | solution.py:493
  59.2 1.3 collective-permute-start.12
  60.7 1.4 %collective-permute-done.10 = f16[384,256]{1,0:T(8,128)(2,1)S(1)} collective-permute-done((f16[384,256]{1,0:T(8,128)(2,1)S(1)}, f16[384,256]{1,0:T(8,128)(2,1)S(1)}, u32[]{:S(2)}, u32[]{:S(2)}) %collective-permute-start.10) | collective-permute-done | bytes 196640 | tf_op jit(solution)/shard_map/ppermute | solution.py:524
  62.2 0.9 collective-permute-start.11
  63.1 7.2 %collective-permute-done.11 = f16[384,256]{1,0:T(8,128)(2,1)S(1)} collective-permute-done((f16[384,256]{1,0:T(8,128)(2,1)S(1)}, f16[384,256]{1,0:T(8,128)(2,1)S(1)}, u32[]{:S(2)}, u32[]{:S(2)}) %collective-permute-start.11) | collective-permute-done | bytes 196640 | tf_op jit(solution)/shard_map/ppermute | solution.py:532
  70.6 2.5 %finish_second_kernel.1 = (f32[16,16,8,256]{3,2,1,0:T(8,128)S(1)}, f32[8,16,256]{2,1,0:T(8,128)S(1)}, f32[3,8,128]{2,1,0:T(8,128)S(1)}) custom-call(f32[16,16,8,256]{3,2,1,0:T(8,128)S(1)} %volume_bulk.4.bulk_ref, f32[8,16,256]{2,1,0:T(8,128)S(1)} %bitcast.155, f32[16,8,256]{2,1,0:T(8,128)S(1)} %get-tuple-element.46.before_ref, ...), custom_call_target="tpu_custom_call" | custom-call | flops 10485760 | bytes 6291456 | tf_op jit(solution)/shard_map/finish_second_kernel/pallas_call | solution.py:264
  73.2 2.6 %bem_partial.4 = f32[4,256,256]{2,1,0:T(8,128)S(1)} custom-call(s32[9]{0:T(128)S(1)} %stack.53.place_ref, bf16[2,512,1024]{2,1,0:T(8,128)(2,1)S(1)} %copy-done.3, f32[1024,256]{1,0:T(8,128)S(1)} %convert_multiply_fusion.1.s_ref, f32[8,16,256]{2,1,0:T(8,128)S(1)} %neg.6.add_ref), custom_call_target="tpu_custom_call" | custom-call | flops 1073741824 | bytes 4194304 | tf_op jit(solution)/shard_map/bem_partial/pallas_call | solution.py:325
  76.5 2.8 %collective-permute-start.16 = (f16[384,256]{1,0:T(8,128)(2,1)S(1)}, f16[384,256]{1,0:T(8,128)(2,1)S(1)}, u32[]{:S(2)}, u32[]{:S(2)}) collective-permute-start(f16[384,256]{1,0:T(8,128)(2,1)S(1)} %pad_maximum_fusion.11), channel_id=1, source_target_pairs={{0,3},{1,0},{2,1},{3,2},{4,7},{5,4},{6,5},{7,6},{8,11},{9,8},{10,9... | collective-permute-start | bytes 589832 | tf_op jit(solution)/shard_map/ppermute | solution.py:493
  79.5 3.5 %volume_bulk.5.bulk_ref = f32[16,16,8,256]{3,2,1,0:T(8,128)S(1)} custom-call(f32[16,16,8,256]{3,2,1,0:T(8,128)S(1)} %get-tuple-element.15.x_ref.u1_ref, f32[16,16,8,128]{3,2,1,0:T(8,128)S(1)} %broadcast_in_dim.6.mass_ref, bf16[2,128,256]{2,1,0:T(8,128)(2,1)S(1)} %get-tuple-element.10.wide_ref, bf16[2,128,128]{2,1,0:T(8,128)(2,1)S(1)} %copy-done.10), custom_call_target="tpu_custom_call" | custom-call | flops 805306368 | bytes 8388608 | tf_op jit(solution)/shard_map/volume_bulk/pallas_call | solution.py:140
  83.1 1.5 %collective-permute-done.16 = f16[384,256]{1,0:T(8,128)(2,1)S(1)} collective-permute-done((f16[384,256]{1,0:T(8,128)(2,1)S(1)}, f16[384,256]{1,0:T(8,128)(2,1)S(1)}, u32[]{:S(2)}, u32[]{:S(2)}) %collective-permute-start.16) | collective-permute-done | bytes 196640 | tf_op jit(solution)/shard_map/ppermute | solution.py:493
  84.6 4.2 %collective-permute-done.14 = f16[384,256]{1,0:T(8,128)(2,1)S(1)} collective-permute-done((f16[384,256]{1,0:T(8,128)(2,1)S(1)}, f16[384,256]{1,0:T(8,128)(2,1)S(1)}, u32[]{:S(2)}, u32[]{:S(2)}) %collective-permute-start.14) | collective-permute-done | bytes 196640 | tf_op jit(solution)/shard_map/ppermute | solution.py:493
  88.9 1.2 collective-permute-start.19
  90.3 1.4 %collective-permute-done.17 = f16[384,256]{1,0:T(8,128)(2,1)S(1)} collective-permute-done((f16[384,256]{1,0:T(8,128)(2,1)S(1)}, f16[384,256]{1,0:T(8,128)(2,1)S(1)}, u32[]{:S(2)}, u32[]{:S(2)}) %collective-permute-start.17) | collective-permute-done | bytes 196640 | tf_op jit(solution)/shard_map/ppermute | solution.py:524
  91.8 1.2 collective-permute-start.18
  93.0 7.0 %collective-permute-done.18 = f16[384,256]{1,0:T(8,128)(2,1)S(1)} collective-permute-done((f16[384,256]{1,0:T(8,128)(2,1)S(1)}, f16[384,256]{1,0:T(8,128)(2,1)S(1)}, u32[]{:S(2)}, u32[]{:S(2)}) %collective-permute-start.18) | collective-permute-done | bytes 196640 | tf_op jit(solution)/shard_map/ppermute | solution.py:532
  100.2 1.4 %collective-permute-done.20 = f16[384,256]{1,0:T(8,128)(2,1)S(1)} collective-permute-done((f16[384,256]{1,0:T(8,128)(2,1)S(1)}, f16[384,256]{1,0:T(8,128)(2,1)S(1)}, u32[]{:S(2)}, u32[]{:S(2)}) %collective-permute-start.20) | collective-permute-done | bytes 196640 | tf_op jit(solution)/shard_map/ppermute | solution.py:536
  101.8 2.6 %bem_partial.5 = f32[4,256,256]{2,1,0:T(8,128)S(1)} custom-call(s32[9]{0:T(128)S(1)} %stack.53.place_ref, bf16[2,512,1024]{2,1,0:T(8,128)(2,1)S(1)} %copy-done.3, f32[1024,256]{1,0:T(8,128)S(1)} %convert_multiply_fusion.s_ref, f32[8,16,256]{2,1,0:T(8,128)S(1)} %neg.7.add_ref), custom_call_target="tpu_custom_call" | custom-call | flops 1073741824 | bytes 4194304 | tf_op jit(solution)/shard_map/bem_partial/pallas_call | solution.py:325
  104.4 1.8 %collective-permute-start.23 = (f16[128,256]{1,0:T(8,128)(2,1)S(1)}, f16[128,256]{1,0:T(8,128)(2,1)S(1)}, u32[]{:S(2)}, u32[]{:S(2)}) collective-permute-start(f16[128,256]{1,0:T(8,128)(2,1)S(1)} %get-tuple-element.35), channel_id=1, source_target_pairs={{0,3},{1,0},{2,1},{3,2},{4,7},{5,4},{6,5},{7,6},{8,11},{9,8},{10,9... | collective-permute-start | bytes 196616 | tf_op jit(solution)/shard_map/ppermute | solution.py:493
  106.2 1.5 %collective-permute-start.22 = (f16[128,256]{1,0:T(8,128)(2,1)S(1)}, f16[128,256]{1,0:T(8,128)(2,1)S(1)}, u32[]{:S(2)}, u32[]{:S(2)}) collective-permute-start(f16[128,256]{1,0:T(8,128)(2,1)S(1)} %get-tuple-element.36), channel_id=1, source_target_pairs={{0,2},{1,3},{2,0},{3,1},{4,6},{5,7},{6,4},{7,5},{8,10},{9,11},{10,... | collective-permute-start | bytes 196616 | tf_op jit(solution)/shard_map/ppermute | solution.py:493
  107.7 2.7 %finish_third_kernel.1.third_ref = f32[5,8,128]{2,1,0:T(8,128)S(1)} custom-call(f32[16,16,8,256]{3,2,1,0:T(8,128)S(1)} %volume_bulk.5.bulk_ref, f32[8,16,256]{2,1,0:T(8,128)S(1)} %bitcast.157, f32[16,8,256]{2,1,0:T(8,128)S(1)} %get-tuple-element.44.before_ref, f32[16,8,256]{2,1,0:T(8,128)S(1)} %get-tuple-element.43.beyond_ref, ...), custom_call_target="tpu_custom_call" | custom-call | flops 10485760 | bytes 8388608 | tf_op jit(solution)/shard_map/finish_third_kernel/pallas_call | solution.py:264
  110.5 2.3 %collective-permute-done.21 = f16[128,256]{1,0:T(8,128)(2,1)S(1)} collective-permute-done((f16[128,256]{1,0:T(8,128)(2,1)S(1)}, f16[128,256]{1,0:T(8,128)(2,1)S(1)}, u32[]{:S(2)}, u32[]{:S(2)}) %collective-permute-start.21) | collective-permute-done | bytes 65568 | tf_op jit(solution)/shard_map/ppermute | solution.py:493
  113.1 10.3 %all_to_all.5 = f32[32,1,1152]{2,1,0:T(1,128)S(1)} all-to-all(f32[32,1,1152]{2,1,0:T(1,128)S(1)} %broadcast_in_dim.15), channel_id=1, replica_groups=mesh['sector'=8,'slab'=4] {'sector','slab'}, dimensions={0} | all-to-all | bytes 294912 | tf_op jit(solution)/shard_map/all_to_all | solution.py:698
  123.8 1.6 %copy-done.5 = f32[16,16,8,256]{3,2,1,0:T(8,128)S(1)} copy-done((f32[16,16,8,256]{3,2,1,0:T(8,128)S(1)}, f32[16,16,8,256]{3,2,1,0:T(8,128)}, u32[]{:S(2)}) %copy-start.5) | copy-done | bytes 2097176
  125.4 3.7 %final_solution.1 = (f32[16,16,8,256]{3,2,1,0:T(8,128)}, f32[8,16,256]{2,1,0:T(8,128)}) custom-call(f32[9,32,128]{2,1,0:T(8,128)S(1)} %bitcast_bitcast_fusion.gram_ref, f32[16,16,8,256]{3,2,1,0:T(8,128)S(1)} %copy-done.5, f32[16,16,8,256]{3,2,1,0:T(8,128)S(1)} %copy-done.1, f32[16,16,8,256]{3,2,1,0:T(8,128)} %copy-done.2, f32[8,16,256]{2,1,0:T(8,128)S(1)} %copy-done.8, ...), custom_call_target="tpu_custom_call" | custom-call | flops 5242880 | bytes 8388608 | tf_op jit(solution)/shard_map/final_solution/pallas_call | solution.py:463
  (115 shorter events, 9.1 us)
Async XLA Ops:
  0.6 14.1 %copy-start.12 = (f32[3,8,8]{2,1,0:T(8,128)S(1)}, f32[3,8,8]{2,1,0:T(8,128)}, u32[]{:S(2)}) copy-start(f32[3,8,8]{2,1,0:T(8,128)} %stiffness_ref.1) | copy-start | bytes 2308
  0.6 15.2 %copy-start.13 = (f32[8,16,256]{2,1,0:T(8,128)S(1)}, f32[8,16,256]{2,1,0:T(8,128)}, u32[]{:S(2)}) copy-start(f32[8,16,256]{2,1,0:T(8,128)} %param.8) | copy-start | bytes 393220
  0.7 17.1 %copy-start.4 = (f32[16,16,8,256]{3,2,1,0:T(8,128)S(1)}, f32[16,16,8,256]{3,2,1,0:T(8,128)}, u32[]{:S(2)}) copy-start(f32[16,16,8,256]{3,2,1,0:T(8,128)} %x_ref.3) | copy-start | bytes 6291460
  3.9 18.9 %collective-permute-start.2 = (f16[160,256]{1,0:T(8,128)(2,1)}, f16[160,256]{1,0:T(8,128)(2,1)}, u32[]{:S(2)}, u32[]{:S(2)}) collective-permute-start(f16[160,256]{1,0:T(8,128)(2,1)} %pad_maximum_fusion.15), channel_id=1, source_target_pairs={{0,3},{1,0},{2,1},{3,2},{4,7},{5,4},{6,5},{7,6},{8,11},{9,8},{10,9... | collective-permute-start | bytes 245768 | tf_op jit(solution)/shard_map/ppermute | solution.py:493
  7.8 14.9 %collective-permute-start.1 = (f16[32,256]{1,0:T(8,128)(2,1)S(1)}, f16[32,256]{1,0:T(8,128)(2,1)S(1)}, u32[]{:S(2)}, u32[]{:S(2)}) collective-permute-start(f16[32,256]{1,0:T(8,128)(2,1)S(1)} %bitcast.170), channel_id=1, source_target_pairs={{0,2},{1,3},{2,0},{3,1},{4,6},{5,7},{6,4},{7,5},{8,10},{9,11},{10,... | collective-permute-start | bytes 49160 | tf_op jit(solution)/shard_map/ppermute | solution.py:493
  9.0 14.7 %collective-permute-start = (f16[160,256]{1,0:T(8,128)(2,1)}, f16[160,256]{1,0:T(8,128)(2,1)}, u32[]{:S(2)}, u32[]{:S(2)}) collective-permute-start(f16[160,256]{1,0:T(8,128)(2,1)} %pad_maximum_fusion.14), channel_id=1, source_target_pairs={{0,1},{1,2},{2,3},{3,0},{4,5},{5,6},{6,7},{7,4},{8,9},{9,10},{10,1... | collective-permute-start | bytes 245768 | tf_op jit(solution)/shard_map/ppermute | solution.py:493
  15.8 34.0 %copy-start.9 = (bf16[2,128,128]{2,1,0:T(8,128)(2,1)}, bf16[2,128,128]{2,1,0:T(8,128)(2,1)S(1)}, u32[]{:S(2)}) copy-start(bf16[2,128,128]{2,1,0:T(8,128)(2,1)S(1)} %get-tuple-element.11.narrow_ref) | copy-start | bytes 196612
  21.4 1.3 %copy-start.6 = (f32[16,16,8,256]{3,2,1,0:T(8,128)}, f32[16,16,8,256]{3,2,1,0:T(8,128)S(1)}, u32[]{:S(2)}) copy-start(f32[16,16,8,256]{3,2,1,0:T(8,128)S(1)} %volume_bulk.3.bulk_ref) | copy-start | bytes 6291460
  22.7 15.6 %copy-start.8 = (f32[8,16,256]{2,1,0:T(8,128)S(1)}, f32[8,16,256]{2,1,0:T(8,128)}, u32[]{:S(2)}) copy-start(f32[8,16,256]{2,1,0:T(8,128)} %s_ref.3) | copy-start | bytes 393220
  22.8 15.5 %copy-start.7 = (f32[16,16,8,256]{3,2,1,0:T(8,128)S(1)}, f32[16,16,8,256]{3,2,1,0:T(8,128)}, u32[]{:S(2)}) copy-start(f32[16,16,8,256]{3,2,1,0:T(8,128)} %copy-done.6) | copy-start | bytes 6291460
  25.2 12.9 %collective-permute-start.5 = (f16[128,256]{1,0:T(8,128)(2,1)S(1)}, f16[128,256]{1,0:T(8,128)(2,1)S(1)}, u32[]{:S(2)}, u32[]{:S(2)}) collective-permute-start(f16[128,256]{1,0:T(8,128)(2,1)S(1)} %bitcast.162), channel_id=1, source_target_pairs={{0,16},{4,20},{8,24},{12,28},{16,0},{20,4},{24,8},{28,12},{1,17},{... | collective-permute-start | bytes 196616 | tf_op jit(solution)/shard_map/ppermute | solution.py:523
  28.8 1.5 %collective-permute-start.3 = (f16[384,256]{1,0:T(8,128)(2,1)S(1)}, f16[384,256]{1,0:T(8,128)(2,1)S(1)}, u32[]{:S(2)}, u32[]{:S(2)}) collective-permute-start(f16[384,256]{1,0:T(8,128)(2,1)S(1)} %fusion.17), channel_id=1, source_target_pairs={{0,4},{4,0},{8,12},{12,8},{16,20},{20,16},{24,28},{28,24},{1,5},{5... | collective-permute-start | bytes 589832 | tf_op jit(solution)/shard_map/ppermute | solution.py:524
  30.4 7.6 %collective-permute-start.4 = (f16[384,256]{1,0:T(8,128)(2,1)S(1)}, f16[384,256]{1,0:T(8,128)(2,1)S(1)}, u32[]{:S(2)}, u32[]{:S(2)}) collective-permute-start(f16[384,256]{1,0:T(8,128)(2,1)S(1)} %fusion.16), channel_id=1, source_target_pairs={{0,8},{4,28},{8,16},{12,4},{16,24},{20,12},{24,0},{28,20},{1,9},{5... | collective-permute-start | bytes 589832 | tf_op jit(solution)/shard_map/ppermute | solution.py:532
  38.2 2.5 %collective-permute-start.6 = (f16[384,256]{1,0:T(8,128)(2,1)S(1)}, f16[384,256]{1,0:T(8,128)(2,1)S(1)}, u32[]{:S(2)}, u32[]{:S(2)}) collective-permute-start(f16[384,256]{1,0:T(8,128)(2,1)S(1)} %pad_maximum_fusion.6), channel_id=1, source_target_pairs={{0,4},{4,0},{8,12},{12,8},{16,20},{20,16},{24,28},{28,24},{1,5},{5... | collective-permute-start | bytes 589832 | tf_op jit(solution)/shard_map/ppermute | solution.py:536
  40.6 9.2 %copy-start = (f32[16,16,8,256]{3,2,1,0:T(8,128)}, f32[16,16,8,256]{3,2,1,0:T(8,128)S(1)}, u32[]{:S(2)}) copy-start(f32[16,16,8,256]{3,2,1,0:T(8,128)S(1)} %get-tuple-element.13.x_ref.u0_ref) | copy-start | bytes 6291460
  40.6 2.4 %copy-start.3 = (bf16[2,512,1024]{2,1,0:T(8,128)(2,1)S(1)}, bf16[2,512,1024]{2,1,0:T(8,128)(2,1)}, u32[]{:S(2)}) copy-start(bf16[2,512,1024]{2,1,0:T(8,128)(2,1)} %m_ref.5) | copy-start | bytes 6291460
  40.6 2.3 %copy-start.11 = (f32[8,16,256]{2,1,0:T(8,128)S(1)}, f32[8,16,256]{2,1,0:T(8,128)}, u32[]{:S(2)}) copy-start(f32[8,16,256]{2,1,0:T(8,128)} %fusion.34.add_ref) | copy-start | bytes 393220
  45.6 7.8 %collective-permute-start.8 = (f16[256,256]{1,0:T(8,128)(2,1)S(1)}, f16[256,256]{1,0:T(8,128)(2,1)S(1)}, u32[]{:S(2)}, u32[]{:S(2)}) collective-permute-start(f16[256,256]{1,0:T(8,128)(2,1)S(1)} %get-tuple-element.42), channel_id=1, source_target_pairs={{0,2},{1,3},{2,0},{3,1},{4,6},{5,7},{6,4},{7,5},{8,10},{9,11},{10,... | collective-permute-start | bytes 393224 | tf_op jit(solution)/shard_map/ppermute | solution.py:493
  46.6 8.3 %collective-permute-start.9 = (f16[384,256]{1,0:T(8,128)(2,1)S(1)}, f16[384,256]{1,0:T(8,128)(2,1)S(1)}, u32[]{:S(2)}, u32[]{:S(2)}) collective-permute-start(f16[384,256]{1,0:T(8,128)(2,1)S(1)} %pad_maximum_fusion.8), channel_id=1, source_target_pairs={{0,3},{1,0},{2,1},{3,2},{4,7},{5,4},{6,5},{7,6},{8,11},{9,8},{10,9... | collective-permute-start | bytes 589832 | tf_op jit(solution)/shard_map/ppermute | solution.py:493
  49.7 9.4 %collective-permute-start.7 = (f16[384,256]{1,0:T(8,128)(2,1)S(1)}, f16[384,256]{1,0:T(8,128)(2,1)S(1)}, u32[]{:S(2)}, u32[]{:S(2)}) collective-permute-start(f16[384,256]{1,0:T(8,128)(2,1)S(1)} %pad_maximum_fusion.7), channel_id=1, source_target_pairs={{0,1},{1,2},{2,3},{3,0},{4,5},{5,6},{6,7},{7,4},{8,9},{9,10},{10,1... | collective-permute-start | bytes 589832 | tf_op jit(solution)/shard_map/ppermute | solution.py:493
  59.2 11.1 %collective-permute-start.12 = (f16[128,256]{1,0:T(8,128)(2,1)S(1)}, f16[128,256]{1,0:T(8,128)(2,1)S(1)}, u32[]{:S(2)}, u32[]{:S(2)}) collective-permute-start(f16[128,256]{1,0:T(8,128)(2,1)S(1)} %get-tuple-element.21), channel_id=1, source_target_pairs={{0,16},{4,20},{8,24},{12,28},{16,0},{20,4},{24,8},{28,12},{1,17},{... | collective-permute-start | bytes 196616 | tf_op jit(solution)/shard_map/ppermute | solution.py:523
  60.6 1.5 %collective-permute-start.10 = (f16[384,256]{1,0:T(8,128)(2,1)S(1)}, f16[384,256]{1,0:T(8,128)(2,1)S(1)}, u32[]{:S(2)}, u32[]{:S(2)}) collective-permute-start(f16[384,256]{1,0:T(8,128)(2,1)S(1)} %fusion.15), channel_id=1, source_target_pairs={{0,4},{4,0},{8,12},{12,8},{16,20},{20,16},{24,28},{28,24},{1,5},{5... | collective-permute-start | bytes 589832 | tf_op jit(solution)/shard_map/ppermute | solution.py:524
  62.2 8.1 %collective-permute-start.11 = (f16[384,256]{1,0:T(8,128)(2,1)S(1)}, f16[384,256]{1,0:T(8,128)(2,1)S(1)}, u32[]{:S(2)}, u32[]{:S(2)}) collective-permute-start(f16[384,256]{1,0:T(8,128)(2,1)S(1)} %fusion.14), channel_id=1, source_target_pairs={{0,8},{4,28},{8,16},{12,4},{16,24},{20,12},{24,0},{28,20},{1,9},{5... | collective-permute-start | bytes 589832 | tf_op jit(solution)/shard_map/ppermute | solution.py:532
  70.4 2.7 %collective-permute-start.13 = (f16[384,256]{1,0:T(8,128)(2,1)S(1)}, f16[384,256]{1,0:T(8,128)(2,1)S(1)}, u32[]{:S(2)}, u32[]{:S(2)}) collective-permute-start(f16[384,256]{1,0:T(8,128)(2,1)S(1)} %pad_maximum_fusion.9), channel_id=1, source_target_pairs={{0,4},{4,0},{8,12},{12,8},{16,20},{20,16},{24,28},{28,24},{1,5},{5... | collective-permute-start | bytes 589832 | tf_op jit(solution)/shard_map/ppermute | solution.py:536
  73.0 6.5 %copy-start.2 = (f32[16,16,8,256]{3,2,1,0:T(8,128)}, f32[16,16,8,256]{3,2,1,0:T(8,128)S(1)}, u32[]{:S(2)}) copy-start(f32[16,16,8,256]{3,2,1,0:T(8,128)S(1)} %get-tuple-element.15.x_ref.u1_ref) | copy-start | bytes 6291460
  75.8 3.7 %copy-start.10 = (bf16[2,128,128]{2,1,0:T(8,128)(2,1)S(1)}, bf16[2,128,128]{2,1,0:T(8,128)(2,1)}, u32[]{:S(2)}) copy-start(bf16[2,128,128]{2,1,0:T(8,128)(2,1)} %copy-done.9) | copy-start | bytes 196612
  75.9 7.2 %collective-permute-start.15 = (f16[256,256]{1,0:T(8,128)(2,1)S(1)}, f16[256,256]{1,0:T(8,128)(2,1)S(1)}, u32[]{:S(2)}, u32[]{:S(2)}) collective-permute-start(f16[256,256]{1,0:T(8,128)(2,1)S(1)} %get-tuple-element.39), channel_id=1, source_target_pairs={{0,2},{1,3},{2,0},{3,1},{4,6},{5,7},{6,4},{7,5},{8,10},{9,11},{10,... | collective-permute-start | bytes 393224 | tf_op jit(solution)/shard_map/ppermute | solution.py:493
  76.5 8.1 %collective-permute-start.16 = (f16[384,256]{1,0:T(8,128)(2,1)S(1)}, f16[384,256]{1,0:T(8,128)(2,1)S(1)}, u32[]{:S(2)}, u32[]{:S(2)}) collective-permute-start(f16[384,256]{1,0:T(8,128)(2,1)S(1)} %pad_maximum_fusion.11), channel_id=1, source_target_pairs={{0,3},{1,0},{2,1},{3,2},{4,7},{5,4},{6,5},{7,6},{8,11},{9,8},{10,9... | collective-permute-start | bytes 589832 | tf_op jit(solution)/shard_map/ppermute | solution.py:493
  79.4 9.4 %collective-permute-start.14 = (f16[384,256]{1,0:T(8,128)(2,1)S(1)}, f16[384,256]{1,0:T(8,128)(2,1)S(1)}, u32[]{:S(2)}, u32[]{:S(2)}) collective-permute-start(f16[384,256]{1,0:T(8,128)(2,1)S(1)} %pad_maximum_fusion.10), channel_id=1, source_target_pairs={{0,1},{1,2},{2,3},{3,0},{4,5},{5,6},{6,7},{7,4},{8,9},{9,10},{10,1... | collective-permute-start | bytes 589832 | tf_op jit(solution)/shard_map/ppermute | solution.py:493
  88.9 11.1 %collective-permute-start.19 = (f16[128,256]{1,0:T(8,128)(2,1)S(1)}, f16[128,256]{1,0:T(8,128)(2,1)S(1)}, u32[]{:S(2)}, u32[]{:S(2)}) collective-permute-start(f16[128,256]{1,0:T(8,128)(2,1)S(1)} %get-tuple-element.19), channel_id=1, source_target_pairs={{0,16},{4,20},{8,24},{12,28},{16,0},{20,4},{24,8},{28,12},{1,17},{... | collective-permute-start | bytes 196616 | tf_op jit(solution)/shard_map/ppermute | solution.py:523
  90.2 1.5 %collective-permute-start.17 = (f16[384,256]{1,0:T(8,128)(2,1)S(1)}, f16[384,256]{1,0:T(8,128)(2,1)S(1)}, u32[]{:S(2)}, u32[]{:S(2)}) collective-permute-start(f16[384,256]{1,0:T(8,128)(2,1)S(1)} %fusion.13), channel_id=1, source_target_pairs={{0,4},{4,0},{8,12},{12,8},{16,20},{20,16},{24,28},{28,24},{1,5},{5... | collective-permute-start | bytes 589832 | tf_op jit(solution)/shard_map/ppermute | solution.py:524
  91.8 8.2 %collective-permute-start.18 = (f16[384,256]{1,0:T(8,128)(2,1)S(1)}, f16[384,256]{1,0:T(8,128)(2,1)S(1)}, u32[]{:S(2)}, u32[]{:S(2)}) collective-permute-start(f16[384,256]{1,0:T(8,128)(2,1)S(1)} %fusion.12), channel_id=1, source_target_pairs={{0,8},{4,28},{8,16},{12,4},{16,24},{20,12},{24,0},{28,20},{1,9},{5... | collective-permute-start | bytes 589832 | tf_op jit(solution)/shard_map/ppermute | solution.py:532
  100.1 1.5 %collective-permute-start.20 = (f16[384,256]{1,0:T(8,128)(2,1)S(1)}, f16[384,256]{1,0:T(8,128)(2,1)S(1)}, u32[]{:S(2)}, u32[]{:S(2)}) collective-permute-start(f16[384,256]{1,0:T(8,128)(2,1)S(1)} %pad_maximum_fusion.12), channel_id=1, source_target_pairs={{0,4},{4,0},{8,12},{12,8},{16,20},{20,16},{24,28},{28,24},{1,5},{5... | collective-permute-start | bytes 589832 | tf_op jit(solution)/shard_map/ppermute | solution.py:536
  101.8 6.0 %copy-start.1 = (f32[16,16,8,256]{3,2,1,0:T(8,128)S(1)}, f32[16,16,8,256]{3,2,1,0:T(8,128)}, u32[]{:S(2)}) copy-start(f32[16,16,8,256]{3,2,1,0:T(8,128)} %copy-done) | copy-start | bytes 6291460
  104.4 6.1 %collective-permute-start.23 = (f16[128,256]{1,0:T(8,128)(2,1)S(1)}, f16[128,256]{1,0:T(8,128)(2,1)S(1)}, u32[]{:S(2)}, u32[]{:S(2)}) collective-permute-start(f16[128,256]{1,0:T(8,128)(2,1)S(1)} %get-tuple-element.35), channel_id=1, source_target_pairs={{0,3},{1,0},{2,1},{3,2},{4,7},{5,4},{6,5},{7,6},{8,11},{9,8},{10,9... | collective-permute-start | bytes 196616 | tf_op jit(solution)/shard_map/ppermute | solution.py:493
  106.2 4.3 %collective-permute-start.22 = (f16[128,256]{1,0:T(8,128)(2,1)S(1)}, f16[128,256]{1,0:T(8,128)(2,1)S(1)}, u32[]{:S(2)}, u32[]{:S(2)}) collective-permute-start(f16[128,256]{1,0:T(8,128)(2,1)S(1)} %get-tuple-element.36), channel_id=1, source_target_pairs={{0,2},{1,3},{2,0},{3,1},{4,6},{5,7},{6,4},{7,5},{8,10},{9,11},{10,... | collective-permute-start | bytes 196616 | tf_op jit(solution)/shard_map/ppermute | solution.py:493
  107.7 5.2 %collective-permute-start.21 = (f16[128,256]{1,0:T(8,128)(2,1)S(1)}, f16[128,256]{1,0:T(8,128)(2,1)S(1)}, u32[]{:S(2)}, u32[]{:S(2)}) collective-permute-start(f16[128,256]{1,0:T(8,128)(2,1)S(1)} %get-tuple-element.34), channel_id=1, source_target_pairs={{0,1},{1,2},{2,3},{3,0},{4,5},{5,6},{6,7},{7,4},{8,9},{9,10},{10,1... | collective-permute-start | bytes 196616 | tf_op jit(solution)/shard_map/ppermute | solution.py:493
  123.8 1.6 %copy-start.5 = (f32[16,16,8,256]{3,2,1,0:T(8,128)S(1)}, f32[16,16,8,256]{3,2,1,0:T(8,128)}, u32[]{:S(2)}) copy-start(f32[16,16,8,256]{3,2,1,0:T(8,128)} %x_ref.3) | copy-start | bytes 6291460
where the time goes:
time: 130 us; the launch traced here: 129 us
  waiting for transfers between devices  37.9 us (29%)
  Pallas kernels  30.7 us (24%)
  starting transfers between devices  25.1 us (19%)
  other arithmetic  13.3 us (10%)
  local copies, waits for them, and re-layouts  10.3 us (8%)
  blocking collectives  10.3 us (8%)
  between operations  1.46 us (1%)
    ppermute x3, waiting for transfers between devices, sector_gather(): arrived.append(lax.ppermute(message, 'sector', up_down(shift)))  19.3 us
    ppermute x12, starting transfers between devices, slab_exchange(): lax.ppermute(messages[shift], 'slab', shift_perm(slabs, shift))  15.7 us
    ppermute x12, waiting for transfers between devices, slab_exchange(): lax.ppermute(messages[shift], 'slab', shift_perm(slabs, shift))  13.8 us
    pallas_call x3, Pallas kernels, volume_bulk(): call(bulk_kernel, shape(*x.shape), 0, 4, flops=2 * 2 * 3 * x.size * rows,...  10.6 us
    all_to_all x1, blocking collectives, per_device(): lax.all_to_all(copies, ('sector', 'slab'), split_axis=0, concat_axis=0, t...  10.3 us
    pallas_call x3, Pallas kernels, bem_partial(): call(functools.partial(bem_kernel, sign, chunk), shape(slabs, 2 * chunk,...  7.68 us
    pallas_call x3, Pallas kernels, finish(): call(kernel, outs, 0, 6 + len(others), flops=20 * bulk.size, bytes_access...  7.44 us
    unnamed x34, local copies, waits for them, and re-layouts  6.75 us
  transfers between devices with their start and end apart: 24, of which 12 were waited for; matrix products, arithmetic and copies ran while one was open for 10% of the time, Pallas kernels for 15%

commit v1 on v0

--- a/solution.py
+++ b/solution.py
@@ -15,24 +15,35 @@
 WIRE = jnp.float16
 LANES = 256
 HALF = 128
-VMEM_LIMIT = 48 * 1024 * 1024
+VMEM_LIMIT = 8 * 1024 * 1024
 WHOLE = pl.BlockSpec(memory_space=pltpu.VMEM)
 SCALARS = pl.BlockSpec(memory_space=pltpu.SMEM)
-
-
-def call(kernel, out_shape, n_scalars, n_arrays, scratch=(), flops=0, bytes_accessed=0, name=None):
-    return pl.pallas_call(
-        kernel,
+ANYWHERE = pl.BlockSpec(memory_space=pl.ANY)
+
+
+def call(
+    kernel, out_shape, n_scalars, n_arrays, scratch=(), flops=0, bytes_accessed=0, name=None,
+    after=(), out_specs=None, aliases=None,
+):
+    n_read = n_scalars + n_arrays
+
+    def body(*refs):
+        kernel(*refs[:n_read], *refs[n_read + len(after) :])
+
+    called = pl.pallas_call(
+        body,
         out_shape=out_shape,
-        in_specs=[SCALARS] * n_scalars + [WHOLE] * n_arrays,
-        out_specs=jax.tree.map(lambda _: WHOLE, out_shape),
+        in_specs=[SCALARS] * n_scalars + [WHOLE] * n_arrays + [ANYWHERE] * len(after),
+        out_specs=out_specs or jax.tree.map(lambda _: WHOLE, out_shape),
         scratch_shapes=list(scratch),
+        input_output_aliases=aliases or {},
         compiler_params=pltpu.CompilerParams(vmem_limit_bytes=VMEM_LIMIT),
         cost_estimate=pl.CostEstimate(
             flops=flops, bytes_accessed=bytes_accessed, transcendentals=0
         ),
         name=name,
     )
+    return lambda *args: called(*args, *after)
 
 
 def shape(*dims):
@@ -106,7 +117,7 @@
     )(stiffness)
 
 
-def bulk_kernel(x_ref, mass_ref, wide_ref, narrow_ref, y_ref):
+def bulk_kernel(x_ref, mass_ref, wide_ref, narrow_ref, y_ref, *face_refs):
     n_theta, n_axial, radial, lanes = x_ref.shape
 
     def product(index, values):
@@ -133,18 +144,24 @@
 
     lax.fori_loop(0, n_axial, along_theta, 0, unroll=2)
     lax.fori_loop(0, n_theta, along_axial, 0, unroll=2)
-
-
-def volume_bulk(x, mass, wide, narrow):
-    rows = x.shape[1] * x.shape[2]
+    for face_ref in face_refs:
+        put_faces(x_ref, face_ref)
+
+
+def volume_bulk(x, mass, wide, narrow, with_face=False, after=()):
+    n_theta, n_axial, radial, lanes = x.shape
+    outs = (shape(*x.shape),)
+    if with_face:
+        outs = outs + (shape(n_theta // 2, n_axial, lanes),)
     return call(
         bulk_kernel,
-        shape(*x.shape),
+        outs,
         0,
         4,
-        flops=2 * 2 * 3 * x.size * rows,
+        flops=2 * 2 * 3 * x.size * n_axial * radial,
         bytes_accessed=16 * x.size,
         name="volume_bulk",
+        after=after,
     )(x, mass, wide, narrow)
 
 
@@ -236,7 +253,8 @@
 
 
 def finish_third_kernel(
-    bulk_ref, s_ref, before_ref, beyond_ref, ax_before_ref, ax_beyond_ref, u0_ref, u1_ref, sums_ref
+    bulk_ref, s_ref, before_ref, beyond_ref, ax_before_ref, ax_beyond_ref, u0_ref, u1_ref,
+    x_ref, sums_ref, *passed_refs,
 ):
     n_theta = bulk_ref.shape[0]
     sums_ref[...] = jnp.zeros_like(sums_ref)
@@ -256,11 +274,15 @@
     over_rows(n_theta, body)
 
 
-def finish(kernel, n_sums, with_result, bulk, s, halos, *others):
+def finish(kernel, n_sums, with_result, bulk, s, halos, *others, after=()):
     n_theta, n_axial, radial, lanes = bulk.shape
     outs = (shape(n_sums, radial, HALF),)
+    aliases = {}
     if with_result:
         outs = (shape(*bulk.shape), shape(n_theta // 2, n_axial, lanes)) + outs
+    else:
+        outs = outs + (shape(*bulk.shape),) * len(others)
+        aliases = {6 + index: 1 + index for index in range(len(others))}
     return call(
         kernel,
         outs,
@@ -269,21 +291,42 @@
         flops=20 * bulk.size,
         bytes_accessed=4 * bulk.size * (2 + len(others)),
         name=kernel.__name__,
+        after=after,
+        aliases=aliases,
     )(bulk, s, *halos, *others)
 
 
-def bem_kernel(sign, chunk, place_ref, m_ref, s_ref, add_ref, out_ref, upper_ref, lower_ref, p_ref):
-    pairs, n_axial, lanes = add_ref.shape
+def bem_kernel(sign, behind, place_ref, m_ref, face_ref, *rest):
+    n_pieces = m_ref.shape[2] // (out_chunk := rest[-4].shape[1] // 2)
+    s_refs, rhs_refs = rest[:n_pieces], rest[n_pieces:-4]
+    out_ref, upper_ref, lower_ref, p_ref = rest[-4:]
+    pairs, n_axial, lanes = face_ref.shape
     slabs = out_ref.shape[0]
     axial_all = p_ref.shape[1]
-    columns = s_ref.shape[0]
     rows = m_ref.shape[1]
-    for piece in range(columns // chunk):
-        values = s_ref[piece * chunk : (piece + 1) * chunk, :]
-        upper, lower = split_bf16(values)
-        at = pl.ds(pl.multiple_of(place_ref[1 + piece], chunk), chunk)
+    slab = place_ref[0]
+    turns = pairs // slabs
+
+    def place_rows(s_ref, first, count, start):
+        upper, lower = split_bf16(s_ref[first : first + count, :])
+        at = pl.ds(pl.multiple_of(start, count), count)
         upper_ref[at, :] = upper
         lower_ref[at, :] = lower
+
+    for which, s_ref in enumerate(s_refs):
+        start = place_ref[1 + which]
+        if not behind:
+            place_rows(s_ref, 0, out_chunk, start)
+            continue
+        for distance in range(slabs):
+            source = lax.rem(slab - distance + slabs, slabs)
+            for turn in range(turns):
+                place_rows(
+                    s_ref,
+                    (distance * turns + turn) * n_axial,
+                    n_axial,
+                    start + turn * axial_all + source * n_axial,
+                )
 
     step = 2 * axial_all if axial_all < 128 else axial_all
 
@@ -304,29 +347,32 @@
         return carry
 
     lax.fori_loop(0, rows // step, block, 0)
-    slab = place_ref[0]
     own = pl.ds(pl.multiple_of(slab * n_axial, n_axial), n_axial)
-    p_ref[:, own, :] += add_ref[...]
+    add = -sign * face_ref[...]
+    for rhs_ref in rhs_refs:
+        add = add + rhs_ref[...]
+    p_ref[:, own, :] += add
     for shift in range(slabs):
         target = lax.rem(slab + shift, slabs)
-        for turn in range(pairs // slabs):
+        for turn in range(turns):
             out_ref[shift, turn * axial_all : (turn + 1) * axial_all, :] = p_ref[
                 target + turn * slabs
             ]
         there = pl.ds(pl.multiple_of(target * n_axial, n_axial), n_axial)
-        out_ref[shift, chunk:, :] = p_ref[:, there, :].reshape(pairs * n_axial, lanes)
-
-
-def bem_partial(sign, place, matrix, gathered, add, slabs):
-    pairs, n_axial, lanes = add.shape
-    axial_all = n_axial * slabs
-    chunk = pairs // slabs * axial_all
+        out_ref[shift, out_chunk:, :] = p_ref[:, there, :].reshape(out_chunk, lanes)
+
+
+def bem_partial(sign, behind, place, matrix, face, gathered, *rhs, after=()):
+    pairs, n_axial, lanes = face.shape
+    chunk = gathered[0].shape[0]
     rows, columns = matrix.shape[1:]
+    axial_all = rows // pairs
+    slabs = axial_all // n_axial
     return call(
-        functools.partial(bem_kernel, sign, chunk),
+        functools.partial(bem_kernel, sign, behind),
         shape(slabs, 2 * chunk, lanes),
         1,
-        3,
+        2 + len(gathered) + len(rhs),
         scratch=[
             pltpu.VMEM((columns, lanes), BF16),
             pltpu.VMEM((columns, lanes), BF16),
@@ -335,7 +381,8 @@
         flops=2 * 4 * rows * columns * lanes,
         bytes_accessed=4 * rows * columns + 4 * columns * lanes + 8 * chunk * slabs * lanes,
         name="bem_partial",
-    )(place, matrix, gathered, add)
+        after=after,
+    )(place, matrix, face, *gathered, *rhs)
 
 
 def surface_sums(u0, u1, u2):
@@ -442,21 +489,28 @@
 
 
 def solution_kernel(
-    gram_ref, x_ref, u0_ref, u1_ref, s_ref, s0_ref, s1_ref, volume_ref, surface_ref
+    gram_ref, x_ref, u0_ref, u1_ref, s_ref, s0_ref, s1_ref,
+    volume_ref, surface_ref, row_ref, copied,
 ):
-    rows = [jnp.sum(gram_ref[row], axis=0, keepdims=True) for row in range(9)]
-    first, second = coefficients(rows)
+    sums = [jnp.sum(gram_ref[row], axis=0, keepdims=True) for row in range(9)]
+    first, second = coefficients(sums)
+    n_theta = x_ref.shape[0]
+
+    def copy(a):
+        return pltpu.make_async_copy(row_ref.at[a], volume_ref.at[a], copied.at[a])
+
+    def body(a, carry):
+        real, imag = combine(first, second, x_ref[a], u0_ref[a], u1_ref[a])
+        row_ref[a, :, :, :HALF] = real
+        row_ref[a, :, :, HALF:] = imag
+        copy(a).start()
+        return carry
+
+    lax.fori_loop(0, n_theta, body, 0)
     real, imag = combine(first, second, s_ref[...], s0_ref[...], s1_ref[...])
     surface_ref[..., :HALF] = real
     surface_ref[..., HALF:] = imag
-
-    def body(a, carry):
-        real, imag = combine(first, second, x_ref[a], u0_ref[a], u1_ref[a])
-        volume_ref[a, :, :, :HALF] = real
-        volume_ref[a, :, :, HALF:] = imag
-        return carry
-
-    lax.fori_loop(0, x_ref.shape[0], body, 0)
+    lax.fori_loop(0, n_theta, lambda a, carry: (copy(a).wait(), carry)[1], 0)
 
 
 def final_solution(gram_all, x, u0, u1, s, s0, s1):
@@ -465,9 +519,11 @@
         (shape(*x.shape), shape(*s.shape)),
         0,
         7,
+        scratch=[pltpu.VMEM(x.shape, F32), pltpu.SemaphoreType.DMA((x.shape[0],))],
         flops=10 * x.size,
         bytes_accessed=16 * x.size,
         name="final_solution",
+        out_specs=(ANYWHERE, WHOLE),
     )(gram_all, x, u0, u1, s, s0, s1)
 
 
@@ -495,98 +551,51 @@
     ]
 
 
-def axial_halos(received_first, received_last, scale, tail):
+def halo_exchange(volume, scale):
+    def both_ways(axis, first, last):
+        peers = lax.axis_size(axis)
+        before = lax.ppermute(to_wire(last, scale), axis, shift_perm(peers, 1))
+        beyond = lax.ppermute(to_wire(first, scale), axis, shift_perm(peers, -1))
+        return from_wire(before, scale), from_wire(beyond, scale)
+
+    theta = both_ways("sector", volume[0], volume[-1])
+    before, beyond = both_ways("slab", volume[:, 0], volume[:, -1])
     slab, slabs = lax.axis_index("slab"), lax.axis_size("slab")
-    before = from_wire(received_first[-tail:], scale) * (slab > 0).astype(F32)
-    beyond = from_wire(received_last[-tail:], scale) * (slab < slabs - 1).astype(F32)
-    return before, beyond
-
-
-def sector_gather(values, scale, layers, layer_scale):
+    return theta + (
+        jnp.where(slab > 0, before, 0.0),
+        jnp.where(slab < slabs - 1, beyond, 0.0),
+    )
+
+
+def sector_gather(own, scale):
     sectors = lax.axis_size("sector")
-    chips = sectors // 2
-    core = lax.rem(lax.axis_index("sector"), 2)
-    chunk = values.shape[0]
-    tail = layers[0].shape[0]
-    own = to_wire(values, scale)
-    first, last = (to_wire(layer, layer_scale) for layer in layers)
     sibling = [(i, i ^ 1) for i in range(sectors)]
-
-    def up_down(shift):
-        pairs = []
-        for i in range(sectors):
-            chip, c = i // 2, i % 2
-            pairs.append((i, (chip + (shift if c == 0 else -shift)) % chips * 2 + c))
-        return pairs
-
-    half = [(i, (i + sectors // 2) % sectors) for i in range(sectors)]
-    from_half = lax.ppermute(own, "sector", half)
-    beside = lax.ppermute(jnp.concatenate([own, first, last]), "sector", sibling)
-    beside_first, beside_last = beside[chunk : chunk + tail], beside[chunk + tail :]
-    far = jnp.where(core == 0, beside_last, beside_first)
-    near = jnp.where(core == 0, beside_first, beside_last)
-    both = jnp.concatenate([own, beside[:chunk]])
-    arrived = []
-    for shift in range(1, chips // 2):
-        message = jnp.concatenate([both, far]) if shift == 1 else both
-        arrived.append(lax.ppermute(message, "sector", up_down(shift)))
-    far_halo = arrived[0][2 * chunk :]
-    arrived = [message[: 2 * chunk] for message in arrived]
-    here = jnp.concatenate(arrived + [from_half])
-    there = lax.ppermute(here, "sector", sibling)
-    gathered = from_wire(jnp.concatenate([both, here, there]), scale)
-    before = from_wire(jnp.where(core == 0, far_halo, near), layer_scale)
-    beyond = from_wire(jnp.where(core == 0, near, far_halo), layer_scale)
-    return gathered, (before, beyond)
+    shares = [own]
+    for shift in range(1, sectors // 2):
+        shares.append(lax.ppermute(own, "sector", shift_perm(sectors, 2 * shift)))
+    gathered = []
+    for share in shares:
+        gathered += [share, lax.ppermute(share, "sector", sibling)]
+    return [from_wire(share, scale) for share in gathered]
 
 
 def gather_places(chunk):
     sectors = lax.axis_size("sector")
-    chips = sectors // 2
     sector = lax.axis_index("sector")
-    chip, core = sector // 2, lax.rem(sector, 2)
-
-    def place(chip_shift, other):
-        source = lax.rem(chip + chip_shift + 2 * chips, chips)
-        return (2 * source + jnp.where(other, 1 - core, core)) * chunk
-
-    up = jnp.where(core == 0, -1, 1)
-    places = [lax.axis_index("slab"), place(0, False), place(0, True)]
-    for mirrored in (False, True):
-        sign = -1 if mirrored else 1
-        for shift in range(1, chips // 2):
-            places.append(place(sign * up * shift, mirrored))
-            places.append(place(sign * up * shift, not mirrored))
-        places.append(place(chips // 2, mirrored))
+    places = [lax.axis_index("slab")]
+    for shift in range(sectors // 2):
+        source = lax.rem(sector - 2 * shift + sectors, sectors)
+        places += [source * chunk, (source + 1 - 2 * lax.rem(source, 2)) * chunk]
     return jnp.stack([jnp.asarray(value, jnp.int32) for value in places])
 
 
-def edge_rows(volume):
-    lanes = volume.shape[-1]
-    theta = (volume[0].reshape(-1, lanes), volume[-1].reshape(-1, lanes))
-    axial = (volume[:, 0].reshape(-1, lanes), volume[:, -1].reshape(-1, lanes))
-    return theta, axial
-
-
-def scatter_sum(parts, scale, axial, layer_scale):
+def scatter_sum(parts, scale):
     slabs = parts.shape[0]
-    rows = parts.shape[1]
-    messages = [None]
-    for shift in range(1, slabs):
-        message = to_wire(parts[shift], scale)
-        if axial is not None and shift == 1:
-            message = jnp.concatenate([message, to_wire(axial[1], layer_scale)])
-        if axial is not None and shift == slabs - 1:
-            message = jnp.concatenate([message, to_wire(axial[0], layer_scale)])
-        messages.append(message)
-    received = slab_exchange(messages)
+    messages = [None] + [to_wire(parts[shift], scale) for shift in range(1, slabs)]
     total = parts[0]
-    for message in received:
-        total = total + from_wire(message[:rows], scale)
-    halos = None
-    if axial is not None:
-        halos = axial_halos(received[0], received[-1], layer_scale, axial[0].shape[0])
-    return total, halos
+    for message in slab_exchange(messages):
+        total = total + from_wire(message, scale)
+    return total
 
 
 def per_device(
@@ -618,86 +627,60 @@
     ]
 
     place = gather_places(chunk)
+
+    by_owner = surface_guess.reshape(turns, slabs, n_axial, lanes)
+    shares = [
+        to_wire(
+            lax.dynamic_index_in_dim(
+                by_owner, lax.rem(slab + shift, slabs), axis=1, keepdims=False
+            ),
+            scale_s[0],
+        ).reshape(turns * n_axial, lanes)
+        for shift in range(slabs)
+    ]
+    columns = jnp.concatenate([shares[0]] + slab_exchange(shares))
+
+    halos = halo_exchange(volume_guess, scale_v[0])
+    gathered = sector_gather(columns, scale_s[0])
     wide, narrow = volume_matrices(stiffness, n_theta, radial)
     mass = jnp.broadcast_to(mass_shift[..., None], mass_shift.shape + (HALF,))
-
-    def layers(rows, count):
-        return rows.reshape(count, radial, lanes)
-
-    def shaped(theta, axial):
-        return (
-            layers(theta[0], n_axial),
-            layers(theta[1], n_axial),
-            layers(axial[0], n_theta),
-            layers(axial[1], n_theta),
-        )
-
-    theta_edges, axial_edges = edge_rows(volume_guess)
-    by_owner = surface_guess.reshape(turns, slabs, n_axial, lanes)
-    messages = [None]
-    for shift in range(1, slabs):
-        share = lax.dynamic_index_in_dim(
-            by_owner, lax.rem(slab + shift, slabs), axis=1, keepdims=False
-        ).reshape(turns * n_axial, lanes)
-        message = to_wire(share, scale_s[0])
-        if shift == 1:
-            message = jnp.concatenate([message, to_wire(axial_edges[1], scale_v[0])])
-        if shift == slabs - 1:
-            message = jnp.concatenate([message, to_wire(axial_edges[0], scale_v[0])])
-        messages.append(message)
-    received = slab_exchange(messages)
-    axial = axial_halos(received[0], received[-1], scale_v[0], n_theta * radial)
-    share = lax.dynamic_index_in_dim(by_owner, slab, axis=1, keepdims=False)
-    parts = [share] + [
-        from_wire(message[: turns * n_axial], scale_s[0]).reshape(turns, n_axial, lanes)
-        for message in received
-    ]
-    columns = jnp.concatenate(
-        [
-            lax.dynamic_index_in_dim(
-                jnp.stack(parts), lax.rem(slab - owner + slabs, slabs), axis=0, keepdims=False
-            )
-            for owner in range(slabs)
-        ],
-        axis=1,
-    ).reshape(chunk, lanes)
-
-    bulk = volume_bulk(volume_guess, mass, wide, narrow)
-    gathered, theta = sector_gather(columns, scale_s[0], theta_edges, scale_v[0])
-    outer = volume_guess[:, :, radial - 1, :].reshape(pairs, 2, n_axial, lanes)
-    add = surface_rhs + 0.5 * (outer[:, 0] + outer[:, 1])
-    u0, face0, first = finish(
-        finish_first_kernel, 1, True, bulk, surface_guess, shaped(theta, axial), volume_rhs
-    )
-    theta_edges, axial_edges = edge_rows(u0)
-    partial = bem_partial(-1.0, place, bem_matrix, gathered, add, slabs)
-    total, axial = scatter_sum(partial, scale_p[0], axial_edges, scale_v[1])
+    bulk, face = volume_bulk(
+        volume_guess, mass, wide, narrow, with_face=True, after=(gathered[0],)
+    )
+    partial = bem_partial(
+        -1.0, True, place, bem_matrix, face, gathered, surface_rhs, after=(bulk,)
+    )
+    u0, face, first = finish(
+        finish_first_kernel, 1, True, bulk, surface_guess, halos, volume_rhs, after=(partial,)
+    )
+    total = scatter_sum(partial, scale_p[0])
     s0_owner, s0 = total[:chunk], total[chunk:].reshape(pairs, n_axial, lanes)
 
-    bulk = volume_bulk(u0, mass, wide, narrow)
-    gathered, theta = sector_gather(s0_owner, scale_s[1], theta_edges, scale_v[1])
-    u1, face1, second = finish(
-        finish_second_kernel, 3, True, bulk, s0, shaped(theta, axial), u0
-    )
-    theta_edges, axial_edges = edge_rows(u1)
-    partial = bem_partial(1.0, place, bem_matrix, gathered, -face0, slabs)
-    total, axial = scatter_sum(partial, scale_p[1], axial_edges, scale_v[2])
+    halos = halo_exchange(u0, scale_v[1])
+    gathered = sector_gather(to_wire(s0_owner, scale_s[1]), scale_s[1])
+    (bulk,) = volume_bulk(u0, mass, wide, narrow, after=(s0_owner,))
+    partial = bem_partial(1.0, False, place, bem_matrix, face, gathered, after=(bulk,))
+    u1, face, second = finish(
+        finish_second_kernel, 3, True, bulk, s0, halos, u0, after=(partial,)
+    )
+    total = scatter_sum(partial, scale_p[1])
     s1_owner, s1 = total[:chunk], total[chunk:].reshape(pairs, n_axial, lanes)
 
-    bulk = volume_bulk(u1, mass, wide, narrow)
-    gathered, theta = sector_gather(s1_owner, scale_s[2], theta_edges, scale_v[2])
-    (third,) = finish(
-        finish_third_kernel, 5, False, bulk, s1, shaped(theta, axial), u0, u1
-    )
-    partial = bem_partial(1.0, place, bem_matrix, gathered, -face1, slabs)
-    total, _ = scatter_sum(partial[:, :chunk], scale_p[2], None, 1.0)
+    halos = halo_exchange(u1, scale_v[2])
+    gathered = sector_gather(to_wire(s1_owner, scale_s[2]), scale_s[2])
+    (bulk,) = volume_bulk(u1, mass, wide, narrow, after=(s1_owner,))
+    partial = bem_partial(1.0, False, place, bem_matrix, face, gathered, after=(bulk,))
+    third, u0, u1, guess = finish(
+        finish_third_kernel, 5, False, bulk, s1, halos, u0, u1, volume_guess, after=(partial,)
+    )
+    total = scatter_sum(partial[:, :chunk], scale_p[2])
 
     gram = local_gram(first, second, third, s0_owner, s1_owner, total)
     devices = sectors * slabs
     copies = jnp.broadcast_to(gram.reshape(1, 1, -1), (devices, 1, gram.size))
     gram_all = lax.all_to_all(copies, ("sector", "slab"), split_axis=0, concat_axis=0, tiled=True)
     gram_all = jnp.swapaxes(gram_all.reshape(devices, 9, HALF), 0, 1)
-    return final_solution(gram_all, volume_guess, u0, u1, surface_guess, s0, s1)
+    return final_solution(gram_all, guess, u0, u1, surface_guess, s0, s1)
 
 
 def solution(mesh):

time: 130 us -> 116 us (0.89)
  starting transfers between devices: 25.1 us -> 51 us
  waiting for transfers between devices: 37.9 us -> 16.2 us
  other arithmetic: 13.3 us -> 1.59 us
  Pallas kernels: 30.7 us -> 25 us
  blocking collectives: 10.3 us -> 12.6 us
  local copies, waits for them, and re-layouts: 10.3 us -> 8.11 us
    ppermute x12 -> x33, starting transfers between devices: 9.34 us -> 31 us  [the longest x9 14.4 us: sector_gather(): shares.append(lax.ppermute(own, 'sector', shift_perm(sectors, 2 * shift)))]
    ppermute x12 -> x33, waiting for transfers between devices: 24.1 us -> 8.94 us  [the longest x9 4.72 us: sector_gather(): shares.append(lax.ppermute(own, 'sector', shift_perm(sectors, 2 * shift)))]
    ppermute x12, waiting for transfers between devices: 13.8 us -> 7.25 us  [slab_exchange(): lax.ppermute(messages[shift], 'slab', shift_perm(slabs, shift))]
    pallas_call x12, Pallas kernels: 30.7 us -> 25 us  [call(): return lambda *args: called(*args, *after)]
    ppermute x12, starting transfers between devices: 15.7 us -> 20 us  [slab_exchange(): lax.ppermute(messages[shift], 'slab', shift_perm(slabs, shift))]
    concatenate x15 -> x1, other arithmetic: 2.88 us -> 0.03 us  [per_device(): columns = jnp.concatenate([shares[0]] + slab_exchange(shares))]
    convert_element_type x10, other arithmetic: 3.1 us -> 0.38 us  [to_wire(): return (values * scale).astype(WIRE)]
    all_to_all x1, blocking collectives: 10.3 us -> 12.6 us  [per_device(): lax.all_to_all(copies, ('sector', 'slab'), split_axis=0, concat_axis=0, t...]
  transfers between devices with their start and end apart: 24 -> 45, of which waited for: 12 -> 13; matrix products, arithmetic and copies ran while one was open for 10% -> 1% of each run, Pallas kernels for 15% -> 14%
where the time goes in v1:
time: 116 us
  starting transfers between devices  51 us (44%)
  Pallas kernels  25 us (22%)
  waiting for transfers between devices  16.2 us (14%)
  blocking collectives  12.6 us (11%)
  local copies, waits for them, and re-layouts  8.11 us (7%)
  other arithmetic  1.59 us (1%)
  between operations  1.39 us (1%)
    pallas_call x12, Pallas kernels, call(): return lambda *args: called(*args, *after)  25 us
    ppermute x12, starting transfers between devices, slab_exchange(): lax.ppermute(messages[shift], 'slab', shift_perm(slabs, shift))  20 us
    ppermute x9, starting transfers between devices, sector_gather(): shares.append(lax.ppermute(own, 'sector', shift_perm(sectors, 2 * shift)))  14.4 us
    all_to_all x1, blocking collectives, per_device(): lax.all_to_all(copies, ('sector', 'slab'), split_axis=0, concat_axis=0, t...  12.6 us
    ppermute x6, starting transfers between devices, both_ways(): beyond = lax.ppermute(to_wire(first, scale), axis, shift_perm(peers, -1))  11.4 us
    unnamed x26, local copies, waits for them, and re-layouts  7.6 us
    ppermute x12, waiting for transfers between devices, slab_exchange(): lax.ppermute(messages[shift], 'slab', shift_perm(slabs, shift))  7.25 us
    ppermute x9, waiting for transfers between devices, sector_gather(): shares.append(lax.ppermute(own, 'sector', shift_perm(sectors, 2 * shift)))  4.72 us
  transfers between devices with their start and end apart: 45, of which 13 were waited for; matrix products, arithmetic and copies ran while one was open for 1% of the time, Pallas kernels for 14%

profile of v1, /device:TPU:0, one launch (start us, length us, event | category | flops | bytes accessed | tf_op | source)
XLA Modules:
  0.0 115.9 jit_solution(6136795490890435860)
XLA Ops:
  0.7 1.6 %copy.63.refs_0_.refs_8_ = f32[16,16,8,256]{3,2,1,0:T(8,128)S(1)} copy(f32[16,16,8,256]{3,2,1,0:T(8,128)} %param.9) | data formatting | bytes 4194304
  2.3 3.0 %collective-permute-start.1 = (f16[32,256]{1,0:T(8,128)(2,1)S(1)}, f16[32,256]{1,0:T(8,128)(2,1)S(1)}, u32[]{:S(2)}, u32[]{:S(2)}) collective-permute-start(f16[32,256]{1,0:T(8,128)(2,1)S(1)} %bitcast.136), channel_id=1, source_target_pairs={{0,2},{1,3},{2,0},{3,1},{4,6},{5,7},{6,4},{7,5},{8,10},{9,11},{10,... | collective-permute-start | bytes 49160 | tf_op jit(solution)/shard_map/ppermute | solution.py:549
  5.4 1.5 %collective-permute-start = (f16[32,256]{1,0:T(8,128)(2,1)S(1)}, f16[32,256]{1,0:T(8,128)(2,1)S(1)}, u32[]{:S(2)}, u32[]{:S(2)}) collective-permute-start(f16[32,256]{1,0:T(8,128)(2,1)S(1)} %bitcast.135), channel_id=1, source_target_pairs={{0,1},{1,2},{2,3},{3,0},{4,5},{5,6},{6,7},{7,4},{8,9},{9,10},{10,1... | collective-permute-start | bytes 49160 | tf_op jit(solution)/shard_map/ppermute | solution.py:549
  6.9 1.4 %collective-permute-start.2 = (f16[32,256]{1,0:T(8,128)(2,1)S(1)}, f16[32,256]{1,0:T(8,128)(2,1)S(1)}, u32[]{:S(2)}, u32[]{:S(2)}) collective-permute-start(f16[32,256]{1,0:T(8,128)(2,1)S(1)} %bitcast.134), channel_id=1, source_target_pairs={{0,3},{1,0},{2,1},{3,2},{4,7},{5,4},{6,5},{7,6},{8,11},{9,8},{10,9... | collective-permute-start | bytes 49160 | tf_op jit(solution)/shard_map/ppermute | solution.py:549
  8.3 2.3 %collective-permute-start.4 = (f16[16,8,256]{2,1,0:T(8,128)(2,1)S(1)}, f16[16,8,256]{2,1,0:T(8,128)(2,1)S(1)}, u32[]{:S(2)}, u32[]{:S(2)}) collective-permute-start(f16[16,8,256]{2,1,0:T(8,128)(2,1)S(1)} %get-tuple-element.44), channel_id=1, source_target_pairs={{0,28},{4,0},{8,4},{12,8},{16,12},{20,16},{24,20},{28,24},{1,29},{... | collective-permute-start | bytes 196616 | tf_op jit(solution)/shard_map/ppermute | solution.py:558
  10.8 1.1 volume_matrices.1
  12.6 1.5 %collective-permute-start.5 = (f16[16,8,256]{2,1,0:T(8,128)(2,1)S(1)}, f16[16,8,256]{2,1,0:T(8,128)(2,1)S(1)}, u32[]{:S(2)}, u32[]{:S(2)}) collective-permute-start(f16[16,8,256]{2,1,0:T(8,128)(2,1)S(1)} %get-tuple-element.43), channel_id=1, source_target_pairs={{0,1},{1,2},{2,3},{3,0},{4,5},{5,6},{6,7},{7,4},{8,9},{9,10},{10,1... | collective-permute-start | bytes 196616 | tf_op jit(solution)/shard_map/ppermute | solution.py:557
  14.1 1.0 collective-permute-start.10
  15.5 3.7 %volume_bulk.3 = (f32[16,16,8,256]{3,2,1,0:T(8,128)S(1)}, f32[8,16,256]{2,1,0:T(8,128)S(1)}) custom-call(f32[16,16,8,256]{3,2,1,0:T(8,128)S(1)} %copy.63.refs_0_.refs_8_, f32[16,16,8,128]{3,2,1,0:T(8,128)S(1)} %broadcast_in_dim.22.refs_1_, bf16[2,128,256]{2,1,0:T(8,128)(2,1)S(1)} %get-tuple-element.16.refs_2_, ...), custom_call_target="tpu_custom_call" | custom-call | flops 805306368 | bytes 8388608 | tf_op jit(solution)/shard_map/volume_bulk/pallas_call | solution.py:46
  19.2 1.6 %collective-permute-start.8 = (f16[128,256]{1,0:T(8,128)(2,1)S(1)}, f16[128,256]{1,0:T(8,128)(2,1)S(1)}, u32[]{:S(2)}, u32[]{:S(2)}) collective-permute-start(f16[128,256]{1,0:T(8,128)(2,1)S(1)} %pad_maximum_fusion), channel_id=1, source_target_pairs={{0,8},{4,12},{8,16},{12,20},{16,24},{20,28},{24,0},{28,4},{1,9},{5... | collective-permute-start | bytes 196616 | tf_op jit(solution)/shard_map/ppermute | solution.py:575
  20.9 1.0 collective-permute-start.7
  21.9 1.6 %collective-permute-start.12 = (f16[128,256]{1,0:T(8,128)(2,1)S(1)}, f16[128,256]{1,0:T(8,128)(2,1)S(1)}, u32[]{:S(2)}, u32[]{:S(2)}) collective-permute-start(f16[128,256]{1,0:T(8,128)(2,1)S(1)} %pad_maximum_fusion), channel_id=1, source_target_pairs={{0,24},{4,28},{8,0},{12,4},{16,8},{20,12},{24,16},{28,20},{1,25},{... | collective-permute-start | bytes 196616 | tf_op jit(solution)/shard_map/ppermute | solution.py:575
  23.5 3.4 %collective-permute-done.12 = f16[128,256]{1,0:T(8,128)(2,1)S(1)} collective-permute-done((f16[128,256]{1,0:T(8,128)(2,1)S(1)}, f16[128,256]{1,0:T(8,128)(2,1)S(1)}, u32[]{:S(2)}, u32[]{:S(2)}) %collective-permute-start.12) | collective-permute-done | bytes 65568 | tf_op jit(solution)/shard_map/ppermute | solution.py:575
  27.6 1.2 %collective-permute-done.11 = f16[128,256]{1,0:T(8,128)(2,1)S(1)} collective-permute-done((f16[128,256]{1,0:T(8,128)(2,1)S(1)}, f16[128,256]{1,0:T(8,128)(2,1)S(1)}, u32[]{:S(2)}, u32[]{:S(2)}) %collective-permute-start.11) | collective-permute-done | bytes 65568 | tf_op jit(solution)/shard_map/ppermute | solution.py:578
  28.9 2.7 %bem_partial.3.refs_7_ = f32[4,256,256]{2,1,0:T(8,128)S(1)} custom-call(s32[9]{0:T(128)S(1)} %stack.39.refs_0_, bf16[2,512,1024]{2,1,0:T(8,128)(2,1)S(1)} %copy-done.6, f32[8,16,256]{2,1,0:T(8,128)S(1)} %get-tuple-element.19.refs_2_, f32[128,256]{1,0:T(8,128)S(1)} %convert_multiply_fusion.29.refs_4_.refs_3_, f32[128,256]{1,0:T(8,128)S(1)} %convert_multiply_fusion.26.refs_4_, ...), custom_call_target="tpu_custom_call" | custom-call | flops 1073741824 | bytes 4194304 | tf_op jit(solution)/shard_map/bem_partial/pallas_call | solution.py:46
  32.5 1.5 %collective-permute-start.20 = (f16[16,8,256]{2,1,0:T(8,128)(2,1)S(1)}, f16[16,8,256]{2,1,0:T(8,128)(2,1)S(1)}, u32[]{:S(2)}, u32[]{:S(2)}) collective-permute-start(f16[16,8,256]{2,1,0:T(8,128)(2,1)S(1)} %get-tuple-element.38), channel_id=1, source_target_pairs={{0,3},{1,0},{2,1},{3,2},{4,7},{5,4},{6,5},{7,6},{8,11},{9,8},{10,9... | collective-permute-start | bytes 196616 | tf_op jit(solution)/shard_map/ppermute | solution.py:558
  34.6 1.9 %collective-permute-start.18 = (f16[16,8,256]{2,1,0:T(8,128)(2,1)S(1)}, f16[16,8,256]{2,1,0:T(8,128)(2,1)S(1)}, u32[]{:S(2)}, u32[]{:S(2)}) collective-permute-start(f16[16,8,256]{2,1,0:T(8,128)(2,1)S(1)} %get-tuple-element.40), channel_id=1, source_target_pairs={{0,28},{4,0},{8,4},{12,8},{16,12},{20,16},{24,20},{28,24},{1,29},{... | collective-permute-start | bytes 196616 | tf_op jit(solution)/shard_map/ppermute | solution.py:558
  36.5 2.4 %collective-permute-start.14 = (f16[256,256]{1,0:T(8,128)(2,1)S(1)}, f16[256,256]{1,0:T(8,128)(2,1)S(1)}, u32[]{:S(2)}, u32[]{:S(2)}) collective-permute-start(f16[256,256]{1,0:T(8,128)(2,1)S(1)} %get-tuple-element.52), channel_id=1, source_target_pairs={{0,1},{1,2},{2,3},{3,0},{4,5},{5,6},{6,7},{7,4},{8,9},{9,10},{10,1... | collective-permute-start | bytes 393224 | tf_op jit(solution)/shard_map/ppermute | solution.py:549
  39.7 1.6 %collective-permute-start.15 = (f16[256,256]{1,0:T(8,128)(2,1)S(1)}, f16[256,256]{1,0:T(8,128)(2,1)S(1)}, u32[]{:S(2)}, u32[]{:S(2)}) collective-permute-start(f16[256,256]{1,0:T(8,128)(2,1)S(1)} %get-tuple-element.54), channel_id=1, source_target_pairs={{0,2},{1,3},{2,0},{3,1},{4,6},{5,7},{6,4},{7,5},{8,10},{9,11},{10,... | collective-permute-start | bytes 393224 | tf_op jit(solution)/shard_map/ppermute | solution.py:549
  42.0 1.8 %collective-permute-done.14 = f16[256,256]{1,0:T(8,128)(2,1)S(1)} collective-permute-done((f16[256,256]{1,0:T(8,128)(2,1)S(1)}, f16[256,256]{1,0:T(8,128)(2,1)S(1)}, u32[]{:S(2)}, u32[]{:S(2)}) %collective-permute-start.14) | collective-permute-done | bytes 131104 | tf_op jit(solution)/shard_map/ppermute | solution.py:549
  43.8 1.1 collective-permute-done.16
  45.4 1.3 %collective-permute-start.24 = (f16[128,256]{1,0:T(8,128)(2,1)S(1)}, f16[128,256]{1,0:T(8,128)(2,1)S(1)}, u32[]{:S(2)}, u32[]{:S(2)}) collective-permute-start(f16[128,256]{1,0:T(8,128)(2,1)S(1)} %get-tuple-element.33), channel_id=1, source_target_pairs={{0,16},{4,20},{8,24},{12,28},{16,0},{20,4},{24,8},{28,12},{1,17},{... | collective-permute-start | bytes 196616 | tf_op jit(solution)/shard_map/ppermute | solution.py:575
  46.7 3.0 %collective-permute-start.22 = (f16[128,256]{1,0:T(8,128)(2,1)S(1)}, f16[128,256]{1,0:T(8,128)(2,1)S(1)}, u32[]{:S(2)}, u32[]{:S(2)}) collective-permute-start(f16[128,256]{1,0:T(8,128)(2,1)S(1)} %get-tuple-element.33), channel_id=1, source_target_pairs={{0,8},{4,12},{8,16},{12,20},{16,24},{20,28},{24,0},{28,4},{1,9},{5... | collective-permute-start | bytes 196616 | tf_op jit(solution)/shard_map/ppermute | solution.py:575
  50.5 3.6 %volume_bulk.4.refs_11_.refs_0_ = f32[16,16,8,256]{3,2,1,0:T(8,128)S(1)} custom-call(f32[16,16,8,256]{3,2,1,0:T(8,128)S(1)} %get-tuple-element.21.refs_0_.refs_6_, f32[16,16,8,128]{3,2,1,0:T(8,128)S(1)} %broadcast_in_dim.22.refs_1_, bf16[2,128,256]{2,1,0:T(8,128)(2,1)S(1)} %get-tuple-element.16.refs_2_, bf16[2,128,128]{2,1,0:T(8,128)(2,1)S(1)} %get-tuple-element.17.refs_3_, ...), custom_call_target="tpu_custom_call" | custom-call | flops 805306368 | bytes 8388608 | tf_op jit(solution)/shard_map/volume_bulk/pallas_call | solution.py:46
  55.7 1.2 %collective-permute-done.25 = f16[128,256]{1,0:T(8,128)(2,1)S(1)} collective-permute-done((f16[128,256]{1,0:T(8,128)(2,1)S(1)}, f16[128,256]{1,0:T(8,128)(2,1)S(1)}, u32[]{:S(2)}, u32[]{:S(2)}) %collective-permute-start.25) | collective-permute-done | bytes 65568 | tf_op jit(solution)/shard_map/ppermute | solution.py:578
  56.9 2.6 %bem_partial.4.refs_7_ = f32[4,256,256]{2,1,0:T(8,128)S(1)} custom-call(s32[9]{0:T(128)S(1)} %stack.39.refs_0_, bf16[2,512,1024]{2,1,0:T(8,128)(2,1)S(1)} %copy-done.6, f32[8,16,256]{2,1,0:T(8,128)S(1)} %get-tuple-element.22.refs_2_, f32[128,256]{1,0:T(8,128)S(1)} %get-tuple-element.32.refs_3_, f32[128,256]{1,0:T(8,128)S(1)} %convert_multiply_fusion.16.refs_4_, ...), custom_call_target="tpu_custom_call" | custom-call | flops 1073741824 | bytes 4194304 | tf_op jit(solution)/shard_map/bem_partial/pallas_call | solution.py:46
  60.6 3.1 %collective-permute-start.34 = (f16[16,8,256]{2,1,0:T(8,128)(2,1)S(1)}, f16[16,8,256]{2,1,0:T(8,128)(2,1)S(1)}, u32[]{:S(2)}, u32[]{:S(2)}) collective-permute-start(f16[16,8,256]{2,1,0:T(8,128)(2,1)S(1)} %get-tuple-element.34), channel_id=1, source_target_pairs={{0,3},{1,0},{2,1},{3,2},{4,7},{5,4},{6,5},{7,6},{8,11},{9,8},{10,9... | collective-permute-start | bytes 196616 | tf_op jit(solution)/shard_map/ppermute | solution.py:558
  63.7 2.1 %collective-permute-start.32 = (f16[16,8,256]{2,1,0:T(8,128)(2,1)S(1)}, f16[16,8,256]{2,1,0:T(8,128)(2,1)S(1)}, u32[]{:S(2)}, u32[]{:S(2)}) collective-permute-start(f16[16,8,256]{2,1,0:T(8,128)(2,1)S(1)} %get-tuple-element.36), channel_id=1, source_target_pairs={{0,28},{4,0},{8,4},{12,8},{16,12},{20,16},{24,20},{28,24},{1,29},{... | collective-permute-start | bytes 196616 | tf_op jit(solution)/shard_map/ppermute | solution.py:558
  65.9 1.6 %collective-permute-start.28 = (f16[256,256]{1,0:T(8,128)(2,1)S(1)}, f16[256,256]{1,0:T(8,128)(2,1)S(1)}, u32[]{:S(2)}, u32[]{:S(2)}) collective-permute-start(f16[256,256]{1,0:T(8,128)(2,1)S(1)} %get-tuple-element.49), channel_id=1, source_target_pairs={{0,1},{1,2},{2,3},{3,0},{4,5},{5,6},{6,7},{7,4},{8,9},{9,10},{10,1... | collective-permute-start | bytes 393224 | tf_op jit(solution)/shard_map/ppermute | solution.py:549
  67.5 1.9 %collective-permute-start.30 = (f16[256,256]{1,0:T(8,128)(2,1)S(1)}, f16[256,256]{1,0:T(8,128)(2,1)S(1)}, u32[]{:S(2)}, u32[]{:S(2)}) collective-permute-start(f16[256,256]{1,0:T(8,128)(2,1)S(1)} %get-tuple-element.50), channel_id=1, source_target_pairs={{0,3},{1,0},{2,1},{3,2},{4,7},{5,4},{6,5},{7,6},{8,11},{9,8},{10,9... | collective-permute-start | bytes 393224 | tf_op jit(solution)/shard_map/ppermute | solution.py:549
  69.4 1.1 collective-permute-start.29
  70.6 2.6 %collective-permute-done.28 = f16[256,256]{1,0:T(8,128)(2,1)S(1)} collective-permute-done((f16[256,256]{1,0:T(8,128)(2,1)S(1)}, f16[256,256]{1,0:T(8,128)(2,1)S(1)}, u32[]{:S(2)}, u32[]{:S(2)}) %collective-permute-start.28) | collective-permute-done | bytes 131104 | tf_op jit(solution)/shard_map/ppermute | solution.py:549
  73.2 0.9 collective-permute-done.30
  74.8 1.3 %collective-permute-start.38 = (f16[128,256]{1,0:T(8,128)(2,1)S(1)}, f16[128,256]{1,0:T(8,128)(2,1)S(1)}, u32[]{:S(2)}, u32[]{:S(2)}) collective-permute-start(f16[128,256]{1,0:T(8,128)(2,1)S(1)} %get-tuple-element.31), channel_id=1, source_target_pairs={{0,16},{4,20},{8,24},{12,28},{16,0},{20,4},{24,8},{28,12},{1,17},{... | collective-permute-start | bytes 196616 | tf_op jit(solution)/shard_map/ppermute | solution.py:575
  76.1 2.9 %collective-permute-start.36 = (f16[128,256]{1,0:T(8,128)(2,1)S(1)}, f16[128,256]{1,0:T(8,128)(2,1)S(1)}, u32[]{:S(2)}, u32[]{:S(2)}) collective-permute-start(f16[128,256]{1,0:T(8,128)(2,1)S(1)} %get-tuple-element.31), channel_id=1, source_target_pairs={{0,8},{4,12},{8,16},{12,20},{16,24},{20,28},{24,0},{28,4},{1,9},{5... | collective-permute-start | bytes 196616 | tf_op jit(solution)/shard_map/ppermute | solution.py:575
  79.0 0.9 collective-permute-start.40
  79.9 3.6 %volume_bulk.5.refs_11_.refs_0_ = f32[16,16,8,256]{3,2,1,0:T(8,128)S(1)} custom-call(f32[16,16,8,256]{3,2,1,0:T(8,128)S(1)} %get-tuple-element.24.refs_0_.refs_7_, f32[16,16,8,128]{3,2,1,0:T(8,128)S(1)} %broadcast_in_dim.22.refs_1_, bf16[2,128,256]{2,1,0:T(8,128)(2,1)S(1)} %get-tuple-element.16.refs_2_, bf16[2,128,128]{2,1,0:T(8,128)(2,1)S(1)} %get-tuple-element.17.refs_3_, ...), custom_call_target="tpu_custom_call" | custom-call | flops 805306368 | bytes 8388608 | tf_op jit(solution)/shard_map/volume_bulk/pallas_call | solution.py:46
  84.8 1.2 %collective-permute-done.39 = f16[128,256]{1,0:T(8,128)(2,1)S(1)} collective-permute-done((f16[128,256]{1,0:T(8,128)(2,1)S(1)}, f16[128,256]{1,0:T(8,128)(2,1)S(1)}, u32[]{:S(2)}, u32[]{:S(2)}) %collective-permute-start.39) | collective-permute-done | bytes 65568 | tf_op jit(solution)/shard_map/ppermute | solution.py:578
  86.1 2.6 %bem_partial.5.refs_9_ = f32[4,256,256]{2,1,0:T(8,128)S(1)} custom-call(s32[9]{0:T(128)S(1)} %stack.39.refs_0_, bf16[2,512,1024]{2,1,0:T(8,128)(2,1)S(1)} %copy-done.6, f32[8,16,256]{2,1,0:T(8,128)S(1)} %get-tuple-element.25.refs_2_, f32[128,256]{1,0:T(8,128)S(1)} %get-tuple-element.30.refs_3_, f32[128,256]{1,0:T(8,128)S(1)} %convert_multiply_fusion.6.refs_4_, ...), custom_call_target="tpu_custom_call" | custom-call | flops 1073741824 | bytes 4194304 | tf_op jit(solution)/shard_map/bem_partial/pallas_call | solution.py:46
  88.8 3.0 %collective-permute-start.42 = (f16[128,256]{1,0:T(8,128)(2,1)S(1)}, f16[128,256]{1,0:T(8,128)(2,1)S(1)}, u32[]{:S(2)}, u32[]{:S(2)}) collective-permute-start(f16[128,256]{1,0:T(8,128)(2,1)S(1)} %get-tuple-element.46), channel_id=1, source_target_pairs={{0,1},{1,2},{2,3},{3,0},{4,5},{5,6},{6,7},{7,4},{8,9},{9,10},{10,1... | collective-permute-start | bytes 196616 | tf_op jit(solution)/shard_map/ppermute | solution.py:549
  92.3 1.1 collective-permute-start.43
  93.4 1.2 %finish_third_kernel.1 = (f32[5,8,128]{2,1,0:T(8,128)S(1)}, f32[16,16,8,256]{3,2,1,0:T(8,128)S(1)}, f32[16,16,8,256]{3,2,1,0:T(8,128)S(1)}, f32[16,16,8,256]{3,2,1,0:T(8,128)S(1)}) custom-call(f32[16,16,8,256]{3,2,1,0:T(8,128)S(1)} %volume_bulk.5.refs_11_.refs_0_, ...), custom_call_target="tpu_custom_call", output_to_operand_aliasing={{1}: (6, {}), {2}: (7, {}), {3}: (8, {})} | custom-call | flops 10485760 | bytes 10485760 | tf_op jit(solution)/shard_map/finish_third_kernel/pallas_call | solution.py:46
  94.6 1.3 %copy-done.2 = f32[16,16,8,256]{3,2,1,0:T(8,128)} copy-done((f32[16,16,8,256]{3,2,1,0:T(8,128)}, f32[16,16,8,256]{3,2,1,0:T(8,128)S(1)}, u32[]{:S(2)}) %copy-start.2) | copy-done | bytes 2097176
  95.9 1.3 %copy-done.4 = f32[16,16,8,256]{3,2,1,0:T(8,128)} copy-done((f32[16,16,8,256]{3,2,1,0:T(8,128)}, f32[16,16,8,256]{3,2,1,0:T(8,128)S(1)}, u32[]{:S(2)}) %copy-start.4) | copy-done | bytes 2097176
  97.5 12.6 %all_to_all.5 = f32[32,1,1152]{2,1,0:T(1,128)S(1)} all-to-all(f32[32,1,1152]{2,1,0:T(1,128)S(1)} %broadcast_in_dim.25), channel_id=1, replica_groups=mesh['sector'=8,'slab'=4] {'sector','slab'}, dimensions={0} | all-to-all | bytes 294912 | tf_op jit(solution)/shard_map/all_to_all | solution.py:681
  110.5 1.6 %copy-done.3 = f32[16,16,8,256]{3,2,1,0:T(8,128)S(1)} copy-done((f32[16,16,8,256]{3,2,1,0:T(8,128)S(1)}, f32[16,16,8,256]{3,2,1,0:T(8,128)}, u32[]{:S(2)}) %copy-start.3) | copy-done | bytes 2097176
  112.1 1.6 %copy-done.5 = f32[16,16,8,256]{3,2,1,0:T(8,128)S(1)} copy-done((f32[16,16,8,256]{3,2,1,0:T(8,128)S(1)}, f32[16,16,8,256]{3,2,1,0:T(8,128)}, u32[]{:S(2)}) %copy-start.5) | copy-done | bytes 2097176
  113.7 2.2 %final_solution.1 = (f32[16,16,8,256]{3,2,1,0:T(8,128)}, f32[8,16,256]{2,1,0:T(8,128)}) custom-call(f32[9,32,128]{2,1,0:T(8,128)S(1)} %bitcast_bitcast_fusion.refs_0_, f32[16,16,8,256]{3,2,1,0:T(8,128)S(1)} %copy-done.3, f32[16,16,8,256]{3,2,1,0:T(8,128)S(1)} %get-tuple-element.28.refs_2_, f32[16,16,8,256]{3,2,1,0:T(8,128)S(1)} %copy-done.5, ...), custom_call_target="tpu_custom_call" | custom-call | flops 5242880 | bytes 8388608 | tf_op jit(solution)/shard_map/final_solution/pallas_call | solution.py:46
  (136 shorter events, 12.0 us)
Async XLA Ops:
  2.3 16.9 %copy-start = (f32[16,16,8,256]{3,2,1,0:T(8,128)}, f32[16,16,8,256]{3,2,1,0:T(8,128)S(1)}, u32[]{:S(2)}) copy-start(f32[16,16,8,256]{3,2,1,0:T(8,128)S(1)} %copy.63.refs_0_.refs_8_) | copy-start | bytes 6291460
  2.3 9.7 %collective-permute-start.1 = (f16[32,256]{1,0:T(8,128)(2,1)S(1)}, f16[32,256]{1,0:T(8,128)(2,1)S(1)}, u32[]{:S(2)}, u32[]{:S(2)}) collective-permute-start(f16[32,256]{1,0:T(8,128)(2,1)S(1)} %bitcast.136), channel_id=1, source_target_pairs={{0,2},{1,3},{2,0},{3,1},{4,6},{5,7},{6,4},{7,5},{8,10},{9,11},{10,... | collective-permute-start | bytes 49160 | tf_op jit(solution)/shard_map/ppermute | solution.py:549
  5.4 7.2 %collective-permute-start = (f16[32,256]{1,0:T(8,128)(2,1)S(1)}, f16[32,256]{1,0:T(8,128)(2,1)S(1)}, u32[]{:S(2)}, u32[]{:S(2)}) collective-permute-start(f16[32,256]{1,0:T(8,128)(2,1)S(1)} %bitcast.135), channel_id=1, source_target_pairs={{0,1},{1,2},{2,3},{3,0},{4,5},{5,6},{6,7},{7,4},{8,9},{9,10},{10,1... | collective-permute-start | bytes 49160 | tf_op jit(solution)/shard_map/ppermute | solution.py:549
  6.9 7.2 %collective-permute-start.2 = (f16[32,256]{1,0:T(8,128)(2,1)S(1)}, f16[32,256]{1,0:T(8,128)(2,1)S(1)}, u32[]{:S(2)}, u32[]{:S(2)}) collective-permute-start(f16[32,256]{1,0:T(8,128)(2,1)S(1)} %bitcast.134), channel_id=1, source_target_pairs={{0,3},{1,0},{2,1},{3,2},{4,7},{5,4},{6,5},{7,6},{8,11},{9,8},{10,9... | collective-permute-start | bytes 49160 | tf_op jit(solution)/shard_map/ppermute | solution.py:549
  8.3 10.9 %collective-permute-start.4 = (f16[16,8,256]{2,1,0:T(8,128)(2,1)S(1)}, f16[16,8,256]{2,1,0:T(8,128)(2,1)S(1)}, u32[]{:S(2)}, u32[]{:S(2)}) collective-permute-start(f16[16,8,256]{2,1,0:T(8,128)(2,1)S(1)} %get-tuple-element.44), channel_id=1, source_target_pairs={{0,28},{4,0},{8,4},{12,8},{16,12},{20,16},{24,20},{28,24},{1,29},{... | collective-permute-start | bytes 196616 | tf_op jit(solution)/shard_map/ppermute | solution.py:558
  10.6 10.3 %collective-permute-start.3 = (f16[16,8,256]{2,1,0:T(8,128)(2,1)S(1)}, f16[16,8,256]{2,1,0:T(8,128)(2,1)S(1)}, u32[]{:S(2)}, u32[]{:S(2)}) collective-permute-start(f16[16,8,256]{2,1,0:T(8,128)(2,1)S(1)} %get-tuple-element.45), channel_id=1, source_target_pairs={{0,4},{4,8},{8,12},{12,16},{16,20},{20,24},{24,28},{28,0},{1,5},{5... | collective-permute-start | bytes 196616 | tf_op jit(solution)/shard_map/ppermute | solution.py:557
  12.0 9.8 %collective-permute-start.6 = (f16[16,8,256]{2,1,0:T(8,128)(2,1)S(1)}, f16[16,8,256]{2,1,0:T(8,128)(2,1)S(1)}, u32[]{:S(2)}, u32[]{:S(2)}) collective-permute-start(f16[16,8,256]{2,1,0:T(8,128)(2,1)S(1)} %get-tuple-element.42), channel_id=1, source_target_pairs={{0,3},{1,0},{2,1},{3,2},{4,7},{5,4},{6,5},{7,6},{8,11},{9,8},{10,9... | collective-permute-start | bytes 196616 | tf_op jit(solution)/shard_map/ppermute | solution.py:558
  12.6 10.8 %collective-permute-start.5 = (f16[16,8,256]{2,1,0:T(8,128)(2,1)S(1)}, f16[16,8,256]{2,1,0:T(8,128)(2,1)S(1)}, u32[]{:S(2)}, u32[]{:S(2)}) collective-permute-start(f16[16,8,256]{2,1,0:T(8,128)(2,1)S(1)} %get-tuple-element.43), channel_id=1, source_target_pairs={{0,1},{1,2},{2,3},{3,0},{4,5},{5,6},{6,7},{7,4},{8,9},{9,10},{10,1... | collective-permute-start | bytes 196616 | tf_op jit(solution)/shard_map/ppermute | solution.py:557
  14.1 13.4 %collective-permute-start.10 = (f16[128,256]{1,0:T(8,128)(2,1)S(1)}, f16[128,256]{1,0:T(8,128)(2,1)S(1)}, u32[]{:S(2)}, u32[]{:S(2)}) collective-permute-start(f16[128,256]{1,0:T(8,128)(2,1)S(1)} %pad_maximum_fusion), channel_id=1, source_target_pairs={{0,16},{4,20},{8,24},{12,28},{16,0},{20,4},{24,8},{28,12},{1,17},{... | collective-permute-start | bytes 196616 | tf_op jit(solution)/shard_map/ppermute | solution.py:575
  15.4 13.5 %copy-start.6 = (bf16[2,512,1024]{2,1,0:T(8,128)(2,1)S(1)}, bf16[2,512,1024]{2,1,0:T(8,128)(2,1)}, u32[]{:S(2)}) copy-start(bf16[2,512,1024]{2,1,0:T(8,128)(2,1)} %refs_1_.7) | copy-start | bytes 6291460
  15.5 13.5 %copy-start.9 = (f32[8,16,256]{2,1,0:T(8,128)S(1)}, f32[8,16,256]{2,1,0:T(8,128)}, u32[]{:S(2)}) copy-start(f32[8,16,256]{2,1,0:T(8,128)} %refs_11_.1) | copy-start | bytes 393220
  19.2 7.7 %collective-permute-start.8 = (f16[128,256]{1,0:T(8,128)(2,1)S(1)}, f16[128,256]{1,0:T(8,128)(2,1)S(1)}, u32[]{:S(2)}, u32[]{:S(2)}) collective-permute-start(f16[128,256]{1,0:T(8,128)(2,1)S(1)} %pad_maximum_fusion), channel_id=1, source_target_pairs={{0,8},{4,12},{8,16},{12,20},{16,24},{20,28},{24,0},{28,4},{1,9},{5... | collective-permute-start | bytes 196616 | tf_op jit(solution)/shard_map/ppermute | solution.py:575
  20.9 6.8 %collective-permute-start.7 = (f16[128,256]{1,0:T(8,128)(2,1)S(1)}, f16[128,256]{1,0:T(8,128)(2,1)S(1)}, u32[]{:S(2)}, u32[]{:S(2)}) collective-permute-start(f16[128,256]{1,0:T(8,128)(2,1)S(1)} %pad_maximum_fusion), channel_id=1, source_target_pairs={{0,4},{4,0},{8,12},{12,8},{16,20},{20,16},{24,28},{28,24},{1,5},{5... | collective-permute-start | bytes 196616 | tf_op jit(solution)/shard_map/ppermute | solution.py:578
  21.9 5.0 %collective-permute-start.12 = (f16[128,256]{1,0:T(8,128)(2,1)S(1)}, f16[128,256]{1,0:T(8,128)(2,1)S(1)}, u32[]{:S(2)}, u32[]{:S(2)}) collective-permute-start(f16[128,256]{1,0:T(8,128)(2,1)S(1)} %pad_maximum_fusion), channel_id=1, source_target_pairs={{0,24},{4,28},{8,0},{12,4},{16,8},{20,12},{24,16},{28,20},{1,25},{... | collective-permute-start | bytes 196616 | tf_op jit(solution)/shard_map/ppermute | solution.py:575
  26.9 2.0 %collective-permute-start.13 = (f16[128,256]{1,0:T(8,128)(2,1)S(1)}, f16[128,256]{1,0:T(8,128)(2,1)S(1)}, u32[]{:S(2)}, u32[]{:S(2)}) collective-permute-start(f16[128,256]{1,0:T(8,128)(2,1)S(1)} %collective-permute-done.12), channel_id=1, source_target_pairs={{0,4},{4,0},{8,12},{12,8},{16,20},{20,16},{24,28},{28,24},{1,5},{5... | collective-permute-start | bytes 196616 | tf_op jit(solution)/shard_map/ppermute | solution.py:578
  26.9 1.9 %collective-permute-start.9 = (f16[128,256]{1,0:T(8,128)(2,1)S(1)}, f16[128,256]{1,0:T(8,128)(2,1)S(1)}, u32[]{:S(2)}, u32[]{:S(2)}) collective-permute-start(f16[128,256]{1,0:T(8,128)(2,1)S(1)} %collective-permute-done.8), channel_id=1, source_target_pairs={{0,4},{4,0},{8,12},{12,8},{16,20},{20,16},{24,28},{28,24},{1,5},{5... | collective-permute-start | bytes 196616 | tf_op jit(solution)/shard_map/ppermute | solution.py:578
  27.5 1.3 %collective-permute-start.11 = (f16[128,256]{1,0:T(8,128)(2,1)S(1)}, f16[128,256]{1,0:T(8,128)(2,1)S(1)}, u32[]{:S(2)}, u32[]{:S(2)}) collective-permute-start(f16[128,256]{1,0:T(8,128)(2,1)S(1)} %collective-permute-done.10), channel_id=1, source_target_pairs={{0,4},{4,0},{8,12},{12,8},{16,20},{20,16},{24,28},{28,24},{1,5},{5... | collective-permute-start | bytes 196616 | tf_op jit(solution)/shard_map/ppermute | solution.py:578
  32.5 6.4 %collective-permute-start.20 = (f16[16,8,256]{2,1,0:T(8,128)(2,1)S(1)}, f16[16,8,256]{2,1,0:T(8,128)(2,1)S(1)}, u32[]{:S(2)}, u32[]{:S(2)}) collective-permute-start(f16[16,8,256]{2,1,0:T(8,128)(2,1)S(1)} %get-tuple-element.38), channel_id=1, source_target_pairs={{0,3},{1,0},{2,1},{3,2},{4,7},{5,4},{6,5},{7,6},{8,11},{9,8},{10,9... | collective-permute-start | bytes 196616 | tf_op jit(solution)/shard_map/ppermute | solution.py:558
  34.0 5.8 %collective-permute-start.19 = (f16[16,8,256]{2,1,0:T(8,128)(2,1)S(1)}, f16[16,8,256]{2,1,0:T(8,128)(2,1)S(1)}, u32[]{:S(2)}, u32[]{:S(2)}) collective-permute-start(f16[16,8,256]{2,1,0:T(8,128)(2,1)S(1)} %get-tuple-element.39), channel_id=1, source_target_pairs={{0,1},{1,2},{2,3},{3,0},{4,5},{5,6},{6,7},{7,4},{8,9},{9,10},{10,1... | collective-permute-start | bytes 196616 | tf_op jit(solution)/shard_map/ppermute | solution.py:557
  34.6 6.7 %collective-permute-start.18 = (f16[16,8,256]{2,1,0:T(8,128)(2,1)S(1)}, f16[16,8,256]{2,1,0:T(8,128)(2,1)S(1)}, u32[]{:S(2)}, u32[]{:S(2)}) collective-permute-start(f16[16,8,256]{2,1,0:T(8,128)(2,1)S(1)} %get-tuple-element.40), channel_id=1, source_target_pairs={{0,28},{4,0},{8,4},{12,8},{16,12},{20,16},{24,20},{28,24},{1,29},{... | collective-permute-start | bytes 196616 | tf_op jit(solution)/shard_map/ppermute | solution.py:558
  36.5 5.5 %collective-permute-start.17 = (f16[16,8,256]{2,1,0:T(8,128)(2,1)S(1)}, f16[16,8,256]{2,1,0:T(8,128)(2,1)S(1)}, u32[]{:S(2)}, u32[]{:S(2)}) collective-permute-start(f16[16,8,256]{2,1,0:T(8,128)(2,1)S(1)} %get-tuple-element.41), channel_id=1, source_target_pairs={{0,4},{4,8},{8,12},{12,16},{16,20},{20,24},{24,28},{28,0},{1,5},{5... | collective-permute-start | bytes 196616 | tf_op jit(solution)/shard_map/ppermute | solution.py:557
  36.5 7.3 %collective-permute-start.14 = (f16[256,256]{1,0:T(8,128)(2,1)S(1)}, f16[256,256]{1,0:T(8,128)(2,1)S(1)}, u32[]{:S(2)}, u32[]{:S(2)}) collective-permute-start(f16[256,256]{1,0:T(8,128)(2,1)S(1)} %get-tuple-element.52), channel_id=1, source_target_pairs={{0,1},{1,2},{2,3},{3,0},{4,5},{5,6},{6,7},{7,4},{8,9},{9,10},{10,1... | collective-permute-start | bytes 393224 | tf_op jit(solution)/shard_map/ppermute | solution.py:549
  38.9 6.0 %collective-permute-start.16 = (f16[256,256]{1,0:T(8,128)(2,1)S(1)}, f16[256,256]{1,0:T(8,128)(2,1)S(1)}, u32[]{:S(2)}, u32[]{:S(2)}) collective-permute-start(f16[256,256]{1,0:T(8,128)(2,1)S(1)} %get-tuple-element.53), channel_id=1, source_target_pairs={{0,3},{1,0},{2,1},{3,2},{4,7},{5,4},{6,5},{7,6},{8,11},{9,8},{10,9... | collective-permute-start | bytes 393224 | tf_op jit(solution)/shard_map/ppermute | solution.py:549
  39.7 5.5 %collective-permute-start.15 = (f16[256,256]{1,0:T(8,128)(2,1)S(1)}, f16[256,256]{1,0:T(8,128)(2,1)S(1)}, u32[]{:S(2)}, u32[]{:S(2)}) collective-permute-start(f16[256,256]{1,0:T(8,128)(2,1)S(1)} %get-tuple-element.54), channel_id=1, source_target_pairs={{0,2},{1,3},{2,0},{3,1},{4,6},{5,7},{6,4},{7,5},{8,10},{9,11},{10,... | collective-permute-start | bytes 393224 | tf_op jit(solution)/shard_map/ppermute | solution.py:549
  45.4 10.1 %collective-permute-start.24 = (f16[128,256]{1,0:T(8,128)(2,1)S(1)}, f16[128,256]{1,0:T(8,128)(2,1)S(1)}, u32[]{:S(2)}, u32[]{:S(2)}) collective-permute-start(f16[128,256]{1,0:T(8,128)(2,1)S(1)} %get-tuple-element.33), channel_id=1, source_target_pairs={{0,16},{4,20},{8,24},{12,28},{16,0},{20,4},{24,8},{28,12},{1,17},{... | collective-permute-start | bytes 196616 | tf_op jit(solution)/shard_map/ppermute | solution.py:575
  46.7 8.2 %collective-permute-start.22 = (f16[128,256]{1,0:T(8,128)(2,1)S(1)}, f16[128,256]{1,0:T(8,128)(2,1)S(1)}, u32[]{:S(2)}, u32[]{:S(2)}) collective-permute-start(f16[128,256]{1,0:T(8,128)(2,1)S(1)} %get-tuple-element.33), channel_id=1, source_target_pairs={{0,8},{4,12},{8,16},{12,20},{16,24},{20,28},{24,0},{28,4},{1,9},{5... | collective-permute-start | bytes 196616 | tf_op jit(solution)/shard_map/ppermute | solution.py:575
  49.7 5.9 %collective-permute-start.21 = (f16[128,256]{1,0:T(8,128)(2,1)S(1)}, f16[128,256]{1,0:T(8,128)(2,1)S(1)}, u32[]{:S(2)}, u32[]{:S(2)}) collective-permute-start(f16[128,256]{1,0:T(8,128)(2,1)S(1)} %get-tuple-element.33), channel_id=1, source_target_pairs={{0,4},{4,0},{8,12},{12,8},{16,20},{20,16},{24,28},{28,24},{1,5},{5... | collective-permute-start | bytes 196616 | tf_op jit(solution)/shard_map/ppermute | solution.py:578
  49.7 5.2 %collective-permute-start.26 = (f16[128,256]{1,0:T(8,128)(2,1)S(1)}, f16[128,256]{1,0:T(8,128)(2,1)S(1)}, u32[]{:S(2)}, u32[]{:S(2)}) collective-permute-start(f16[128,256]{1,0:T(8,128)(2,1)S(1)} %get-tuple-element.33), channel_id=1, source_target_pairs={{0,24},{4,28},{8,0},{12,4},{16,8},{20,12},{24,16},{28,20},{1,25},{... | collective-permute-start | bytes 196616 | tf_op jit(solution)/shard_map/ppermute | solution.py:575
  54.9 2.0 %collective-permute-start.27 = (f16[128,256]{1,0:T(8,128)(2,1)S(1)}, f16[128,256]{1,0:T(8,128)(2,1)S(1)}, u32[]{:S(2)}, u32[]{:S(2)}) collective-permute-start(f16[128,256]{1,0:T(8,128)(2,1)S(1)} %collective-permute-done.26), channel_id=1, source_target_pairs={{0,4},{4,0},{8,12},{12,8},{16,20},{20,16},{24,28},{28,24},{1,5},{5... | collective-permute-start | bytes 196616 | tf_op jit(solution)/shard_map/ppermute | solution.py:578
  54.9 1.9 %collective-permute-start.23 = (f16[128,256]{1,0:T(8,128)(2,1)S(1)}, f16[128,256]{1,0:T(8,128)(2,1)S(1)}, u32[]{:S(2)}, u32[]{:S(2)}) collective-permute-start(f16[128,256]{1,0:T(8,128)(2,1)S(1)} %collective-permute-done.22), channel_id=1, source_target_pairs={{0,4},{4,0},{8,12},{12,8},{16,20},{20,16},{24,28},{28,24},{1,5},{5... | collective-permute-start | bytes 196616 | tf_op jit(solution)/shard_map/ppermute | solution.py:578
  55.5 1.3 %collective-permute-start.25 = (f16[128,256]{1,0:T(8,128)(2,1)S(1)}, f16[128,256]{1,0:T(8,128)(2,1)S(1)}, u32[]{:S(2)}, u32[]{:S(2)}) collective-permute-start(f16[128,256]{1,0:T(8,128)(2,1)S(1)} %collective-permute-done.24), channel_id=1, source_target_pairs={{0,4},{4,0},{8,12},{12,8},{16,20},{20,16},{24,28},{28,24},{1,5},{5... | collective-permute-start | bytes 196616 | tf_op jit(solution)/shard_map/ppermute | solution.py:578
  60.6 6.9 %collective-permute-start.34 = (f16[16,8,256]{2,1,0:T(8,128)(2,1)S(1)}, f16[16,8,256]{2,1,0:T(8,128)(2,1)S(1)}, u32[]{:S(2)}, u32[]{:S(2)}) collective-permute-start(f16[16,8,256]{2,1,0:T(8,128)(2,1)S(1)} %get-tuple-element.34), channel_id=1, source_target_pairs={{0,3},{1,0},{2,1},{3,2},{4,7},{5,4},{6,5},{7,6},{8,11},{9,8},{10,9... | collective-permute-start | bytes 196616 | tf_op jit(solution)/shard_map/ppermute | solution.py:558
  63.7 5.8 %collective-permute-start.33 = (f16[16,8,256]{2,1,0:T(8,128)(2,1)S(1)}, f16[16,8,256]{2,1,0:T(8,128)(2,1)S(1)}, u32[]{:S(2)}, u32[]{:S(2)}) collective-permute-start(f16[16,8,256]{2,1,0:T(8,128)(2,1)S(1)} %get-tuple-element.35), channel_id=1, source_target_pairs={{0,1},{1,2},{2,3},{3,0},{4,5},{5,6},{6,7},{7,4},{8,9},{9,10},{10,1... | collective-permute-start | bytes 196616 | tf_op jit(solution)/shard_map/ppermute | solution.py:557
  63.7 6.8 %collective-permute-start.32 = (f16[16,8,256]{2,1,0:T(8,128)(2,1)S(1)}, f16[16,8,256]{2,1,0:T(8,128)(2,1)S(1)}, u32[]{:S(2)}, u32[]{:S(2)}) collective-permute-start(f16[16,8,256]{2,1,0:T(8,128)(2,1)S(1)} %get-tuple-element.36), channel_id=1, source_target_pairs={{0,28},{4,0},{8,4},{12,8},{16,12},{20,16},{24,20},{28,24},{1,29},{... | collective-permute-start | bytes 196616 | tf_op jit(solution)/shard_map/ppermute | solution.py:558
  65.9 27.5 %collective-permute-start.31 = (f16[16,8,256]{2,1,0:T(8,128)(2,1)S(1)}, f16[16,8,256]{2,1,0:T(8,128)(2,1)S(1)}, u32[]{:S(2)}, u32[]{:S(2)}) collective-permute-start(f16[16,8,256]{2,1,0:T(8,128)(2,1)S(1)} %get-tuple-element.37), channel_id=1, source_target_pairs={{0,4},{4,8},{8,12},{12,16},{16,20},{20,24},{24,28},{28,0},{1,5},{5... | collective-permute-start | bytes 196616 | tf_op jit(solution)/shard_map/ppermute | solution.py:557
  65.9 7.3 %collective-permute-start.28 = (f16[256,256]{1,0:T(8,128)(2,1)S(1)}, f16[256,256]{1,0:T(8,128)(2,1)S(1)}, u32[]{:S(2)}, u32[]{:S(2)}) collective-permute-start(f16[256,256]{1,0:T(8,128)(2,1)S(1)} %get-tuple-element.49), channel_id=1, source_target_pairs={{0,1},{1,2},{2,3},{3,0},{4,5},{5,6},{6,7},{7,4},{8,9},{9,10},{10,1... | collective-permute-start | bytes 393224 | tf_op jit(solution)/shard_map/ppermute | solution.py:549
  67.5 6.6 %collective-permute-start.30 = (f16[256,256]{1,0:T(8,128)(2,1)S(1)}, f16[256,256]{1,0:T(8,128)(2,1)S(1)}, u32[]{:S(2)}, u32[]{:S(2)}) collective-permute-start(f16[256,256]{1,0:T(8,128)(2,1)S(1)} %get-tuple-element.50), channel_id=1, source_target_pairs={{0,3},{1,0},{2,1},{3,2},{4,7},{5,4},{6,5},{7,6},{8,11},{9,8},{10,9... | collective-permute-start | bytes 393224 | tf_op jit(solution)/shard_map/ppermute | solution.py:549
  69.4 5.2 %collective-permute-start.29 = (f16[256,256]{1,0:T(8,128)(2,1)S(1)}, f16[256,256]{1,0:T(8,128)(2,1)S(1)}, u32[]{:S(2)}, u32[]{:S(2)}) collective-permute-start(f16[256,256]{1,0:T(8,128)(2,1)S(1)} %get-tuple-element.51), channel_id=1, source_target_pairs={{0,2},{1,3},{2,0},{3,1},{4,6},{5,7},{6,4},{7,5},{8,10},{9,11},{10,... | collective-permute-start | bytes 393224 | tf_op jit(solution)/shard_map/ppermute | solution.py:549
  74.8 9.9 %collective-permute-start.38 = (f16[128,256]{1,0:T(8,128)(2,1)S(1)}, f16[128,256]{1,0:T(8,128)(2,1)S(1)}, u32[]{:S(2)}, u32[]{:S(2)}) collective-permute-start(f16[128,256]{1,0:T(8,128)(2,1)S(1)} %get-tuple-element.31), channel_id=1, source_target_pairs={{0,16},{4,20},{8,24},{12,28},{16,0},{20,4},{24,8},{28,12},{1,17},{... | collective-permute-start | bytes 196616 | tf_op jit(solution)/shard_map/ppermute | solution.py:575
  76.1 8.0 %collective-permute-start.36 = (f16[128,256]{1,0:T(8,128)(2,1)S(1)}, f16[128,256]{1,0:T(8,128)(2,1)S(1)}, u32[]{:S(2)}, u32[]{:S(2)}) collective-permute-start(f16[128,256]{1,0:T(8,128)(2,1)S(1)} %get-tuple-element.31), channel_id=1, source_target_pairs={{0,8},{4,12},{8,16},{12,20},{16,24},{20,28},{24,0},{28,4},{1,9},{5... | collective-permute-start | bytes 196616 | tf_op jit(solution)/shard_map/ppermute | solution.py:575
  79.0 5.8 %collective-permute-start.35 = (f16[128,256]{1,0:T(8,128)(2,1)S(1)}, f16[128,256]{1,0:T(8,128)(2,1)S(1)}, u32[]{:S(2)}, u32[]{:S(2)}) collective-permute-start(f16[128,256]{1,0:T(8,128)(2,1)S(1)} %get-tuple-element.31), channel_id=1, source_target_pairs={{0,4},{4,0},{8,12},{12,8},{16,20},{20,16},{24,28},{28,24},{1,5},{5... | collective-permute-start | bytes 196616 | tf_op jit(solution)/shard_map/ppermute | solution.py:578
  79.0 5.1 %collective-permute-start.40 = (f16[128,256]{1,0:T(8,128)(2,1)S(1)}, f16[128,256]{1,0:T(8,128)(2,1)S(1)}, u32[]{:S(2)}, u32[]{:S(2)}) collective-permute-start(f16[128,256]{1,0:T(8,128)(2,1)S(1)} %get-tuple-element.31), channel_id=1, source_target_pairs={{0,24},{4,28},{8,0},{12,4},{16,8},{20,12},{24,16},{28,20},{1,25},{... | collective-permute-start | bytes 196616 | tf_op jit(solution)/shard_map/ppermute | solution.py:575
  84.1 2.0 %collective-permute-start.41 = (f16[128,256]{1,0:T(8,128)(2,1)S(1)}, f16[128,256]{1,0:T(8,128)(2,1)S(1)}, u32[]{:S(2)}, u32[]{:S(2)}) collective-permute-start(f16[128,256]{1,0:T(8,128)(2,1)S(1)} %collective-permute-done.40), channel_id=1, source_target_pairs={{0,4},{4,0},{8,12},{12,8},{16,20},{20,16},{24,28},{28,24},{1,5},{5... | collective-permute-start | bytes 196616 | tf_op jit(solution)/shard_map/ppermute | solution.py:578
  84.1 1.9 %collective-permute-start.37 = (f16[128,256]{1,0:T(8,128)(2,1)S(1)}, f16[128,256]{1,0:T(8,128)(2,1)S(1)}, u32[]{:S(2)}, u32[]{:S(2)}) collective-permute-start(f16[128,256]{1,0:T(8,128)(2,1)S(1)} %collective-permute-done.36), channel_id=1, source_target_pairs={{0,4},{4,0},{8,12},{12,8},{16,20},{20,16},{24,28},{28,24},{1,5},{5... | collective-permute-start | bytes 196616 | tf_op jit(solution)/shard_map/ppermute | solution.py:578
  84.7 1.3 %collective-permute-start.39 = (f16[128,256]{1,0:T(8,128)(2,1)S(1)}, f16[128,256]{1,0:T(8,128)(2,1)S(1)}, u32[]{:S(2)}, u32[]{:S(2)}) collective-permute-start(f16[128,256]{1,0:T(8,128)(2,1)S(1)} %collective-permute-done.38), channel_id=1, source_target_pairs={{0,4},{4,0},{8,12},{12,8},{16,20},{20,16},{24,28},{28,24},{1,5},{5... | collective-permute-start | bytes 196616 | tf_op jit(solution)/shard_map/ppermute | solution.py:578
  88.8 8.4 %collective-permute-start.42 = (f16[128,256]{1,0:T(8,128)(2,1)S(1)}, f16[128,256]{1,0:T(8,128)(2,1)S(1)}, u32[]{:S(2)}, u32[]{:S(2)}) collective-permute-start(f16[128,256]{1,0:T(8,128)(2,1)S(1)} %get-tuple-element.46), channel_id=1, source_target_pairs={{0,1},{1,2},{2,3},{3,0},{4,5},{5,6},{6,7},{7,4},{8,9},{9,10},{10,1... | collective-permute-start | bytes 196616 | tf_op jit(solution)/shard_map/ppermute | solution.py:549
  91.8 5.4 %collective-permute-start.44 = (f16[128,256]{1,0:T(8,128)(2,1)S(1)}, f16[128,256]{1,0:T(8,128)(2,1)S(1)}, u32[]{:S(2)}, u32[]{:S(2)}) collective-permute-start(f16[128,256]{1,0:T(8,128)(2,1)S(1)} %get-tuple-element.47), channel_id=1, source_target_pairs={{0,3},{1,0},{2,1},{3,2},{4,7},{5,4},{6,5},{7,6},{8,11},{9,8},{10,9... | collective-permute-start | bytes 196616 | tf_op jit(solution)/shard_map/ppermute | solution.py:549
  92.3 4.9 %collective-permute-start.43 = (f16[128,256]{1,0:T(8,128)(2,1)S(1)}, f16[128,256]{1,0:T(8,128)(2,1)S(1)}, u32[]{:S(2)}, u32[]{:S(2)}) collective-permute-start(f16[128,256]{1,0:T(8,128)(2,1)S(1)} %get-tuple-element.48), channel_id=1, source_target_pairs={{0,2},{1,3},{2,0},{3,1},{4,6},{5,7},{6,4},{7,5},{8,10},{9,11},{10,... | collective-permute-start | bytes 196616 | tf_op jit(solution)/shard_map/ppermute | solution.py:549
  (9 other events, 37.8 us)

commit v2 on v1

--- a/solution.py
+++ b/solution.py
@@ -22,10 +22,9 @@
 
 
 def call(
-    kernel, out_shape, n_scalars, n_arrays, scratch=(), flops=0, bytes_accessed=0, name=None,
-    after=(), out_specs=None, aliases=None,
+    kernel, out_shape, n_scalars, n_arrays, n_anywhere=0, scratch=(), name=None, after=(), out_specs=None, aliases=None, vmem=VMEM_LIMIT,
 ):
-    n_read = n_scalars + n_arrays
+    n_read = n_scalars + n_arrays + n_anywhere
 
     def body(*refs):
         kernel(*refs[:n_read], *refs[n_read + len(after) :])
@@ -33,14 +32,14 @@
     called = pl.pallas_call(
         body,
         out_shape=out_shape,
-        in_specs=[SCALARS] * n_scalars + [WHOLE] * n_arrays + [ANYWHERE] * len(after),
+        in_specs=[SCALARS] * n_scalars
+        + [WHOLE] * n_arrays
+        + [ANYWHERE] * (n_anywhere + len(after)),
         out_specs=out_specs or jax.tree.map(lambda _: WHOLE, out_shape),
         scratch_shapes=list(scratch),
         input_output_aliases=aliases or {},
-        compiler_params=pltpu.CompilerParams(vmem_limit_bytes=VMEM_LIMIT),
-        cost_estimate=pl.CostEstimate(
-            flops=flops, bytes_accessed=bytes_accessed, transcendentals=0
-        ),
+        compiler_params=pltpu.CompilerParams(vmem_limit_bytes=vmem),
+        cost_estimate=pl.CostEstimate(flops=1000, bytes_accessed=1000, transcendentals=0),
         name=name,
     )
     return lambda *args: called(*args, *after)
@@ -103,7 +102,7 @@
         narrow_ref[index] = lower
 
 
-def volume_matrices(stiffness, nodes, radial):
+def volume_matrices(stiffness, nodes, radial, after=()):
     rows = nodes * radial
     return call(
         functools.partial(matrices_kernel, nodes, radial),
@@ -114,10 +113,11 @@
         0,
         1,
         name="volume_matrices",
+        after=after,
     )(stiffness)
 
 
-def bulk_kernel(x_ref, mass_ref, wide_ref, narrow_ref, y_ref, *face_refs):
+def bulk_kernel(x_ref, mass_ref, wide_ref, narrow_ref, own_ref, y_ref, passed_ref):
     n_theta, n_axial, radial, lanes = x_ref.shape
 
     def product(index, values):
@@ -142,27 +142,56 @@
         y_ref[a, :, :, HALF:] = old[:, :, HALF:] + mass * x[:, :, HALF:]
         return carry
 
-    lax.fori_loop(0, n_axial, along_theta, 0, unroll=2)
-    lax.fori_loop(0, n_theta, along_axial, 0, unroll=2)
-    for face_ref in face_refs:
-        put_faces(x_ref, face_ref)
-
-
-def volume_bulk(x, mass, wide, narrow, with_face=False, after=()):
+    lax.fori_loop(0, n_axial, along_theta, 0, unroll=True)
+    lax.fori_loop(0, n_theta, along_axial, 0, unroll=True)
+
+
+def volume_bulk(x, mass, wide, narrow, own, after=()):
     n_theta, n_axial, radial, lanes = x.shape
-    outs = (shape(*x.shape),)
-    if with_face:
-        outs = outs + (shape(n_theta // 2, n_axial, lanes),)
     return call(
         bulk_kernel,
-        outs,
+        (shape(*x.shape), shape(*own.shape)),
         0,
-        4,
-        flops=2 * 2 * 3 * x.size * n_axial * radial,
-        bytes_accessed=16 * x.size,
+        5,
         name="volume_bulk",
+        aliases={4: 1},
         after=after,
-    )(x, mass, wide, narrow)
+    )(x, mass, wide, narrow, own)
+
+
+def edges_kernel(x_ref, first_ref, last_ref, axial_first_ref, axial_last_ref, face_ref, copy_ref):
+    n_theta, n_axial = x_ref.shape[:2]
+    first_ref[...] = x_ref[0]
+    last_ref[...] = x_ref[n_theta - 1]
+    axial_first_ref[...] = x_ref[:, 0]
+    axial_last_ref[...] = x_ref[:, n_axial - 1]
+    put_faces(x_ref, face_ref)
+    copy_ref[...] = x_ref[...]
+
+
+def volume_edges(x):
+    n_theta, n_axial, radial, lanes = x.shape
+    theta, axial = shape(n_axial, radial, lanes), shape(n_theta, radial, lanes)
+    *layers, face, copy = call(
+        edges_kernel,
+        (theta, theta, axial, axial, shape(n_theta // 2, n_axial, lanes), shape(*x.shape)),
+        0,
+        1,
+        name="volume_edges",
+    )(x)
+    return layers, face, copy
+
+
+def pass_after(values, *earlier):
+    return call(
+        lambda values_ref, out_ref: None,
+        shape(*values.shape),
+        0,
+        1,
+        name="pass_after",
+        after=earlier,
+        aliases={0: 0},
+    )(values)
 
 
 def pair_sums(left, right):
@@ -254,7 +283,7 @@
 
 def finish_third_kernel(
     bulk_ref, s_ref, before_ref, beyond_ref, ax_before_ref, ax_beyond_ref, u0_ref, u1_ref,
-    x_ref, sums_ref, *passed_refs,
+    sums_ref,
 ):
     n_theta = bulk_ref.shape[0]
     sums_ref[...] = jnp.zeros_like(sums_ref)
@@ -277,31 +306,25 @@
 def finish(kernel, n_sums, with_result, bulk, s, halos, *others, after=()):
     n_theta, n_axial, radial, lanes = bulk.shape
     outs = (shape(n_sums, radial, HALF),)
-    aliases = {}
     if with_result:
         outs = (shape(*bulk.shape), shape(n_theta // 2, n_axial, lanes)) + outs
-    else:
-        outs = outs + (shape(*bulk.shape),) * len(others)
-        aliases = {6 + index: 1 + index for index in range(len(others))}
     return call(
         kernel,
         outs,
         0,
         6 + len(others),
-        flops=20 * bulk.size,
-        bytes_accessed=4 * bulk.size * (2 + len(others)),
         name=kernel.__name__,
         after=after,
-        aliases=aliases,
     )(bulk, s, *halos, *others)
 
 
-def bem_kernel(sign, behind, place_ref, m_ref, face_ref, *rest):
-    n_pieces = m_ref.shape[2] // (out_chunk := rest[-4].shape[1] // 2)
-    s_refs, rhs_refs = rest[:n_pieces], rest[n_pieces:-4]
-    out_ref, upper_ref, lower_ref, p_ref = rest[-4:]
+def bem_kernel(sign, by_source, place_ref, m_ref, face_ref, *rest):
+    own_ref, out_ref, upper_ref, lower_ref, p_ref = rest[-5:]
+    out_chunk = own_ref.shape[0] // 2
+    n_pieces = m_ref.shape[2] // out_chunk
+    s_refs, rhs_refs = rest[:n_pieces], rest[n_pieces:-5]
     pairs, n_axial, lanes = face_ref.shape
-    slabs = out_ref.shape[0]
+    slabs = out_ref.shape[0] + 1
     axial_all = p_ref.shape[1]
     rows = m_ref.shape[1]
     slab = place_ref[0]
@@ -315,15 +338,14 @@
 
     for which, s_ref in enumerate(s_refs):
         start = place_ref[1 + which]
-        if not behind:
+        if not by_source:
             place_rows(s_ref, 0, out_chunk, start)
             continue
-        for distance in range(slabs):
-            source = lax.rem(slab - distance + slabs, slabs)
+        for source in range(slabs):
             for turn in range(turns):
                 place_rows(
                     s_ref,
-                    (distance * turns + turn) * n_axial,
+                    (source * turns + turn) * n_axial,
                     n_axial,
                     start + turn * axial_all + source * n_axial,
                 )
@@ -346,31 +368,30 @@
         p_ref[here, :, HALF:] = sign * (by_real[:, HALF:] + by_imag[:, :HALF]).reshape(three)
         return carry
 
-    lax.fori_loop(0, rows // step, block, 0)
+    lax.fori_loop(0, rows // step, block, 0, unroll=True)
     own = pl.ds(pl.multiple_of(slab * n_axial, n_axial), n_axial)
     add = -sign * face_ref[...]
     for rhs_ref in rhs_refs:
         add = add + rhs_ref[...]
     p_ref[:, own, :] += add
     for shift in range(slabs):
-        target = lax.rem(slab + shift, slabs)
+        target = partner(slab, shift, slabs)
+        part_ref = own_ref if shift == 0 else out_ref.at[shift - 1]
         for turn in range(turns):
-            out_ref[shift, turn * axial_all : (turn + 1) * axial_all, :] = p_ref[
-                target + turn * slabs
-            ]
+            part_ref[turn * axial_all : (turn + 1) * axial_all, :] = p_ref[target + turn * slabs]
         there = pl.ds(pl.multiple_of(target * n_axial, n_axial), n_axial)
-        out_ref[shift, out_chunk:, :] = p_ref[:, there, :].reshape(out_chunk, lanes)
-
-
-def bem_partial(sign, behind, place, matrix, face, gathered, *rhs, after=()):
+        part_ref[out_chunk:, :] = p_ref[:, there, :].reshape(out_chunk, lanes)
+
+
+def bem_partial(sign, by_source, place, matrix, face, gathered, *rhs, after=()):
     pairs, n_axial, lanes = face.shape
     chunk = gathered[0].shape[0]
     rows, columns = matrix.shape[1:]
     axial_all = rows // pairs
     slabs = axial_all // n_axial
     return call(
-        functools.partial(bem_kernel, sign, behind),
-        shape(slabs, 2 * chunk, lanes),
+        functools.partial(bem_kernel, sign, by_source),
+        (shape(2 * chunk, lanes), shape(slabs - 1, 2 * chunk, lanes)),
         1,
         2 + len(gathered) + len(rhs),
         scratch=[
@@ -378,8 +399,6 @@
             pltpu.VMEM((columns, lanes), BF16),
             pltpu.VMEM((pairs, axial_all, lanes), F32),
         ],
-        flops=2 * 4 * rows * columns * lanes,
-        bytes_accessed=4 * rows * columns + 4 * columns * lanes + 8 * chunk * slabs * lanes,
         name="bem_partial",
         after=after,
     )(place, matrix, face, *gathered, *rhs)
@@ -398,14 +417,14 @@
     )
     surface = surface_sums(s0_ref[...], s1_ref[...], s2_ref[...])
     for row, (one, two) in enumerate(zip(volume, surface)):
-        out_ref[row : row + 1, :] = jnp.sum(one, axis=0, keepdims=True) + jnp.sum(
-            two, axis=0, keepdims=True
-        )
-
-
-def local_gram(first, second, third, s0, s1, s2):
+        total = jnp.sum(one, axis=0, keepdims=True) + jnp.sum(two, axis=0, keepdims=True)
+        for device in range(out_ref.shape[0]):
+            out_ref[device, :, row * HALF : (row + 1) * HALF] = total
+
+
+def local_gram(devices, first, second, third, s0, s1, s2):
     tiles = [values.reshape(-1, 8, LANES) for values in (s0, s1, s2)]
-    return call(gram_kernel, shape(9, HALF), 0, 6, name="local_gram")(
+    return call(gram_kernel, shape(devices, 1, 9 * HALF), 0, 6, name="local_gram")(
         first, second, third, *tiles
     )
 
@@ -490,27 +509,26 @@
 
 def solution_kernel(
     gram_ref, x_ref, u0_ref, u1_ref, s_ref, s0_ref, s1_ref,
-    volume_ref, surface_ref, row_ref, copied,
+    volume_ref, surface_ref, row_ref, stored,
 ):
-    sums = [jnp.sum(gram_ref[row], axis=0, keepdims=True) for row in range(9)]
+    total = jnp.sum(gram_ref[...], axis=0)
+    sums = [total[:, row * HALF : (row + 1) * HALF] for row in range(9)]
     first, second = coefficients(sums)
     n_theta = x_ref.shape[0]
 
-    def copy(a):
-        return pltpu.make_async_copy(row_ref.at[a], volume_ref.at[a], copied.at[a])
-
-    def body(a, carry):
+    def store(a):
+        return pltpu.make_async_copy(row_ref.at[a], volume_ref.at[a], stored.at[a])
+
+    for a in range(n_theta):
         real, imag = combine(first, second, x_ref[a], u0_ref[a], u1_ref[a])
         row_ref[a, :, :, :HALF] = real
         row_ref[a, :, :, HALF:] = imag
-        copy(a).start()
-        return carry
-
-    lax.fori_loop(0, n_theta, body, 0)
+        store(a).start()
     real, imag = combine(first, second, s_ref[...], s0_ref[...], s1_ref[...])
     surface_ref[..., :HALF] = real
     surface_ref[..., HALF:] = imag
-    lax.fori_loop(0, n_theta, lambda a, carry: (copy(a).wait(), carry)[1], 0)
+    for a in range(n_theta):
+        store(a).wait()
 
 
 def final_solution(gram_all, x, u0, u1, s, s0, s1):
@@ -520,8 +538,6 @@
         0,
         7,
         scratch=[pltpu.VMEM(x.shape, F32), pltpu.SemaphoreType.DMA((x.shape[0],))],
-        flops=10 * x.size,
-        bytes_accessed=16 * x.size,
         name="final_solution",
         out_specs=(ANYWHERE, WHOLE),
     )(gram_all, x, u0, u1, s, s0, s1)
@@ -539,63 +555,134 @@
     return values.astype(F32) * (1.0 / scale)
 
 
-def shift_perm(peers, shift):
-    return [(i, (i + shift) % peers) for i in range(peers)]
+def partner(index, distance, peers):
+    if peers & (peers - 1) == 0:
+        return index ^ distance
+    return lax.rem(index + distance, peers)
+
+
+def partner_perm(peers, distance):
+    if peers & (peers - 1) == 0:
+        return [(i, i ^ distance) for i in range(peers)]
+    return [(i, (i + distance) % peers) for i in range(peers)]
 
 
 def slab_exchange(messages):
     slabs = lax.axis_size("slab")
     return [
-        lax.ppermute(messages[shift], "slab", shift_perm(slabs, shift))
-        for shift in range(1, slabs)
+        lax.ppermute(messages[distance], "slab", partner_perm(slabs, distance))
+        for distance in range(1, slabs)
     ]
 
 
-def halo_exchange(volume, scale):
-    def both_ways(axis, first, last):
-        peers = lax.axis_size(axis)
-        before = lax.ppermute(to_wire(last, scale), axis, shift_perm(peers, 1))
-        beyond = lax.ppermute(to_wire(first, scale), axis, shift_perm(peers, -1))
-        return from_wire(before, scale), from_wire(beyond, scale)
-
-    theta = both_ways("sector", volume[0], volume[-1])
-    before, beyond = both_ways("slab", volume[:, 0], volume[:, -1])
-    slab, slabs = lax.axis_index("slab"), lax.axis_size("slab")
-    return theta + (
-        jnp.where(slab > 0, before, 0.0),
-        jnp.where(slab < slabs - 1, beyond, 0.0),
-    )
+def neighbour_swap(axis, first, last, scale, wrap):
+    peers = lax.axis_size(axis)
+    odd = lax.rem(lax.axis_index(axis), 2) == 1
+    first, last = to_wire(first, scale), to_wire(last, scale)
+    within = [(i, i ^ 1) for i in range(peers)]
+    across = [
+        pair
+        for i in range(1, peers if wrap else peers - 1, 2)
+        for pair in ((i, (i + 1) % peers), ((i + 1) % peers, i))
+    ]
+    inner = lax.ppermute(jnp.where(odd, first, last), axis, within)
+    outer = lax.ppermute(jnp.where(odd, last, first), axis, across)
+    before = from_wire(jnp.where(odd, inner, outer), scale)
+    beyond = from_wire(jnp.where(odd, outer, inner), scale)
+    return before, beyond
+
+
+def theta_halos(layers, scale):
+    return neighbour_swap("sector", *layers[:2], scale, True)
+
+
+def axial_halos(layers, scale):
+    return neighbour_swap("slab", *layers[2:], scale, False)
+
+
+def edge_layers(volume):
+    return volume[0], volume[-1], volume[:, 0], volume[:, -1]
+
+
+def sibling_perm():
+    return [(i, i ^ 1) for i in range(lax.axis_size("sector"))]
 
 
 def sector_gather(own, scale):
     sectors = lax.axis_size("sector")
-    sibling = [(i, i ^ 1) for i in range(sectors)]
     shares = [own]
-    for shift in range(1, sectors // 2):
-        shares.append(lax.ppermute(own, "sector", shift_perm(sectors, 2 * shift)))
+    for distance in range(1, sectors // 2):
+        perm = [
+            (2 * i + core, 2 * j + core)
+            for i, j in partner_perm(sectors // 2, distance)
+            for core in range(2)
+        ]
+        shares.append(lax.ppermute(own, "sector", perm))
     gathered = []
     for share in shares:
-        gathered += [share, lax.ppermute(share, "sector", sibling)]
+        gathered += [share, lax.ppermute(share, "sector", sibling_perm())]
     return [from_wire(share, scale) for share in gathered]
 
 
 def gather_places(chunk):
+    chips = lax.axis_size("sector") // 2
+    sector = lax.axis_index("sector")
+    chip, core = sector // 2, lax.rem(sector, 2)
+    places = [lax.axis_index("slab")]
+    for distance in range(chips):
+        mutual = chips & (chips - 1) == 0
+        source = chip ^ distance if mutual else lax.rem(chip - distance + chips, chips)
+        places += [(2 * source + core) * chunk, (2 * source + 1 - core) * chunk]
+    return jnp.stack([jnp.asarray(value, jnp.int32) for value in places])
+
+
+def first_gather(surface, scale):
+    sectors, slabs = lax.axis_size("sector"), lax.axis_size("slab")
+    chips = sectors // 2
+    pairs, n_axial, lanes = surface.shape
+    turns = pairs // slabs
+    by_owner = to_wire(surface, scale).reshape(turns, slabs, n_axial, lanes)
+    by_owner = jnp.swapaxes(by_owner, 0, 1).reshape(1, slabs, turns * n_axial, lanes)
+    messages = jnp.broadcast_to(by_owner, (chips,) + by_owner.shape[1:])
+    groups = [
+        [(2 * chip + core) * slabs + slab for chip in range(chips) for slab in range(slabs)]
+        for core in range(2)
+    ]
+    mine = lax.all_to_all(
+        messages.reshape(chips * slabs, turns * n_axial, lanes),
+        ("sector", "slab"),
+        split_axis=0,
+        concat_axis=0,
+        axis_index_groups=groups,
+        tiled=True,
+    )
+    other = lax.ppermute(mine, "sector", sibling_perm())
+    mine, other = (
+        from_wire(values, scale).reshape(chips, slabs * turns * n_axial, lanes)
+        for values in (mine, other)
+    )
+    return [values[chip] for chip in range(chips) for values in (mine, other)]
+
+
+def first_places(chunk):
     sectors = lax.axis_size("sector")
-    sector = lax.axis_index("sector")
+    core = lax.rem(lax.axis_index("sector"), 2)
     places = [lax.axis_index("slab")]
-    for shift in range(sectors // 2):
-        source = lax.rem(sector - 2 * shift + sectors, sectors)
-        places += [source * chunk, (source + 1 - 2 * lax.rem(source, 2)) * chunk]
+    for chip in range(sectors // 2):
+        places += [(2 * chip + core) * chunk, (2 * chip + 1 - core) * chunk]
     return jnp.stack([jnp.asarray(value, jnp.int32) for value in places])
 
 
-def scatter_sum(parts, scale):
-    slabs = parts.shape[0]
-    messages = [None] + [to_wire(parts[shift], scale) for shift in range(1, slabs)]
-    total = parts[0]
-    for message in slab_exchange(messages):
-        total = total + from_wire(message, scale)
-    return total
+def scatter(parts, scale):
+    messages = [None] + [to_wire(parts[which], scale) for which in range(parts.shape[0])]
+    meanwhile = lax.ppermute(messages[1][:16, :HALF], "sector", sibling_perm())
+    return slab_exchange(messages), meanwhile.astype(F32)
+
+
+def scatter_sum(own, received, scale):
+    for message in received:
+        own = own + from_wire(message, scale)
+    return own
 
 
 def per_device(
@@ -628,58 +715,50 @@
 
     place = gather_places(chunk)
 
-    by_owner = surface_guess.reshape(turns, slabs, n_axial, lanes)
-    shares = [
-        to_wire(
-            lax.dynamic_index_in_dim(
-                by_owner, lax.rem(slab + shift, slabs), axis=1, keepdims=False
-            ),
-            scale_s[0],
-        ).reshape(turns * n_axial, lanes)
-        for shift in range(slabs)
-    ]
-    columns = jnp.concatenate([shares[0]] + slab_exchange(shares))
-
-    halos = halo_exchange(volume_guess, scale_v[0])
-    gathered = sector_gather(columns, scale_s[0])
+    def surface_parts(total):
+        return total[:chunk], total[chunk:].reshape(pairs, n_axial, lanes)
+
+    gathered = first_gather(surface_guess, scale_s[0])
+    mass = jnp.broadcast_to(mass_shift[..., None], mass_shift.shape + (HALF,))
     wide, narrow = volume_matrices(stiffness, n_theta, radial)
-    mass = jnp.broadcast_to(mass_shift[..., None], mass_shift.shape + (HALF,))
-    bulk, face = volume_bulk(
-        volume_guess, mass, wide, narrow, with_face=True, after=(gathered[0],)
-    )
-    partial = bem_partial(
-        -1.0, True, place, bem_matrix, face, gathered, surface_rhs, after=(bulk,)
-    )
+    layers, face, guess = volume_edges(volume_guess)
+    halos = theta_halos(layers, scale_v[0]) + axial_halos(layers, scale_v[0])
+    own, parts = bem_partial(
+        -1.0, True, first_places(chunk), bem_matrix, face, gathered, surface_rhs
+    )
+    received, meanwhile = scatter(parts, scale_p[0])
+    bulk, own = volume_bulk(guess, mass, wide, narrow, own, after=(meanwhile,))
     u0, face, first = finish(
-        finish_first_kernel, 1, True, bulk, surface_guess, halos, volume_rhs, after=(partial,)
-    )
-    total = scatter_sum(partial, scale_p[0])
-    s0_owner, s0 = total[:chunk], total[chunk:].reshape(pairs, n_axial, lanes)
-
-    halos = halo_exchange(u0, scale_v[1])
+        finish_first_kernel, 1, True, bulk, surface_guess, halos, volume_rhs
+    )
+    theta = theta_halos(edge_layers(u0), scale_v[1])
+    bulk, own = volume_bulk(u0, mass, wide, narrow, own)
+    s0_owner, s0 = surface_parts(scatter_sum(own, received, scale_p[0]))
+
     gathered = sector_gather(to_wire(s0_owner, scale_s[1]), scale_s[1])
-    (bulk,) = volume_bulk(u0, mass, wide, narrow, after=(s0_owner,))
-    partial = bem_partial(1.0, False, place, bem_matrix, face, gathered, after=(bulk,))
+    u0 = pass_after(u0, gathered[1])
+    halos = theta + axial_halos(edge_layers(u0), scale_v[1])
+    own, parts = bem_partial(1.0, False, place, bem_matrix, face, gathered)
+    received, meanwhile = scatter(parts, scale_p[1])
     u1, face, second = finish(
-        finish_second_kernel, 3, True, bulk, s0, halos, u0, after=(partial,)
-    )
-    total = scatter_sum(partial, scale_p[1])
-    s1_owner, s1 = total[:chunk], total[chunk:].reshape(pairs, n_axial, lanes)
-
-    halos = halo_exchange(u1, scale_v[2])
+        finish_second_kernel, 3, True, bulk, s0, halos, u0, after=(meanwhile,)
+    )
+    theta = theta_halos(edge_layers(u1), scale_v[2])
+    bulk, own = volume_bulk(u1, mass, wide, narrow, own)
+    s1_owner, s1 = surface_parts(scatter_sum(own, received, scale_p[1]))
+
     gathered = sector_gather(to_wire(s1_owner, scale_s[2]), scale_s[2])
-    (bulk,) = volume_bulk(u1, mass, wide, narrow, after=(s1_owner,))
-    partial = bem_partial(1.0, False, place, bem_matrix, face, gathered, after=(bulk,))
-    third, u0, u1, guess = finish(
-        finish_third_kernel, 5, False, bulk, s1, halos, u0, u1, volume_guess, after=(partial,)
-    )
-    total = scatter_sum(partial[:, :chunk], scale_p[2])
-
-    gram = local_gram(first, second, third, s0_owner, s1_owner, total)
-    devices = sectors * slabs
-    copies = jnp.broadcast_to(gram.reshape(1, 1, -1), (devices, 1, gram.size))
-    gram_all = lax.all_to_all(copies, ("sector", "slab"), split_axis=0, concat_axis=0, tiled=True)
-    gram_all = jnp.swapaxes(gram_all.reshape(devices, 9, HALF), 0, 1)
+    u1 = pass_after(u1, gathered[1])
+    halos = theta + axial_halos(edge_layers(u1), scale_v[2])
+    own, parts = bem_partial(1.0, False, place, bem_matrix, face, gathered)
+    received, meanwhile = scatter(parts[:, :chunk], scale_p[2])
+    (third,) = finish(
+        finish_third_kernel, 5, False, bulk, s1, halos, u0, u1, after=(meanwhile,)
+    )
+    total = scatter_sum(own[:chunk], received, scale_p[2])
+
+    gram = local_gram(sectors * slabs, first, second, third, s0_owner, s1_owner, total)
+    gram_all = lax.all_to_all(gram, ("sector", "slab"), split_axis=0, concat_axis=0, tiled=True)
     return final_solution(gram_all, guess, u0, u1, surface_guess, s0, s1)
 
 

time: 116 us -> 100 us (0.86)
  Pallas kernels: 25 us -> 17.3 us
  starting transfers between devices: 51 us -> 45.6 us
  local copies, waits for them, and re-layouts: 8.11 us -> 4.47 us
  blocking collectives: 12.6 us -> 10.7 us
  other arithmetic: 1.59 us -> 3.1 us
    ppermute x45 -> x39, starting transfers between devices: 51 us -> 37.3 us  [the longest x9 14.3 us: slab_exchange(): lax.ppermute(messages[distance], 'slab', partner_perm(slabs, distance))]
    all_to_all x0 -> x1, starting transfers between devices: none -> 8.31 us  [first_gather(): lax.all_to_all(messages.reshape(chips * slabs, turns * n_axial, lanes), (...]
    pallas_call x12 -> x15, Pallas kernels: 25 us -> 17.3 us  [call(): return lambda *args: called(*args, *after)]
    unnamed x26 -> x19, local copies, waits for them, and re-layouts: 7.6 us -> 3.09 us
    all_to_all x1, blocking collectives: 12.6 us -> 10.7 us  [per_device(): lax.all_to_all(gram, ('sector', 'slab'), split_axis=0, concat_axis=0, til...]
    ppermute x45 -> x39, waiting for transfers between devices: 16.2 us -> 17.2 us  [the longest x9 7.7 us: slab_exchange(): lax.ppermute(messages[distance], 'slab', partner_perm(slabs, distance))]
  transfers between devices with their start and end apart: 45 -> 40, of which waited for: 13 -> 13; matrix products, arithmetic and copies ran while one was open for 1% -> 3% of each run, Pallas kernels for 14% -> 15%
where the time goes in v2:
time: 100 us; the launch traced here: 99.9 us
  starting transfers between devices  45.6 us (46%)
  Pallas kernels  17.3 us (17%)
  waiting for transfers between devices  17.2 us (17%)
  blocking collectives  10.7 us (11%)
  local copies, waits for them, and re-layouts  4.47 us (4%)
  other arithmetic  3.1 us (3%)
  between operations  1.54 us (2%)
    pallas_call x15, Pallas kernels, call(): return lambda *args: called(*args, *after)  17.3 us
    ppermute x9, starting transfers between devices, slab_exchange(): lax.ppermute(messages[distance], 'slab', partner_perm(slabs, distance))  14.3 us
    all_to_all x1, blocking collectives, per_device(): lax.all_to_all(gram, ('sector', 'slab'), split_axis=0, concat_axis=0, til...  10.7 us
    ppermute x6, starting transfers between devices, sector_gather(): shares.append(lax.ppermute(own, 'sector', perm))  9 us
    all_to_all x1, starting transfers between devices, first_gather(): lax.all_to_all(messages.reshape(chips * slabs, turns * n_axial, lanes), (...  8.31 us
    ppermute x9, waiting for transfers between devices, slab_exchange(): lax.ppermute(messages[distance], 'slab', partner_perm(slabs, distance))  7.7 us
    ppermute x6, starting transfers between devices, neighbour_swap(): outer = lax.ppermute(jnp.where(odd, last, first), axis, across)  6.65 us
    ppermute x6, starting transfers between devices, neighbour_swap(): inner = lax.ppermute(jnp.where(odd, first, last), axis, within)  5.63 us
  transfers between devices with their start and end apart: 40, of which 13 were waited for; matrix products, arithmetic and copies ran while one was open for 3% of the time, Pallas kernels for 15%

profile of v2, /device:TPU:0, one launch (start us, length us, event | category | flops | bytes accessed | tf_op | source)
XLA Modules:
  0.0 99.9 jit_solution(3011023938615164821)
XLA Ops:
  0.6 1.0 multiply_convert_fusion.19
  1.6 0.8 broadcast_in_dim.15
  2.4 8.3 %all-to-all-start = ((f16[16,32,256]{2,1,0:T(8,128)(2,1)}), f16[16,32,256]{2,1,0:T(8,128)(2,1)S(1)}, u32[]{:S(2)}, u32[]{:S(2)}) async-start(f16[16,32,256]{2,1,0:T(8,128)(2,1)} %bitcast.12), calls=%async_computation | async-start | bytes 524288 | tf_op jit(solution)/shard_map/all_to_all | solution.py:651
  10.7 1.6 %copy-done.4 = f32[16,16,8,256]{3,2,1,0:T(8,128)S(1)} copy-done((f32[16,16,8,256]{3,2,1,0:T(8,128)S(1)}, f32[16,16,8,256]{3,2,1,0:T(8,128)}, u32[]{:S(2)}) %copy-start.4) | copy-done | bytes 2097176
  12.6 1.3 %copy-done.1 = f32[16,16,8,256]{3,2,1,0:T(8,128)} copy-done((f32[16,16,8,256]{3,2,1,0:T(8,128)}, f32[16,16,8,256]{3,2,1,0:T(8,128)S(1)}, u32[]{:S(2)}) %copy-start.1) | copy-done | bytes 2097176
  14.0 3.8 %collective-permute-start.3 = (f16[16,8,256]{2,1,0:T(8,128)(2,1)S(1)}, f16[16,8,256]{2,1,0:T(8,128)(2,1)}, u32[]{:S(2)}, u32[]{:S(2)}) collective-permute-start(f16[16,8,256]{2,1,0:T(8,128)(2,1)S(1)} %get-tuple-element.89), channel_id=1, source_target_pairs={{4,8},{8,4},{12,16},{16,12},{20,24},{24,20},{28,0},{0,28},{5,9},{9... | collective-permute-start | bytes 196616 | tf_op jit(solution)/shard_map/ppermute | solution.py:589
  17.9 1.5 %collective-permute-start.4 = (f16[16,8,256]{2,1,0:T(8,128)(2,1)S(1)}, f16[16,8,256]{2,1,0:T(8,128)(2,1)S(1)}, u32[]{:S(2)}, u32[]{:S(2)}) collective-permute-start(f16[16,8,256]{2,1,0:T(8,128)(2,1)S(1)} %get-tuple-element.88), channel_id=1, source_target_pairs={{0,1},{1,0},{2,3},{3,2},{4,5},{5,4},{6,7},{7,6},{8,9},{9,8},{10,11... | collective-permute-start | bytes 196616 | tf_op jit(solution)/shard_map/ppermute | solution.py:588
  19.4 0.7 collective-permute-start.5
  20.1 1.1 %volume_matrices.1 = (bf16[2,128,256]{2,1,0:T(8,128)(2,1)S(1)}, bf16[2,128,128]{2,1,0:T(8,128)(2,1)S(1)}) custom-call(f32[3,8,8]{2,1,0:T(8,128)S(1)} %copy-done.7), custom_call_target="tpu_custom_call" | custom-call | flops 1000 | bytes 1000 | tf_op jit(solution)/shard_map/volume_matrices/pallas_call | solution.py:45
  21.6 1.0 convert_multiply_fusion.28
  22.8 1.4 %collective-permute-done = f16[16,32,256]{2,1,0:T(8,128)(2,1)S(1)} collective-permute-done((f16[16,32,256]{2,1,0:T(8,128)(2,1)S(1)}, f16[16,32,256]{2,1,0:T(8,128)(2,1)S(1)}, u32[]{:S(2)}, u32[]{:S(2)}) %collective-permute-start) | collective-permute-done | bytes 262176 | tf_op jit(solution)/shard_map/ppermute | solution.py:659
  24.3 2.0 %bem_partial.3 = (f32[256,256]{1,0:T(8,128)S(1)}, f32[3,256,256]{2,1,0:T(8,128)S(1)}) custom-call(s32[9]{0:T(128)S(1)} %stack.67.refs_0_, bf16[2,512,1024]{2,1,0:T(8,128)(2,1)S(1)} %copy-done, f32[8,16,256]{2,1,0:T(8,128)S(1)} %get-tuple-element.31.refs_2_, f32[128,256]{1,0:T(8,128)S(1)} %bitcast.119, f32[128,256]{1,0:T(8,128)S(1)} %bitcast.123, ...), custom_call_target="tpu_custom_call" | custom-call | flops 1000 | bytes 1000 | tf_op jit(solution)/shard_map/bem_partial/pallas_call | solution.py:45
  26.7 4.2 %collective-permute-start.6 = (f16[256,256]{1,0:T(8,128)(2,1)S(1)}, f16[256,256]{1,0:T(8,128)(2,1)S(1)}, u32[]{:S(2)}, u32[]{:S(2)}) collective-permute-start(f16[256,256]{1,0:T(8,128)(2,1)S(1)} %get-tuple-element.74), channel_id=1, source_target_pairs={{0,1},{1,0},{2,3},{3,2},{4,5},{5,4},{6,7},{7,6},{8,9},{9,8},{10,11... | collective-permute-start | bytes 393224 | tf_op jit(solution)/shard_map/ppermute | solution.py:573
  30.9 1.5 %collective-permute-start.8 = (f16[256,256]{1,0:T(8,128)(2,1)S(1)}, f16[256,256]{1,0:T(8,128)(2,1)S(1)}, u32[]{:S(2)}, u32[]{:S(2)}) collective-permute-start(f16[256,256]{1,0:T(8,128)(2,1)S(1)} %get-tuple-element.73), channel_id=1, source_target_pairs={{0,3},{1,2},{2,1},{3,0},{4,7},{5,6},{6,5},{7,4},{8,11},{9,10},{10,... | collective-permute-start | bytes 393224 | tf_op jit(solution)/shard_map/ppermute | solution.py:573
  32.9 1.5 %volume_bulk.3 = (f32[16,16,8,256]{3,2,1,0:T(8,128)S(1)}, f32[256,256]{1,0:T(8,128)S(1)}) custom-call(f32[16,16,8,256]{3,2,1,0:T(8,128)S(1)} %copy-done.2, f32[16,16,8,128]{3,2,1,0:T(8,128)S(1)} %broadcast_in_dim.6.refs_1_, bf16[2,128,256]{2,1,0:T(8,128)(2,1)S(1)} %get-tuple-element.29.refs_2_, ...), custom_call_target="tpu_custom_call", output_to_operand_aliasing={{1}: (4, {})} | custom-call | flops 1000 | bytes 1000 | tf_op jit(solution)/shard_map/volume_bulk/pallas_call | solution.py:45
  34.4 0.7 finish_first_kernel.1
  35.2 1.5 %volume_bulk.4 = (f32[16,16,8,256]{3,2,1,0:T(8,128)S(1)}, f32[256,256]{1,0:T(8,128)S(1)}) custom-call(f32[16,16,8,256]{3,2,1,0:T(8,128)S(1)} %get-tuple-element.40.refs_0_, f32[16,16,8,128]{3,2,1,0:T(8,128)S(1)} %broadcast_in_dim.6.refs_1_, bf16[2,128,256]{2,1,0:T(8,128)(2,1)S(1)} %get-tuple-element.29.refs_2_, ...), custom_call_target="tpu_custom_call", output_to_operand_aliasing={{1}: (4, {})} | custom-call | flops 1000 | bytes 1000 | tf_op jit(solution)/shard_map/volume_bulk/pallas_call | solution.py:45
  36.9 2.3 %collective-permute-done.7 = f16[256,256]{1,0:T(8,128)(2,1)S(1)} collective-permute-done((f16[256,256]{1,0:T(8,128)(2,1)S(1)}, f16[256,256]{1,0:T(8,128)(2,1)S(1)}, u32[]{:S(2)}, u32[]{:S(2)}) %collective-permute-start.7) | collective-permute-done | bytes 131104 | tf_op jit(solution)/shard_map/ppermute | solution.py:573
  39.4 2.9 %collective-permute-done.10 = f16[16,8,256]{2,1,0:T(8,128)(2,1)S(1)} collective-permute-done((f16[16,8,256]{2,1,0:T(8,128)(2,1)S(1)}, f16[16,8,256]{2,1,0:T(8,128)(2,1)S(1)}, u32[]{:S(2)}, u32[]{:S(2)}) %collective-permute-start.10) | collective-permute-done | bytes 65568 | tf_op jit(solution)/shard_map/ppermute | solution.py:589
  42.6 4.3 %collective-permute-start.14 = (f16[128,256]{1,0:T(8,128)(2,1)S(1)}, f16[128,256]{1,0:T(8,128)(2,1)S(1)}, u32[]{:S(2)}, u32[]{:S(2)}) collective-permute-start(f16[128,256]{1,0:T(8,128)(2,1)S(1)} %get-tuple-element.57), channel_id=1, source_target_pairs={{0,8},{4,12},{8,0},{12,4},{16,24},{20,28},{24,16},{28,20},{1,9},{5... | collective-permute-start | bytes 196616 | tf_op jit(solution)/shard_map/ppermute | solution.py:620
  47.0 2.0 %collective-permute-start.12 = (f16[16,8,256]{2,1,0:T(8,128)(2,1)S(1)}, f16[16,8,256]{2,1,0:T(8,128)(2,1)S(1)}, u32[]{:S(2)}, u32[]{:S(2)}) collective-permute-start(f16[16,8,256]{2,1,0:T(8,128)(2,1)S(1)} %get-tuple-element.63), channel_id=1, source_target_pairs={{0,1},{1,0},{2,3},{3,2},{4,5},{5,4},{6,7},{7,6},{8,9},{9,8},{10,11... | collective-permute-start | bytes 196616 | tf_op jit(solution)/shard_map/ppermute | solution.py:588
  49.0 0.8 collective-permute-start.13
  49.9 0.6 collective-permute-start.17
  50.6 0.5 collective-permute-done.19
  51.4 0.4 collective-permute-done.15
  51.9 2.1 %bem_partial.4 = (f32[256,256]{1,0:T(8,128)S(1)}, f32[3,256,256]{2,1,0:T(8,128)S(1)}) custom-call(s32[9]{0:T(128)S(1)} %stack.76.refs_0_, bf16[2,512,1024]{2,1,0:T(8,128)(2,1)S(1)} %copy-done, f32[8,16,256]{2,1,0:T(8,128)S(1)} %get-tuple-element.44.refs_2_, f32[128,256]{1,0:T(8,128)S(1)} %get-tuple-element.56.refs_3_, ...), custom_call_target="tpu_custom_call" | custom-call | flops 1000 | bytes 1000 | tf_op jit(solution)/shard_map/bem_partial/pallas_call | solution.py:45
  54.0 2.8 %collective-permute-start.21 = (f16[256,256]{1,0:T(8,128)(2,1)S(1)}, f16[256,256]{1,0:T(8,128)(2,1)S(1)}, u32[]{:S(2)}, u32[]{:S(2)}) collective-permute-start(f16[256,256]{1,0:T(8,128)(2,1)S(1)} %get-tuple-element.71), channel_id=1, source_target_pairs={{0,1},{1,0},{2,3},{3,2},{4,5},{5,4},{6,7},{7,6},{8,9},{9,8},{10,11... | collective-permute-start | bytes 393224 | tf_op jit(solution)/shard_map/ppermute | solution.py:573
  57.1 1.4 %collective-permute-start.23 = (f16[256,256]{1,0:T(8,128)(2,1)S(1)}, f16[256,256]{1,0:T(8,128)(2,1)S(1)}, u32[]{:S(2)}, u32[]{:S(2)}) collective-permute-start(f16[256,256]{1,0:T(8,128)(2,1)S(1)} %get-tuple-element.70), channel_id=1, source_target_pairs={{0,3},{1,2},{2,1},{3,0},{4,7},{5,6},{6,5},{7,4},{8,11},{9,10},{10,... | collective-permute-start | bytes 393224 | tf_op jit(solution)/shard_map/ppermute | solution.py:573
  58.6 0.9 finish_second_kernel.1
  59.5 1.5 %volume_bulk.5 = (f32[16,16,8,256]{3,2,1,0:T(8,128)S(1)}, f32[256,256]{1,0:T(8,128)S(1)}) custom-call(f32[16,16,8,256]{3,2,1,0:T(8,128)S(1)} %get-tuple-element.47.refs_0_, f32[16,16,8,128]{3,2,1,0:T(8,128)S(1)} %broadcast_in_dim.6.refs_1_, bf16[2,128,256]{2,1,0:T(8,128)(2,1)S(1)} %get-tuple-element.29.refs_2_, ...), custom_call_target="tpu_custom_call", output_to_operand_aliasing={{1}: (4, {})} | custom-call | flops 1000 | bytes 1000 | tf_op jit(solution)/shard_map/volume_bulk/pallas_call | solution.py:45
  61.2 0.6 collective-permute-start.25
  61.8 3.7 %collective-permute-done.22 = f16[256,256]{1,0:T(8,128)(2,1)S(1)} collective-permute-done((f16[256,256]{1,0:T(8,128)(2,1)S(1)}, f16[256,256]{1,0:T(8,128)(2,1)S(1)}, u32[]{:S(2)}, u32[]{:S(2)}) %collective-permute-start.22) | collective-permute-done | bytes 131104 | tf_op jit(solution)/shard_map/ppermute | solution.py:573
  65.8 0.9 collective-permute-done.25
  66.8 0.6 collective-permute-start.31
  67.4 3.9 %collective-permute-start.29 = (f16[128,256]{1,0:T(8,128)(2,1)S(1)}, f16[128,256]{1,0:T(8,128)(2,1)S(1)}, u32[]{:S(2)}, u32[]{:S(2)}) collective-permute-start(f16[128,256]{1,0:T(8,128)(2,1)S(1)} %get-tuple-element.55), channel_id=1, source_target_pairs={{0,8},{4,12},{8,0},{12,4},{16,24},{20,28},{24,16},{28,20},{1,9},{5... | collective-permute-start | bytes 196616 | tf_op jit(solution)/shard_map/ppermute | solution.py:620
  71.3 1.8 %collective-permute-start.27 = (f16[16,8,256]{2,1,0:T(8,128)(2,1)S(1)}, f16[16,8,256]{2,1,0:T(8,128)(2,1)S(1)}, u32[]{:S(2)}, u32[]{:S(2)}) collective-permute-start(f16[16,8,256]{2,1,0:T(8,128)(2,1)S(1)} %get-tuple-element.59), channel_id=1, source_target_pairs={{0,1},{1,0},{2,3},{3,2},{4,5},{5,4},{6,7},{7,6},{8,9},{9,8},{10,11... | collective-permute-start | bytes 196616 | tf_op jit(solution)/shard_map/ppermute | solution.py:588
  73.1 0.7 collective-permute-start.28
  73.9 1.1 %collective-permute-done.31 = f16[128,256]{1,0:T(8,128)(2,1)S(1)} collective-permute-done((f16[128,256]{1,0:T(8,128)(2,1)S(1)}, f16[128,256]{1,0:T(8,128)(2,1)S(1)}, u32[]{:S(2)}, u32[]{:S(2)}) %collective-permute-start.31) | collective-permute-done | bytes 65568 | tf_op jit(solution)/shard_map/ppermute | solution.py:620
  75.1 0.5 collective-permute-start.30
  75.6 0.6 collective-permute-done.32
  76.5 2.1 %bem_partial.5 = (f32[256,256]{1,0:T(8,128)S(1)}, f32[3,256,256]{2,1,0:T(8,128)S(1)}) custom-call(s32[9]{0:T(128)S(1)} %stack.76.refs_0_, bf16[2,512,1024]{2,1,0:T(8,128)(2,1)S(1)} %copy-done, f32[8,16,256]{2,1,0:T(8,128)S(1)} %get-tuple-element.51.refs_2_, f32[128,256]{1,0:T(8,128)S(1)} %get-tuple-element.54.refs_3_, ...), custom_call_target="tpu_custom_call" | custom-call | flops 1000 | bytes 1000 | tf_op jit(solution)/shard_map/bem_partial/pallas_call | solution.py:45
  78.6 2.4 %collective-permute-start.36 = (f16[128,256]{1,0:T(8,128)(2,1)S(1)}, f16[128,256]{1,0:T(8,128)(2,1)S(1)}, u32[]{:S(2)}, u32[]{:S(2)}) collective-permute-start(f16[128,256]{1,0:T(8,128)(2,1)S(1)} %get-tuple-element.68), channel_id=1, source_target_pairs={{0,1},{1,0},{2,3},{3,2},{4,5},{5,4},{6,7},{7,6},{8,9},{9,8},{10,11... | collective-permute-start | bytes 196616 | tf_op jit(solution)/shard_map/ppermute | solution.py:573
  81.1 1.5 %collective-permute-start.38 = (f16[128,256]{1,0:T(8,128)(2,1)S(1)}, f16[128,256]{1,0:T(8,128)(2,1)S(1)}, u32[]{:S(2)}, u32[]{:S(2)}) collective-permute-start(f16[128,256]{1,0:T(8,128)(2,1)S(1)} %get-tuple-element.67), channel_id=1, source_target_pairs={{0,3},{1,2},{2,1},{3,0},{4,7},{5,6},{6,5},{7,4},{8,11},{9,10},{10,... | collective-permute-start | bytes 196616 | tf_op jit(solution)/shard_map/ppermute | solution.py:573
  82.7 1.1 %collective-permute-done.35 = f16[16,128]{1,0:T(8,128)(2,1)S(1)} collective-permute-done((f16[16,128]{1,0:T(8,128)(2,1)S(1)}, f16[16,128]{1,0:T(8,128)(2,1)S(1)}, u32[]{:S(2)}, u32[]{:S(2)}) %collective-permute-start.35) | collective-permute-done | bytes 4128 | tf_op jit(solution)/shard_map/ppermute | solution.py:678
  83.8 1.2 %finish_third_kernel.1.refs_2_ = f32[5,8,128]{2,1,0:T(8,128)S(1)} custom-call(f32[16,16,8,256]{3,2,1,0:T(8,128)S(1)} %get-tuple-element.49.refs_0_, f32[8,16,256]{2,1,0:T(8,128)S(1)} %bitcast.114, f32[16,8,256]{2,1,0:T(8,128)S(1)} %get-tuple-element.94.refs_2_, f32[16,8,256]{2,1,0:T(8,128)S(1)} %get-tuple-element.93.refs_3_, ...), custom_call_target="tpu_custom_call" | custom-call | flops 1000 | bytes 1000 | tf_op jit(solution)/shard_map/finish_third_kernel/pallas_call | solution.py:45
  85.0 1.6 %collective-permute-done.37 = f16[128,256]{1,0:T(8,128)(2,1)S(1)} collective-permute-done((f16[128,256]{1,0:T(8,128)(2,1)S(1)}, f16[128,256]{1,0:T(8,128)(2,1)S(1)}, u32[]{:S(2)}, u32[]{:S(2)}) %collective-permute-start.37) | collective-permute-done | bytes 65568 | tf_op jit(solution)/shard_map/ppermute | solution.py:573
  86.8 10.7 %all_to_all.10.refs_0_ = f32[32,1,1152]{2,1,0:T(1,128)S(1)} all-to-all(f32[32,1,1152]{2,1,0:T(1,128)S(1)} %local_gram.1), channel_id=1, replica_groups=mesh['sector'=8,'slab'=4] {'sector','slab'}, dimensions={0} | all-to-all | bytes 294912 | tf_op jit(solution)/shard_map/all_to_all | solution.py:761
  97.5 2.2 %final_solution.1 = (f32[16,16,8,256]{3,2,1,0:T(8,128)}, f32[8,16,256]{2,1,0:T(8,128)}) custom-call(f32[32,1,1152]{2,1,0:T(1,128)S(1)} %all_to_all.10.refs_0_, f32[16,16,8,256]{3,2,1,0:T(8,128)S(1)} %copy-done.2, f32[16,16,8,256]{3,2,1,0:T(8,128)S(1)} %pass_after.2.refs_6_.refs_2_, f32[16,16,8,256]{3,2,1,0:T(8,128)S(1)} %pass_after.3.refs_7_.refs_3_, ...), custom_call_target="tpu_custom_call" | custom-call | flops 1000 | bytes 1000 | tf_op jit(solution)/shard_map/final_solution/pallas_call | solution.py:45
  (117 shorter events, 4.6 us)
Async XLA Ops:
  0.6 19.4 %copy-start.7 = (f32[3,8,8]{2,1,0:T(8,128)S(1)}, f32[3,8,8]{2,1,0:T(8,128)}, u32[]{:S(2)}) copy-start(f32[3,8,8]{2,1,0:T(8,128)} %refs_0_.3) | copy-start | bytes 2308
  0.6 20.6 %copy-start.8 = (f32[16,16,8]{1,2,0:T(8,128)S(1)}, f32[16,16,8]{1,2,0:T(8,128)}, u32[]{:S(2)}) copy-start(f32[16,16,8]{1,2,0:T(8,128)} %param.13) | copy-start | bytes 24580
  2.4 20.2 %all-to-all-start = ((f16[16,32,256]{2,1,0:T(8,128)(2,1)}), f16[16,32,256]{2,1,0:T(8,128)(2,1)S(1)}, u32[]{:S(2)}, u32[]{:S(2)}) async-start(f16[16,32,256]{2,1,0:T(8,128)(2,1)} %bitcast.12), calls=%async_computation | async-start | bytes 524288 | tf_op jit(solution)/shard_map/all_to_all | solution.py:651
  10.7 1.6 %copy-start.4 = (f32[16,16,8,256]{3,2,1,0:T(8,128)S(1)}, f32[16,16,8,256]{3,2,1,0:T(8,128)}, u32[]{:S(2)}) copy-start(f32[16,16,8,256]{3,2,1,0:T(8,128)} %refs_0_.2) | copy-start | bytes 6291460
  13.9 7.6 %collective-permute-start.2 = (f16[16,8,256]{2,1,0:T(8,128)(2,1)S(1)}, f16[16,8,256]{2,1,0:T(8,128)(2,1)S(1)}, u32[]{:S(2)}, u32[]{:S(2)}) collective-permute-start(f16[16,8,256]{2,1,0:T(8,128)(2,1)S(1)} %get-tuple-element.90), channel_id=1, source_target_pairs={{0,4},{4,0},{8,12},{12,8},{16,20},{20,16},{24,28},{28,24},{1,5},{5... | collective-permute-start | bytes 196616 | tf_op jit(solution)/shard_map/ppermute | solution.py:588
  14.0 7.6 %collective-permute-start.3 = (f16[16,8,256]{2,1,0:T(8,128)(2,1)S(1)}, f16[16,8,256]{2,1,0:T(8,128)(2,1)}, u32[]{:S(2)}, u32[]{:S(2)}) collective-permute-start(f16[16,8,256]{2,1,0:T(8,128)(2,1)S(1)} %get-tuple-element.89), channel_id=1, source_target_pairs={{4,8},{8,4},{12,16},{16,12},{20,24},{24,20},{28,0},{0,28},{5,9},{9... | collective-permute-start | bytes 196616 | tf_op jit(solution)/shard_map/ppermute | solution.py:589
  17.9 8.8 %collective-permute-start.4 = (f16[16,8,256]{2,1,0:T(8,128)(2,1)S(1)}, f16[16,8,256]{2,1,0:T(8,128)(2,1)S(1)}, u32[]{:S(2)}, u32[]{:S(2)}) collective-permute-start(f16[16,8,256]{2,1,0:T(8,128)(2,1)S(1)} %get-tuple-element.88), channel_id=1, source_target_pairs={{0,1},{1,0},{2,3},{3,2},{4,5},{5,4},{6,7},{7,6},{8,9},{9,8},{10,11... | collective-permute-start | bytes 196616 | tf_op jit(solution)/shard_map/ppermute | solution.py:588
  19.4 7.3 %collective-permute-start.5 = (f16[16,8,256]{2,1,0:T(8,128)(2,1)S(1)}, f16[16,8,256]{2,1,0:T(8,128)(2,1)S(1)}, u32[]{:S(2)}, u32[]{:S(2)}) collective-permute-start(f16[16,8,256]{2,1,0:T(8,128)(2,1)S(1)} %get-tuple-element.87), channel_id=1, source_target_pairs={{1,2},{2,1},{5,6},{6,5},{9,10},{10,9},{13,14},{14,13},{17,18},{18,... | collective-permute-start | bytes 196616 | tf_op jit(solution)/shard_map/ppermute | solution.py:589
  21.3 3.0 %copy-start = (bf16[2,512,1024]{2,1,0:T(8,128)(2,1)S(1)}, bf16[2,512,1024]{2,1,0:T(8,128)(2,1)}, u32[]{:S(2)}) copy-start(bf16[2,512,1024]{2,1,0:T(8,128)(2,1)} %refs_1_.7) | copy-start | bytes 6291460
  21.3 3.0 %copy-start.6 = (f32[8,16,256]{2,1,0:T(8,128)S(1)}, f32[8,16,256]{2,1,0:T(8,128)}, u32[]{:S(2)}) copy-start(f32[8,16,256]{2,1,0:T(8,128)} %refs_11_.1) | copy-start | bytes 393220
  22.6 1.6 %collective-permute-start = (f16[16,32,256]{2,1,0:T(8,128)(2,1)S(1)}, f16[16,32,256]{2,1,0:T(8,128)(2,1)S(1)}, u32[]{:S(2)}, u32[]{:S(2)}) collective-permute-start(f16[16,32,256]{2,1,0:T(8,128)(2,1)S(1)} %all-to-all-done), channel_id=1, source_target_pairs={{0,4},{4,0},{8,12},{12,8},{16,20},{20,16},{24,28},{28,24},{1,5},{5... | collective-permute-start | bytes 786440 | tf_op jit(solution)/shard_map/ppermute | solution.py:659
  26.3 6.5 %copy-start.2 = (f32[16,16,8,256]{3,2,1,0:T(8,128)S(1)}, f32[16,16,8,256]{3,2,1,0:T(8,128)}, u32[]{:S(2)}) copy-start(f32[16,16,8,256]{3,2,1,0:T(8,128)} %copy-done.1) | copy-start | bytes 6291460
  26.4 6.0 %collective-permute-start.1 = (f16[16,128]{1,0:T(8,128)(2,1)S(1)}, f16[16,128]{1,0:T(8,128)(2,1)S(1)}, u32[]{:S(2)}, u32[]{:S(2)}) collective-permute-start(f16[16,128]{1,0:T(8,128)(2,1)S(1)} %slice.152), channel_id=1, source_target_pairs={{0,4},{4,0},{8,12},{12,8},{16,20},{20,16},{24,28},{28,24},{1,5},{5... | collective-permute-start | bytes 12296 | tf_op jit(solution)/shard_map/ppermute | solution.py:678
  26.7 10.2 %collective-permute-start.6 = (f16[256,256]{1,0:T(8,128)(2,1)S(1)}, f16[256,256]{1,0:T(8,128)(2,1)S(1)}, u32[]{:S(2)}, u32[]{:S(2)}) collective-permute-start(f16[256,256]{1,0:T(8,128)(2,1)S(1)} %get-tuple-element.74), channel_id=1, source_target_pairs={{0,1},{1,0},{2,3},{3,2},{4,5},{5,4},{6,7},{7,6},{8,9},{9,8},{10,11... | collective-permute-start | bytes 393224 | tf_op jit(solution)/shard_map/ppermute | solution.py:573
  30.9 8.3 %collective-permute-start.7 = (f16[256,256]{1,0:T(8,128)(2,1)S(1)}, f16[256,256]{1,0:T(8,128)(2,1)S(1)}, u32[]{:S(2)}, u32[]{:S(2)}) collective-permute-start(f16[256,256]{1,0:T(8,128)(2,1)S(1)} %get-tuple-element.72), channel_id=1, source_target_pairs={{0,2},{1,3},{2,0},{3,1},{4,6},{5,7},{6,4},{7,5},{8,10},{9,11},{10,... | collective-permute-start | bytes 393224 | tf_op jit(solution)/shard_map/ppermute | solution.py:573
  30.9 8.3 %collective-permute-start.8 = (f16[256,256]{1,0:T(8,128)(2,1)S(1)}, f16[256,256]{1,0:T(8,128)(2,1)S(1)}, u32[]{:S(2)}, u32[]{:S(2)}) collective-permute-start(f16[256,256]{1,0:T(8,128)(2,1)S(1)} %get-tuple-element.73), channel_id=1, source_target_pairs={{0,3},{1,2},{2,1},{3,0},{4,7},{5,6},{6,5},{7,4},{8,11},{9,10},{10,... | collective-permute-start | bytes 393224 | tf_op jit(solution)/shard_map/ppermute | solution.py:573
  32.8 1.6 %copy-start.3 = (f32[16,16,8,256]{3,2,1,0:T(8,128)S(1)}, f32[16,16,8,256]{3,2,1,0:T(8,128)}, u32[]{:S(2)}) copy-start(f32[16,16,8,256]{3,2,1,0:T(8,128)} %refs_6_.1) | copy-start | bytes 6291460
  32.8 1.6 %copy-start.5 = (f32[8,16,256]{2,1,0:T(8,128)S(1)}, f32[8,16,256]{2,1,0:T(8,128)}, u32[]{:S(2)}) copy-start(f32[8,16,256]{2,1,0:T(8,128)} %refs_4_.1) | copy-start | bytes 393220
  36.8 5.6 %collective-permute-start.10 = (f16[16,8,256]{2,1,0:T(8,128)(2,1)S(1)}, f16[16,8,256]{2,1,0:T(8,128)(2,1)S(1)}, u32[]{:S(2)}, u32[]{:S(2)}) collective-permute-start(f16[16,8,256]{2,1,0:T(8,128)(2,1)S(1)} %get-tuple-element.64), channel_id=1, source_target_pairs={{4,8},{8,4},{12,16},{16,12},{20,24},{24,20},{28,0},{0,28},{5,9},{9... | collective-permute-start | bytes 196616 | tf_op jit(solution)/shard_map/ppermute | solution.py:589
  36.8 5.5 %collective-permute-start.9 = (f16[16,8,256]{2,1,0:T(8,128)(2,1)S(1)}, f16[16,8,256]{2,1,0:T(8,128)(2,1)S(1)}, u32[]{:S(2)}, u32[]{:S(2)}) collective-permute-start(f16[16,8,256]{2,1,0:T(8,128)(2,1)S(1)} %get-tuple-element.65), channel_id=1, source_target_pairs={{0,4},{4,0},{8,12},{12,8},{16,20},{20,16},{24,28},{28,24},{1,5},{5... | collective-permute-start | bytes 196616 | tf_op jit(solution)/shard_map/ppermute | solution.py:588
  39.4 3.2 %collective-permute-start.11 = (f16[128,256]{1,0:T(8,128)(2,1)S(1)}, f16[128,256]{1,0:T(8,128)(2,1)S(1)}, u32[]{:S(2)}, u32[]{:S(2)}) collective-permute-start(f16[128,256]{1,0:T(8,128)(2,1)S(1)} %get-tuple-element.57), channel_id=1, source_target_pairs={{0,4},{4,0},{8,12},{12,8},{16,20},{20,16},{24,28},{28,24},{1,5},{5... | collective-permute-start | bytes 196616 | tf_op jit(solution)/shard_map/ppermute | solution.py:623
  42.4 7.4 %collective-permute-start.18 = (f16[128,256]{1,0:T(8,128)(2,1)S(1)}, f16[128,256]{1,0:T(8,128)(2,1)S(1)}, u32[]{:S(2)}, u32[]{:S(2)}) collective-permute-start(f16[128,256]{1,0:T(8,128)(2,1)S(1)} %get-tuple-element.57), channel_id=1, source_target_pairs={{0,24},{4,28},{8,16},{12,20},{16,8},{20,12},{24,0},{28,4},{1,25},{... | collective-permute-start | bytes 196616 | tf_op jit(solution)/shard_map/ppermute | solution.py:620
  42.5 7.5 %collective-permute-start.16 = (f16[128,256]{1,0:T(8,128)(2,1)S(1)}, f16[128,256]{1,0:T(8,128)(2,1)S(1)}, u32[]{:S(2)}, u32[]{:S(2)}) collective-permute-start(f16[128,256]{1,0:T(8,128)(2,1)S(1)} %get-tuple-element.57), channel_id=1, source_target_pairs={{0,16},{4,20},{8,24},{12,28},{16,0},{20,4},{24,8},{28,12},{1,17},{... | collective-permute-start | bytes 196616 | tf_op jit(solution)/shard_map/ppermute | solution.py:620
  42.6 7.9 %collective-permute-start.14 = (f16[128,256]{1,0:T(8,128)(2,1)S(1)}, f16[128,256]{1,0:T(8,128)(2,1)S(1)}, u32[]{:S(2)}, u32[]{:S(2)}) collective-permute-start(f16[128,256]{1,0:T(8,128)(2,1)S(1)} %get-tuple-element.57), channel_id=1, source_target_pairs={{0,8},{4,12},{8,0},{12,4},{16,24},{20,28},{24,16},{28,20},{1,9},{5... | collective-permute-start | bytes 196616 | tf_op jit(solution)/shard_map/ppermute | solution.py:620
  47.0 10.2 %collective-permute-start.12 = (f16[16,8,256]{2,1,0:T(8,128)(2,1)S(1)}, f16[16,8,256]{2,1,0:T(8,128)(2,1)S(1)}, u32[]{:S(2)}, u32[]{:S(2)}) collective-permute-start(f16[16,8,256]{2,1,0:T(8,128)(2,1)S(1)} %get-tuple-element.63), channel_id=1, source_target_pairs={{0,1},{1,0},{2,3},{3,2},{4,5},{5,4},{6,7},{7,6},{8,9},{9,8},{10,11... | collective-permute-start | bytes 196616 | tf_op jit(solution)/shard_map/ppermute | solution.py:588
  49.0 9.6 %collective-permute-start.13 = (f16[16,8,256]{2,1,0:T(8,128)(2,1)S(1)}, f16[16,8,256]{2,1,0:T(8,128)(2,1)S(1)}, u32[]{:S(2)}, u32[]{:S(2)}) collective-permute-start(f16[16,8,256]{2,1,0:T(8,128)(2,1)S(1)} %get-tuple-element.62), channel_id=1, source_target_pairs={{1,2},{2,1},{5,6},{6,5},{9,10},{10,9},{13,14},{14,13},{17,18},{18,... | collective-permute-start | bytes 196616 | tf_op jit(solution)/shard_map/ppermute | solution.py:589
  49.8 1.3 %collective-permute-start.19 = (f16[128,256]{1,0:T(8,128)(2,1)S(1)}, f16[128,256]{1,0:T(8,128)(2,1)S(1)}, u32[]{:S(2)}, u32[]{:S(2)}) collective-permute-start(f16[128,256]{1,0:T(8,128)(2,1)S(1)} %collective-permute-done.18), channel_id=1, source_target_pairs={{0,4},{4,0},{8,12},{12,8},{16,20},{20,16},{24,28},{28,24},{1,5},{5... | collective-permute-start | bytes 196616 | tf_op jit(solution)/shard_map/ppermute | solution.py:623
  49.9 1.5 %collective-permute-start.17 = (f16[128,256]{1,0:T(8,128)(2,1)S(1)}, f16[128,256]{1,0:T(8,128)(2,1)S(1)}, u32[]{:S(2)}, u32[]{:S(2)}) collective-permute-start(f16[128,256]{1,0:T(8,128)(2,1)S(1)} %collective-permute-done.16), channel_id=1, source_target_pairs={{0,4},{4,0},{8,12},{12,8},{16,20},{20,16},{24,28},{28,24},{1,5},{5... | collective-permute-start | bytes 196616 | tf_op jit(solution)/shard_map/ppermute | solution.py:623
  50.5 1.3 %collective-permute-start.15 = (f16[128,256]{1,0:T(8,128)(2,1)S(1)}, f16[128,256]{1,0:T(8,128)(2,1)S(1)}, u32[]{:S(2)}, u32[]{:S(2)}) collective-permute-start(f16[128,256]{1,0:T(8,128)(2,1)S(1)} %collective-permute-done.14), channel_id=1, source_target_pairs={{0,4},{4,0},{8,12},{12,8},{16,20},{20,16},{24,28},{28,24},{1,5},{5... | collective-permute-start | bytes 196616 | tf_op jit(solution)/shard_map/ppermute | solution.py:623
  54.0 7.8 %collective-permute-start.21 = (f16[256,256]{1,0:T(8,128)(2,1)S(1)}, f16[256,256]{1,0:T(8,128)(2,1)S(1)}, u32[]{:S(2)}, u32[]{:S(2)}) collective-permute-start(f16[256,256]{1,0:T(8,128)(2,1)S(1)} %get-tuple-element.71), channel_id=1, source_target_pairs={{0,1},{1,0},{2,3},{3,2},{4,5},{5,4},{6,7},{7,6},{8,9},{9,8},{10,11... | collective-permute-start | bytes 393224 | tf_op jit(solution)/shard_map/ppermute | solution.py:573
  56.8 1.8 %collective-permute-start.20 = (f16[16,128]{1,0:T(8,128)(2,1)S(1)}, f16[16,128]{1,0:T(8,128)(2,1)S(1)}, u32[]{:S(2)}, u32[]{:S(2)}) collective-permute-start(f16[16,128]{1,0:T(8,128)(2,1)S(1)} %slice.157), channel_id=1, source_target_pairs={{0,4},{4,0},{8,12},{12,8},{16,20},{20,16},{24,28},{28,24},{1,5},{5... | collective-permute-start | bytes 12296 | tf_op jit(solution)/shard_map/ppermute | solution.py:678
  56.8 8.7 %collective-permute-start.22 = (f16[256,256]{1,0:T(8,128)(2,1)S(1)}, f16[256,256]{1,0:T(8,128)(2,1)S(1)}, u32[]{:S(2)}, u32[]{:S(2)}) collective-permute-start(f16[256,256]{1,0:T(8,128)(2,1)S(1)} %get-tuple-element.69), channel_id=1, source_target_pairs={{0,2},{1,3},{2,0},{3,1},{4,6},{5,7},{6,4},{7,5},{8,10},{9,11},{10,... | collective-permute-start | bytes 393224 | tf_op jit(solution)/shard_map/ppermute | solution.py:573
  57.1 8.4 %collective-permute-start.23 = (f16[256,256]{1,0:T(8,128)(2,1)S(1)}, f16[256,256]{1,0:T(8,128)(2,1)S(1)}, u32[]{:S(2)}, u32[]{:S(2)}) collective-permute-start(f16[256,256]{1,0:T(8,128)(2,1)S(1)} %get-tuple-element.70), channel_id=1, source_target_pairs={{0,3},{1,2},{2,1},{3,0},{4,7},{5,6},{6,5},{7,4},{8,11},{9,10},{10,... | collective-permute-start | bytes 393224 | tf_op jit(solution)/shard_map/ppermute | solution.py:573
  61.0 4.7 %collective-permute-start.24 = (f16[16,8,256]{2,1,0:T(8,128)(2,1)S(1)}, f16[16,8,256]{2,1,0:T(8,128)(2,1)S(1)}, u32[]{:S(2)}, u32[]{:S(2)}) collective-permute-start(f16[16,8,256]{2,1,0:T(8,128)(2,1)S(1)} %get-tuple-element.61), channel_id=1, source_target_pairs={{0,4},{4,0},{8,12},{12,8},{16,20},{20,16},{24,28},{28,24},{1,5},{5... | collective-permute-start | bytes 196616 | tf_op jit(solution)/shard_map/ppermute | solution.py:588
  61.2 5.5 %collective-permute-start.25 = (f16[16,8,256]{2,1,0:T(8,128)(2,1)S(1)}, f16[16,8,256]{2,1,0:T(8,128)(2,1)S(1)}, u32[]{:S(2)}, u32[]{:S(2)}) collective-permute-start(f16[16,8,256]{2,1,0:T(8,128)(2,1)S(1)} %get-tuple-element.60), channel_id=1, source_target_pairs={{4,8},{8,4},{12,16},{16,12},{20,24},{24,20},{28,0},{0,28},{5,9},{9... | collective-permute-start | bytes 196616 | tf_op jit(solution)/shard_map/ppermute | solution.py:589
  65.7 1.7 %collective-permute-start.26 = (f16[128,256]{1,0:T(8,128)(2,1)S(1)}, f16[128,256]{1,0:T(8,128)(2,1)S(1)}, u32[]{:S(2)}, u32[]{:S(2)}) collective-permute-start(f16[128,256]{1,0:T(8,128)(2,1)S(1)} %get-tuple-element.55), channel_id=1, source_target_pairs={{0,4},{4,0},{8,12},{12,8},{16,20},{20,16},{24,28},{28,24},{1,5},{5... | collective-permute-start | bytes 196616 | tf_op jit(solution)/shard_map/ppermute | solution.py:623
  66.7 7.1 %collective-permute-start.33 = (f16[128,256]{1,0:T(8,128)(2,1)S(1)}, f16[128,256]{1,0:T(8,128)(2,1)S(1)}, u32[]{:S(2)}, u32[]{:S(2)}) collective-permute-start(f16[128,256]{1,0:T(8,128)(2,1)S(1)} %get-tuple-element.55), channel_id=1, source_target_pairs={{0,24},{4,28},{8,16},{12,20},{16,8},{20,12},{24,0},{28,4},{1,25},{... | collective-permute-start | bytes 196616 | tf_op jit(solution)/shard_map/ppermute | solution.py:620
  66.8 8.2 %collective-permute-start.31 = (f16[128,256]{1,0:T(8,128)(2,1)S(1)}, f16[128,256]{1,0:T(8,128)(2,1)S(1)}, u32[]{:S(2)}, u32[]{:S(2)}) collective-permute-start(f16[128,256]{1,0:T(8,128)(2,1)S(1)} %get-tuple-element.55), channel_id=1, source_target_pairs={{0,16},{4,20},{8,24},{12,28},{16,0},{20,4},{24,8},{28,12},{1,17},{... | collective-permute-start | bytes 196616 | tf_op jit(solution)/shard_map/ppermute | solution.py:620
  67.4 7.7 %collective-permute-start.29 = (f16[128,256]{1,0:T(8,128)(2,1)S(1)}, f16[128,256]{1,0:T(8,128)(2,1)S(1)}, u32[]{:S(2)}, u32[]{:S(2)}) collective-permute-start(f16[128,256]{1,0:T(8,128)(2,1)S(1)} %get-tuple-element.55), channel_id=1, source_target_pairs={{0,8},{4,12},{8,0},{12,4},{16,24},{20,28},{24,16},{28,20},{1,9},{5... | collective-permute-start | bytes 196616 | tf_op jit(solution)/shard_map/ppermute | solution.py:620
  71.3 11.3 %collective-permute-start.27 = (f16[16,8,256]{2,1,0:T(8,128)(2,1)S(1)}, f16[16,8,256]{2,1,0:T(8,128)(2,1)S(1)}, u32[]{:S(2)}, u32[]{:S(2)}) collective-permute-start(f16[16,8,256]{2,1,0:T(8,128)(2,1)S(1)} %get-tuple-element.59), channel_id=1, source_target_pairs={{0,1},{1,0},{2,3},{3,2},{4,5},{5,4},{6,7},{7,6},{8,9},{9,8},{10,11... | collective-permute-start | bytes 196616 | tf_op jit(solution)/shard_map/ppermute | solution.py:588
  73.1 9.5 %collective-permute-start.28 = (f16[16,8,256]{2,1,0:T(8,128)(2,1)S(1)}, f16[16,8,256]{2,1,0:T(8,128)(2,1)S(1)}, u32[]{:S(2)}, u32[]{:S(2)}) collective-permute-start(f16[16,8,256]{2,1,0:T(8,128)(2,1)S(1)} %get-tuple-element.58), channel_id=1, source_target_pairs={{1,2},{2,1},{5,6},{6,5},{9,10},{10,9},{13,14},{14,13},{17,18},{18,... | collective-permute-start | bytes 196616 | tf_op jit(solution)/shard_map/ppermute | solution.py:589
  73.8 1.8 %collective-permute-start.34 = (f16[128,256]{1,0:T(8,128)(2,1)S(1)}, f16[128,256]{1,0:T(8,128)(2,1)S(1)}, u32[]{:S(2)}, u32[]{:S(2)}) collective-permute-start(f16[128,256]{1,0:T(8,128)(2,1)S(1)} %collective-permute-done.33), channel_id=1, source_target_pairs={{0,4},{4,0},{8,12},{12,8},{16,20},{20,16},{24,28},{28,24},{1,5},{5... | collective-permute-start | bytes 196616 | tf_op jit(solution)/shard_map/ppermute | solution.py:623
  75.0 1.3 %collective-permute-start.32 = (f16[128,256]{1,0:T(8,128)(2,1)S(1)}, f16[128,256]{1,0:T(8,128)(2,1)S(1)}, u32[]{:S(2)}, u32[]{:S(2)}) collective-permute-start(f16[128,256]{1,0:T(8,128)(2,1)S(1)} %collective-permute-done.31), channel_id=1, source_target_pairs={{0,4},{4,0},{8,12},{12,8},{16,20},{20,16},{24,28},{28,24},{1,5},{5... | collective-permute-start | bytes 196616 | tf_op jit(solution)/shard_map/ppermute | solution.py:623
  75.1 1.4 %collective-permute-start.30 = (f16[128,256]{1,0:T(8,128)(2,1)S(1)}, f16[128,256]{1,0:T(8,128)(2,1)S(1)}, u32[]{:S(2)}, u32[]{:S(2)}) collective-permute-start(f16[128,256]{1,0:T(8,128)(2,1)S(1)} %collective-permute-done.29), channel_id=1, source_target_pairs={{0,4},{4,0},{8,12},{12,8},{16,20},{20,16},{24,28},{28,24},{1,5},{5... | collective-permute-start | bytes 196616 | tf_op jit(solution)/shard_map/ppermute | solution.py:623
  78.6 6.3 %collective-permute-start.36 = (f16[128,256]{1,0:T(8,128)(2,1)S(1)}, f16[128,256]{1,0:T(8,128)(2,1)S(1)}, u32[]{:S(2)}, u32[]{:S(2)}) collective-permute-start(f16[128,256]{1,0:T(8,128)(2,1)S(1)} %get-tuple-element.68), channel_id=1, source_target_pairs={{0,1},{1,0},{2,3},{3,2},{4,5},{5,4},{6,7},{7,6},{8,9},{9,8},{10,11... | collective-permute-start | bytes 196616 | tf_op jit(solution)/shard_map/ppermute | solution.py:573
  81.1 5.5 %collective-permute-start.37 = (f16[128,256]{1,0:T(8,128)(2,1)S(1)}, f16[128,256]{1,0:T(8,128)(2,1)S(1)}, u32[]{:S(2)}, u32[]{:S(2)}) collective-permute-start(f16[128,256]{1,0:T(8,128)(2,1)S(1)} %get-tuple-element.66), channel_id=1, source_target_pairs={{0,2},{1,3},{2,0},{3,1},{4,6},{5,7},{6,4},{7,5},{8,10},{9,11},{10,... | collective-permute-start | bytes 196616 | tf_op jit(solution)/shard_map/ppermute | solution.py:573
  81.1 5.5 %collective-permute-start.38 = (f16[128,256]{1,0:T(8,128)(2,1)S(1)}, f16[128,256]{1,0:T(8,128)(2,1)S(1)}, u32[]{:S(2)}, u32[]{:S(2)}) collective-permute-start(f16[128,256]{1,0:T(8,128)(2,1)S(1)} %get-tuple-element.67), channel_id=1, source_target_pairs={{0,3},{1,2},{2,1},{3,0},{4,7},{5,6},{6,5},{7,4},{8,11},{9,10},{10,... | collective-permute-start | bytes 196616 | tf_op jit(solution)/shard_map/ppermute | solution.py:573
  82.6 1.2 %collective-permute-start.35 = (f16[16,128]{1,0:T(8,128)(2,1)S(1)}, f16[16,128]{1,0:T(8,128)(2,1)S(1)}, u32[]{:S(2)}, u32[]{:S(2)}) collective-permute-start(f16[16,128]{1,0:T(8,128)(2,1)S(1)} %slice.162), channel_id=1, source_target_pairs={{0,4},{4,0},{8,12},{12,8},{16,20},{20,16},{24,28},{28,24},{1,5},{5... | collective-permute-start | bytes 12296 | tf_op jit(solution)/shard_map/ppermute | solution.py:678
  (1 other events, 1.3 us)

commit v3 on v2

--- a/solution.py
+++ b/solution.py
@@ -117,7 +117,9 @@
     )(stiffness)
 
 
-def bulk_kernel(x_ref, mass_ref, wide_ref, narrow_ref, own_ref, y_ref, passed_ref):
+def bulk_kernel(
+    x_ref, mass_ref, wide_ref, narrow_ref, own_ref, y_ref, passed_ref, *copy_refs
+):
     n_theta, n_axial, radial, lanes = x_ref.shape
 
     def product(index, values):
@@ -144,13 +146,15 @@
 
     lax.fori_loop(0, n_axial, along_theta, 0, unroll=True)
     lax.fori_loop(0, n_theta, along_axial, 0, unroll=True)
-
-
-def volume_bulk(x, mass, wide, narrow, own, after=()):
-    n_theta, n_axial, radial, lanes = x.shape
+    for copy_ref in copy_refs:
+        copy_ref[...] = x_ref[...]
+
+
+def volume_bulk(x, mass, wide, narrow, own, copied=False, after=()):
+    outs = (shape(*x.shape), shape(*own.shape)) + ((shape(*x.shape),) if copied else ())
     return call(
         bulk_kernel,
-        (shape(*x.shape), shape(*own.shape)),
+        outs,
         0,
         5,
         name="volume_bulk",
@@ -159,27 +163,46 @@
     )(x, mass, wide, narrow, own)
 
 
-def edges_kernel(x_ref, first_ref, last_ref, axial_first_ref, axial_last_ref, face_ref, copy_ref):
-    n_theta, n_axial = x_ref.shape[:2]
-    first_ref[...] = x_ref[0]
-    last_ref[...] = x_ref[n_theta - 1]
-    axial_first_ref[...] = x_ref[:, 0]
-    axial_last_ref[...] = x_ref[:, n_axial - 1]
-    put_faces(x_ref, face_ref)
-    copy_ref[...] = x_ref[...]
+def edges_kernel(
+    x_ref, first_ref, last_ref, axial_first_ref, axial_last_ref, face_ref, outer_ref, copied
+):
+    n_theta, n_axial, radial, _ = x_ref.shape
+    copies = [
+        pltpu.make_async_copy(source, target, copied.at[index])
+        for index, (source, target) in enumerate(
+            (
+                (x_ref.at[0], first_ref),
+                (x_ref.at[n_theta - 1], last_ref),
+                (x_ref.at[:, 0], axial_first_ref),
+                (x_ref.at[:, n_axial - 1], axial_last_ref),
+                (x_ref.at[:, :, radial - 1], outer_ref),
+            )
+        )
+    ]
+    for copy in copies:
+        copy.start()
+    for copy in copies:
+        copy.wait()
+    for pair in range(face_ref.shape[0]):
+        face_ref[pair] = 0.5 * (outer_ref[2 * pair] + outer_ref[2 * pair + 1])
 
 
 def volume_edges(x):
     n_theta, n_axial, radial, lanes = x.shape
     theta, axial = shape(n_axial, radial, lanes), shape(n_theta, radial, lanes)
-    *layers, face, copy = call(
+    *layers, face = call(
         edges_kernel,
-        (theta, theta, axial, axial, shape(n_theta // 2, n_axial, lanes), shape(*x.shape)),
+        (theta, theta, axial, axial, shape(n_theta // 2, n_axial, lanes)),
+        0,
         0,
         1,
+        scratch=[
+            pltpu.VMEM((n_theta, n_axial, lanes), F32),
+            pltpu.SemaphoreType.DMA((5,)),
+        ],
         name="volume_edges",
     )(x)
-    return layers, face, copy
+    return layers, face
 
 
 def pass_after(values, *earlier):
@@ -318,7 +341,7 @@
     )(bulk, s, *halos, *others)
 
 
-def bem_kernel(sign, by_source, place_ref, m_ref, face_ref, *rest):
+def bem_kernel(sign, by_source, split, place_ref, m_ref, face_ref, *rest):
     own_ref, out_ref, upper_ref, lower_ref, p_ref = rest[-5:]
     out_chunk = own_ref.shape[0] // 2
     n_pieces = m_ref.shape[2] // out_chunk
@@ -356,12 +379,11 @@
         at = pl.ds(pl.multiple_of(index * step, step), step)
         real = m_ref[0, at, :]
         imag = m_ref[1, at, :]
-        by_real = jnp.dot(real, upper_ref[...], preferred_element_type=F32) + jnp.dot(
-            real, lower_ref[...], preferred_element_type=F32
-        )
-        by_imag = jnp.dot(imag, upper_ref[...], preferred_element_type=F32) + jnp.dot(
-            imag, lower_ref[...], preferred_element_type=F32
-        )
+        by_real = jnp.dot(real, upper_ref[...], preferred_element_type=F32)
+        by_imag = jnp.dot(imag, upper_ref[...], preferred_element_type=F32)
+        if split:
+            by_real += jnp.dot(real, lower_ref[...], preferred_element_type=F32)
+            by_imag += jnp.dot(imag, lower_ref[...], preferred_element_type=F32)
         here = pl.ds(index * (step // axial_all), step // axial_all)
         three = (step // axial_all, axial_all, HALF)
         p_ref[here, :, :HALF] = sign * (by_real[:, :HALF] - by_imag[:, HALF:]).reshape(three)
@@ -383,14 +405,14 @@
         part_ref[out_chunk:, :] = p_ref[:, there, :].reshape(out_chunk, lanes)
 
 
-def bem_partial(sign, by_source, place, matrix, face, gathered, *rhs, after=()):
+def bem_partial(sign, by_source, place, matrix, face, gathered, *rhs, split=True, after=()):
     pairs, n_axial, lanes = face.shape
     chunk = gathered[0].shape[0]
     rows, columns = matrix.shape[1:]
     axial_all = rows // pairs
     slabs = axial_all // n_axial
     return call(
-        functools.partial(bem_kernel, sign, by_source),
+        functools.partial(bem_kernel, sign, by_source, split),
         (shape(2 * chunk, lanes), shape(slabs - 1, 2 * chunk, lanes)),
         1,
         2 + len(gathered) + len(rhs),
@@ -721,13 +743,15 @@
     gathered = first_gather(surface_guess, scale_s[0])
     mass = jnp.broadcast_to(mass_shift[..., None], mass_shift.shape + (HALF,))
     wide, narrow = volume_matrices(stiffness, n_theta, radial)
-    layers, face, guess = volume_edges(volume_guess)
+    layers, face = volume_edges(volume_guess)
     halos = theta_halos(layers, scale_v[0]) + axial_halos(layers, scale_v[0])
     own, parts = bem_partial(
         -1.0, True, first_places(chunk), bem_matrix, face, gathered, surface_rhs
     )
     received, meanwhile = scatter(parts, scale_p[0])
-    bulk, own = volume_bulk(guess, mass, wide, narrow, own, after=(meanwhile,))
+    bulk, own, guess = volume_bulk(
+        volume_guess, mass, wide, narrow, own, copied=True, after=(meanwhile,)
+    )
     u0, face, first = finish(
         finish_first_kernel, 1, True, bulk, surface_guess, halos, volume_rhs
     )
@@ -750,7 +774,7 @@
     gathered = sector_gather(to_wire(s1_owner, scale_s[2]), scale_s[2])
     u1 = pass_after(u1, gathered[1])
     halos = theta + axial_halos(edge_layers(u1), scale_v[2])
-    own, parts = bem_partial(1.0, False, place, bem_matrix, face, gathered)
+    own, parts = bem_partial(1.0, False, place, bem_matrix, face, gathered, split=False)
     received, meanwhile = scatter(parts[:, :chunk], scale_p[2])
     (third,) = finish(
         finish_third_kernel, 5, False, bulk, s1, halos, u0, u1, after=(meanwhile,)

time: 100 us -> 98.6 us (0.986)
  local copies, waits for them, and re-layouts: 4.47 us -> 3.07 us
    unnamed x19 -> x17, local copies, waits for them, and re-layouts: 3.09 us -> 1.71 us
where the time goes in v3:
time: 98.6 us; the launch traced here: 98.3 us
  starting transfers between devices  45.7 us (46%)
  waiting for transfers between devices  17.2 us (17%)
  Pallas kernels  17 us (17%)
  blocking collectives  10.7 us (11%)
  other arithmetic  3.13 us (3%)
  local copies, waits for them, and re-layouts  3.07 us (3%)
  between operations  1.55 us (2%)
    pallas_call x15, Pallas kernels, call(): return lambda *args: called(*args, *after)  17 us
    ppermute x9, starting transfers between devices, slab_exchange(): lax.ppermute(messages[distance], 'slab', partner_perm(slabs, distance))  14.3 us
    all_to_all x1, blocking collectives, per_device(): lax.all_to_all(gram, ('sector', 'slab'), split_axis=0, concat_axis=0, til...  10.7 us
    ppermute x6, starting transfers between devices, sector_gather(): shares.append(lax.ppermute(own, 'sector', perm))  9 us
    all_to_all x1, starting transfers between devices, first_gather(): lax.all_to_all(messages.reshape(chips * slabs, turns * n_axial, lanes), (...  8.31 us
    ppermute x9, waiting for transfers between devices, slab_exchange(): lax.ppermute(messages[distance], 'slab', partner_perm(slabs, distance))  7.62 us
    ppermute x6, starting transfers between devices, neighbour_swap(): outer = lax.ppermute(jnp.where(odd, last, first), axis, across)  6.66 us
    ppermute x6, starting transfers between devices, neighbour_swap(): inner = lax.ppermute(jnp.where(odd, first, last), axis, within)  5.66 us
  transfers between devices with their start and end apart: 40, of which 13 were waited for; matrix products, arithmetic and copies ran while one was open for 3% of the time, Pallas kernels for 15%

profile of v3, /device:TPU:0, one launch (start us, length us, event | category | flops | bytes accessed | tf_op | source)
XLA Modules:
  0.0 98.3 jit_solution(8906630946325361423)
XLA Ops:
  0.6 1.0 multiply_convert_fusion.19
  1.6 0.7 broadcast_in_dim.15
  2.4 8.3 %all-to-all-start = ((f16[16,32,256]{2,1,0:T(8,128)(2,1)}), f16[16,32,256]{2,1,0:T(8,128)(2,1)S(1)}, u32[]{:S(2)}, u32[]{:S(2)}) async-start(f16[16,32,256]{2,1,0:T(8,128)(2,1)} %bitcast.12), calls=%async_computation | async-start | bytes 524288 | tf_op jit(solution)/shard_map/all_to_all | solution.py:673
  10.7 1.6 %copy-done.1 = f32[16,16,8,256]{3,2,1,0:T(8,128)S(1)} copy-done((f32[16,16,8,256]{3,2,1,0:T(8,128)S(1)}, f32[16,16,8,256]{3,2,1,0:T(8,128)}, u32[]{:S(2)}) %copy-start.1) | copy-done | bytes 2097176
  12.3 0.6 volume_edges.1
  13.0 3.8 %collective-permute-start.3 = (f16[16,8,256]{2,1,0:T(8,128)(2,1)S(1)}, f16[16,8,256]{2,1,0:T(8,128)(2,1)}, u32[]{:S(2)}, u32[]{:S(2)}) collective-permute-start(f16[16,8,256]{2,1,0:T(8,128)(2,1)S(1)} %get-tuple-element.89), channel_id=1, source_target_pairs={{4,8},{8,4},{12,16},{16,12},{20,24},{24,20},{28,0},{0,28},{5,9},{9... | collective-permute-start | bytes 196616 | tf_op jit(solution)/shard_map/ppermute | solution.py:611
  16.9 1.5 %collective-permute-start.4 = (f16[16,8,256]{2,1,0:T(8,128)(2,1)S(1)}, f16[16,8,256]{2,1,0:T(8,128)(2,1)S(1)}, u32[]{:S(2)}, u32[]{:S(2)}) collective-permute-start(f16[16,8,256]{2,1,0:T(8,128)(2,1)S(1)} %get-tuple-element.88), channel_id=1, source_target_pairs={{0,1},{1,0},{2,3},{3,2},{4,5},{5,4},{6,7},{7,6},{8,9},{9,8},{10,11... | collective-permute-start | bytes 196616 | tf_op jit(solution)/shard_map/ppermute | solution.py:610
  18.4 0.7 collective-permute-start.5
  19.1 1.1 %volume_matrices.1 = (bf16[2,128,256]{2,1,0:T(8,128)(2,1)S(1)}, bf16[2,128,128]{2,1,0:T(8,128)(2,1)S(1)}) custom-call(f32[3,8,8]{2,1,0:T(8,128)S(1)} %copy-done.6), custom_call_target="tpu_custom_call" | custom-call | flops 1000 | bytes 1000 | tf_op jit(solution)/shard_map/volume_matrices/pallas_call | solution.py:45
  20.6 1.0 %convert_multiply_fusion.28 = (f32[16,8,256]{2,1,0:T(8,128)S(1)}, f32[16,8,256]{2,1,0:T(8,128)S(1)}) fusion(f16[16,8,256]{2,1,0:T(8,128)(2,1)} %collective-permute-done.3, f16[16,8,256]{2,1,0:T(8,128)(2,1)S(1)} %collective-permute-done.2, pred[]{:T(512)S(6)} %eq.4), kind=kLoop, calls=%fused_computation.66 | loop fusion | flops 196608 | bytes 393217 | tf_op jit(solution)/shard_map/mul | solution.py:577
  21.8 1.4 %collective-permute-done = f16[16,32,256]{2,1,0:T(8,128)(2,1)S(1)} collective-permute-done((f16[16,32,256]{2,1,0:T(8,128)(2,1)S(1)}, f16[16,32,256]{2,1,0:T(8,128)(2,1)S(1)}, u32[]{:S(2)}, u32[]{:S(2)}) %collective-permute-start) | collective-permute-done | bytes 262176 | tf_op jit(solution)/shard_map/ppermute | solution.py:681
  23.3 2.0 %bem_partial.3 = (f32[256,256]{1,0:T(8,128)S(1)}, f32[3,256,256]{2,1,0:T(8,128)S(1)}) custom-call(s32[9]{0:T(128)S(1)} %stack.67.refs_0_, bf16[2,512,1024]{2,1,0:T(8,128)(2,1)S(1)} %copy-done, f32[8,16,256]{2,1,0:T(8,128)S(1)} %get-tuple-element.30.refs_2_, f32[128,256]{1,0:T(8,128)S(1)} %bitcast.119, f32[128,256]{1,0:T(8,128)S(1)} %bitcast.123, ...), custom_call_target="tpu_custom_call" | custom-call | flops 1000 | bytes 1000 | tf_op jit(solution)/shard_map/bem_partial/pallas_call | solution.py:45
  25.7 4.2 %collective-permute-start.6 = (f16[256,256]{1,0:T(8,128)(2,1)S(1)}, f16[256,256]{1,0:T(8,128)(2,1)S(1)}, u32[]{:S(2)}, u32[]{:S(2)}) collective-permute-start(f16[256,256]{1,0:T(8,128)(2,1)S(1)} %get-tuple-element.74), channel_id=1, source_target_pairs={{0,1},{1,0},{2,3},{3,2},{4,5},{5,4},{6,7},{7,6},{8,9},{9,8},{10,11... | collective-permute-start | bytes 393224 | tf_op jit(solution)/shard_map/ppermute | solution.py:595
  30.0 1.5 %collective-permute-start.8 = (f16[256,256]{1,0:T(8,128)(2,1)S(1)}, f16[256,256]{1,0:T(8,128)(2,1)S(1)}, u32[]{:S(2)}, u32[]{:S(2)}) collective-permute-start(f16[256,256]{1,0:T(8,128)(2,1)S(1)} %get-tuple-element.73), channel_id=1, source_target_pairs={{0,3},{1,2},{2,1},{3,0},{4,7},{5,6},{6,5},{7,4},{8,11},{9,10},{10,... | collective-permute-start | bytes 393224 | tf_op jit(solution)/shard_map/ppermute | solution.py:595
  31.9 1.6 %volume_bulk.3 = (f32[16,16,8,256]{3,2,1,0:T(8,128)S(1)}, f32[256,256]{1,0:T(8,128)S(1)}, f32[16,16,8,256]{3,2,1,0:T(8,128)S(1)}) custom-call(f32[16,16,8,256]{3,2,1,0:T(8,128)S(1)} %copy-done.2, f32[16,16,8,128]{3,2,1,0:T(8,128)S(1)} %broadcast_in_dim.6.refs_1_, ...), custom_call_target="tpu_custom_call", output_to_operand_aliasing={{1}: (4, {})} | custom-call | flops 1000 | bytes 1000 | tf_op jit(solution)/shard_map/volume_bulk/pallas_call | solution.py:45
  33.5 0.7 finish_first_kernel.1
  34.2 1.5 %volume_bulk.4 = (f32[16,16,8,256]{3,2,1,0:T(8,128)S(1)}, f32[256,256]{1,0:T(8,128)S(1)}) custom-call(f32[16,16,8,256]{3,2,1,0:T(8,128)S(1)} %get-tuple-element.39.refs_0_, f32[16,16,8,128]{3,2,1,0:T(8,128)S(1)} %broadcast_in_dim.6.refs_1_, bf16[2,128,256]{2,1,0:T(8,128)(2,1)S(1)} %get-tuple-element.28.refs_2_, ...), custom_call_target="tpu_custom_call", output_to_operand_aliasing={{1}: (4, {})} | custom-call | flops 1000 | bytes 1000 | tf_op jit(solution)/shard_map/volume_bulk/pallas_call | solution.py:45
  36.0 2.2 %collective-permute-done.7 = f16[256,256]{1,0:T(8,128)(2,1)S(1)} collective-permute-done((f16[256,256]{1,0:T(8,128)(2,1)S(1)}, f16[256,256]{1,0:T(8,128)(2,1)S(1)}, u32[]{:S(2)}, u32[]{:S(2)}) %collective-permute-start.7) | collective-permute-done | bytes 131104 | tf_op jit(solution)/shard_map/ppermute | solution.py:595
  38.5 3.0 %collective-permute-done.10 = f16[16,8,256]{2,1,0:T(8,128)(2,1)S(1)} collective-permute-done((f16[16,8,256]{2,1,0:T(8,128)(2,1)S(1)}, f16[16,8,256]{2,1,0:T(8,128)(2,1)S(1)}, u32[]{:S(2)}, u32[]{:S(2)}) %collective-permute-start.10) | collective-permute-done | bytes 65568 | tf_op jit(solution)/shard_map/ppermute | solution.py:611
  41.7 4.3 %collective-permute-start.14 = (f16[128,256]{1,0:T(8,128)(2,1)S(1)}, f16[128,256]{1,0:T(8,128)(2,1)S(1)}, u32[]{:S(2)}, u32[]{:S(2)}) collective-permute-start(f16[128,256]{1,0:T(8,128)(2,1)S(1)} %get-tuple-element.57), channel_id=1, source_target_pairs={{0,8},{4,12},{8,0},{12,4},{16,24},{20,28},{24,16},{28,20},{1,9},{5... | collective-permute-start | bytes 196616 | tf_op jit(solution)/shard_map/ppermute | solution.py:642
  46.1 2.0 %collective-permute-start.12 = (f16[16,8,256]{2,1,0:T(8,128)(2,1)S(1)}, f16[16,8,256]{2,1,0:T(8,128)(2,1)S(1)}, u32[]{:S(2)}, u32[]{:S(2)}) collective-permute-start(f16[16,8,256]{2,1,0:T(8,128)(2,1)S(1)} %get-tuple-element.63), channel_id=1, source_target_pairs={{0,1},{1,0},{2,3},{3,2},{4,5},{5,4},{6,7},{7,6},{8,9},{9,8},{10,11... | collective-permute-start | bytes 196616 | tf_op jit(solution)/shard_map/ppermute | solution.py:610
  48.1 0.8 collective-permute-start.13
  49.0 0.6 collective-permute-start.17
  49.7 0.5 collective-permute-done.19
  50.5 0.4 collective-permute-done.15
  50.9 2.1 %bem_partial.4 = (f32[256,256]{1,0:T(8,128)S(1)}, f32[3,256,256]{2,1,0:T(8,128)S(1)}) custom-call(s32[9]{0:T(128)S(1)} %stack.76.refs_0_, bf16[2,512,1024]{2,1,0:T(8,128)(2,1)S(1)} %copy-done, f32[8,16,256]{2,1,0:T(8,128)S(1)} %get-tuple-element.43.refs_2_, f32[128,256]{1,0:T(8,128)S(1)} %get-tuple-element.56.refs_3_, ...), custom_call_target="tpu_custom_call" | custom-call | flops 1000 | bytes 1000 | tf_op jit(solution)/shard_map/bem_partial/pallas_call | solution.py:45
  53.1 2.8 %collective-permute-start.21 = (f16[256,256]{1,0:T(8,128)(2,1)S(1)}, f16[256,256]{1,0:T(8,128)(2,1)S(1)}, u32[]{:S(2)}, u32[]{:S(2)}) collective-permute-start(f16[256,256]{1,0:T(8,128)(2,1)S(1)} %get-tuple-element.71), channel_id=1, source_target_pairs={{0,1},{1,0},{2,3},{3,2},{4,5},{5,4},{6,7},{7,6},{8,9},{9,8},{10,11... | collective-permute-start | bytes 393224 | tf_op jit(solution)/shard_map/ppermute | solution.py:595
  56.2 1.4 %collective-permute-start.23 = (f16[256,256]{1,0:T(8,128)(2,1)S(1)}, f16[256,256]{1,0:T(8,128)(2,1)S(1)}, u32[]{:S(2)}, u32[]{:S(2)}) collective-permute-start(f16[256,256]{1,0:T(8,128)(2,1)S(1)} %get-tuple-element.70), channel_id=1, source_target_pairs={{0,3},{1,2},{2,1},{3,0},{4,7},{5,6},{6,5},{7,4},{8,11},{9,10},{10,... | collective-permute-start | bytes 393224 | tf_op jit(solution)/shard_map/ppermute | solution.py:595
  57.7 0.9 finish_second_kernel.1
  58.6 1.5 %volume_bulk.5 = (f32[16,16,8,256]{3,2,1,0:T(8,128)S(1)}, f32[256,256]{1,0:T(8,128)S(1)}) custom-call(f32[16,16,8,256]{3,2,1,0:T(8,128)S(1)} %get-tuple-element.46.refs_0_, f32[16,16,8,128]{3,2,1,0:T(8,128)S(1)} %broadcast_in_dim.6.refs_1_, bf16[2,128,256]{2,1,0:T(8,128)(2,1)S(1)} %get-tuple-element.28.refs_2_, ...), custom_call_target="tpu_custom_call", output_to_operand_aliasing={{1}: (4, {})} | custom-call | flops 1000 | bytes 1000 | tf_op jit(solution)/shard_map/volume_bulk/pallas_call | solution.py:45
  60.3 0.6 collective-permute-start.25
  60.9 3.7 %collective-permute-done.22 = f16[256,256]{1,0:T(8,128)(2,1)S(1)} collective-permute-done((f16[256,256]{1,0:T(8,128)(2,1)S(1)}, f16[256,256]{1,0:T(8,128)(2,1)S(1)}, u32[]{:S(2)}, u32[]{:S(2)}) %collective-permute-start.22) | collective-permute-done | bytes 131104 | tf_op jit(solution)/shard_map/ppermute | solution.py:595
  64.9 0.9 collective-permute-done.25
  65.9 0.6 collective-permute-start.31
  66.5 3.8 %collective-permute-start.29 = (f16[128,256]{1,0:T(8,128)(2,1)S(1)}, f16[128,256]{1,0:T(8,128)(2,1)S(1)}, u32[]{:S(2)}, u32[]{:S(2)}) collective-permute-start(f16[128,256]{1,0:T(8,128)(2,1)S(1)} %get-tuple-element.55), channel_id=1, source_target_pairs={{0,8},{4,12},{8,0},{12,4},{16,24},{20,28},{24,16},{28,20},{1,9},{5... | collective-permute-start | bytes 196616 | tf_op jit(solution)/shard_map/ppermute | solution.py:642
  70.4 1.8 %collective-permute-start.27 = (f16[16,8,256]{2,1,0:T(8,128)(2,1)S(1)}, f16[16,8,256]{2,1,0:T(8,128)(2,1)S(1)}, u32[]{:S(2)}, u32[]{:S(2)}) collective-permute-start(f16[16,8,256]{2,1,0:T(8,128)(2,1)S(1)} %get-tuple-element.59), channel_id=1, source_target_pairs={{0,1},{1,0},{2,3},{3,2},{4,5},{5,4},{6,7},{7,6},{8,9},{9,8},{10,11... | collective-permute-start | bytes 196616 | tf_op jit(solution)/shard_map/ppermute | solution.py:610
  72.2 0.7 collective-permute-start.28
  73.0 1.1 %collective-permute-done.31 = f16[128,256]{1,0:T(8,128)(2,1)S(1)} collective-permute-done((f16[128,256]{1,0:T(8,128)(2,1)S(1)}, f16[128,256]{1,0:T(8,128)(2,1)S(1)}, u32[]{:S(2)}, u32[]{:S(2)}) %collective-permute-start.31) | collective-permute-done | bytes 65568 | tf_op jit(solution)/shard_map/ppermute | solution.py:642
  74.2 0.5 collective-permute-start.30
  74.7 0.6 collective-permute-done.32
  75.6 1.4 %bem_partial.5 = (f32[256,256]{1,0:T(8,128)S(1)}, f32[3,256,256]{2,1,0:T(8,128)S(1)}) custom-call(s32[9]{0:T(128)S(1)} %stack.76.refs_0_, bf16[2,512,1024]{2,1,0:T(8,128)(2,1)S(1)} %copy-done, f32[8,16,256]{2,1,0:T(8,128)S(1)} %get-tuple-element.50.refs_2_, f32[128,256]{1,0:T(8,128)S(1)} %get-tuple-element.54.refs_3_, ...), custom_call_target="tpu_custom_call" | custom-call | flops 1000 | bytes 1000 | tf_op jit(solution)/shard_map/bem_partial/pallas_call | solution.py:45
  77.0 2.4 %collective-permute-start.36 = (f16[128,256]{1,0:T(8,128)(2,1)S(1)}, f16[128,256]{1,0:T(8,128)(2,1)S(1)}, u32[]{:S(2)}, u32[]{:S(2)}) collective-permute-start(f16[128,256]{1,0:T(8,128)(2,1)S(1)} %get-tuple-element.68), channel_id=1, source_target_pairs={{0,1},{1,0},{2,3},{3,2},{4,5},{5,4},{6,7},{7,6},{8,9},{9,8},{10,11... | collective-permute-start | bytes 196616 | tf_op jit(solution)/shard_map/ppermute | solution.py:595
  79.5 1.5 %collective-permute-start.38 = (f16[128,256]{1,0:T(8,128)(2,1)S(1)}, f16[128,256]{1,0:T(8,128)(2,1)S(1)}, u32[]{:S(2)}, u32[]{:S(2)}) collective-permute-start(f16[128,256]{1,0:T(8,128)(2,1)S(1)} %get-tuple-element.67), channel_id=1, source_target_pairs={{0,3},{1,2},{2,1},{3,0},{4,7},{5,6},{6,5},{7,4},{8,11},{9,10},{10,... | collective-permute-start | bytes 196616 | tf_op jit(solution)/shard_map/ppermute | solution.py:595
  81.1 1.1 %collective-permute-done.35 = f16[16,128]{1,0:T(8,128)(2,1)S(1)} collective-permute-done((f16[16,128]{1,0:T(8,128)(2,1)S(1)}, f16[16,128]{1,0:T(8,128)(2,1)S(1)}, u32[]{:S(2)}, u32[]{:S(2)}) %collective-permute-start.35) | collective-permute-done | bytes 4128 | tf_op jit(solution)/shard_map/ppermute | solution.py:700
  82.2 1.2 %finish_third_kernel.1.refs_2_ = f32[5,8,128]{2,1,0:T(8,128)S(1)} custom-call(f32[16,16,8,256]{3,2,1,0:T(8,128)S(1)} %get-tuple-element.48.refs_0_, f32[8,16,256]{2,1,0:T(8,128)S(1)} %bitcast.114, f32[16,8,256]{2,1,0:T(8,128)S(1)} %get-tuple-element.94.refs_2_, f32[16,8,256]{2,1,0:T(8,128)S(1)} %get-tuple-element.93.refs_3_, ...), custom_call_target="tpu_custom_call" | custom-call | flops 1000 | bytes 1000 | tf_op jit(solution)/shard_map/finish_third_kernel/pallas_call | solution.py:45
  83.4 1.6 %collective-permute-done.37 = f16[128,256]{1,0:T(8,128)(2,1)S(1)} collective-permute-done((f16[128,256]{1,0:T(8,128)(2,1)S(1)}, f16[128,256]{1,0:T(8,128)(2,1)S(1)}, u32[]{:S(2)}, u32[]{:S(2)}) %collective-permute-start.37) | collective-permute-done | bytes 65568 | tf_op jit(solution)/shard_map/ppermute | solution.py:595
  85.2 10.7 %all_to_all.10.refs_0_ = f32[32,1,1152]{2,1,0:T(1,128)S(1)} all-to-all(f32[32,1,1152]{2,1,0:T(1,128)S(1)} %local_gram.1), channel_id=1, replica_groups=mesh['sector'=8,'slab'=4] {'sector','slab'}, dimensions={0} | all-to-all | bytes 294912 | tf_op jit(solution)/shard_map/all_to_all | solution.py:785
  95.9 2.2 %final_solution.1 = (f32[16,16,8,256]{3,2,1,0:T(8,128)}, f32[8,16,256]{2,1,0:T(8,128)}) custom-call(f32[32,1,1152]{2,1,0:T(1,128)S(1)} %all_to_all.10.refs_0_, f32[16,16,8,256]{3,2,1,0:T(8,128)S(1)} %get-tuple-element.53.refs_1_, f32[16,16,8,256]{3,2,1,0:T(8,128)S(1)} %pass_after.2.refs_6_.refs_2_, f32[16,16,8,256]{3,2,1,0:T(8,128)S(1)} %pass_after.3.refs_7_.refs_3_, ...), custom_call_target="tpu_custom_call" | custom-call | flops 1000 | bytes 1000 | tf_op jit(solution)/shard_map/final_solution/pallas_call | solution.py:45
  (115 shorter events, 4.3 us)
Async XLA Ops:
  0.6 18.4 %copy-start.6 = (f32[3,8,8]{2,1,0:T(8,128)S(1)}, f32[3,8,8]{2,1,0:T(8,128)}, u32[]{:S(2)}) copy-start(f32[3,8,8]{2,1,0:T(8,128)} %refs_0_.3) | copy-start | bytes 2308
  0.6 19.6 %copy-start.7 = (f32[16,16,8]{1,2,0:T(8,128)S(1)}, f32[16,16,8]{1,2,0:T(8,128)}, u32[]{:S(2)}) copy-start(f32[16,16,8]{1,2,0:T(8,128)} %param.13) | copy-start | bytes 24580
  2.4 19.2 %all-to-all-start = ((f16[16,32,256]{2,1,0:T(8,128)(2,1)}), f16[16,32,256]{2,1,0:T(8,128)(2,1)S(1)}, u32[]{:S(2)}, u32[]{:S(2)}) async-start(f16[16,32,256]{2,1,0:T(8,128)(2,1)} %bitcast.12), calls=%async_computation | async-start | bytes 524288 | tf_op jit(solution)/shard_map/all_to_all | solution.py:673
  10.7 1.6 %copy-start.1 = (f32[16,16,8,256]{3,2,1,0:T(8,128)S(1)}, f32[16,16,8,256]{3,2,1,0:T(8,128)}, u32[]{:S(2)}) copy-start(f32[16,16,8,256]{3,2,1,0:T(8,128)} %refs_0_.5) | copy-start | bytes 6291460
  12.9 7.6 %collective-permute-start.2 = (f16[16,8,256]{2,1,0:T(8,128)(2,1)S(1)}, f16[16,8,256]{2,1,0:T(8,128)(2,1)S(1)}, u32[]{:S(2)}, u32[]{:S(2)}) collective-permute-start(f16[16,8,256]{2,1,0:T(8,128)(2,1)S(1)} %get-tuple-element.90), channel_id=1, source_target_pairs={{0,4},{4,0},{8,12},{12,8},{16,20},{20,16},{24,28},{28,24},{1,5},{5... | collective-permute-start | bytes 196616 | tf_op jit(solution)/shard_map/ppermute | solution.py:610
  13.0 7.6 %collective-permute-start.3 = (f16[16,8,256]{2,1,0:T(8,128)(2,1)S(1)}, f16[16,8,256]{2,1,0:T(8,128)(2,1)}, u32[]{:S(2)}, u32[]{:S(2)}) collective-permute-start(f16[16,8,256]{2,1,0:T(8,128)(2,1)S(1)} %get-tuple-element.89), channel_id=1, source_target_pairs={{4,8},{8,4},{12,16},{16,12},{20,24},{24,20},{28,0},{0,28},{5,9},{9... | collective-permute-start | bytes 196616 | tf_op jit(solution)/shard_map/ppermute | solution.py:611
  16.9 8.8 %collective-permute-start.4 = (f16[16,8,256]{2,1,0:T(8,128)(2,1)S(1)}, f16[16,8,256]{2,1,0:T(8,128)(2,1)S(1)}, u32[]{:S(2)}, u32[]{:S(2)}) collective-permute-start(f16[16,8,256]{2,1,0:T(8,128)(2,1)S(1)} %get-tuple-element.88), channel_id=1, source_target_pairs={{0,1},{1,0},{2,3},{3,2},{4,5},{5,4},{6,7},{7,6},{8,9},{9,8},{10,11... | collective-permute-start | bytes 196616 | tf_op jit(solution)/shard_map/ppermute | solution.py:610
  18.4 7.3 %collective-permute-start.5 = (f16[16,8,256]{2,1,0:T(8,128)(2,1)S(1)}, f16[16,8,256]{2,1,0:T(8,128)(2,1)S(1)}, u32[]{:S(2)}, u32[]{:S(2)}) collective-permute-start(f16[16,8,256]{2,1,0:T(8,128)(2,1)S(1)} %get-tuple-element.87), channel_id=1, source_target_pairs={{1,2},{2,1},{5,6},{6,5},{9,10},{10,9},{13,14},{14,13},{17,18},{18,... | collective-permute-start | bytes 196616 | tf_op jit(solution)/shard_map/ppermute | solution.py:611
  20.3 3.0 %copy-start = (bf16[2,512,1024]{2,1,0:T(8,128)(2,1)S(1)}, bf16[2,512,1024]{2,1,0:T(8,128)(2,1)}, u32[]{:S(2)}) copy-start(bf16[2,512,1024]{2,1,0:T(8,128)(2,1)} %refs_1_.7) | copy-start | bytes 6291460
  20.4 3.0 %copy-start.5 = (f32[8,16,256]{2,1,0:T(8,128)S(1)}, f32[8,16,256]{2,1,0:T(8,128)}, u32[]{:S(2)}) copy-start(f32[8,16,256]{2,1,0:T(8,128)} %refs_11_.1) | copy-start | bytes 393220
  21.6 1.6 %collective-permute-start = (f16[16,32,256]{2,1,0:T(8,128)(2,1)S(1)}, f16[16,32,256]{2,1,0:T(8,128)(2,1)S(1)}, u32[]{:S(2)}, u32[]{:S(2)}) collective-permute-start(f16[16,32,256]{2,1,0:T(8,128)(2,1)S(1)} %all-to-all-done), channel_id=1, source_target_pairs={{0,4},{4,0},{8,12},{12,8},{16,20},{20,16},{24,28},{28,24},{1,5},{5... | collective-permute-start | bytes 786440 | tf_op jit(solution)/shard_map/ppermute | solution.py:681
  25.3 6.5 %copy-start.2 = (f32[16,16,8,256]{3,2,1,0:T(8,128)S(1)}, f32[16,16,8,256]{3,2,1,0:T(8,128)}, u32[]{:S(2)}) copy-start(f32[16,16,8,256]{3,2,1,0:T(8,128)} %refs_0_.5) | copy-start | bytes 6291460
  25.5 6.0 %collective-permute-start.1 = (f16[16,128]{1,0:T(8,128)(2,1)S(1)}, f16[16,128]{1,0:T(8,128)(2,1)S(1)}, u32[]{:S(2)}, u32[]{:S(2)}) collective-permute-start(f16[16,128]{1,0:T(8,128)(2,1)S(1)} %slice.152), channel_id=1, source_target_pairs={{0,4},{4,0},{8,12},{12,8},{16,20},{20,16},{24,28},{28,24},{1,5},{5... | collective-permute-start | bytes 12296 | tf_op jit(solution)/shard_map/ppermute | solution.py:700
  25.7 10.3 %collective-permute-start.6 = (f16[256,256]{1,0:T(8,128)(2,1)S(1)}, f16[256,256]{1,0:T(8,128)(2,1)S(1)}, u32[]{:S(2)}, u32[]{:S(2)}) collective-permute-start(f16[256,256]{1,0:T(8,128)(2,1)S(1)} %get-tuple-element.74), channel_id=1, source_target_pairs={{0,1},{1,0},{2,3},{3,2},{4,5},{5,4},{6,7},{7,6},{8,9},{9,8},{10,11... | collective-permute-start | bytes 393224 | tf_op jit(solution)/shard_map/ppermute | solution.py:595
  30.0 8.3 %collective-permute-start.7 = (f16[256,256]{1,0:T(8,128)(2,1)S(1)}, f16[256,256]{1,0:T(8,128)(2,1)S(1)}, u32[]{:S(2)}, u32[]{:S(2)}) collective-permute-start(f16[256,256]{1,0:T(8,128)(2,1)S(1)} %get-tuple-element.72), channel_id=1, source_target_pairs={{0,2},{1,3},{2,0},{3,1},{4,6},{5,7},{6,4},{7,5},{8,10},{9,11},{10,... | collective-permute-start | bytes 393224 | tf_op jit(solution)/shard_map/ppermute | solution.py:595
  30.0 8.3 %collective-permute-start.8 = (f16[256,256]{1,0:T(8,128)(2,1)S(1)}, f16[256,256]{1,0:T(8,128)(2,1)S(1)}, u32[]{:S(2)}, u32[]{:S(2)}) collective-permute-start(f16[256,256]{1,0:T(8,128)(2,1)S(1)} %get-tuple-element.73), channel_id=1, source_target_pairs={{0,3},{1,2},{2,1},{3,0},{4,7},{5,6},{6,5},{7,4},{8,11},{9,10},{10,... | collective-permute-start | bytes 393224 | tf_op jit(solution)/shard_map/ppermute | solution.py:595
  31.9 1.7 %copy-start.3 = (f32[16,16,8,256]{3,2,1,0:T(8,128)S(1)}, f32[16,16,8,256]{3,2,1,0:T(8,128)}, u32[]{:S(2)}) copy-start(f32[16,16,8,256]{3,2,1,0:T(8,128)} %refs_6_.1) | copy-start | bytes 6291460
  31.9 1.7 %copy-start.4 = (f32[8,16,256]{2,1,0:T(8,128)S(1)}, f32[8,16,256]{2,1,0:T(8,128)}, u32[]{:S(2)}) copy-start(f32[8,16,256]{2,1,0:T(8,128)} %refs_4_.1) | copy-start | bytes 393220
  35.8 5.6 %collective-permute-start.10 = (f16[16,8,256]{2,1,0:T(8,128)(2,1)S(1)}, f16[16,8,256]{2,1,0:T(8,128)(2,1)S(1)}, u32[]{:S(2)}, u32[]{:S(2)}) collective-permute-start(f16[16,8,256]{2,1,0:T(8,128)(2,1)S(1)} %get-tuple-element.64), channel_id=1, source_target_pairs={{4,8},{8,4},{12,16},{16,12},{20,24},{24,20},{28,0},{0,28},{5,9},{9... | collective-permute-start | bytes 196616 | tf_op jit(solution)/shard_map/ppermute | solution.py:611
  35.9 5.5 %collective-permute-start.9 = (f16[16,8,256]{2,1,0:T(8,128)(2,1)S(1)}, f16[16,8,256]{2,1,0:T(8,128)(2,1)S(1)}, u32[]{:S(2)}, u32[]{:S(2)}) collective-permute-start(f16[16,8,256]{2,1,0:T(8,128)(2,1)S(1)} %get-tuple-element.65), channel_id=1, source_target_pairs={{0,4},{4,0},{8,12},{12,8},{16,20},{20,16},{24,28},{28,24},{1,5},{5... | collective-permute-start | bytes 196616 | tf_op jit(solution)/shard_map/ppermute | solution.py:610
  38.4 3.3 %collective-permute-start.11 = (f16[128,256]{1,0:T(8,128)(2,1)S(1)}, f16[128,256]{1,0:T(8,128)(2,1)S(1)}, u32[]{:S(2)}, u32[]{:S(2)}) collective-permute-start(f16[128,256]{1,0:T(8,128)(2,1)S(1)} %get-tuple-element.57), channel_id=1, source_target_pairs={{0,4},{4,0},{8,12},{12,8},{16,20},{20,16},{24,28},{28,24},{1,5},{5... | collective-permute-start | bytes 196616 | tf_op jit(solution)/shard_map/ppermute | solution.py:645
  41.5 7.4 %collective-permute-start.18 = (f16[128,256]{1,0:T(8,128)(2,1)S(1)}, f16[128,256]{1,0:T(8,128)(2,1)S(1)}, u32[]{:S(2)}, u32[]{:S(2)}) collective-permute-start(f16[128,256]{1,0:T(8,128)(2,1)S(1)} %get-tuple-element.57), channel_id=1, source_target_pairs={{0,24},{4,28},{8,16},{12,20},{16,8},{20,12},{24,0},{28,4},{1,25},{... | collective-permute-start | bytes 196616 | tf_op jit(solution)/shard_map/ppermute | solution.py:642
  41.6 7.5 %collective-permute-start.16 = (f16[128,256]{1,0:T(8,128)(2,1)S(1)}, f16[128,256]{1,0:T(8,128)(2,1)S(1)}, u32[]{:S(2)}, u32[]{:S(2)}) collective-permute-start(f16[128,256]{1,0:T(8,128)(2,1)S(1)} %get-tuple-element.57), channel_id=1, source_target_pairs={{0,16},{4,20},{8,24},{12,28},{16,0},{20,4},{24,8},{28,12},{1,17},{... | collective-permute-start | bytes 196616 | tf_op jit(solution)/shard_map/ppermute | solution.py:642
  41.7 7.9 %collective-permute-start.14 = (f16[128,256]{1,0:T(8,128)(2,1)S(1)}, f16[128,256]{1,0:T(8,128)(2,1)S(1)}, u32[]{:S(2)}, u32[]{:S(2)}) collective-permute-start(f16[128,256]{1,0:T(8,128)(2,1)S(1)} %get-tuple-element.57), channel_id=1, source_target_pairs={{0,8},{4,12},{8,0},{12,4},{16,24},{20,28},{24,16},{28,20},{1,9},{5... | collective-permute-start | bytes 196616 | tf_op jit(solution)/shard_map/ppermute | solution.py:642
  46.1 10.2 %collective-permute-start.12 = (f16[16,8,256]{2,1,0:T(8,128)(2,1)S(1)}, f16[16,8,256]{2,1,0:T(8,128)(2,1)S(1)}, u32[]{:S(2)}, u32[]{:S(2)}) collective-permute-start(f16[16,8,256]{2,1,0:T(8,128)(2,1)S(1)} %get-tuple-element.63), channel_id=1, source_target_pairs={{0,1},{1,0},{2,3},{3,2},{4,5},{5,4},{6,7},{7,6},{8,9},{9,8},{10,11... | collective-permute-start | bytes 196616 | tf_op jit(solution)/shard_map/ppermute | solution.py:610
  48.1 9.6 %collective-permute-start.13 = (f16[16,8,256]{2,1,0:T(8,128)(2,1)S(1)}, f16[16,8,256]{2,1,0:T(8,128)(2,1)S(1)}, u32[]{:S(2)}, u32[]{:S(2)}) collective-permute-start(f16[16,8,256]{2,1,0:T(8,128)(2,1)S(1)} %get-tuple-element.62), channel_id=1, source_target_pairs={{1,2},{2,1},{5,6},{6,5},{9,10},{10,9},{13,14},{14,13},{17,18},{18,... | collective-permute-start | bytes 196616 | tf_op jit(solution)/shard_map/ppermute | solution.py:611
  48.9 1.3 %collective-permute-start.19 = (f16[128,256]{1,0:T(8,128)(2,1)S(1)}, f16[128,256]{1,0:T(8,128)(2,1)S(1)}, u32[]{:S(2)}, u32[]{:S(2)}) collective-permute-start(f16[128,256]{1,0:T(8,128)(2,1)S(1)} %collective-permute-done.18), channel_id=1, source_target_pairs={{0,4},{4,0},{8,12},{12,8},{16,20},{20,16},{24,28},{28,24},{1,5},{5... | collective-permute-start | bytes 196616 | tf_op jit(solution)/shard_map/ppermute | solution.py:645
  49.0 1.5 %collective-permute-start.17 = (f16[128,256]{1,0:T(8,128)(2,1)S(1)}, f16[128,256]{1,0:T(8,128)(2,1)S(1)}, u32[]{:S(2)}, u32[]{:S(2)}) collective-permute-start(f16[128,256]{1,0:T(8,128)(2,1)S(1)} %collective-permute-done.16), channel_id=1, source_target_pairs={{0,4},{4,0},{8,12},{12,8},{16,20},{20,16},{24,28},{28,24},{1,5},{5... | collective-permute-start | bytes 196616 | tf_op jit(solution)/shard_map/ppermute | solution.py:645
  49.6 1.3 %collective-permute-start.15 = (f16[128,256]{1,0:T(8,128)(2,1)S(1)}, f16[128,256]{1,0:T(8,128)(2,1)S(1)}, u32[]{:S(2)}, u32[]{:S(2)}) collective-permute-start(f16[128,256]{1,0:T(8,128)(2,1)S(1)} %collective-permute-done.14), channel_id=1, source_target_pairs={{0,4},{4,0},{8,12},{12,8},{16,20},{20,16},{24,28},{28,24},{1,5},{5... | collective-permute-start | bytes 196616 | tf_op jit(solution)/shard_map/ppermute | solution.py:645
  53.1 7.8 %collective-permute-start.21 = (f16[256,256]{1,0:T(8,128)(2,1)S(1)}, f16[256,256]{1,0:T(8,128)(2,1)S(1)}, u32[]{:S(2)}, u32[]{:S(2)}) collective-permute-start(f16[256,256]{1,0:T(8,128)(2,1)S(1)} %get-tuple-element.71), channel_id=1, source_target_pairs={{0,1},{1,0},{2,3},{3,2},{4,5},{5,4},{6,7},{7,6},{8,9},{9,8},{10,11... | collective-permute-start | bytes 393224 | tf_op jit(solution)/shard_map/ppermute | solution.py:595
  55.9 1.8 %collective-permute-start.20 = (f16[16,128]{1,0:T(8,128)(2,1)S(1)}, f16[16,128]{1,0:T(8,128)(2,1)S(1)}, u32[]{:S(2)}, u32[]{:S(2)}) collective-permute-start(f16[16,128]{1,0:T(8,128)(2,1)S(1)} %slice.157), channel_id=1, source_target_pairs={{0,4},{4,0},{8,12},{12,8},{16,20},{20,16},{24,28},{28,24},{1,5},{5... | collective-permute-start | bytes 12296 | tf_op jit(solution)/shard_map/ppermute | solution.py:700
  55.9 8.7 %collective-permute-start.22 = (f16[256,256]{1,0:T(8,128)(2,1)S(1)}, f16[256,256]{1,0:T(8,128)(2,1)S(1)}, u32[]{:S(2)}, u32[]{:S(2)}) collective-permute-start(f16[256,256]{1,0:T(8,128)(2,1)S(1)} %get-tuple-element.69), channel_id=1, source_target_pairs={{0,2},{1,3},{2,0},{3,1},{4,6},{5,7},{6,4},{7,5},{8,10},{9,11},{10,... | collective-permute-start | bytes 393224 | tf_op jit(solution)/shard_map/ppermute | solution.py:595
  56.2 8.4 %collective-permute-start.23 = (f16[256,256]{1,0:T(8,128)(2,1)S(1)}, f16[256,256]{1,0:T(8,128)(2,1)S(1)}, u32[]{:S(2)}, u32[]{:S(2)}) collective-permute-start(f16[256,256]{1,0:T(8,128)(2,1)S(1)} %get-tuple-element.70), channel_id=1, source_target_pairs={{0,3},{1,2},{2,1},{3,0},{4,7},{5,6},{6,5},{7,4},{8,11},{9,10},{10,... | collective-permute-start | bytes 393224 | tf_op jit(solution)/shard_map/ppermute | solution.py:595
  60.1 4.7 %collective-permute-start.24 = (f16[16,8,256]{2,1,0:T(8,128)(2,1)S(1)}, f16[16,8,256]{2,1,0:T(8,128)(2,1)S(1)}, u32[]{:S(2)}, u32[]{:S(2)}) collective-permute-start(f16[16,8,256]{2,1,0:T(8,128)(2,1)S(1)} %get-tuple-element.61), channel_id=1, source_target_pairs={{0,4},{4,0},{8,12},{12,8},{16,20},{20,16},{24,28},{28,24},{1,5},{5... | collective-permute-start | bytes 196616 | tf_op jit(solution)/shard_map/ppermute | solution.py:610
  60.3 5.5 %collective-permute-start.25 = (f16[16,8,256]{2,1,0:T(8,128)(2,1)S(1)}, f16[16,8,256]{2,1,0:T(8,128)(2,1)S(1)}, u32[]{:S(2)}, u32[]{:S(2)}) collective-permute-start(f16[16,8,256]{2,1,0:T(8,128)(2,1)S(1)} %get-tuple-element.60), channel_id=1, source_target_pairs={{4,8},{8,4},{12,16},{16,12},{20,24},{24,20},{28,0},{0,28},{5,9},{9... | collective-permute-start | bytes 196616 | tf_op jit(solution)/shard_map/ppermute | solution.py:611
  64.8 1.7 %collective-permute-start.26 = (f16[128,256]{1,0:T(8,128)(2,1)S(1)}, f16[128,256]{1,0:T(8,128)(2,1)S(1)}, u32[]{:S(2)}, u32[]{:S(2)}) collective-permute-start(f16[128,256]{1,0:T(8,128)(2,1)S(1)} %get-tuple-element.55), channel_id=1, source_target_pairs={{0,4},{4,0},{8,12},{12,8},{16,20},{20,16},{24,28},{28,24},{1,5},{5... | collective-permute-start | bytes 196616 | tf_op jit(solution)/shard_map/ppermute | solution.py:645
  65.8 7.1 %collective-permute-start.33 = (f16[128,256]{1,0:T(8,128)(2,1)S(1)}, f16[128,256]{1,0:T(8,128)(2,1)S(1)}, u32[]{:S(2)}, u32[]{:S(2)}) collective-permute-start(f16[128,256]{1,0:T(8,128)(2,1)S(1)} %get-tuple-element.55), channel_id=1, source_target_pairs={{0,24},{4,28},{8,16},{12,20},{16,8},{20,12},{24,0},{28,4},{1,25},{... | collective-permute-start | bytes 196616 | tf_op jit(solution)/shard_map/ppermute | solution.py:642
  65.9 8.2 %collective-permute-start.31 = (f16[128,256]{1,0:T(8,128)(2,1)S(1)}, f16[128,256]{1,0:T(8,128)(2,1)S(1)}, u32[]{:S(2)}, u32[]{:S(2)}) collective-permute-start(f16[128,256]{1,0:T(8,128)(2,1)S(1)} %get-tuple-element.55), channel_id=1, source_target_pairs={{0,16},{4,20},{8,24},{12,28},{16,0},{20,4},{24,8},{28,12},{1,17},{... | collective-permute-start | bytes 196616 | tf_op jit(solution)/shard_map/ppermute | solution.py:642
  66.5 7.7 %collective-permute-start.29 = (f16[128,256]{1,0:T(8,128)(2,1)S(1)}, f16[128,256]{1,0:T(8,128)(2,1)S(1)}, u32[]{:S(2)}, u32[]{:S(2)}) collective-permute-start(f16[128,256]{1,0:T(8,128)(2,1)S(1)} %get-tuple-element.55), channel_id=1, source_target_pairs={{0,8},{4,12},{8,0},{12,4},{16,24},{20,28},{24,16},{28,20},{1,9},{5... | collective-permute-start | bytes 196616 | tf_op jit(solution)/shard_map/ppermute | solution.py:642
  70.4 10.7 %collective-permute-start.27 = (f16[16,8,256]{2,1,0:T(8,128)(2,1)S(1)}, f16[16,8,256]{2,1,0:T(8,128)(2,1)S(1)}, u32[]{:S(2)}, u32[]{:S(2)}) collective-permute-start(f16[16,8,256]{2,1,0:T(8,128)(2,1)S(1)} %get-tuple-element.59), channel_id=1, source_target_pairs={{0,1},{1,0},{2,3},{3,2},{4,5},{5,4},{6,7},{7,6},{8,9},{9,8},{10,11... | collective-permute-start | bytes 196616 | tf_op jit(solution)/shard_map/ppermute | solution.py:610
  72.2 8.8 %collective-permute-start.28 = (f16[16,8,256]{2,1,0:T(8,128)(2,1)S(1)}, f16[16,8,256]{2,1,0:T(8,128)(2,1)S(1)}, u32[]{:S(2)}, u32[]{:S(2)}) collective-permute-start(f16[16,8,256]{2,1,0:T(8,128)(2,1)S(1)} %get-tuple-element.58), channel_id=1, source_target_pairs={{1,2},{2,1},{5,6},{6,5},{9,10},{10,9},{13,14},{14,13},{17,18},{18,... | collective-permute-start | bytes 196616 | tf_op jit(solution)/shard_map/ppermute | solution.py:611
  72.9 1.8 %collective-permute-start.34 = (f16[128,256]{1,0:T(8,128)(2,1)S(1)}, f16[128,256]{1,0:T(8,128)(2,1)S(1)}, u32[]{:S(2)}, u32[]{:S(2)}) collective-permute-start(f16[128,256]{1,0:T(8,128)(2,1)S(1)} %collective-permute-done.33), channel_id=1, source_target_pairs={{0,4},{4,0},{8,12},{12,8},{16,20},{20,16},{24,28},{28,24},{1,5},{5... | collective-permute-start | bytes 196616 | tf_op jit(solution)/shard_map/ppermute | solution.py:645
  74.1 1.3 %collective-permute-start.32 = (f16[128,256]{1,0:T(8,128)(2,1)S(1)}, f16[128,256]{1,0:T(8,128)(2,1)S(1)}, u32[]{:S(2)}, u32[]{:S(2)}) collective-permute-start(f16[128,256]{1,0:T(8,128)(2,1)S(1)} %collective-permute-done.31), channel_id=1, source_target_pairs={{0,4},{4,0},{8,12},{12,8},{16,20},{20,16},{24,28},{28,24},{1,5},{5... | collective-permute-start | bytes 196616 | tf_op jit(solution)/shard_map/ppermute | solution.py:645
  74.2 1.4 %collective-permute-start.30 = (f16[128,256]{1,0:T(8,128)(2,1)S(1)}, f16[128,256]{1,0:T(8,128)(2,1)S(1)}, u32[]{:S(2)}, u32[]{:S(2)}) collective-permute-start(f16[128,256]{1,0:T(8,128)(2,1)S(1)} %collective-permute-done.29), channel_id=1, source_target_pairs={{0,4},{4,0},{8,12},{12,8},{16,20},{20,16},{24,28},{28,24},{1,5},{5... | collective-permute-start | bytes 196616 | tf_op jit(solution)/shard_map/ppermute | solution.py:645
  77.0 6.3 %collective-permute-start.36 = (f16[128,256]{1,0:T(8,128)(2,1)S(1)}, f16[128,256]{1,0:T(8,128)(2,1)S(1)}, u32[]{:S(2)}, u32[]{:S(2)}) collective-permute-start(f16[128,256]{1,0:T(8,128)(2,1)S(1)} %get-tuple-element.68), channel_id=1, source_target_pairs={{0,1},{1,0},{2,3},{3,2},{4,5},{5,4},{6,7},{7,6},{8,9},{9,8},{10,11... | collective-permute-start | bytes 196616 | tf_op jit(solution)/shard_map/ppermute | solution.py:595
  79.5 5.5 %collective-permute-start.37 = (f16[128,256]{1,0:T(8,128)(2,1)S(1)}, f16[128,256]{1,0:T(8,128)(2,1)S(1)}, u32[]{:S(2)}, u32[]{:S(2)}) collective-permute-start(f16[128,256]{1,0:T(8,128)(2,1)S(1)} %get-tuple-element.66), channel_id=1, source_target_pairs={{0,2},{1,3},{2,0},{3,1},{4,6},{5,7},{6,4},{7,5},{8,10},{9,11},{10,... | collective-permute-start | bytes 196616 | tf_op jit(solution)/shard_map/ppermute | solution.py:595
  79.5 5.5 %collective-permute-start.38 = (f16[128,256]{1,0:T(8,128)(2,1)S(1)}, f16[128,256]{1,0:T(8,128)(2,1)S(1)}, u32[]{:S(2)}, u32[]{:S(2)}) collective-permute-start(f16[128,256]{1,0:T(8,128)(2,1)S(1)} %get-tuple-element.67), channel_id=1, source_target_pairs={{0,3},{1,2},{2,1},{3,0},{4,7},{5,6},{6,5},{7,4},{8,11},{9,10},{10,... | collective-permute-start | bytes 196616 | tf_op jit(solution)/shard_map/ppermute | solution.py:595
  81.0 1.2 %collective-permute-start.35 = (f16[16,128]{1,0:T(8,128)(2,1)S(1)}, f16[16,128]{1,0:T(8,128)(2,1)S(1)}, u32[]{:S(2)}, u32[]{:S(2)}) collective-permute-start(f16[16,128]{1,0:T(8,128)(2,1)S(1)} %slice.162), channel_id=1, source_target_pairs={{0,4},{4,0},{8,12},{12,8},{16,20},{20,16},{24,28},{28,24},{1,5},{5... | collective-permute-start | bytes 12296 | tf_op jit(solution)/shard_map/ppermute | solution.py:700

commit v4 on v3

--- a/solution.py
+++ b/solution.py
@@ -636,7 +636,7 @@
     for distance in range(1, sectors // 2):
         perm = [
             (2 * i + core, 2 * j + core)
-            for i, j in partner_perm(sectors // 2, distance)
+            for i, j in [(i, (i + distance) % (sectors // 2)) for i in range(sectors // 2)]
             for core in range(2)
         ]
         shares.append(lax.ppermute(own, "sector", perm))
@@ -652,7 +652,7 @@
     chip, core = sector // 2, lax.rem(sector, 2)
     places = [lax.axis_index("slab")]
     for distance in range(chips):
-        mutual = chips & (chips - 1) == 0
+        mutual = False
         source = chip ^ distance if mutual else lax.rem(chip - distance + chips, chips)
         places += [(2 * source + core) * chunk, (2 * source + 1 - core) * chunk]
     return jnp.stack([jnp.asarray(value, jnp.int32) for value in places])
@@ -742,13 +742,13 @@
 
     gathered = first_gather(surface_guess, scale_s[0])
     mass = jnp.broadcast_to(mass_shift[..., None], mass_shift.shape + (HALF,))
-    wide, narrow = volume_matrices(stiffness, n_theta, radial)
     layers, face = volume_edges(volume_guess)
     halos = theta_halos(layers, scale_v[0]) + axial_halos(layers, scale_v[0])
     own, parts = bem_partial(
         -1.0, True, first_places(chunk), bem_matrix, face, gathered, surface_rhs
     )
     received, meanwhile = scatter(parts, scale_p[0])
+    wide, narrow = volume_matrices(stiffness, n_theta, radial, after=(meanwhile,))
     bulk, own, guess = volume_bulk(
         volume_guess, mass, wide, narrow, own, copied=True, after=(meanwhile,)
     )

time: 98.6 us -> 97 us (0.984)
  starting transfers between devices: 45.7 us -> 41.3 us
  waiting for transfers between devices: 17.2 us -> 20.3 us
    ppermute x6, starting transfers between devices: 9 us -> 4.65 us  [sector_gather(): shares.append(lax.ppermute(own, 'sector', perm))]
    ppermute x9, waiting for transfers between devices: 7.62 us -> 4.3 us  [slab_exchange(): lax.ppermute(messages[distance], 'slab', partner_perm(slabs, distance))]
    ppermute x6, waiting for transfers between devices: 1.09 us -> 4.29 us  [sector_gather(): shares.append(lax.ppermute(own, 'sector', perm))]
    ppermute x9, starting transfers between devices: 14.3 us -> 11.6 us  [slab_exchange(): lax.ppermute(messages[distance], 'slab', partner_perm(slabs, distance))]
    ppermute x6, waiting for transfers between devices: 3.88 us -> 5.78 us  [neighbour_swap(): outer = lax.ppermute(jnp.where(odd, last, first), axis, across)]
    ppermute x8, starting transfers between devices: 1.5 us -> 3.11 us  [sector_gather(): gathered += [share, lax.ppermute(share, 'sector', sibling_perm())]]
    all_to_all x1, waiting for transfers between devices: 0.01 us -> 1.35 us  [first_gather(): lax.all_to_all(messages.reshape(chips * slabs, turns * n_axial, lanes), (...]
  transfers between devices with their start and end apart: 40 -> 40, of which waited for: 13 -> 15; matrix products, arithmetic and copies ran while one was open for 3% -> 2% of each run, Pallas kernels for 15% -> 15%
where the time goes in v4:
time: 97 us; the launch traced here: 96.7 us
  starting transfers between devices  41.3 us (43%)
  waiting for transfers between devices  20.3 us (21%)
  Pallas kernels  17 us (18%)
  blocking collectives  11.3 us (12%)
  local copies, waits for them, and re-layouts  3.07 us (3%)
  other arithmetic  2.17 us (2%)
  between operations  1.55 us (2%)
    pallas_call x15, Pallas kernels, call(): return lambda *args: called(*args, *after)  17 us
    ppermute x9, starting transfers between devices, slab_exchange(): lax.ppermute(messages[distance], 'slab', partner_perm(slabs, distance))  11.6 us
    all_to_all x1, blocking collectives, per_device(): lax.all_to_all(gram, ('sector', 'slab'), split_axis=0, concat_axis=0, til...  11.3 us
    all_to_all x1, starting transfers between devices, first_gather(): lax.all_to_all(messages.reshape(chips * slabs, turns * n_axial, lanes), (...  8.31 us
    ppermute x6, starting transfers between devices, neighbour_swap(): outer = lax.ppermute(jnp.where(odd, last, first), axis, across)  7.64 us
    ppermute x6, starting transfers between devices, neighbour_swap(): inner = lax.ppermute(jnp.where(odd, first, last), axis, within)  5.79 us
    ppermute x6, waiting for transfers between devices, neighbour_swap(): outer = lax.ppermute(jnp.where(odd, last, first), axis, across)  5.78 us
    ppermute x6, starting transfers between devices, sector_gather(): shares.append(lax.ppermute(own, 'sector', perm))  4.65 us
  transfers between devices with their start and end apart: 40, of which 15 were waited for; matrix products, arithmetic and copies ran while one was open for 2% of the time, Pallas kernels for 15%

profile of v4, /device:TPU:0, one launch (start us, length us, event | category | flops | bytes accessed | tf_op | source)
XLA Modules:
  0.0 96.7 jit_solution(4118931240857941444)
XLA Ops:
  0.6 1.0 multiply_convert_fusion.19
  1.6 0.7 broadcast_in_dim.15
  2.4 8.3 %all-to-all-start = ((f16[16,32,256]{2,1,0:T(8,128)(2,1)}), f16[16,32,256]{2,1,0:T(8,128)(2,1)S(1)}, u32[]{:S(2)}, u32[]{:S(2)}) async-start(f16[16,32,256]{2,1,0:T(8,128)(2,1)} %bitcast.12), calls=%async_computation | async-start | bytes 524288 | tf_op jit(solution)/shard_map/all_to_all | solution.py:673
  10.7 1.6 %copy-done.1 = f32[16,16,8,256]{3,2,1,0:T(8,128)S(1)} copy-done((f32[16,16,8,256]{3,2,1,0:T(8,128)S(1)}, f32[16,16,8,256]{3,2,1,0:T(8,128)}, u32[]{:S(2)}) %copy-start.1) | copy-done | bytes 2097176
  13.0 3.8 %collective-permute-start.3 = (f16[16,8,256]{2,1,0:T(8,128)(2,1)S(1)}, f16[16,8,256]{2,1,0:T(8,128)(2,1)S(1)}, u32[]{:S(2)}, u32[]{:S(2)}) collective-permute-start(f16[16,8,256]{2,1,0:T(8,128)(2,1)S(1)} %get-tuple-element.89), channel_id=1, source_target_pairs={{4,8},{8,4},{12,16},{16,12},{20,24},{24,20},{28,0},{0,28},{5,9},{9... | collective-permute-start | bytes 196616 | tf_op jit(solution)/shard_map/ppermute | solution.py:611
  16.9 1.5 %collective-permute-start.4 = (f16[16,8,256]{2,1,0:T(8,128)(2,1)S(1)}, f16[16,8,256]{2,1,0:T(8,128)(2,1)S(1)}, u32[]{:S(2)}, u32[]{:S(2)}) collective-permute-start(f16[16,8,256]{2,1,0:T(8,128)(2,1)S(1)} %get-tuple-element.88), channel_id=1, source_target_pairs={{0,1},{1,0},{2,3},{3,2},{4,5},{5,4},{6,7},{7,6},{8,9},{9,8},{10,11... | collective-permute-start | bytes 196616 | tf_op jit(solution)/shard_map/ppermute | solution.py:610
  18.4 0.7 collective-permute-start.5
  19.6 1.3 %all-to-all-done = f16[16,32,256]{2,1,0:T(8,128)(2,1)S(1)} async-done(((f16[16,32,256]{2,1,0:T(8,128)(2,1)}), f16[16,32,256]{2,1,0:T(8,128)(2,1)S(1)}, u32[]{:S(2)}, u32[]{:S(2)}) %all-to-all-start) | async-done | bytes 262176 | tf_op jit(solution)/shard_map/all_to_all | solution.py:673
  21.0 1.4 %collective-permute-done = f16[16,32,256]{2,1,0:T(8,128)(2,1)S(1)} collective-permute-done((f16[16,32,256]{2,1,0:T(8,128)(2,1)S(1)}, f16[16,32,256]{2,1,0:T(8,128)(2,1)S(1)}, u32[]{:S(2)}, u32[]{:S(2)}) %collective-permute-start) | collective-permute-done | bytes 262176 | tf_op jit(solution)/shard_map/ppermute | solution.py:681
  22.6 2.0 %bem_partial.3 = (f32[256,256]{1,0:T(8,128)S(1)}, f32[3,256,256]{2,1,0:T(8,128)S(1)}) custom-call(s32[9]{0:T(128)S(1)} %stack.67.refs_0_, bf16[2,512,1024]{2,1,0:T(8,128)(2,1)S(1)} %copy-done, f32[8,16,256]{2,1,0:T(8,128)S(1)} %get-tuple-element.28.refs_2_, f32[128,256]{1,0:T(8,128)S(1)} %bitcast.119, f32[128,256]{1,0:T(8,128)S(1)} %bitcast.123, ...), custom_call_target="tpu_custom_call" | custom-call | flops 1000 | bytes 1000 | tf_op jit(solution)/shard_map/bem_partial/pallas_call | solution.py:45
  25.0 2.9 %collective-permute-start.6 = (f16[256,256]{1,0:T(8,128)(2,1)S(1)}, f16[256,256]{1,0:T(8,128)(2,1)S(1)}, u32[]{:S(2)}, u32[]{:S(2)}) collective-permute-start(f16[256,256]{1,0:T(8,128)(2,1)S(1)} %get-tuple-element.74), channel_id=1, source_target_pairs={{0,1},{1,0},{2,3},{3,2},{4,5},{5,4},{6,7},{7,6},{8,9},{9,8},{10,11... | collective-permute-start | bytes 393224 | tf_op jit(solution)/shard_map/ppermute | solution.py:595
  27.9 1.5 %collective-permute-start.8 = (f16[256,256]{1,0:T(8,128)(2,1)S(1)}, f16[256,256]{1,0:T(8,128)(2,1)S(1)}, u32[]{:S(2)}, u32[]{:S(2)}) collective-permute-start(f16[256,256]{1,0:T(8,128)(2,1)S(1)} %get-tuple-element.73), channel_id=1, source_target_pairs={{0,3},{1,2},{2,1},{3,0},{4,7},{5,6},{6,5},{7,4},{8,11},{9,10},{10,... | collective-permute-start | bytes 393224 | tf_op jit(solution)/shard_map/ppermute | solution.py:595
  29.4 1.1 %volume_matrices.1 = (bf16[2,128,256]{2,1,0:T(8,128)(2,1)S(1)}, bf16[2,128,128]{2,1,0:T(8,128)(2,1)S(1)}) custom-call(f32[3,8,8]{2,1,0:T(8,128)S(1)} %copy-done.6, f32[16,128]{1,0:T(8,128)S(1)} %convert_element_type.238.refs_1_.refs_5_), custom_call_target="tpu_custom_call" | custom-call | flops 1000 | bytes 1000 | tf_op jit(solution)/shard_map/volume_matrices/pallas_call | solution.py:45
  30.9 1.6 %volume_bulk.3 = (f32[16,16,8,256]{3,2,1,0:T(8,128)S(1)}, f32[256,256]{1,0:T(8,128)S(1)}, f32[16,16,8,256]{3,2,1,0:T(8,128)S(1)}) custom-call(f32[16,16,8,256]{3,2,1,0:T(8,128)S(1)} %copy-done.2, f32[16,16,8,128]{3,2,1,0:T(8,128)S(1)} %broadcast_in_dim.6.refs_1_, ...), custom_call_target="tpu_custom_call", output_to_operand_aliasing={{1}: (4, {})} | custom-call | flops 1000 | bytes 1000 | tf_op jit(solution)/shard_map/volume_bulk/pallas_call | solution.py:45
  32.6 0.7 finish_first_kernel.1
  33.3 1.5 %volume_bulk.4 = (f32[16,16,8,256]{3,2,1,0:T(8,128)S(1)}, f32[256,256]{1,0:T(8,128)S(1)}) custom-call(f32[16,16,8,256]{3,2,1,0:T(8,128)S(1)} %get-tuple-element.39.refs_0_, f32[16,16,8,128]{3,2,1,0:T(8,128)S(1)} %broadcast_in_dim.6.refs_1_, bf16[2,128,256]{2,1,0:T(8,128)(2,1)S(1)} %get-tuple-element.30.refs_2_, ...), custom_call_target="tpu_custom_call", output_to_operand_aliasing={{1}: (4, {})} | custom-call | flops 1000 | bytes 1000 | tf_op jit(solution)/shard_map/volume_bulk/pallas_call | solution.py:45
  34.9 0.6 collective-permute-start.9
  36.4 4.0 %collective-permute-done.10 = f16[16,8,256]{2,1,0:T(8,128)(2,1)S(1)} collective-permute-done((f16[16,8,256]{2,1,0:T(8,128)(2,1)S(1)}, f16[16,8,256]{2,1,0:T(8,128)(2,1)S(1)}, u32[]{:S(2)}, u32[]{:S(2)}) %collective-permute-start.10) | collective-permute-done | bytes 65568 | tf_op jit(solution)/shard_map/ppermute | solution.py:611
  40.5 0.9 collective-permute-start.16
  41.4 1.2 %collective-permute-start.14 = (f16[128,256]{1,0:T(8,128)(2,1)S(1)}, f16[128,256]{1,0:T(8,128)(2,1)S(1)}, u32[]{:S(2)}, u32[]{:S(2)}) collective-permute-start(f16[128,256]{1,0:T(8,128)(2,1)S(1)} %get-tuple-element.57), channel_id=1, source_target_pairs={{0,8},{4,12},{8,16},{12,20},{16,24},{20,28},{24,0},{28,4},{1,9},{5... | collective-permute-start | bytes 196616 | tf_op jit(solution)/shard_map/ppermute | solution.py:642
  42.7 2.1 %collective-permute-start.12 = (f16[16,8,256]{2,1,0:T(8,128)(2,1)S(1)}, f16[16,8,256]{2,1,0:T(8,128)(2,1)S(1)}, u32[]{:S(2)}, u32[]{:S(2)}) collective-permute-start(f16[16,8,256]{2,1,0:T(8,128)(2,1)S(1)} %get-tuple-element.63), channel_id=1, source_target_pairs={{0,1},{1,0},{2,3},{3,2},{4,5},{5,4},{6,7},{7,6},{8,9},{9,8},{10,11... | collective-permute-start | bytes 196616 | tf_op jit(solution)/shard_map/ppermute | solution.py:610
  44.7 0.7 collective-permute-start.13
  45.5 2.8 %collective-permute-done.16 = f16[128,256]{1,0:T(8,128)(2,1)S(1)} collective-permute-done((f16[128,256]{1,0:T(8,128)(2,1)S(1)}, f16[128,256]{1,0:T(8,128)(2,1)S(1)}, u32[]{:S(2)}, u32[]{:S(2)}) %collective-permute-start.16) | collective-permute-done | bytes 65568 | tf_op jit(solution)/shard_map/ppermute | solution.py:642
  49.0 0.6 collective-permute-done.17
  49.8 2.1 %bem_partial.4 = (f32[256,256]{1,0:T(8,128)S(1)}, f32[3,256,256]{2,1,0:T(8,128)S(1)}) custom-call(s32[9]{0:T(128)S(1)} %stack.76.refs_0_, bf16[2,512,1024]{2,1,0:T(8,128)(2,1)S(1)} %copy-done, f32[8,16,256]{2,1,0:T(8,128)S(1)} %get-tuple-element.43.refs_2_, f32[128,256]{1,0:T(8,128)S(1)} %get-tuple-element.56.refs_3_, ...), custom_call_target="tpu_custom_call" | custom-call | flops 1000 | bytes 1000 | tf_op jit(solution)/shard_map/bem_partial/pallas_call | solution.py:45
  52.0 1.4 %collective-permute-start.21 = (f16[256,256]{1,0:T(8,128)(2,1)S(1)}, f16[256,256]{1,0:T(8,128)(2,1)S(1)}, u32[]{:S(2)}, u32[]{:S(2)}) collective-permute-start(f16[256,256]{1,0:T(8,128)(2,1)S(1)} %get-tuple-element.71), channel_id=1, source_target_pairs={{0,1},{1,0},{2,3},{3,2},{4,5},{5,4},{6,7},{7,6},{8,9},{9,8},{10,11... | collective-permute-start | bytes 393224 | tf_op jit(solution)/shard_map/ppermute | solution.py:595
  53.4 0.8 collective-permute-start.22
  54.2 1.5 %collective-permute-start.23 = (f16[256,256]{1,0:T(8,128)(2,1)S(1)}, f16[256,256]{1,0:T(8,128)(2,1)S(1)}, u32[]{:S(2)}, u32[]{:S(2)}) collective-permute-start(f16[256,256]{1,0:T(8,128)(2,1)S(1)} %get-tuple-element.70), channel_id=1, source_target_pairs={{0,3},{1,2},{2,1},{3,0},{4,7},{5,6},{6,5},{7,4},{8,11},{9,10},{10,... | collective-permute-start | bytes 393224 | tf_op jit(solution)/shard_map/ppermute | solution.py:595
  55.7 0.9 finish_second_kernel.1
  56.6 1.5 %volume_bulk.5 = (f32[16,16,8,256]{3,2,1,0:T(8,128)S(1)}, f32[256,256]{1,0:T(8,128)S(1)}) custom-call(f32[16,16,8,256]{3,2,1,0:T(8,128)S(1)} %get-tuple-element.46.refs_0_, f32[16,16,8,128]{3,2,1,0:T(8,128)S(1)} %broadcast_in_dim.6.refs_1_, bf16[2,128,256]{2,1,0:T(8,128)(2,1)S(1)} %get-tuple-element.30.refs_2_, ...), custom_call_target="tpu_custom_call", output_to_operand_aliasing={{1}: (4, {})} | custom-call | flops 1000 | bytes 1000 | tf_op jit(solution)/shard_map/volume_bulk/pallas_call | solution.py:45
  58.2 1.8 %collective-permute-start.25 = (f16[16,8,256]{2,1,0:T(8,128)(2,1)S(1)}, f16[16,8,256]{2,1,0:T(8,128)(2,1)S(1)}, u32[]{:S(2)}, u32[]{:S(2)}) collective-permute-start(f16[16,8,256]{2,1,0:T(8,128)(2,1)S(1)} %get-tuple-element.60), channel_id=1, source_target_pairs={{4,8},{8,4},{12,16},{16,12},{20,24},{24,20},{28,0},{0,28},{5,9},{9... | collective-permute-start | bytes 196616 | tf_op jit(solution)/shard_map/ppermute | solution.py:611
  60.0 2.1 %collective-permute-done.22 = f16[256,256]{1,0:T(8,128)(2,1)S(1)} collective-permute-done((f16[256,256]{1,0:T(8,128)(2,1)S(1)}, f16[256,256]{1,0:T(8,128)(2,1)S(1)}, u32[]{:S(2)}, u32[]{:S(2)}) %collective-permute-start.22) | collective-permute-done | bytes 131104 | tf_op jit(solution)/shard_map/ppermute | solution.py:595
  62.3 1.7 %collective-permute-done.25 = f16[16,8,256]{2,1,0:T(8,128)(2,1)S(1)} collective-permute-done((f16[16,8,256]{2,1,0:T(8,128)(2,1)S(1)}, f16[16,8,256]{2,1,0:T(8,128)(2,1)S(1)}, u32[]{:S(2)}, u32[]{:S(2)}) %collective-permute-start.25) | collective-permute-done | bytes 65568 | tf_op jit(solution)/shard_map/ppermute | solution.py:611
  64.6 2.0 %collective-permute-start.29 = (f16[128,256]{1,0:T(8,128)(2,1)S(1)}, f16[128,256]{1,0:T(8,128)(2,1)S(1)}, u32[]{:S(2)}, u32[]{:S(2)}) collective-permute-start(f16[128,256]{1,0:T(8,128)(2,1)S(1)} %get-tuple-element.55), channel_id=1, source_target_pairs={{0,8},{4,12},{8,16},{12,20},{16,24},{20,28},{24,0},{28,4},{1,9},{5... | collective-permute-start | bytes 196616 | tf_op jit(solution)/shard_map/ppermute | solution.py:642
  66.6 1.4 %collective-permute-start.27 = (f16[16,8,256]{2,1,0:T(8,128)(2,1)S(1)}, f16[16,8,256]{2,1,0:T(8,128)(2,1)S(1)}, u32[]{:S(2)}, u32[]{:S(2)}) collective-permute-start(f16[16,8,256]{2,1,0:T(8,128)(2,1)S(1)} %get-tuple-element.59), channel_id=1, source_target_pairs={{0,1},{1,0},{2,3},{3,2},{4,5},{5,4},{6,7},{7,6},{8,9},{9,8},{10,11... | collective-permute-start | bytes 196616 | tf_op jit(solution)/shard_map/ppermute | solution.py:610
  68.0 0.7 collective-permute-start.28
  68.8 1.5 %collective-permute-done.31 = f16[128,256]{1,0:T(8,128)(2,1)S(1)} collective-permute-done((f16[128,256]{1,0:T(8,128)(2,1)S(1)}, f16[128,256]{1,0:T(8,128)(2,1)S(1)}, u32[]{:S(2)}, u32[]{:S(2)}) %collective-permute-start.31) | collective-permute-done | bytes 65568 | tf_op jit(solution)/shard_map/ppermute | solution.py:642
  70.3 2.2 %collective-permute-start.32 = (f16[128,256]{1,0:T(8,128)(2,1)S(1)}, f16[128,256]{1,0:T(8,128)(2,1)S(1)}, u32[]{:S(2)}, u32[]{:S(2)}) collective-permute-start(f16[128,256]{1,0:T(8,128)(2,1)S(1)} %collective-permute-done.31), channel_id=1, source_target_pairs={{0,4},{4,0},{8,12},{12,8},{16,20},{20,16},{24,28},{28,24},{1,5},{5... | collective-permute-start | bytes 196616 | tf_op jit(solution)/shard_map/ppermute | solution.py:645
  72.6 0.7 collective-permute-done.32
  73.8 1.4 %bem_partial.5 = (f32[256,256]{1,0:T(8,128)S(1)}, f32[3,256,256]{2,1,0:T(8,128)S(1)}) custom-call(s32[9]{0:T(128)S(1)} %stack.76.refs_0_, bf16[2,512,1024]{2,1,0:T(8,128)(2,1)S(1)} %copy-done, f32[8,16,256]{2,1,0:T(8,128)S(1)} %get-tuple-element.50.refs_2_, f32[128,256]{1,0:T(8,128)S(1)} %get-tuple-element.54.refs_3_, ...), custom_call_target="tpu_custom_call" | custom-call | flops 1000 | bytes 1000 | tf_op jit(solution)/shard_map/bem_partial/pallas_call | solution.py:45
  75.3 1.4 %collective-permute-start.36 = (f16[128,256]{1,0:T(8,128)(2,1)S(1)}, f16[128,256]{1,0:T(8,128)(2,1)S(1)}, u32[]{:S(2)}, u32[]{:S(2)}) collective-permute-start(f16[128,256]{1,0:T(8,128)(2,1)S(1)} %get-tuple-element.68), channel_id=1, source_target_pairs={{0,1},{1,0},{2,3},{3,2},{4,5},{5,4},{6,7},{7,6},{8,9},{9,8},{10,11... | collective-permute-start | bytes 196616 | tf_op jit(solution)/shard_map/ppermute | solution.py:595
  76.7 0.9 collective-permute-start.37
  77.6 1.2 %collective-permute-start.38 = (f16[128,256]{1,0:T(8,128)(2,1)S(1)}, f16[128,256]{1,0:T(8,128)(2,1)S(1)}, u32[]{:S(2)}, u32[]{:S(2)}) collective-permute-start(f16[128,256]{1,0:T(8,128)(2,1)S(1)} %get-tuple-element.67), channel_id=1, source_target_pairs={{0,3},{1,2},{2,1},{3,0},{4,7},{5,6},{6,5},{7,4},{8,11},{9,10},{10,... | collective-permute-start | bytes 196616 | tf_op jit(solution)/shard_map/ppermute | solution.py:595
  78.9 1.1 %collective-permute-done.35 = f16[16,128]{1,0:T(8,128)(2,1)S(1)} collective-permute-done((f16[16,128]{1,0:T(8,128)(2,1)S(1)}, f16[16,128]{1,0:T(8,128)(2,1)S(1)}, u32[]{:S(2)}, u32[]{:S(2)}) %collective-permute-start.35) | collective-permute-done | bytes 4128 | tf_op jit(solution)/shard_map/ppermute | solution.py:700
  80.0 1.2 %finish_third_kernel.1.refs_2_ = f32[5,8,128]{2,1,0:T(8,128)S(1)} custom-call(f32[16,16,8,256]{3,2,1,0:T(8,128)S(1)} %get-tuple-element.48.refs_0_, f32[8,16,256]{2,1,0:T(8,128)S(1)} %bitcast.114, f32[16,8,256]{2,1,0:T(8,128)S(1)} %get-tuple-element.94.refs_2_, f32[16,8,256]{2,1,0:T(8,128)S(1)} %get-tuple-element.93.refs_3_, ...), custom_call_target="tpu_custom_call" | custom-call | flops 1000 | bytes 1000 | tf_op jit(solution)/shard_map/finish_third_kernel/pallas_call | solution.py:45
  81.2 1.6 %collective-permute-done.38 = f16[128,256]{1,0:T(8,128)(2,1)S(1)} collective-permute-done((f16[128,256]{1,0:T(8,128)(2,1)S(1)}, f16[128,256]{1,0:T(8,128)(2,1)S(1)}, u32[]{:S(2)}, u32[]{:S(2)}) %collective-permute-start.38) | collective-permute-done | bytes 65568 | tf_op jit(solution)/shard_map/ppermute | solution.py:595
  83.0 11.3 %all_to_all.10.refs_0_ = f32[32,1,1152]{2,1,0:T(1,128)S(1)} all-to-all(f32[32,1,1152]{2,1,0:T(1,128)S(1)} %local_gram.1), channel_id=1, replica_groups=mesh['sector'=8,'slab'=4] {'sector','slab'}, dimensions={0} | all-to-all | bytes 294912 | tf_op jit(solution)/shard_map/all_to_all | solution.py:785
  94.3 2.2 %final_solution.1 = (f32[16,16,8,256]{3,2,1,0:T(8,128)}, f32[8,16,256]{2,1,0:T(8,128)}) custom-call(f32[32,1,1152]{2,1,0:T(1,128)S(1)} %all_to_all.10.refs_0_, f32[16,16,8,256]{3,2,1,0:T(8,128)S(1)} %get-tuple-element.53.refs_1_, f32[16,16,8,256]{3,2,1,0:T(8,128)S(1)} %pass_after.2.refs_6_.refs_2_, f32[16,16,8,256]{3,2,1,0:T(8,128)S(1)} %pass_after.3.refs_7_.refs_3_, ...), custom_call_target="tpu_custom_call" | custom-call | flops 1000 | bytes 1000 | tf_op jit(solution)/shard_map/final_solution/pallas_call | solution.py:45
  (115 shorter events, 6.0 us)
Async XLA Ops:
  0.6 18.5 %copy-start.7 = (f32[16,16,8]{1,2,0:T(8,128)S(1)}, f32[16,16,8]{1,2,0:T(8,128)}, u32[]{:S(2)}) copy-start(f32[16,16,8]{1,2,0:T(8,128)} %param.13) | copy-start | bytes 24580
  2.4 18.6 %all-to-all-start = ((f16[16,32,256]{2,1,0:T(8,128)(2,1)}), f16[16,32,256]{2,1,0:T(8,128)(2,1)S(1)}, u32[]{:S(2)}, u32[]{:S(2)}) async-start(f16[16,32,256]{2,1,0:T(8,128)(2,1)} %bitcast.12), calls=%async_computation | async-start | bytes 524288 | tf_op jit(solution)/shard_map/all_to_all | solution.py:673
  10.7 1.6 %copy-start.1 = (f32[16,16,8,256]{3,2,1,0:T(8,128)S(1)}, f32[16,16,8,256]{3,2,1,0:T(8,128)}, u32[]{:S(2)}) copy-start(f32[16,16,8,256]{3,2,1,0:T(8,128)} %refs_0_.5) | copy-start | bytes 6291460
  12.9 6.5 %collective-permute-start.2 = (f16[16,8,256]{2,1,0:T(8,128)(2,1)S(1)}, f16[16,8,256]{2,1,0:T(8,128)(2,1)S(1)}, u32[]{:S(2)}, u32[]{:S(2)}) collective-permute-start(f16[16,8,256]{2,1,0:T(8,128)(2,1)S(1)} %get-tuple-element.90), channel_id=1, source_target_pairs={{0,4},{4,0},{8,12},{12,8},{16,20},{20,16},{24,28},{28,24},{1,5},{5... | collective-permute-start | bytes 196616 | tf_op jit(solution)/shard_map/ppermute | solution.py:610
  13.0 6.5 %collective-permute-start.3 = (f16[16,8,256]{2,1,0:T(8,128)(2,1)S(1)}, f16[16,8,256]{2,1,0:T(8,128)(2,1)S(1)}, u32[]{:S(2)}, u32[]{:S(2)}) collective-permute-start(f16[16,8,256]{2,1,0:T(8,128)(2,1)S(1)} %get-tuple-element.89), channel_id=1, source_target_pairs={{4,8},{8,4},{12,16},{16,12},{20,24},{24,20},{28,0},{0,28},{5,9},{9... | collective-permute-start | bytes 196616 | tf_op jit(solution)/shard_map/ppermute | solution.py:611
  16.9 8.1 %collective-permute-start.4 = (f16[16,8,256]{2,1,0:T(8,128)(2,1)S(1)}, f16[16,8,256]{2,1,0:T(8,128)(2,1)S(1)}, u32[]{:S(2)}, u32[]{:S(2)}) collective-permute-start(f16[16,8,256]{2,1,0:T(8,128)(2,1)S(1)} %get-tuple-element.88), channel_id=1, source_target_pairs={{0,1},{1,0},{2,3},{3,2},{4,5},{5,4},{6,7},{7,6},{8,9},{9,8},{10,11... | collective-permute-start | bytes 196616 | tf_op jit(solution)/shard_map/ppermute | solution.py:610
  18.4 6.6 %collective-permute-start.5 = (f16[16,8,256]{2,1,0:T(8,128)(2,1)S(1)}, f16[16,8,256]{2,1,0:T(8,128)(2,1)S(1)}, u32[]{:S(2)}, u32[]{:S(2)}) collective-permute-start(f16[16,8,256]{2,1,0:T(8,128)(2,1)S(1)} %get-tuple-element.87), channel_id=1, source_target_pairs={{1,2},{2,1},{5,6},{6,5},{9,10},{10,9},{13,14},{14,13},{17,18},{18,... | collective-permute-start | bytes 196616 | tf_op jit(solution)/shard_map/ppermute | solution.py:611
  19.2 3.3 %copy-start = (bf16[2,512,1024]{2,1,0:T(8,128)(2,1)S(1)}, bf16[2,512,1024]{2,1,0:T(8,128)(2,1)}, u32[]{:S(2)}) copy-start(bf16[2,512,1024]{2,1,0:T(8,128)(2,1)} %refs_1_.7) | copy-start | bytes 6291460
  19.2 3.3 %copy-start.5 = (f32[8,16,256]{2,1,0:T(8,128)S(1)}, f32[8,16,256]{2,1,0:T(8,128)}, u32[]{:S(2)}) copy-start(f32[8,16,256]{2,1,0:T(8,128)} %refs_11_.1) | copy-start | bytes 393220
  20.9 1.5 %collective-permute-start = (f16[16,32,256]{2,1,0:T(8,128)(2,1)S(1)}, f16[16,32,256]{2,1,0:T(8,128)(2,1)S(1)}, u32[]{:S(2)}, u32[]{:S(2)}) collective-permute-start(f16[16,32,256]{2,1,0:T(8,128)(2,1)S(1)} %all-to-all-done), channel_id=1, source_target_pairs={{0,4},{4,0},{8,12},{12,8},{16,20},{20,16},{24,28},{28,24},{1,5},{5... | collective-permute-start | bytes 786440 | tf_op jit(solution)/shard_map/ppermute | solution.py:681
  22.6 6.9 %copy-start.6 = (f32[3,8,8]{2,1,0:T(8,128)S(1)}, f32[3,8,8]{2,1,0:T(8,128)}, u32[]{:S(2)}) copy-start(f32[3,8,8]{2,1,0:T(8,128)} %refs_0_.4) | copy-start | bytes 2308
  24.6 6.3 %copy-start.2 = (f32[16,16,8,256]{3,2,1,0:T(8,128)S(1)}, f32[16,16,8,256]{3,2,1,0:T(8,128)}, u32[]{:S(2)}) copy-start(f32[16,16,8,256]{3,2,1,0:T(8,128)} %refs_0_.5) | copy-start | bytes 6291460
  24.7 4.7 %collective-permute-start.1 = (f16[16,128]{1,0:T(8,128)(2,1)S(1)}, f16[16,128]{1,0:T(8,128)(2,1)S(1)}, u32[]{:S(2)}, u32[]{:S(2)}) collective-permute-start(f16[16,128]{1,0:T(8,128)(2,1)S(1)} %slice.152), channel_id=1, source_target_pairs={{0,4},{4,0},{8,12},{12,8},{16,20},{20,16},{24,28},{28,24},{1,5},{5... | collective-permute-start | bytes 12296 | tf_op jit(solution)/shard_map/ppermute | solution.py:700
  25.0 10.6 %collective-permute-start.6 = (f16[256,256]{1,0:T(8,128)(2,1)S(1)}, f16[256,256]{1,0:T(8,128)(2,1)S(1)}, u32[]{:S(2)}, u32[]{:S(2)}) collective-permute-start(f16[256,256]{1,0:T(8,128)(2,1)S(1)} %get-tuple-element.74), channel_id=1, source_target_pairs={{0,1},{1,0},{2,3},{3,2},{4,5},{5,4},{6,7},{7,6},{8,9},{9,8},{10,11... | collective-permute-start | bytes 393224 | tf_op jit(solution)/shard_map/ppermute | solution.py:595
  27.9 8.3 %collective-permute-start.7 = (f16[256,256]{1,0:T(8,128)(2,1)S(1)}, f16[256,256]{1,0:T(8,128)(2,1)S(1)}, u32[]{:S(2)}, u32[]{:S(2)}) collective-permute-start(f16[256,256]{1,0:T(8,128)(2,1)S(1)} %get-tuple-element.72), channel_id=1, source_target_pairs={{0,2},{1,3},{2,0},{3,1},{4,6},{5,7},{6,4},{7,5},{8,10},{9,11},{10,... | collective-permute-start | bytes 393224 | tf_op jit(solution)/shard_map/ppermute | solution.py:595
  27.9 8.3 %collective-permute-start.8 = (f16[256,256]{1,0:T(8,128)(2,1)S(1)}, f16[256,256]{1,0:T(8,128)(2,1)S(1)}, u32[]{:S(2)}, u32[]{:S(2)}) collective-permute-start(f16[256,256]{1,0:T(8,128)(2,1)S(1)} %get-tuple-element.73), channel_id=1, source_target_pairs={{0,3},{1,2},{2,1},{3,0},{4,7},{5,6},{6,5},{7,4},{8,11},{9,10},{10,... | collective-permute-start | bytes 393224 | tf_op jit(solution)/shard_map/ppermute | solution.py:595
  30.9 1.7 %copy-start.3 = (f32[16,16,8,256]{3,2,1,0:T(8,128)S(1)}, f32[16,16,8,256]{3,2,1,0:T(8,128)}, u32[]{:S(2)}) copy-start(f32[16,16,8,256]{3,2,1,0:T(8,128)} %refs_6_.1) | copy-start | bytes 6291460
  30.9 1.7 %copy-start.4 = (f32[8,16,256]{2,1,0:T(8,128)S(1)}, f32[8,16,256]{2,1,0:T(8,128)}, u32[]{:S(2)}) copy-start(f32[8,16,256]{2,1,0:T(8,128)} %refs_4_.1) | copy-start | bytes 393220
  34.9 5.6 %collective-permute-start.10 = (f16[16,8,256]{2,1,0:T(8,128)(2,1)S(1)}, f16[16,8,256]{2,1,0:T(8,128)(2,1)S(1)}, u32[]{:S(2)}, u32[]{:S(2)}) collective-permute-start(f16[16,8,256]{2,1,0:T(8,128)(2,1)S(1)} %get-tuple-element.64), channel_id=1, source_target_pairs={{4,8},{8,4},{12,16},{16,12},{20,24},{24,20},{28,0},{0,28},{5,9},{9... | collective-permute-start | bytes 196616 | tf_op jit(solution)/shard_map/ppermute | solution.py:611
  34.9 5.5 %collective-permute-start.9 = (f16[16,8,256]{2,1,0:T(8,128)(2,1)S(1)}, f16[16,8,256]{2,1,0:T(8,128)(2,1)S(1)}, u32[]{:S(2)}, u32[]{:S(2)}) collective-permute-start(f16[16,8,256]{2,1,0:T(8,128)(2,1)S(1)} %get-tuple-element.65), channel_id=1, source_target_pairs={{0,4},{4,0},{8,12},{12,8},{16,20},{20,16},{24,28},{28,24},{1,5},{5... | collective-permute-start | bytes 196616 | tf_op jit(solution)/shard_map/ppermute | solution.py:610
  36.3 5.0 %collective-permute-start.11 = (f16[128,256]{1,0:T(8,128)(2,1)S(1)}, f16[128,256]{1,0:T(8,128)(2,1)S(1)}, u32[]{:S(2)}, u32[]{:S(2)}) collective-permute-start(f16[128,256]{1,0:T(8,128)(2,1)S(1)} %get-tuple-element.57), channel_id=1, source_target_pairs={{0,4},{4,0},{8,12},{12,8},{16,20},{20,16},{24,28},{28,24},{1,5},{5... | collective-permute-start | bytes 196616 | tf_op jit(solution)/shard_map/ppermute | solution.py:645
  40.5 4.9 %collective-permute-start.18 = (f16[128,256]{1,0:T(8,128)(2,1)S(1)}, f16[128,256]{1,0:T(8,128)(2,1)S(1)}, u32[]{:S(2)}, u32[]{:S(2)}) collective-permute-start(f16[128,256]{1,0:T(8,128)(2,1)S(1)} %get-tuple-element.57), channel_id=1, source_target_pairs={{0,24},{4,28},{8,0},{12,4},{16,8},{20,12},{24,16},{28,20},{1,25},{... | collective-permute-start | bytes 196616 | tf_op jit(solution)/shard_map/ppermute | solution.py:642
  40.5 7.8 %collective-permute-start.16 = (f16[128,256]{1,0:T(8,128)(2,1)S(1)}, f16[128,256]{1,0:T(8,128)(2,1)S(1)}, u32[]{:S(2)}, u32[]{:S(2)}) collective-permute-start(f16[128,256]{1,0:T(8,128)(2,1)S(1)} %get-tuple-element.57), channel_id=1, source_target_pairs={{0,16},{4,20},{8,24},{12,28},{16,0},{20,4},{24,8},{28,12},{1,17},{... | collective-permute-start | bytes 196616 | tf_op jit(solution)/shard_map/ppermute | solution.py:642
  41.4 6.9 %collective-permute-start.14 = (f16[128,256]{1,0:T(8,128)(2,1)S(1)}, f16[128,256]{1,0:T(8,128)(2,1)S(1)}, u32[]{:S(2)}, u32[]{:S(2)}) collective-permute-start(f16[128,256]{1,0:T(8,128)(2,1)S(1)} %get-tuple-element.57), channel_id=1, source_target_pairs={{0,8},{4,12},{8,16},{12,20},{16,24},{20,28},{24,0},{28,4},{1,9},{5... | collective-permute-start | bytes 196616 | tf_op jit(solution)/shard_map/ppermute | solution.py:642
  42.7 11.5 %collective-permute-start.12 = (f16[16,8,256]{2,1,0:T(8,128)(2,1)S(1)}, f16[16,8,256]{2,1,0:T(8,128)(2,1)S(1)}, u32[]{:S(2)}, u32[]{:S(2)}) collective-permute-start(f16[16,8,256]{2,1,0:T(8,128)(2,1)S(1)} %get-tuple-element.63), channel_id=1, source_target_pairs={{0,1},{1,0},{2,3},{3,2},{4,5},{5,4},{6,7},{7,6},{8,9},{9,8},{10,11... | collective-permute-start | bytes 196616 | tf_op jit(solution)/shard_map/ppermute | solution.py:610
  44.7 10.9 %collective-permute-start.13 = (f16[16,8,256]{2,1,0:T(8,128)(2,1)S(1)}, f16[16,8,256]{2,1,0:T(8,128)(2,1)S(1)}, u32[]{:S(2)}, u32[]{:S(2)}) collective-permute-start(f16[16,8,256]{2,1,0:T(8,128)(2,1)S(1)} %get-tuple-element.62), channel_id=1, source_target_pairs={{1,2},{2,1},{5,6},{6,5},{9,10},{10,9},{13,14},{14,13},{17,18},{18,... | collective-permute-start | bytes 196616 | tf_op jit(solution)/shard_map/ppermute | solution.py:611
  45.4 3.5 %collective-permute-start.19 = (f16[128,256]{1,0:T(8,128)(2,1)S(1)}, f16[128,256]{1,0:T(8,128)(2,1)S(1)}, u32[]{:S(2)}, u32[]{:S(2)}) collective-permute-start(f16[128,256]{1,0:T(8,128)(2,1)S(1)} %collective-permute-done.18), channel_id=1, source_target_pairs={{0,4},{4,0},{8,12},{12,8},{16,20},{20,16},{24,28},{28,24},{1,5},{5... | collective-permute-start | bytes 196616 | tf_op jit(solution)/shard_map/ppermute | solution.py:645
  48.3 1.3 %collective-permute-start.17 = (f16[128,256]{1,0:T(8,128)(2,1)S(1)}, f16[128,256]{1,0:T(8,128)(2,1)S(1)}, u32[]{:S(2)}, u32[]{:S(2)}) collective-permute-start(f16[128,256]{1,0:T(8,128)(2,1)S(1)} %collective-permute-done.16), channel_id=1, source_target_pairs={{0,4},{4,0},{8,12},{12,8},{16,20},{20,16},{24,28},{28,24},{1,5},{5... | collective-permute-start | bytes 196616 | tf_op jit(solution)/shard_map/ppermute | solution.py:645
  48.3 1.5 %collective-permute-start.15 = (f16[128,256]{1,0:T(8,128)(2,1)S(1)}, f16[128,256]{1,0:T(8,128)(2,1)S(1)}, u32[]{:S(2)}, u32[]{:S(2)}) collective-permute-start(f16[128,256]{1,0:T(8,128)(2,1)S(1)} %collective-permute-done.14), channel_id=1, source_target_pairs={{0,4},{4,0},{8,12},{12,8},{16,20},{20,16},{24,28},{28,24},{1,5},{5... | collective-permute-start | bytes 196616 | tf_op jit(solution)/shard_map/ppermute | solution.py:645
  52.0 8.0 %collective-permute-start.21 = (f16[256,256]{1,0:T(8,128)(2,1)S(1)}, f16[256,256]{1,0:T(8,128)(2,1)S(1)}, u32[]{:S(2)}, u32[]{:S(2)}) collective-permute-start(f16[256,256]{1,0:T(8,128)(2,1)S(1)} %get-tuple-element.71), channel_id=1, source_target_pairs={{0,1},{1,0},{2,3},{3,2},{4,5},{5,4},{6,7},{7,6},{8,9},{9,8},{10,11... | collective-permute-start | bytes 393224 | tf_op jit(solution)/shard_map/ppermute | solution.py:595
  53.4 2.3 %collective-permute-start.20 = (f16[16,128]{1,0:T(8,128)(2,1)S(1)}, f16[16,128]{1,0:T(8,128)(2,1)S(1)}, u32[]{:S(2)}, u32[]{:S(2)}) collective-permute-start(f16[16,128]{1,0:T(8,128)(2,1)S(1)} %slice.157), channel_id=1, source_target_pairs={{0,4},{4,0},{8,12},{12,8},{16,20},{20,16},{24,28},{28,24},{1,5},{5... | collective-permute-start | bytes 12296 | tf_op jit(solution)/shard_map/ppermute | solution.py:700
  53.4 8.7 %collective-permute-start.22 = (f16[256,256]{1,0:T(8,128)(2,1)S(1)}, f16[256,256]{1,0:T(8,128)(2,1)S(1)}, u32[]{:S(2)}, u32[]{:S(2)}) collective-permute-start(f16[256,256]{1,0:T(8,128)(2,1)S(1)} %get-tuple-element.69), channel_id=1, source_target_pairs={{0,2},{1,3},{2,0},{3,1},{4,6},{5,7},{6,4},{7,5},{8,10},{9,11},{10,... | collective-permute-start | bytes 393224 | tf_op jit(solution)/shard_map/ppermute | solution.py:595
  54.2 7.9 %collective-permute-start.23 = (f16[256,256]{1,0:T(8,128)(2,1)S(1)}, f16[256,256]{1,0:T(8,128)(2,1)S(1)}, u32[]{:S(2)}, u32[]{:S(2)}) collective-permute-start(f16[256,256]{1,0:T(8,128)(2,1)S(1)} %get-tuple-element.70), channel_id=1, source_target_pairs={{0,3},{1,2},{2,1},{3,0},{4,7},{5,6},{6,5},{7,4},{8,11},{9,10},{10,... | collective-permute-start | bytes 393224 | tf_op jit(solution)/shard_map/ppermute | solution.py:595
  58.1 4.2 %collective-permute-start.24 = (f16[16,8,256]{2,1,0:T(8,128)(2,1)S(1)}, f16[16,8,256]{2,1,0:T(8,128)(2,1)S(1)}, u32[]{:S(2)}, u32[]{:S(2)}) collective-permute-start(f16[16,8,256]{2,1,0:T(8,128)(2,1)S(1)} %get-tuple-element.61), channel_id=1, source_target_pairs={{0,4},{4,0},{8,12},{12,8},{16,20},{20,16},{24,28},{28,24},{1,5},{5... | collective-permute-start | bytes 196616 | tf_op jit(solution)/shard_map/ppermute | solution.py:610
  58.2 5.8 %collective-permute-start.25 = (f16[16,8,256]{2,1,0:T(8,128)(2,1)S(1)}, f16[16,8,256]{2,1,0:T(8,128)(2,1)S(1)}, u32[]{:S(2)}, u32[]{:S(2)}) collective-permute-start(f16[16,8,256]{2,1,0:T(8,128)(2,1)S(1)} %get-tuple-element.60), channel_id=1, source_target_pairs={{4,8},{8,4},{12,16},{16,12},{20,24},{24,20},{28,0},{0,28},{5,9},{9... | collective-permute-start | bytes 196616 | tf_op jit(solution)/shard_map/ppermute | solution.py:611
  62.3 2.3 %collective-permute-start.26 = (f16[128,256]{1,0:T(8,128)(2,1)S(1)}, f16[128,256]{1,0:T(8,128)(2,1)S(1)}, u32[]{:S(2)}, u32[]{:S(2)}) collective-permute-start(f16[128,256]{1,0:T(8,128)(2,1)S(1)} %get-tuple-element.55), channel_id=1, source_target_pairs={{0,4},{4,0},{8,12},{12,8},{16,20},{20,16},{24,28},{28,24},{1,5},{5... | collective-permute-start | bytes 196616 | tf_op jit(solution)/shard_map/ppermute | solution.py:645
  64.1 4.7 %collective-permute-start.33 = (f16[128,256]{1,0:T(8,128)(2,1)S(1)}, f16[128,256]{1,0:T(8,128)(2,1)S(1)}, u32[]{:S(2)}, u32[]{:S(2)}) collective-permute-start(f16[128,256]{1,0:T(8,128)(2,1)S(1)} %get-tuple-element.55), channel_id=1, source_target_pairs={{0,24},{4,28},{8,0},{12,4},{16,8},{20,12},{24,16},{28,20},{1,25},{... | collective-permute-start | bytes 196616 | tf_op jit(solution)/shard_map/ppermute | solution.py:642
  64.5 5.8 %collective-permute-start.31 = (f16[128,256]{1,0:T(8,128)(2,1)S(1)}, f16[128,256]{1,0:T(8,128)(2,1)S(1)}, u32[]{:S(2)}, u32[]{:S(2)}) collective-permute-start(f16[128,256]{1,0:T(8,128)(2,1)S(1)} %get-tuple-element.55), channel_id=1, source_target_pairs={{0,16},{4,20},{8,24},{12,28},{16,0},{20,4},{24,8},{28,12},{1,17},{... | collective-permute-start | bytes 196616 | tf_op jit(solution)/shard_map/ppermute | solution.py:642
  64.6 7.9 %collective-permute-start.29 = (f16[128,256]{1,0:T(8,128)(2,1)S(1)}, f16[128,256]{1,0:T(8,128)(2,1)S(1)}, u32[]{:S(2)}, u32[]{:S(2)}) collective-permute-start(f16[128,256]{1,0:T(8,128)(2,1)S(1)} %get-tuple-element.55), channel_id=1, source_target_pairs={{0,8},{4,12},{8,16},{12,20},{16,24},{20,28},{24,0},{28,4},{1,9},{5... | collective-permute-start | bytes 196616 | tf_op jit(solution)/shard_map/ppermute | solution.py:642
  66.6 12.2 %collective-permute-start.27 = (f16[16,8,256]{2,1,0:T(8,128)(2,1)S(1)}, f16[16,8,256]{2,1,0:T(8,128)(2,1)S(1)}, u32[]{:S(2)}, u32[]{:S(2)}) collective-permute-start(f16[16,8,256]{2,1,0:T(8,128)(2,1)S(1)} %get-tuple-element.59), channel_id=1, source_target_pairs={{0,1},{1,0},{2,3},{3,2},{4,5},{5,4},{6,7},{7,6},{8,9},{9,8},{10,11... | collective-permute-start | bytes 196616 | tf_op jit(solution)/shard_map/ppermute | solution.py:610
  68.0 10.8 %collective-permute-start.28 = (f16[16,8,256]{2,1,0:T(8,128)(2,1)S(1)}, f16[16,8,256]{2,1,0:T(8,128)(2,1)S(1)}, u32[]{:S(2)}, u32[]{:S(2)}) collective-permute-start(f16[16,8,256]{2,1,0:T(8,128)(2,1)S(1)} %get-tuple-element.58), channel_id=1, source_target_pairs={{1,2},{2,1},{5,6},{6,5},{9,10},{10,9},{13,14},{14,13},{17,18},{18,... | collective-permute-start | bytes 196616 | tf_op jit(solution)/shard_map/ppermute | solution.py:611
  68.7 3.9 %collective-permute-start.34 = (f16[128,256]{1,0:T(8,128)(2,1)S(1)}, f16[128,256]{1,0:T(8,128)(2,1)S(1)}, u32[]{:S(2)}, u32[]{:S(2)}) collective-permute-start(f16[128,256]{1,0:T(8,128)(2,1)S(1)} %collective-permute-done.33), channel_id=1, source_target_pairs={{0,4},{4,0},{8,12},{12,8},{16,20},{20,16},{24,28},{28,24},{1,5},{5... | collective-permute-start | bytes 196616 | tf_op jit(solution)/shard_map/ppermute | solution.py:645
  70.3 3.1 %collective-permute-start.32 = (f16[128,256]{1,0:T(8,128)(2,1)S(1)}, f16[128,256]{1,0:T(8,128)(2,1)S(1)}, u32[]{:S(2)}, u32[]{:S(2)}) collective-permute-start(f16[128,256]{1,0:T(8,128)(2,1)S(1)} %collective-permute-done.31), channel_id=1, source_target_pairs={{0,4},{4,0},{8,12},{12,8},{16,20},{20,16},{24,28},{28,24},{1,5},{5... | collective-permute-start | bytes 196616 | tf_op jit(solution)/shard_map/ppermute | solution.py:645
  72.5 1.3 %collective-permute-start.30 = (f16[128,256]{1,0:T(8,128)(2,1)S(1)}, f16[128,256]{1,0:T(8,128)(2,1)S(1)}, u32[]{:S(2)}, u32[]{:S(2)}) collective-permute-start(f16[128,256]{1,0:T(8,128)(2,1)S(1)} %collective-permute-done.29), channel_id=1, source_target_pairs={{0,4},{4,0},{8,12},{12,8},{16,20},{20,16},{24,28},{28,24},{1,5},{5... | collective-permute-start | bytes 196616 | tf_op jit(solution)/shard_map/ppermute | solution.py:645
  75.3 5.9 %collective-permute-start.36 = (f16[128,256]{1,0:T(8,128)(2,1)S(1)}, f16[128,256]{1,0:T(8,128)(2,1)S(1)}, u32[]{:S(2)}, u32[]{:S(2)}) collective-permute-start(f16[128,256]{1,0:T(8,128)(2,1)S(1)} %get-tuple-element.68), channel_id=1, source_target_pairs={{0,1},{1,0},{2,3},{3,2},{4,5},{5,4},{6,7},{7,6},{8,9},{9,8},{10,11... | collective-permute-start | bytes 196616 | tf_op jit(solution)/shard_map/ppermute | solution.py:595
  76.7 4.5 %collective-permute-start.37 = (f16[128,256]{1,0:T(8,128)(2,1)S(1)}, f16[128,256]{1,0:T(8,128)(2,1)S(1)}, u32[]{:S(2)}, u32[]{:S(2)}) collective-permute-start(f16[128,256]{1,0:T(8,128)(2,1)S(1)} %get-tuple-element.66), channel_id=1, source_target_pairs={{0,2},{1,3},{2,0},{3,1},{4,6},{5,7},{6,4},{7,5},{8,10},{9,11},{10,... | collective-permute-start | bytes 196616 | tf_op jit(solution)/shard_map/ppermute | solution.py:595
  77.6 5.2 %collective-permute-start.38 = (f16[128,256]{1,0:T(8,128)(2,1)S(1)}, f16[128,256]{1,0:T(8,128)(2,1)S(1)}, u32[]{:S(2)}, u32[]{:S(2)}) collective-permute-start(f16[128,256]{1,0:T(8,128)(2,1)S(1)} %get-tuple-element.67), channel_id=1, source_target_pairs={{0,3},{1,2},{2,1},{3,0},{4,7},{5,6},{6,5},{7,4},{8,11},{9,10},{10,... | collective-permute-start | bytes 196616 | tf_op jit(solution)/shard_map/ppermute | solution.py:595
  78.9 1.2 %collective-permute-start.35 = (f16[16,128]{1,0:T(8,128)(2,1)S(1)}, f16[16,128]{1,0:T(8,128)(2,1)S(1)}, u32[]{:S(2)}, u32[]{:S(2)}) collective-permute-start(f16[16,128]{1,0:T(8,128)(2,1)S(1)} %slice.162), channel_id=1, source_target_pairs={{0,4},{4,0},{8,12},{12,8},{16,20},{20,16},{24,28},{28,24},{1,5},{5... | collective-permute-start | bytes 12296 | tf_op jit(solution)/shard_map/ppermute | solution.py:700

commit v5 on v4

--- a/solution.py
+++ b/solution.py
@@ -591,10 +591,11 @@
 
 def slab_exchange(messages):
     slabs = lax.axis_size("slab")
-    return [
+    received = [
         lax.ppermute(messages[distance], "slab", partner_perm(slabs, distance))
-        for distance in range(1, slabs)
+        for distance in reversed(range(1, slabs))
     ]
+    return received[::-1]
 
 
 def neighbour_swap(axis, first, last, scale, wrap):
@@ -633,7 +634,7 @@
 def sector_gather(own, scale):
     sectors = lax.axis_size("sector")
     shares = [own]
-    for distance in range(1, sectors // 2):
+    for distance in reversed(range(1, sectors // 2)):
         perm = [
             (2 * i + core, 2 * j + core)
             for i, j in [(i, (i + distance) % (sectors // 2)) for i in range(sectors // 2)]
@@ -651,9 +652,8 @@
     sector = lax.axis_index("sector")
     chip, core = sector // 2, lax.rem(sector, 2)
     places = [lax.axis_index("slab")]
-    for distance in range(chips):
-        mutual = False
-        source = chip ^ distance if mutual else lax.rem(chip - distance + chips, chips)
+    for distance in [0] + list(reversed(range(1, chips))):
+        source = lax.rem(chip - distance + chips, chips)
         places += [(2 * source + core) * chunk, (2 * source + 1 - core) * chunk]
     return jnp.stack([jnp.asarray(value, jnp.int32) for value in places])
 
@@ -697,7 +697,7 @@
 
 def scatter(parts, scale):
     messages = [None] + [to_wire(parts[which], scale) for which in range(parts.shape[0])]
-    meanwhile = lax.ppermute(messages[1][:16, :HALF], "sector", sibling_perm())
+    meanwhile = lax.ppermute(messages[-1][:16, :HALF], "sector", sibling_perm())
     return slab_exchange(messages), meanwhile.astype(F32)
 
 
@@ -720,7 +720,7 @@
     unknowns = sectors * pairs * axial_all
 
     gain = 8.0 * math.sqrt(unknowns)
-    stiff = 3 * (3.0 + 7 * 1.05) + 6 + 3.0
+    stiff = 3 * stiffness.shape[1] * 3.0 + 6 + 3.0
     surface_0 = 6.0
     volume_0 = 6.0
     surface_1 = gain * surface_0 + 12.0

time: 97 us -> 95.1 us (0.980)
  waiting for transfers between devices: 20.3 us -> 14.8 us
  starting transfers between devices: 41.3 us -> 44.9 us
    ppermute x6, starting transfers between devices: 5.79 us -> 12 us  [neighbour_swap(): inner = lax.ppermute(jnp.where(odd, first, last), axis, within)]
    ppermute x6, waiting for transfers between devices: 4.29 us -> 2.65 us  [sector_gather(): shares.append(lax.ppermute(own, 'sector', perm))]
    ppermute x6, waiting for transfers between devices: 5.78 us -> 4.32 us  [neighbour_swap(): outer = lax.ppermute(jnp.where(odd, last, first), axis, across)]
    ppermute x8, starting transfers between devices: 3.11 us -> 1.67 us  [sector_gather(): gathered += [share, lax.ppermute(share, 'sector', sibling_perm())]]
    all_to_all x1, waiting for transfers between devices: 1.35 us -> 0.11 us  [first_gather(): lax.all_to_all(messages.reshape(chips * slabs, turns * n_axial, lanes), (...]
    ppermute x3, waiting for transfers between devices: 1.12 us -> 0.01 us  [scatter(): meanwhile = lax.ppermute(messages[-1][:16, :HALF], 'sector', sibling_perm())]
  transfers between devices with their start and end apart: 40 -> 40, of which waited for: 15 -> 12; matrix products, arithmetic and copies ran while one was open for 2% -> 2% of each run, Pallas kernels for 15% -> 15%
where the time goes in v5:
time: 95.1 us; the launch traced here: 94.8 us
  starting transfers between devices  44.9 us (47%)
  Pallas kernels  17 us (18%)
  waiting for transfers between devices  14.8 us (16%)
  blocking collectives  11 us (12%)
  local copies, waits for them, and re-layouts  3.07 us (3%)
  other arithmetic  2.56 us (3%)
  between operations  1.49 us (2%)
    pallas_call x15, Pallas kernels, call(): return lambda *args: called(*args, *after)  17 us
    ppermute x6, starting transfers between devices, neighbour_swap(): inner = lax.ppermute(jnp.where(odd, first, last), axis, within)  12 us
    all_to_all x1, blocking collectives, per_device(): lax.all_to_all(gram, ('sector', 'slab'), split_axis=0, concat_axis=0, til...  11 us
    ppermute x9, starting transfers between devices, slab_exchange(): lax.ppermute(messages[distance], 'slab', partner_perm(slabs, distance))  10.7 us
    all_to_all x1, starting transfers between devices, first_gather(): lax.all_to_all(messages.reshape(chips * slabs, turns * n_axial, lanes), (...  8.31 us
    ppermute x6, starting transfers between devices, neighbour_swap(): outer = lax.ppermute(jnp.where(odd, last, first), axis, across)  7.5 us
    ppermute x6, starting transfers between devices, sector_gather(): shares.append(lax.ppermute(own, 'sector', perm))  4.6 us
    ppermute x6, waiting for transfers between devices, neighbour_swap(): outer = lax.ppermute(jnp.where(odd, last, first), axis, across)  4.32 us
  transfers between devices with their start and end apart: 40, of which 12 were waited for; matrix products, arithmetic and copies ran while one was open for 2% of the time, Pallas kernels for 15%

profile of v5, /device:TPU:0, one launch (start us, length us, event | category | flops | bytes accessed | tf_op | source)
XLA Modules:
  0.0 94.8 jit_solution(9433135804324541182)
XLA Ops:
  0.6 1.0 %multiply_convert_fusion.17 = f16[8,16,256]{2,1,0:T(8,128)(2,1)S(1)} fusion(f32[8,16,256]{2,1,0:T(8,128)} %refs_4_.1), kind=kLoop, calls=%fused_computation.59 | loop fusion | flops 65536 | bytes 196608 | tf_op jit(solution)/shard_map/convert_element_type | solution.py:573
  1.6 0.7 broadcast_in_dim.15
  2.4 8.3 %all-to-all-start = ((f16[16,32,256]{2,1,0:T(8,128)(2,1)}), f16[16,32,256]{2,1,0:T(8,128)(2,1)S(1)}, u32[]{:S(2)}, u32[]{:S(2)}) async-start(f16[16,32,256]{2,1,0:T(8,128)(2,1)} %bitcast.12), calls=%async_computation | async-start | bytes 524288 | tf_op jit(solution)/shard_map/all_to_all | solution.py:673
  10.7 1.6 %copy-done.1 = f32[16,16,8,256]{3,2,1,0:T(8,128)S(1)} copy-done((f32[16,16,8,256]{3,2,1,0:T(8,128)S(1)}, f32[16,16,8,256]{3,2,1,0:T(8,128)}, u32[]{:S(2)}) %copy-start.1) | copy-done | bytes 2097176
  12.9 2.7 %collective-permute-start.3 = (f16[16,8,256]{2,1,0:T(8,128)(2,1)S(1)}, f16[16,8,256]{2,1,0:T(8,128)(2,1)S(1)}, u32[]{:S(2)}, u32[]{:S(2)}) collective-permute-start(f16[16,8,256]{2,1,0:T(8,128)(2,1)S(1)} %get-tuple-element.89), channel_id=1, source_target_pairs={{4,8},{8,4},{12,16},{16,12},{20,24},{24,20},{28,0},{0,28},{5,9},{9... | collective-permute-start | bytes 196616 | tf_op jit(solution)/shard_map/ppermute | solution.py:612
  15.6 0.7 collective-permute-start.5
  16.3 4.2 %collective-permute-start.4 = (f16[16,8,256]{2,1,0:T(8,128)(2,1)S(1)}, f16[16,8,256]{2,1,0:T(8,128)(2,1)S(1)}, u32[]{:S(2)}, u32[]{:S(2)}) collective-permute-start(f16[16,8,256]{2,1,0:T(8,128)(2,1)S(1)} %get-tuple-element.88), channel_id=1, source_target_pairs={{0,1},{1,0},{2,3},{3,2},{4,5},{5,4},{6,7},{7,6},{8,9},{9,8},{10,11... | collective-permute-start | bytes 196616 | tf_op jit(solution)/shard_map/ppermute | solution.py:611
  21.1 1.4 %collective-permute-done = f16[16,32,256]{2,1,0:T(8,128)(2,1)S(1)} collective-permute-done((f16[16,32,256]{2,1,0:T(8,128)(2,1)S(1)}, f16[16,32,256]{2,1,0:T(8,128)(2,1)S(1)}, u32[]{:S(2)}, u32[]{:S(2)}) %collective-permute-start) | collective-permute-done | bytes 262176 | tf_op jit(solution)/shard_map/ppermute | solution.py:681
  22.7 2.0 %bem_partial.3 = (f32[256,256]{1,0:T(8,128)S(1)}, f32[3,256,256]{2,1,0:T(8,128)S(1)}) custom-call(s32[9]{0:T(128)S(1)} %stack.67.refs_0_, bf16[2,512,1024]{2,1,0:T(8,128)(2,1)S(1)} %copy-done, f32[8,16,256]{2,1,0:T(8,128)S(1)} %get-tuple-element.28.refs_2_, f32[128,256]{1,0:T(8,128)S(1)} %bitcast.99, f32[128,256]{1,0:T(8,128)S(1)} %bitcast.103, ...), custom_call_target="tpu_custom_call" | custom-call | flops 1000 | bytes 1000 | tf_op jit(solution)/shard_map/bem_partial/pallas_call | solution.py:45
  25.1 1.5 %collective-permute-start.8 = (f16[256,256]{1,0:T(8,128)(2,1)S(1)}, f16[256,256]{1,0:T(8,128)(2,1)S(1)}, u32[]{:S(2)}, u32[]{:S(2)}) collective-permute-start(f16[256,256]{1,0:T(8,128)(2,1)S(1)} %get-tuple-element.74), channel_id=1, source_target_pairs={{0,3},{1,2},{2,1},{3,0},{4,7},{5,6},{6,5},{7,4},{8,11},{9,10},{10,... | collective-permute-start | bytes 393224 | tf_op jit(solution)/shard_map/ppermute | solution.py:595
  26.6 1.2 %collective-permute-start.6 = (f16[256,256]{1,0:T(8,128)(2,1)S(1)}, f16[256,256]{1,0:T(8,128)(2,1)S(1)}, u32[]{:S(2)}, u32[]{:S(2)}) collective-permute-start(f16[256,256]{1,0:T(8,128)(2,1)S(1)} %get-tuple-element.72), channel_id=1, source_target_pairs={{0,1},{1,0},{2,3},{3,2},{4,5},{5,4},{6,7},{7,6},{8,9},{9,8},{10,11... | collective-permute-start | bytes 393224 | tf_op jit(solution)/shard_map/ppermute | solution.py:595
  27.8 0.9 collective-permute-start.7
  28.6 1.1 %volume_matrices.1 = (bf16[2,128,256]{2,1,0:T(8,128)(2,1)S(1)}, bf16[2,128,128]{2,1,0:T(8,128)(2,1)S(1)}) custom-call(f32[3,8,8]{2,1,0:T(8,128)S(1)} %copy-done.6, f32[16,128]{1,0:T(8,128)S(1)} %convert_element_type.230.refs_1_.refs_5_), custom_call_target="tpu_custom_call" | custom-call | flops 1000 | bytes 1000 | tf_op jit(solution)/shard_map/volume_matrices/pallas_call | solution.py:45
  30.1 1.6 %volume_bulk.3 = (f32[16,16,8,256]{3,2,1,0:T(8,128)S(1)}, f32[256,256]{1,0:T(8,128)S(1)}, f32[16,16,8,256]{3,2,1,0:T(8,128)S(1)}) custom-call(f32[16,16,8,256]{3,2,1,0:T(8,128)S(1)} %copy-done.2, f32[16,16,8,128]{3,2,1,0:T(8,128)S(1)} %broadcast_in_dim.6.refs_1_, ...), custom_call_target="tpu_custom_call", output_to_operand_aliasing={{1}: (4, {})} | custom-call | flops 1000 | bytes 1000 | tf_op jit(solution)/shard_map/volume_bulk/pallas_call | solution.py:45
  31.8 0.7 finish_first_kernel.1
  32.5 1.2 %collective-permute-start.10 = (f16[16,8,256]{2,1,0:T(8,128)(2,1)S(1)}, f16[16,8,256]{2,1,0:T(8,128)(2,1)S(1)}, u32[]{:S(2)}, u32[]{:S(2)}) collective-permute-start(f16[16,8,256]{2,1,0:T(8,128)(2,1)S(1)} %get-tuple-element.60), channel_id=1, source_target_pairs={{4,8},{8,4},{12,16},{16,12},{20,24},{24,20},{28,0},{0,28},{5,9},{9... | collective-permute-start | bytes 196616 | tf_op jit(solution)/shard_map/ppermute | solution.py:612
  34.1 1.5 %volume_bulk.4 = (f32[16,16,8,256]{3,2,1,0:T(8,128)S(1)}, f32[256,256]{1,0:T(8,128)S(1)}) custom-call(f32[16,16,8,256]{3,2,1,0:T(8,128)S(1)} %get-tuple-element.39.refs_0_, f32[16,16,8,128]{3,2,1,0:T(8,128)S(1)} %broadcast_in_dim.6.refs_1_, bf16[2,128,256]{2,1,0:T(8,128)(2,1)S(1)} %get-tuple-element.30.refs_2_, ...), custom_call_target="tpu_custom_call", output_to_operand_aliasing={{1}: (4, {})} | custom-call | flops 1000 | bytes 1000 | tf_op jit(solution)/shard_map/volume_bulk/pallas_call | solution.py:45
  36.0 2.1 %collective-permute-done.10 = f16[16,8,256]{2,1,0:T(8,128)(2,1)S(1)} collective-permute-done((f16[16,8,256]{2,1,0:T(8,128)(2,1)S(1)}, f16[16,8,256]{2,1,0:T(8,128)(2,1)S(1)}, u32[]{:S(2)}, u32[]{:S(2)}) %collective-permute-start.10) | collective-permute-done | bytes 65568 | tf_op jit(solution)/shard_map/ppermute | solution.py:612
  38.2 2.3 %collective-permute-start.14 = (f16[128,256]{1,0:T(8,128)(2,1)S(1)}, f16[128,256]{1,0:T(8,128)(2,1)S(1)}, u32[]{:S(2)}, u32[]{:S(2)}) collective-permute-start(f16[128,256]{1,0:T(8,128)(2,1)S(1)} %get-tuple-element.57), channel_id=1, source_target_pairs={{0,24},{4,28},{8,0},{12,4},{16,8},{20,12},{24,16},{28,20},{1,25},{... | collective-permute-start | bytes 196616 | tf_op jit(solution)/shard_map/ppermute | solution.py:643
  40.6 0.8 collective-permute-start.13
  41.5 3.8 %collective-permute-start.12 = (f16[16,8,256]{2,1,0:T(8,128)(2,1)S(1)}, f16[16,8,256]{2,1,0:T(8,128)(2,1)S(1)}, u32[]{:S(2)}, u32[]{:S(2)}) collective-permute-start(f16[16,8,256]{2,1,0:T(8,128)(2,1)S(1)} %get-tuple-element.59), channel_id=1, source_target_pairs={{0,1},{1,0},{2,3},{3,2},{4,5},{5,4},{6,7},{7,6},{8,9},{9,8},{10,11... | collective-permute-start | bytes 196616 | tf_op jit(solution)/shard_map/ppermute | solution.py:611
  45.3 1.3 %collective-permute-done.18 = f16[128,256]{1,0:T(8,128)(2,1)S(1)} collective-permute-done((f16[128,256]{1,0:T(8,128)(2,1)S(1)}, f16[128,256]{1,0:T(8,128)(2,1)S(1)}, u32[]{:S(2)}, u32[]{:S(2)}) %collective-permute-start.18) | collective-permute-done | bytes 65568 | tf_op jit(solution)/shard_map/ppermute | solution.py:643
  47.4 1.2 %collective-permute-done.17 = f16[128,256]{1,0:T(8,128)(2,1)S(1)} collective-permute-done((f16[128,256]{1,0:T(8,128)(2,1)S(1)}, f16[128,256]{1,0:T(8,128)(2,1)S(1)}, u32[]{:S(2)}, u32[]{:S(2)}) %collective-permute-start.17) | collective-permute-done | bytes 65568 | tf_op jit(solution)/shard_map/ppermute | solution.py:646
  48.7 2.1 %bem_partial.4 = (f32[256,256]{1,0:T(8,128)S(1)}, f32[3,256,256]{2,1,0:T(8,128)S(1)}) custom-call(s32[9]{0:T(128)S(1)} %stack.76.refs_0_, bf16[2,512,1024]{2,1,0:T(8,128)(2,1)S(1)} %copy-done, f32[8,16,256]{2,1,0:T(8,128)S(1)} %get-tuple-element.43.refs_2_, f32[128,256]{1,0:T(8,128)S(1)} %get-tuple-element.56.refs_3_, ...), custom_call_target="tpu_custom_call" | custom-call | flops 1000 | bytes 1000 | tf_op jit(solution)/shard_map/bem_partial/pallas_call | solution.py:45
  50.8 1.1 %collective-permute-start.23 = (f16[256,256]{1,0:T(8,128)(2,1)S(1)}, f16[256,256]{1,0:T(8,128)(2,1)S(1)}, u32[]{:S(2)}, u32[]{:S(2)}) collective-permute-start(f16[256,256]{1,0:T(8,128)(2,1)S(1)} %get-tuple-element.71), channel_id=1, source_target_pairs={{0,3},{1,2},{2,1},{3,0},{4,7},{5,6},{6,5},{7,4},{8,11},{9,10},{10,... | collective-permute-start | bytes 393224 | tf_op jit(solution)/shard_map/ppermute | solution.py:595
  51.9 1.3 %collective-permute-start.21 = (f16[256,256]{1,0:T(8,128)(2,1)S(1)}, f16[256,256]{1,0:T(8,128)(2,1)S(1)}, u32[]{:S(2)}, u32[]{:S(2)}) collective-permute-start(f16[256,256]{1,0:T(8,128)(2,1)S(1)} %get-tuple-element.69), channel_id=1, source_target_pairs={{0,1},{1,0},{2,3},{3,2},{4,5},{5,4},{6,7},{7,6},{8,9},{9,8},{10,11... | collective-permute-start | bytes 393224 | tf_op jit(solution)/shard_map/ppermute | solution.py:595
  53.2 1.2 %collective-permute-start.22 = (f16[256,256]{1,0:T(8,128)(2,1)S(1)}, f16[256,256]{1,0:T(8,128)(2,1)S(1)}, u32[]{:S(2)}, u32[]{:S(2)}) collective-permute-start(f16[256,256]{1,0:T(8,128)(2,1)S(1)} %get-tuple-element.70), channel_id=1, source_target_pairs={{0,2},{1,3},{2,0},{3,1},{4,6},{5,7},{6,4},{7,5},{8,10},{9,11},{10,... | collective-permute-start | bytes 393224 | tf_op jit(solution)/shard_map/ppermute | solution.py:595
  54.5 0.9 finish_second_kernel.1
  55.6 1.5 %volume_bulk.5 = (f32[16,16,8,256]{3,2,1,0:T(8,128)S(1)}, f32[256,256]{1,0:T(8,128)S(1)}) custom-call(f32[16,16,8,256]{3,2,1,0:T(8,128)S(1)} %get-tuple-element.46.refs_0_, f32[16,16,8,128]{3,2,1,0:T(8,128)S(1)} %broadcast_in_dim.6.refs_1_, bf16[2,128,256]{2,1,0:T(8,128)(2,1)S(1)} %get-tuple-element.30.refs_2_, ...), custom_call_target="tpu_custom_call", output_to_operand_aliasing={{1}: (4, {})} | custom-call | flops 1000 | bytes 1000 | tf_op jit(solution)/shard_map/volume_bulk/pallas_call | solution.py:45
  57.1 1.4 %collective-permute-start.25 = (f16[16,8,256]{2,1,0:T(8,128)(2,1)S(1)}, f16[16,8,256]{2,1,0:T(8,128)(2,1)S(1)}, u32[]{:S(2)}, u32[]{:S(2)}) collective-permute-start(f16[16,8,256]{2,1,0:T(8,128)(2,1)S(1)} %get-tuple-element.64), channel_id=1, source_target_pairs={{4,8},{8,4},{12,16},{16,12},{20,24},{24,20},{28,0},{0,28},{5,9},{9... | collective-permute-start | bytes 196616 | tf_op jit(solution)/shard_map/ppermute | solution.py:612
  58.5 1.1 %collective-permute-done.21 = f16[256,256]{1,0:T(8,128)(2,1)S(1)} collective-permute-done((f16[256,256]{1,0:T(8,128)(2,1)S(1)}, f16[256,256]{1,0:T(8,128)(2,1)S(1)}, u32[]{:S(2)}, u32[]{:S(2)}) %collective-permute-start.21) | collective-permute-done | bytes 131104 | tf_op jit(solution)/shard_map/ppermute | solution.py:595
  59.6 0.6 collective-permute-done.22
  60.4 2.3 %collective-permute-done.25 = f16[16,8,256]{2,1,0:T(8,128)(2,1)S(1)} collective-permute-done((f16[16,8,256]{2,1,0:T(8,128)(2,1)S(1)}, f16[16,8,256]{2,1,0:T(8,128)(2,1)S(1)}, u32[]{:S(2)}, u32[]{:S(2)}) %collective-permute-start.25) | collective-permute-done | bytes 65568 | tf_op jit(solution)/shard_map/ppermute | solution.py:612
  62.8 0.6 collective-permute-start.29
  63.4 1.5 %collective-permute-start.33 = (f16[128,256]{1,0:T(8,128)(2,1)S(1)}, f16[128,256]{1,0:T(8,128)(2,1)S(1)}, u32[]{:S(2)}, u32[]{:S(2)}) collective-permute-start(f16[128,256]{1,0:T(8,128)(2,1)S(1)} %get-tuple-element.55), channel_id=1, source_target_pairs={{0,8},{4,12},{8,16},{12,20},{16,24},{20,28},{24,0},{28,4},{1,9},{5... | collective-permute-start | bytes 196616 | tf_op jit(solution)/shard_map/ppermute | solution.py:643
  65.2 0.7 collective-permute-start.28
  65.8 3.6 %collective-permute-start.27 = (f16[16,8,256]{2,1,0:T(8,128)(2,1)S(1)}, f16[16,8,256]{2,1,0:T(8,128)(2,1)S(1)}, u32[]{:S(2)}, u32[]{:S(2)}) collective-permute-start(f16[16,8,256]{2,1,0:T(8,128)(2,1)S(1)} %get-tuple-element.63), channel_id=1, source_target_pairs={{0,1},{1,0},{2,3},{3,2},{4,5},{5,4},{6,7},{7,6},{8,9},{9,8},{10,11... | collective-permute-start | bytes 196616 | tf_op jit(solution)/shard_map/ppermute | solution.py:611
  69.5 1.3 %collective-permute-done.33 = f16[128,256]{1,0:T(8,128)(2,1)S(1)} collective-permute-done((f16[128,256]{1,0:T(8,128)(2,1)S(1)}, f16[128,256]{1,0:T(8,128)(2,1)S(1)}, u32[]{:S(2)}, u32[]{:S(2)}) %collective-permute-start.33) | collective-permute-done | bytes 65568 | tf_op jit(solution)/shard_map/ppermute | solution.py:643
  71.5 1.2 %collective-permute-done.32 = f16[128,256]{1,0:T(8,128)(2,1)S(1)} collective-permute-done((f16[128,256]{1,0:T(8,128)(2,1)S(1)}, f16[128,256]{1,0:T(8,128)(2,1)S(1)}, u32[]{:S(2)}, u32[]{:S(2)}) %collective-permute-start.32) | collective-permute-done | bytes 65568 | tf_op jit(solution)/shard_map/ppermute | solution.py:646
  72.8 1.4 %bem_partial.5 = (f32[256,256]{1,0:T(8,128)S(1)}, f32[3,256,256]{2,1,0:T(8,128)S(1)}) custom-call(s32[9]{0:T(128)S(1)} %stack.76.refs_0_, bf16[2,512,1024]{2,1,0:T(8,128)(2,1)S(1)} %copy-done, f32[8,16,256]{2,1,0:T(8,128)S(1)} %get-tuple-element.50.refs_2_, f32[128,256]{1,0:T(8,128)S(1)} %get-tuple-element.54.refs_3_, ...), custom_call_target="tpu_custom_call" | custom-call | flops 1000 | bytes 1000 | tf_op jit(solution)/shard_map/bem_partial/pallas_call | solution.py:45
  74.3 1.2 %collective-permute-start.38 = (f16[128,256]{1,0:T(8,128)(2,1)S(1)}, f16[128,256]{1,0:T(8,128)(2,1)S(1)}, u32[]{:S(2)}, u32[]{:S(2)}) collective-permute-start(f16[128,256]{1,0:T(8,128)(2,1)S(1)} %get-tuple-element.68), channel_id=1, source_target_pairs={{0,3},{1,2},{2,1},{3,0},{4,7},{5,6},{6,5},{7,4},{8,11},{9,10},{10,... | collective-permute-start | bytes 196616 | tf_op jit(solution)/shard_map/ppermute | solution.py:595
  75.5 1.1 %collective-permute-start.36 = (f16[128,256]{1,0:T(8,128)(2,1)S(1)}, f16[128,256]{1,0:T(8,128)(2,1)S(1)}, u32[]{:S(2)}, u32[]{:S(2)}) collective-permute-start(f16[128,256]{1,0:T(8,128)(2,1)S(1)} %get-tuple-element.66), channel_id=1, source_target_pairs={{0,1},{1,0},{2,3},{3,2},{4,5},{5,4},{6,7},{7,6},{8,9},{9,8},{10,11... | collective-permute-start | bytes 196616 | tf_op jit(solution)/shard_map/ppermute | solution.py:595
  76.7 1.2 %collective-permute-start.37 = (f16[128,256]{1,0:T(8,128)(2,1)S(1)}, f16[128,256]{1,0:T(8,128)(2,1)S(1)}, u32[]{:S(2)}, u32[]{:S(2)}) collective-permute-start(f16[128,256]{1,0:T(8,128)(2,1)S(1)} %get-tuple-element.67), channel_id=1, source_target_pairs={{0,2},{1,3},{2,0},{3,1},{4,6},{5,7},{6,4},{7,5},{8,10},{9,11},{10,... | collective-permute-start | bytes 196616 | tf_op jit(solution)/shard_map/ppermute | solution.py:595
  77.9 1.2 %finish_third_kernel.1.refs_2_ = f32[5,8,128]{2,1,0:T(8,128)S(1)} custom-call(f32[16,16,8,256]{3,2,1,0:T(8,128)S(1)} %get-tuple-element.48.refs_0_, f32[8,16,256]{2,1,0:T(8,128)S(1)} %bitcast.94, f32[16,8,256]{2,1,0:T(8,128)S(1)} %get-tuple-element.94.refs_2_, f32[16,8,256]{2,1,0:T(8,128)S(1)} %get-tuple-element.93.refs_3_, ...), custom_call_target="tpu_custom_call" | custom-call | flops 1000 | bytes 1000 | tf_op jit(solution)/shard_map/finish_third_kernel/pallas_call | solution.py:45
  79.1 1.3 %collective-permute-done.36 = f16[128,256]{1,0:T(8,128)(2,1)S(1)} collective-permute-done((f16[128,256]{1,0:T(8,128)(2,1)S(1)}, f16[128,256]{1,0:T(8,128)(2,1)S(1)}, u32[]{:S(2)}, u32[]{:S(2)}) %collective-permute-start.36) | collective-permute-done | bytes 65568 | tf_op jit(solution)/shard_map/ppermute | solution.py:595
  80.3 0.9 collective-permute-done.37
  81.4 11.0 %all_to_all.10.refs_0_ = f32[32,1,1152]{2,1,0:T(1,128)S(1)} all-to-all(f32[32,1,1152]{2,1,0:T(1,128)S(1)} %local_gram.1), channel_id=1, replica_groups=mesh['sector'=8,'slab'=4] {'sector','slab'}, dimensions={0} | all-to-all | bytes 294912 | tf_op jit(solution)/shard_map/all_to_all | solution.py:785
  92.4 2.3 %final_solution.1 = (f32[16,16,8,256]{3,2,1,0:T(8,128)}, f32[8,16,256]{2,1,0:T(8,128)}) custom-call(f32[32,1,1152]{2,1,0:T(1,128)S(1)} %all_to_all.10.refs_0_, f32[16,16,8,256]{3,2,1,0:T(8,128)S(1)} %get-tuple-element.53.refs_1_, f32[16,16,8,256]{3,2,1,0:T(8,128)S(1)} %pass_after.2.refs_6_.refs_2_, f32[16,16,8,256]{3,2,1,0:T(8,128)S(1)} %pass_after.3.refs_7_.refs_3_, ...), custom_call_target="tpu_custom_call" | custom-call | flops 1000 | bytes 1000 | tf_op jit(solution)/shard_map/final_solution/pallas_call | solution.py:45
  (117 shorter events, 5.7 us)
Async XLA Ops:
  0.6 19.9 %copy-start.7 = (f32[16,16,8]{1,2,0:T(8,128)S(1)}, f32[16,16,8]{1,2,0:T(8,128)}, u32[]{:S(2)}) copy-start(f32[16,16,8]{1,2,0:T(8,128)} %param.13) | copy-start | bytes 24580
  2.4 18.6 %all-to-all-start = ((f16[16,32,256]{2,1,0:T(8,128)(2,1)}), f16[16,32,256]{2,1,0:T(8,128)(2,1)S(1)}, u32[]{:S(2)}, u32[]{:S(2)}) async-start(f16[16,32,256]{2,1,0:T(8,128)(2,1)} %bitcast.12), calls=%async_computation | async-start | bytes 524288 | tf_op jit(solution)/shard_map/all_to_all | solution.py:673
  10.7 1.6 %copy-start.1 = (f32[16,16,8,256]{3,2,1,0:T(8,128)S(1)}, f32[16,16,8,256]{3,2,1,0:T(8,128)}, u32[]{:S(2)}) copy-start(f32[16,16,8,256]{3,2,1,0:T(8,128)} %refs_0_.5) | copy-start | bytes 6291460
  12.9 7.9 %collective-permute-start.3 = (f16[16,8,256]{2,1,0:T(8,128)(2,1)S(1)}, f16[16,8,256]{2,1,0:T(8,128)(2,1)S(1)}, u32[]{:S(2)}, u32[]{:S(2)}) collective-permute-start(f16[16,8,256]{2,1,0:T(8,128)(2,1)S(1)} %get-tuple-element.89), channel_id=1, source_target_pairs={{4,8},{8,4},{12,16},{16,12},{20,24},{24,20},{28,0},{0,28},{5,9},{9... | collective-permute-start | bytes 196616 | tf_op jit(solution)/shard_map/ppermute | solution.py:612
  15.6 5.3 %collective-permute-start.2 = (f16[16,8,256]{2,1,0:T(8,128)(2,1)S(1)}, f16[16,8,256]{2,1,0:T(8,128)(2,1)S(1)}, u32[]{:S(2)}, u32[]{:S(2)}) collective-permute-start(f16[16,8,256]{2,1,0:T(8,128)(2,1)S(1)} %get-tuple-element.90), channel_id=1, source_target_pairs={{0,4},{4,0},{8,12},{12,8},{16,20},{20,16},{24,28},{28,24},{1,5},{5... | collective-permute-start | bytes 196616 | tf_op jit(solution)/shard_map/ppermute | solution.py:611
  15.6 9.4 %collective-permute-start.5 = (f16[16,8,256]{2,1,0:T(8,128)(2,1)S(1)}, f16[16,8,256]{2,1,0:T(8,128)(2,1)S(1)}, u32[]{:S(2)}, u32[]{:S(2)}) collective-permute-start(f16[16,8,256]{2,1,0:T(8,128)(2,1)S(1)} %get-tuple-element.87), channel_id=1, source_target_pairs={{1,2},{2,1},{5,6},{6,5},{9,10},{10,9},{13,14},{14,13},{17,18},{18,... | collective-permute-start | bytes 196616 | tf_op jit(solution)/shard_map/ppermute | solution.py:612
  16.3 8.7 %collective-permute-start.4 = (f16[16,8,256]{2,1,0:T(8,128)(2,1)S(1)}, f16[16,8,256]{2,1,0:T(8,128)(2,1)S(1)}, u32[]{:S(2)}, u32[]{:S(2)}) collective-permute-start(f16[16,8,256]{2,1,0:T(8,128)(2,1)S(1)} %get-tuple-element.88), channel_id=1, source_target_pairs={{0,1},{1,0},{2,3},{3,2},{4,5},{5,4},{6,7},{7,6},{8,9},{9,8},{10,11... | collective-permute-start | bytes 196616 | tf_op jit(solution)/shard_map/ppermute | solution.py:611
  20.6 2.0 %copy-start = (bf16[2,512,1024]{2,1,0:T(8,128)(2,1)S(1)}, bf16[2,512,1024]{2,1,0:T(8,128)(2,1)}, u32[]{:S(2)}) copy-start(bf16[2,512,1024]{2,1,0:T(8,128)(2,1)} %refs_1_.7) | copy-start | bytes 6291460
  20.6 2.0 %copy-start.5 = (f32[8,16,256]{2,1,0:T(8,128)S(1)}, f32[8,16,256]{2,1,0:T(8,128)}, u32[]{:S(2)}) copy-start(f32[8,16,256]{2,1,0:T(8,128)} %refs_11_.1) | copy-start | bytes 393220
  21.0 1.5 %collective-permute-start = (f16[16,32,256]{2,1,0:T(8,128)(2,1)S(1)}, f16[16,32,256]{2,1,0:T(8,128)(2,1)S(1)}, u32[]{:S(2)}, u32[]{:S(2)}) collective-permute-start(f16[16,32,256]{2,1,0:T(8,128)(2,1)S(1)} %all-to-all-done), channel_id=1, source_target_pairs={{0,4},{4,0},{8,12},{12,8},{16,20},{20,16},{24,28},{28,24},{1,5},{5... | collective-permute-start | bytes 786440 | tf_op jit(solution)/shard_map/ppermute | solution.py:681
  22.7 6.0 %copy-start.6 = (f32[3,8,8]{2,1,0:T(8,128)S(1)}, f32[3,8,8]{2,1,0:T(8,128)}, u32[]{:S(2)}) copy-start(f32[3,8,8]{2,1,0:T(8,128)} %refs_0_.4) | copy-start | bytes 2308
  24.7 5.4 %copy-start.2 = (f32[16,16,8,256]{3,2,1,0:T(8,128)S(1)}, f32[16,16,8,256]{3,2,1,0:T(8,128)}, u32[]{:S(2)}) copy-start(f32[16,16,8,256]{3,2,1,0:T(8,128)} %refs_0_.5) | copy-start | bytes 6291460
  24.8 3.8 %collective-permute-start.1 = (f16[16,128]{1,0:T(8,128)(2,1)S(1)}, f16[16,128]{1,0:T(8,128)(2,1)S(1)}, u32[]{:S(2)}, u32[]{:S(2)}) collective-permute-start(f16[16,128]{1,0:T(8,128)(2,1)S(1)} %slice.156), channel_id=1, source_target_pairs={{0,4},{4,0},{8,12},{12,8},{16,20},{20,16},{24,28},{28,24},{1,5},{5... | collective-permute-start | bytes 12296 | tf_op jit(solution)/shard_map/ppermute | solution.py:700
  25.1 10.6 %collective-permute-start.8 = (f16[256,256]{1,0:T(8,128)(2,1)S(1)}, f16[256,256]{1,0:T(8,128)(2,1)S(1)}, u32[]{:S(2)}, u32[]{:S(2)}) collective-permute-start(f16[256,256]{1,0:T(8,128)(2,1)S(1)} %get-tuple-element.74), channel_id=1, source_target_pairs={{0,3},{1,2},{2,1},{3,0},{4,7},{5,6},{6,5},{7,4},{8,11},{9,10},{10,... | collective-permute-start | bytes 393224 | tf_op jit(solution)/shard_map/ppermute | solution.py:595
  26.6 9.0 %collective-permute-start.6 = (f16[256,256]{1,0:T(8,128)(2,1)S(1)}, f16[256,256]{1,0:T(8,128)(2,1)S(1)}, u32[]{:S(2)}, u32[]{:S(2)}) collective-permute-start(f16[256,256]{1,0:T(8,128)(2,1)S(1)} %get-tuple-element.72), channel_id=1, source_target_pairs={{0,1},{1,0},{2,3},{3,2},{4,5},{5,4},{6,7},{7,6},{8,9},{9,8},{10,11... | collective-permute-start | bytes 393224 | tf_op jit(solution)/shard_map/ppermute | solution.py:595
  27.8 7.8 %collective-permute-start.7 = (f16[256,256]{1,0:T(8,128)(2,1)S(1)}, f16[256,256]{1,0:T(8,128)(2,1)S(1)}, u32[]{:S(2)}, u32[]{:S(2)}) collective-permute-start(f16[256,256]{1,0:T(8,128)(2,1)S(1)} %get-tuple-element.73), channel_id=1, source_target_pairs={{0,2},{1,3},{2,0},{3,1},{4,6},{5,7},{6,4},{7,5},{8,10},{9,11},{10,... | collective-permute-start | bytes 393224 | tf_op jit(solution)/shard_map/ppermute | solution.py:595
  30.1 1.7 %copy-start.3 = (f32[16,16,8,256]{3,2,1,0:T(8,128)S(1)}, f32[16,16,8,256]{3,2,1,0:T(8,128)}, u32[]{:S(2)}) copy-start(f32[16,16,8,256]{3,2,1,0:T(8,128)} %refs_6_.1) | copy-start | bytes 6291460
  30.1 1.7 %copy-start.4 = (f32[8,16,256]{2,1,0:T(8,128)S(1)}, f32[8,16,256]{2,1,0:T(8,128)}, u32[]{:S(2)}) copy-start(f32[8,16,256]{2,1,0:T(8,128)} %refs_4_.1) | copy-start | bytes 393220
  32.5 5.6 %collective-permute-start.10 = (f16[16,8,256]{2,1,0:T(8,128)(2,1)S(1)}, f16[16,8,256]{2,1,0:T(8,128)(2,1)S(1)}, u32[]{:S(2)}, u32[]{:S(2)}) collective-permute-start(f16[16,8,256]{2,1,0:T(8,128)(2,1)S(1)} %get-tuple-element.60), channel_id=1, source_target_pairs={{4,8},{8,4},{12,16},{16,12},{20,24},{24,20},{28,0},{0,28},{5,9},{9... | collective-permute-start | bytes 196616 | tf_op jit(solution)/shard_map/ppermute | solution.py:612
  33.8 4.3 %collective-permute-start.9 = (f16[16,8,256]{2,1,0:T(8,128)(2,1)S(1)}, f16[16,8,256]{2,1,0:T(8,128)(2,1)S(1)}, u32[]{:S(2)}, u32[]{:S(2)}) collective-permute-start(f16[16,8,256]{2,1,0:T(8,128)(2,1)S(1)} %get-tuple-element.61), channel_id=1, source_target_pairs={{0,4},{4,0},{8,12},{12,8},{16,20},{20,16},{24,28},{28,24},{1,5},{5... | collective-permute-start | bytes 196616 | tf_op jit(solution)/shard_map/ppermute | solution.py:611
  35.8 4.7 %collective-permute-start.11 = (f16[128,256]{1,0:T(8,128)(2,1)S(1)}, f16[128,256]{1,0:T(8,128)(2,1)S(1)}, u32[]{:S(2)}, u32[]{:S(2)}) collective-permute-start(f16[128,256]{1,0:T(8,128)(2,1)S(1)} %get-tuple-element.57), channel_id=1, source_target_pairs={{0,4},{4,0},{8,12},{12,8},{16,20},{20,16},{24,28},{28,24},{1,5},{5... | collective-permute-start | bytes 196616 | tf_op jit(solution)/shard_map/ppermute | solution.py:646
  38.1 9.1 %collective-permute-start.16 = (f16[128,256]{1,0:T(8,128)(2,1)S(1)}, f16[128,256]{1,0:T(8,128)(2,1)S(1)}, u32[]{:S(2)}, u32[]{:S(2)}) collective-permute-start(f16[128,256]{1,0:T(8,128)(2,1)S(1)} %get-tuple-element.57), channel_id=1, source_target_pairs={{0,16},{4,20},{8,24},{12,28},{16,0},{20,4},{24,8},{28,12},{1,17},{... | collective-permute-start | bytes 196616 | tf_op jit(solution)/shard_map/ppermute | solution.py:643
  38.2 8.4 %collective-permute-start.14 = (f16[128,256]{1,0:T(8,128)(2,1)S(1)}, f16[128,256]{1,0:T(8,128)(2,1)S(1)}, u32[]{:S(2)}, u32[]{:S(2)}) collective-permute-start(f16[128,256]{1,0:T(8,128)(2,1)S(1)} %get-tuple-element.57), channel_id=1, source_target_pairs={{0,24},{4,28},{8,0},{12,4},{16,8},{20,12},{24,16},{28,20},{1,25},{... | collective-permute-start | bytes 196616 | tf_op jit(solution)/shard_map/ppermute | solution.py:643
  40.5 6.1 %collective-permute-start.18 = (f16[128,256]{1,0:T(8,128)(2,1)S(1)}, f16[128,256]{1,0:T(8,128)(2,1)S(1)}, u32[]{:S(2)}, u32[]{:S(2)}) collective-permute-start(f16[128,256]{1,0:T(8,128)(2,1)S(1)} %get-tuple-element.57), channel_id=1, source_target_pairs={{0,8},{4,12},{8,16},{12,20},{16,24},{20,28},{24,0},{28,4},{1,9},{5... | collective-permute-start | bytes 196616 | tf_op jit(solution)/shard_map/ppermute | solution.py:643
  40.6 12.6 %collective-permute-start.13 = (f16[16,8,256]{2,1,0:T(8,128)(2,1)S(1)}, f16[16,8,256]{2,1,0:T(8,128)(2,1)S(1)}, u32[]{:S(2)}, u32[]{:S(2)}) collective-permute-start(f16[16,8,256]{2,1,0:T(8,128)(2,1)S(1)} %get-tuple-element.58), channel_id=1, source_target_pairs={{1,2},{2,1},{5,6},{6,5},{9,10},{10,9},{13,14},{14,13},{17,18},{18,... | collective-permute-start | bytes 196616 | tf_op jit(solution)/shard_map/ppermute | solution.py:612
  41.5 12.9 %collective-permute-start.12 = (f16[16,8,256]{2,1,0:T(8,128)(2,1)S(1)}, f16[16,8,256]{2,1,0:T(8,128)(2,1)S(1)}, u32[]{:S(2)}, u32[]{:S(2)}) collective-permute-start(f16[16,8,256]{2,1,0:T(8,128)(2,1)S(1)} %get-tuple-element.59), channel_id=1, source_target_pairs={{0,1},{1,0},{2,3},{3,2},{4,5},{5,4},{6,7},{7,6},{8,9},{9,8},{10,11... | collective-permute-start | bytes 196616 | tf_op jit(solution)/shard_map/ppermute | solution.py:611
  46.6 2.0 %collective-permute-start.19 = (f16[128,256]{1,0:T(8,128)(2,1)S(1)}, f16[128,256]{1,0:T(8,128)(2,1)S(1)}, u32[]{:S(2)}, u32[]{:S(2)}) collective-permute-start(f16[128,256]{1,0:T(8,128)(2,1)S(1)} %collective-permute-done.18), channel_id=1, source_target_pairs={{0,4},{4,0},{8,12},{12,8},{16,20},{20,16},{24,28},{28,24},{1,5},{5... | collective-permute-start | bytes 196616 | tf_op jit(solution)/shard_map/ppermute | solution.py:646
  46.7 1.9 %collective-permute-start.15 = (f16[128,256]{1,0:T(8,128)(2,1)S(1)}, f16[128,256]{1,0:T(8,128)(2,1)S(1)}, u32[]{:S(2)}, u32[]{:S(2)}) collective-permute-start(f16[128,256]{1,0:T(8,128)(2,1)S(1)} %collective-permute-done.14), channel_id=1, source_target_pairs={{0,4},{4,0},{8,12},{12,8},{16,20},{20,16},{24,28},{28,24},{1,5},{5... | collective-permute-start | bytes 196616 | tf_op jit(solution)/shard_map/ppermute | solution.py:646
  47.3 1.3 %collective-permute-start.17 = (f16[128,256]{1,0:T(8,128)(2,1)S(1)}, f16[128,256]{1,0:T(8,128)(2,1)S(1)}, u32[]{:S(2)}, u32[]{:S(2)}) collective-permute-start(f16[128,256]{1,0:T(8,128)(2,1)S(1)} %collective-permute-done.16), channel_id=1, source_target_pairs={{0,4},{4,0},{8,12},{12,8},{16,20},{20,16},{24,28},{28,24},{1,5},{5... | collective-permute-start | bytes 196616 | tf_op jit(solution)/shard_map/ppermute | solution.py:646
  50.8 9.3 %collective-permute-start.23 = (f16[256,256]{1,0:T(8,128)(2,1)S(1)}, f16[256,256]{1,0:T(8,128)(2,1)S(1)}, u32[]{:S(2)}, u32[]{:S(2)}) collective-permute-start(f16[256,256]{1,0:T(8,128)(2,1)S(1)} %get-tuple-element.71), channel_id=1, source_target_pairs={{0,3},{1,2},{2,1},{3,0},{4,7},{5,6},{6,5},{7,4},{8,11},{9,10},{10,... | collective-permute-start | bytes 393224 | tf_op jit(solution)/shard_map/ppermute | solution.py:595
  51.9 2.5 %collective-permute-start.20 = (f16[16,128]{1,0:T(8,128)(2,1)S(1)}, f16[16,128]{1,0:T(8,128)(2,1)S(1)}, u32[]{:S(2)}, u32[]{:S(2)}) collective-permute-start(f16[16,128]{1,0:T(8,128)(2,1)S(1)} %slice.161), channel_id=1, source_target_pairs={{0,4},{4,0},{8,12},{12,8},{16,20},{20,16},{24,28},{28,24},{1,5},{5... | collective-permute-start | bytes 12296 | tf_op jit(solution)/shard_map/ppermute | solution.py:700
  51.9 7.6 %collective-permute-start.21 = (f16[256,256]{1,0:T(8,128)(2,1)S(1)}, f16[256,256]{1,0:T(8,128)(2,1)S(1)}, u32[]{:S(2)}, u32[]{:S(2)}) collective-permute-start(f16[256,256]{1,0:T(8,128)(2,1)S(1)} %get-tuple-element.69), channel_id=1, source_target_pairs={{0,1},{1,0},{2,3},{3,2},{4,5},{5,4},{6,7},{7,6},{8,9},{9,8},{10,11... | collective-permute-start | bytes 393224 | tf_op jit(solution)/shard_map/ppermute | solution.py:595
  53.2 6.9 %collective-permute-start.22 = (f16[256,256]{1,0:T(8,128)(2,1)S(1)}, f16[256,256]{1,0:T(8,128)(2,1)S(1)}, u32[]{:S(2)}, u32[]{:S(2)}) collective-permute-start(f16[256,256]{1,0:T(8,128)(2,1)S(1)} %get-tuple-element.70), channel_id=1, source_target_pairs={{0,2},{1,3},{2,0},{3,1},{4,6},{5,7},{6,4},{7,5},{8,10},{9,11},{10,... | collective-permute-start | bytes 393224 | tf_op jit(solution)/shard_map/ppermute | solution.py:595
  57.1 5.6 %collective-permute-start.25 = (f16[16,8,256]{2,1,0:T(8,128)(2,1)S(1)}, f16[16,8,256]{2,1,0:T(8,128)(2,1)S(1)}, u32[]{:S(2)}, u32[]{:S(2)}) collective-permute-start(f16[16,8,256]{2,1,0:T(8,128)(2,1)S(1)} %get-tuple-element.64), channel_id=1, source_target_pairs={{4,8},{8,4},{12,16},{16,12},{20,24},{24,20},{28,0},{0,28},{5,9},{9... | collective-permute-start | bytes 196616 | tf_op jit(solution)/shard_map/ppermute | solution.py:612
  58.5 4.1 %collective-permute-start.24 = (f16[16,8,256]{2,1,0:T(8,128)(2,1)S(1)}, f16[16,8,256]{2,1,0:T(8,128)(2,1)S(1)}, u32[]{:S(2)}, u32[]{:S(2)}) collective-permute-start(f16[16,8,256]{2,1,0:T(8,128)(2,1)S(1)} %get-tuple-element.65), channel_id=1, source_target_pairs={{0,4},{4,0},{8,12},{12,8},{16,20},{20,16},{24,28},{28,24},{1,5},{5... | collective-permute-start | bytes 196616 | tf_op jit(solution)/shard_map/ppermute | solution.py:611
  60.3 3.1 %collective-permute-start.26 = (f16[128,256]{1,0:T(8,128)(2,1)S(1)}, f16[128,256]{1,0:T(8,128)(2,1)S(1)}, u32[]{:S(2)}, u32[]{:S(2)}) collective-permute-start(f16[128,256]{1,0:T(8,128)(2,1)S(1)} %get-tuple-element.55), channel_id=1, source_target_pairs={{0,4},{4,0},{8,12},{12,8},{16,20},{20,16},{24,28},{28,24},{1,5},{5... | collective-permute-start | bytes 196616 | tf_op jit(solution)/shard_map/ppermute | solution.py:646
  62.7 8.7 %collective-permute-start.31 = (f16[128,256]{1,0:T(8,128)(2,1)S(1)}, f16[128,256]{1,0:T(8,128)(2,1)S(1)}, u32[]{:S(2)}, u32[]{:S(2)}) collective-permute-start(f16[128,256]{1,0:T(8,128)(2,1)S(1)} %get-tuple-element.55), channel_id=1, source_target_pairs={{0,16},{4,20},{8,24},{12,28},{16,0},{20,4},{24,8},{28,12},{1,17},{... | collective-permute-start | bytes 196616 | tf_op jit(solution)/shard_map/ppermute | solution.py:643
  62.8 8.0 %collective-permute-start.29 = (f16[128,256]{1,0:T(8,128)(2,1)S(1)}, f16[128,256]{1,0:T(8,128)(2,1)S(1)}, u32[]{:S(2)}, u32[]{:S(2)}) collective-permute-start(f16[128,256]{1,0:T(8,128)(2,1)S(1)} %get-tuple-element.55), channel_id=1, source_target_pairs={{0,24},{4,28},{8,0},{12,4},{16,8},{20,12},{24,16},{28,20},{1,25},{... | collective-permute-start | bytes 196616 | tf_op jit(solution)/shard_map/ppermute | solution.py:643
  63.4 7.4 %collective-permute-start.33 = (f16[128,256]{1,0:T(8,128)(2,1)S(1)}, f16[128,256]{1,0:T(8,128)(2,1)S(1)}, u32[]{:S(2)}, u32[]{:S(2)}) collective-permute-start(f16[128,256]{1,0:T(8,128)(2,1)S(1)} %get-tuple-element.55), channel_id=1, source_target_pairs={{0,8},{4,12},{8,16},{12,20},{16,24},{20,28},{24,0},{28,4},{1,9},{5... | collective-permute-start | bytes 196616 | tf_op jit(solution)/shard_map/ppermute | solution.py:643
  65.2 11.5 %collective-permute-start.28 = (f16[16,8,256]{2,1,0:T(8,128)(2,1)S(1)}, f16[16,8,256]{2,1,0:T(8,128)(2,1)S(1)}, u32[]{:S(2)}, u32[]{:S(2)}) collective-permute-start(f16[16,8,256]{2,1,0:T(8,128)(2,1)S(1)} %get-tuple-element.62), channel_id=1, source_target_pairs={{1,2},{2,1},{5,6},{6,5},{9,10},{10,9},{13,14},{14,13},{17,18},{18,... | collective-permute-start | bytes 196616 | tf_op jit(solution)/shard_map/ppermute | solution.py:612
  65.8 12.0 %collective-permute-start.27 = (f16[16,8,256]{2,1,0:T(8,128)(2,1)S(1)}, f16[16,8,256]{2,1,0:T(8,128)(2,1)S(1)}, u32[]{:S(2)}, u32[]{:S(2)}) collective-permute-start(f16[16,8,256]{2,1,0:T(8,128)(2,1)S(1)} %get-tuple-element.63), channel_id=1, source_target_pairs={{0,1},{1,0},{2,3},{3,2},{4,5},{5,4},{6,7},{7,6},{8,9},{9,8},{10,11... | collective-permute-start | bytes 196616 | tf_op jit(solution)/shard_map/ppermute | solution.py:611
  70.8 2.0 %collective-permute-start.34 = (f16[128,256]{1,0:T(8,128)(2,1)S(1)}, f16[128,256]{1,0:T(8,128)(2,1)S(1)}, u32[]{:S(2)}, u32[]{:S(2)}) collective-permute-start(f16[128,256]{1,0:T(8,128)(2,1)S(1)} %collective-permute-done.33), channel_id=1, source_target_pairs={{0,4},{4,0},{8,12},{12,8},{16,20},{20,16},{24,28},{28,24},{1,5},{5... | collective-permute-start | bytes 196616 | tf_op jit(solution)/shard_map/ppermute | solution.py:646
  70.8 1.9 %collective-permute-start.30 = (f16[128,256]{1,0:T(8,128)(2,1)S(1)}, f16[128,256]{1,0:T(8,128)(2,1)S(1)}, u32[]{:S(2)}, u32[]{:S(2)}) collective-permute-start(f16[128,256]{1,0:T(8,128)(2,1)S(1)} %collective-permute-done.29), channel_id=1, source_target_pairs={{0,4},{4,0},{8,12},{12,8},{16,20},{20,16},{24,28},{28,24},{1,5},{5... | collective-permute-start | bytes 196616 | tf_op jit(solution)/shard_map/ppermute | solution.py:646
  71.4 1.3 %collective-permute-start.32 = (f16[128,256]{1,0:T(8,128)(2,1)S(1)}, f16[128,256]{1,0:T(8,128)(2,1)S(1)}, u32[]{:S(2)}, u32[]{:S(2)}) collective-permute-start(f16[128,256]{1,0:T(8,128)(2,1)S(1)} %collective-permute-done.31), channel_id=1, source_target_pairs={{0,4},{4,0},{8,12},{12,8},{16,20},{20,16},{24,28},{28,24},{1,5},{5... | collective-permute-start | bytes 196616 | tf_op jit(solution)/shard_map/ppermute | solution.py:646
  74.3 6.9 %collective-permute-start.38 = (f16[128,256]{1,0:T(8,128)(2,1)S(1)}, f16[128,256]{1,0:T(8,128)(2,1)S(1)}, u32[]{:S(2)}, u32[]{:S(2)}) collective-permute-start(f16[128,256]{1,0:T(8,128)(2,1)S(1)} %get-tuple-element.68), channel_id=1, source_target_pairs={{0,3},{1,2},{2,1},{3,0},{4,7},{5,6},{6,5},{7,4},{8,11},{9,10},{10,... | collective-permute-start | bytes 196616 | tf_op jit(solution)/shard_map/ppermute | solution.py:595
  75.5 2.3 %collective-permute-start.35 = (f16[16,128]{1,0:T(8,128)(2,1)S(1)}, f16[16,128]{1,0:T(8,128)(2,1)S(1)}, u32[]{:S(2)}, u32[]{:S(2)}) collective-permute-start(f16[16,128]{1,0:T(8,128)(2,1)S(1)} %slice.168), channel_id=1, source_target_pairs={{0,4},{4,0},{8,12},{12,8},{16,20},{20,16},{24,28},{28,24},{1,5},{5... | collective-permute-start | bytes 12296 | tf_op jit(solution)/shard_map/ppermute | solution.py:700
  75.5 4.8 %collective-permute-start.36 = (f16[128,256]{1,0:T(8,128)(2,1)S(1)}, f16[128,256]{1,0:T(8,128)(2,1)S(1)}, u32[]{:S(2)}, u32[]{:S(2)}) collective-permute-start(f16[128,256]{1,0:T(8,128)(2,1)S(1)} %get-tuple-element.66), channel_id=1, source_target_pairs={{0,1},{1,0},{2,3},{3,2},{4,5},{5,4},{6,7},{7,6},{8,9},{9,8},{10,11... | collective-permute-start | bytes 196616 | tf_op jit(solution)/shard_map/ppermute | solution.py:595
  76.7 4.5 %collective-permute-start.37 = (f16[128,256]{1,0:T(8,128)(2,1)S(1)}, f16[128,256]{1,0:T(8,128)(2,1)S(1)}, u32[]{:S(2)}, u32[]{:S(2)}) collective-permute-start(f16[128,256]{1,0:T(8,128)(2,1)S(1)} %get-tuple-element.67), channel_id=1, source_target_pairs={{0,2},{1,3},{2,0},{3,1},{4,6},{5,7},{6,4},{7,5},{8,10},{9,11},{10,... | collective-permute-start | bytes 196616 | tf_op jit(solution)/shard_map/ppermute | solution.py:595

commit v6 on v5

--- a/solution.py
+++ b/solution.py
@@ -357,7 +357,8 @@
         upper, lower = split_bf16(s_ref[first : first + count, :])
         at = pl.ds(pl.multiple_of(start, count), count)
         upper_ref[at, :] = upper
-        lower_ref[at, :] = lower
+        if split:
+            lower_ref[at, :] = lower
 
     for which, s_ref in enumerate(s_refs):
         start = place_ref[1 + which]
@@ -742,13 +743,14 @@
 
     gathered = first_gather(surface_guess, scale_s[0])
     mass = jnp.broadcast_to(mass_shift[..., None], mass_shift.shape + (HALF,))
+    wide, narrow = volume_matrices(stiffness, n_theta, radial, after=(gathered[0],))
     layers, face = volume_edges(volume_guess)
     halos = theta_halos(layers, scale_v[0]) + axial_halos(layers, scale_v[0])
     own, parts = bem_partial(
-        -1.0, True, first_places(chunk), bem_matrix, face, gathered, surface_rhs
+        -1.0, True, first_places(chunk), bem_matrix, face, gathered, surface_rhs,
+        after=(narrow,),
     )
     received, meanwhile = scatter(parts, scale_p[0])
-    wide, narrow = volume_matrices(stiffness, n_theta, radial, after=(meanwhile,))
     bulk, own, guess = volume_bulk(
         volume_guess, mass, wide, narrow, own, copied=True, after=(meanwhile,)
     )

time: 95.1 us -> 94 us (0.988)
  waiting for transfers between devices: 14.8 us -> 13.7 us
    ppermute x1, waiting for transfers between devices: 1.42 us -> 0.29 us  [first_gather(): other = lax.ppermute(mine, 'sector', sibling_perm())]
  transfers between devices with their start and end apart: 40 -> 40, of which waited for: 12 -> 13; matrix products, arithmetic and copies ran while one was open for 2% -> 2% of each run, Pallas kernels for 15% -> 16%
where the time goes in v6:
time: 94 us; the launch traced here: 93.7 us
  starting transfers between devices  44.9 us (48%)
  Pallas kernels  16.9 us (18%)
  waiting for transfers between devices  13.7 us (15%)
  blocking collectives  11 us (12%)
  local copies, waits for them, and re-layouts  3.06 us (3%)
  other arithmetic  2.59 us (3%)
  between operations  1.47 us (2%)
    pallas_call x15, Pallas kernels, call(): return lambda *args: called(*args, *after)  16.9 us
    ppermute x6, starting transfers between devices, neighbour_swap(): inner = lax.ppermute(jnp.where(odd, first, last), axis, within)  12 us
    all_to_all x1, blocking collectives, per_device(): lax.all_to_all(gram, ('sector', 'slab'), split_axis=0, concat_axis=0, til...  11 us
    ppermute x9, starting transfers between devices, slab_exchange(): lax.ppermute(messages[distance], 'slab', partner_perm(slabs, distance))  10.7 us
    all_to_all x1, starting transfers between devices, first_gather(): lax.all_to_all(messages.reshape(chips * slabs, turns * n_axial, lanes), (...  8.31 us
    ppermute x6, starting transfers between devices, neighbour_swap(): outer = lax.ppermute(jnp.where(odd, last, first), axis, across)  7.44 us
    ppermute x6, starting transfers between devices, sector_gather(): shares.append(lax.ppermute(own, 'sector', perm))  4.6 us
    ppermute x6, waiting for transfers between devices, neighbour_swap(): outer = lax.ppermute(jnp.where(odd, last, first), axis, across)  4.37 us
  transfers between devices with their start and end apart: 40, of which 13 were waited for; matrix products, arithmetic and copies ran while one was open for 2% of the time, Pallas kernels for 16%

profile of v6, /device:TPU:0, one launch (start us, length us, event | category | flops | bytes accessed | tf_op | source)
XLA Modules:
  0.0 93.7 jit_solution(7946044174871819637)
XLA Ops:
  0.6 1.0 %multiply_convert_fusion.17 = f16[8,16,256]{2,1,0:T(8,128)(2,1)S(1)} fusion(f32[8,16,256]{2,1,0:T(8,128)} %refs_4_.1), kind=kLoop, calls=%fused_computation.59 | loop fusion | flops 65536 | bytes 196608 | tf_op jit(solution)/shard_map/convert_element_type | solution.py:574
  1.6 0.7 broadcast_in_dim.15
  2.4 8.3 %all-to-all-start = ((f16[16,32,256]{2,1,0:T(8,128)(2,1)}), f16[16,32,256]{2,1,0:T(8,128)(2,1)S(1)}, u32[]{:S(2)}, u32[]{:S(2)}) async-start(f16[16,32,256]{2,1,0:T(8,128)(2,1)} %bitcast.3), calls=%async_computation | async-start | bytes 524288 | tf_op jit(solution)/shard_map/all_to_all | solution.py:674
  10.7 1.6 %copy-done.1 = f32[16,16,8,256]{3,2,1,0:T(8,128)S(1)} copy-done((f32[16,16,8,256]{3,2,1,0:T(8,128)S(1)}, f32[16,16,8,256]{3,2,1,0:T(8,128)}, u32[]{:S(2)}) %copy-start.1) | copy-done | bytes 2097176
  12.3 0.6 volume_edges.1
  12.9 2.7 %collective-permute-start.3 = (f16[16,8,256]{2,1,0:T(8,128)(2,1)S(1)}, f16[16,8,256]{2,1,0:T(8,128)(2,1)S(1)}, u32[]{:S(2)}, u32[]{:S(2)}) collective-permute-start(f16[16,8,256]{2,1,0:T(8,128)(2,1)S(1)} %get-tuple-element.89), channel_id=1, source_target_pairs={{4,8},{8,4},{12,16},{16,12},{20,24},{24,20},{28,0},{0,28},{5,9},{9... | collective-permute-start | bytes 196616 | tf_op jit(solution)/shard_map/ppermute | solution.py:613
  15.6 0.7 collective-permute-start.5
  16.3 4.2 %collective-permute-start.4 = (f16[16,8,256]{2,1,0:T(8,128)(2,1)S(1)}, f16[16,8,256]{2,1,0:T(8,128)(2,1)S(1)}, u32[]{:S(2)}, u32[]{:S(2)}) collective-permute-start(f16[16,8,256]{2,1,0:T(8,128)(2,1)S(1)} %get-tuple-element.88), channel_id=1, source_target_pairs={{0,1},{1,0},{2,3},{3,2},{4,5},{5,4},{6,7},{7,6},{8,9},{9,8},{10,11... | collective-permute-start | bytes 196616 | tf_op jit(solution)/shard_map/ppermute | solution.py:612
  21.1 1.1 %volume_matrices.1 = (bf16[2,128,256]{2,1,0:T(8,128)(2,1)S(1)}, bf16[2,128,128]{2,1,0:T(8,128)(2,1)S(1)}) custom-call(f32[3,8,8]{2,1,0:T(8,128)S(1)} %copy-done.6, f32[128,256]{1,0:T(8,128)S(1)} %bitcast.92), custom_call_target="tpu_custom_call" | custom-call | flops 1000 | bytes 1000 | tf_op jit(solution)/shard_map/volume_matrices/pallas_call | solution.py:45
  22.6 2.0 %bem_partial.3 = (f32[256,256]{1,0:T(8,128)S(1)}, f32[3,256,256]{2,1,0:T(8,128)S(1)}) custom-call(s32[9]{0:T(128)S(1)} %stack.67.refs_0_, bf16[2,512,1024]{2,1,0:T(8,128)(2,1)S(1)} %copy-done, f32[8,16,256]{2,1,0:T(8,128)S(1)} %get-tuple-element.30.refs_2_, f32[128,256]{1,0:T(8,128)S(1)} %bitcast.93, f32[128,256]{1,0:T(8,128)S(1)} %bitcast.104, ...), custom_call_target="tpu_custom_call" | custom-call | flops 1000 | bytes 1000 | tf_op jit(solution)/shard_map/bem_partial/pallas_call | solution.py:45
  25.1 1.5 %collective-permute-start.8 = (f16[256,256]{1,0:T(8,128)(2,1)S(1)}, f16[256,256]{1,0:T(8,128)(2,1)S(1)}, u32[]{:S(2)}, u32[]{:S(2)}) collective-permute-start(f16[256,256]{1,0:T(8,128)(2,1)S(1)} %get-tuple-element.74), channel_id=1, source_target_pairs={{0,3},{1,2},{2,1},{3,0},{4,7},{5,6},{6,5},{7,4},{8,11},{9,10},{10,... | collective-permute-start | bytes 393224 | tf_op jit(solution)/shard_map/ppermute | solution.py:596
  26.6 1.2 %collective-permute-start.6 = (f16[256,256]{1,0:T(8,128)(2,1)S(1)}, f16[256,256]{1,0:T(8,128)(2,1)S(1)}, u32[]{:S(2)}, u32[]{:S(2)}) collective-permute-start(f16[256,256]{1,0:T(8,128)(2,1)S(1)} %get-tuple-element.72), channel_id=1, source_target_pairs={{0,1},{1,0},{2,3},{3,2},{4,5},{5,4},{6,7},{7,6},{8,9},{9,8},{10,11... | collective-permute-start | bytes 393224 | tf_op jit(solution)/shard_map/ppermute | solution.py:596
  27.8 0.8 collective-permute-start.7
  29.1 1.6 %volume_bulk.3 = (f32[16,16,8,256]{3,2,1,0:T(8,128)S(1)}, f32[256,256]{1,0:T(8,128)S(1)}, f32[16,16,8,256]{3,2,1,0:T(8,128)S(1)}) custom-call(f32[16,16,8,256]{3,2,1,0:T(8,128)S(1)} %copy-done.2, f32[16,16,8,128]{3,2,1,0:T(8,128)S(1)} %broadcast_in_dim.6.refs_1_, ...), custom_call_target="tpu_custom_call", output_to_operand_aliasing={{1}: (4, {})} | custom-call | flops 1000 | bytes 1000 | tf_op jit(solution)/shard_map/volume_bulk/pallas_call | solution.py:45
  30.7 0.7 finish_first_kernel.1
  31.4 1.2 %collective-permute-start.10 = (f16[16,8,256]{2,1,0:T(8,128)(2,1)S(1)}, f16[16,8,256]{2,1,0:T(8,128)(2,1)S(1)}, u32[]{:S(2)}, u32[]{:S(2)}) collective-permute-start(f16[16,8,256]{2,1,0:T(8,128)(2,1)S(1)} %get-tuple-element.60), channel_id=1, source_target_pairs={{4,8},{8,4},{12,16},{16,12},{20,24},{24,20},{28,0},{0,28},{5,9},{9... | collective-permute-start | bytes 196616 | tf_op jit(solution)/shard_map/ppermute | solution.py:613
  33.0 1.5 %volume_bulk.4 = (f32[16,16,8,256]{3,2,1,0:T(8,128)S(1)}, f32[256,256]{1,0:T(8,128)S(1)}) custom-call(f32[16,16,8,256]{3,2,1,0:T(8,128)S(1)} %get-tuple-element.39.refs_0_, f32[16,16,8,128]{3,2,1,0:T(8,128)S(1)} %broadcast_in_dim.6.refs_1_, bf16[2,128,256]{2,1,0:T(8,128)(2,1)S(1)} %get-tuple-element.28.refs_2_, ...), custom_call_target="tpu_custom_call", output_to_operand_aliasing={{1}: (4, {})} | custom-call | flops 1000 | bytes 1000 | tf_op jit(solution)/shard_map/volume_bulk/pallas_call | solution.py:45
  34.9 2.1 %collective-permute-done.10 = f16[16,8,256]{2,1,0:T(8,128)(2,1)S(1)} collective-permute-done((f16[16,8,256]{2,1,0:T(8,128)(2,1)S(1)}, f16[16,8,256]{2,1,0:T(8,128)(2,1)S(1)}, u32[]{:S(2)}, u32[]{:S(2)}) %collective-permute-start.10) | collective-permute-done | bytes 65568 | tf_op jit(solution)/shard_map/ppermute | solution.py:613
  37.1 2.3 %collective-permute-start.14 = (f16[128,256]{1,0:T(8,128)(2,1)S(1)}, f16[128,256]{1,0:T(8,128)(2,1)S(1)}, u32[]{:S(2)}, u32[]{:S(2)}) collective-permute-start(f16[128,256]{1,0:T(8,128)(2,1)S(1)} %get-tuple-element.57), channel_id=1, source_target_pairs={{0,24},{4,28},{8,0},{12,4},{16,8},{20,12},{24,16},{28,20},{1,25},{... | collective-permute-start | bytes 196616 | tf_op jit(solution)/shard_map/ppermute | solution.py:644
  39.5 0.8 collective-permute-start.13
  40.4 3.8 %collective-permute-start.12 = (f16[16,8,256]{2,1,0:T(8,128)(2,1)S(1)}, f16[16,8,256]{2,1,0:T(8,128)(2,1)S(1)}, u32[]{:S(2)}, u32[]{:S(2)}) collective-permute-start(f16[16,8,256]{2,1,0:T(8,128)(2,1)S(1)} %get-tuple-element.59), channel_id=1, source_target_pairs={{0,1},{1,0},{2,3},{3,2},{4,5},{5,4},{6,7},{7,6},{8,9},{9,8},{10,11... | collective-permute-start | bytes 196616 | tf_op jit(solution)/shard_map/ppermute | solution.py:612
  44.2 1.3 %collective-permute-done.18 = f16[128,256]{1,0:T(8,128)(2,1)S(1)} collective-permute-done((f16[128,256]{1,0:T(8,128)(2,1)S(1)}, f16[128,256]{1,0:T(8,128)(2,1)S(1)}, u32[]{:S(2)}, u32[]{:S(2)}) %collective-permute-start.18) | collective-permute-done | bytes 65568 | tf_op jit(solution)/shard_map/ppermute | solution.py:644
  46.3 1.2 %collective-permute-done.17 = f16[128,256]{1,0:T(8,128)(2,1)S(1)} collective-permute-done((f16[128,256]{1,0:T(8,128)(2,1)S(1)}, f16[128,256]{1,0:T(8,128)(2,1)S(1)}, u32[]{:S(2)}, u32[]{:S(2)}) %collective-permute-start.17) | collective-permute-done | bytes 65568 | tf_op jit(solution)/shard_map/ppermute | solution.py:647
  47.6 2.1 %bem_partial.4 = (f32[256,256]{1,0:T(8,128)S(1)}, f32[3,256,256]{2,1,0:T(8,128)S(1)}) custom-call(s32[9]{0:T(128)S(1)} %stack.76.refs_0_, bf16[2,512,1024]{2,1,0:T(8,128)(2,1)S(1)} %copy-done, f32[8,16,256]{2,1,0:T(8,128)S(1)} %get-tuple-element.43.refs_2_, f32[128,256]{1,0:T(8,128)S(1)} %get-tuple-element.56.refs_3_, ...), custom_call_target="tpu_custom_call" | custom-call | flops 1000 | bytes 1000 | tf_op jit(solution)/shard_map/bem_partial/pallas_call | solution.py:45
  49.7 1.1 %collective-permute-start.23 = (f16[256,256]{1,0:T(8,128)(2,1)S(1)}, f16[256,256]{1,0:T(8,128)(2,1)S(1)}, u32[]{:S(2)}, u32[]{:S(2)}) collective-permute-start(f16[256,256]{1,0:T(8,128)(2,1)S(1)} %get-tuple-element.71), channel_id=1, source_target_pairs={{0,3},{1,2},{2,1},{3,0},{4,7},{5,6},{6,5},{7,4},{8,11},{9,10},{10,... | collective-permute-start | bytes 393224 | tf_op jit(solution)/shard_map/ppermute | solution.py:596
  50.9 1.3 %collective-permute-start.21 = (f16[256,256]{1,0:T(8,128)(2,1)S(1)}, f16[256,256]{1,0:T(8,128)(2,1)S(1)}, u32[]{:S(2)}, u32[]{:S(2)}) collective-permute-start(f16[256,256]{1,0:T(8,128)(2,1)S(1)} %get-tuple-element.69), channel_id=1, source_target_pairs={{0,1},{1,0},{2,3},{3,2},{4,5},{5,4},{6,7},{7,6},{8,9},{9,8},{10,11... | collective-permute-start | bytes 393224 | tf_op jit(solution)/shard_map/ppermute | solution.py:596
  52.1 1.2 %collective-permute-start.22 = (f16[256,256]{1,0:T(8,128)(2,1)S(1)}, f16[256,256]{1,0:T(8,128)(2,1)S(1)}, u32[]{:S(2)}, u32[]{:S(2)}) collective-permute-start(f16[256,256]{1,0:T(8,128)(2,1)S(1)} %get-tuple-element.70), channel_id=1, source_target_pairs={{0,2},{1,3},{2,0},{3,1},{4,6},{5,7},{6,4},{7,5},{8,10},{9,11},{10,... | collective-permute-start | bytes 393224 | tf_op jit(solution)/shard_map/ppermute | solution.py:596
  53.4 0.9 finish_second_kernel.1
  54.5 1.5 %volume_bulk.5 = (f32[16,16,8,256]{3,2,1,0:T(8,128)S(1)}, f32[256,256]{1,0:T(8,128)S(1)}) custom-call(f32[16,16,8,256]{3,2,1,0:T(8,128)S(1)} %get-tuple-element.46.refs_0_, f32[16,16,8,128]{3,2,1,0:T(8,128)S(1)} %broadcast_in_dim.6.refs_1_, bf16[2,128,256]{2,1,0:T(8,128)(2,1)S(1)} %get-tuple-element.28.refs_2_, ...), custom_call_target="tpu_custom_call", output_to_operand_aliasing={{1}: (4, {})} | custom-call | flops 1000 | bytes 1000 | tf_op jit(solution)/shard_map/volume_bulk/pallas_call | solution.py:45
  56.0 1.4 %collective-permute-start.25 = (f16[16,8,256]{2,1,0:T(8,128)(2,1)S(1)}, f16[16,8,256]{2,1,0:T(8,128)(2,1)S(1)}, u32[]{:S(2)}, u32[]{:S(2)}) collective-permute-start(f16[16,8,256]{2,1,0:T(8,128)(2,1)S(1)} %get-tuple-element.64), channel_id=1, source_target_pairs={{4,8},{8,4},{12,16},{16,12},{20,24},{24,20},{28,0},{0,28},{5,9},{9... | collective-permute-start | bytes 196616 | tf_op jit(solution)/shard_map/ppermute | solution.py:613
  57.4 1.0 %collective-permute-done.21 = f16[256,256]{1,0:T(8,128)(2,1)S(1)} collective-permute-done((f16[256,256]{1,0:T(8,128)(2,1)S(1)}, f16[256,256]{1,0:T(8,128)(2,1)S(1)}, u32[]{:S(2)}, u32[]{:S(2)}) %collective-permute-start.21) | collective-permute-done | bytes 131104 | tf_op jit(solution)/shard_map/ppermute | solution.py:596
  58.5 0.6 collective-permute-done.22
  59.3 2.3 %collective-permute-done.25 = f16[16,8,256]{2,1,0:T(8,128)(2,1)S(1)} collective-permute-done((f16[16,8,256]{2,1,0:T(8,128)(2,1)S(1)}, f16[16,8,256]{2,1,0:T(8,128)(2,1)S(1)}, u32[]{:S(2)}, u32[]{:S(2)}) %collective-permute-start.25) | collective-permute-done | bytes 65568 | tf_op jit(solution)/shard_map/ppermute | solution.py:613
  61.7 0.6 collective-permute-start.29
  62.3 1.5 %collective-permute-start.33 = (f16[128,256]{1,0:T(8,128)(2,1)S(1)}, f16[128,256]{1,0:T(8,128)(2,1)S(1)}, u32[]{:S(2)}, u32[]{:S(2)}) collective-permute-start(f16[128,256]{1,0:T(8,128)(2,1)S(1)} %get-tuple-element.55), channel_id=1, source_target_pairs={{0,8},{4,12},{8,16},{12,20},{16,24},{20,28},{24,0},{28,4},{1,9},{5... | collective-permute-start | bytes 196616 | tf_op jit(solution)/shard_map/ppermute | solution.py:644
  64.1 0.7 collective-permute-start.28
  64.7 3.6 %collective-permute-start.27 = (f16[16,8,256]{2,1,0:T(8,128)(2,1)S(1)}, f16[16,8,256]{2,1,0:T(8,128)(2,1)S(1)}, u32[]{:S(2)}, u32[]{:S(2)}) collective-permute-start(f16[16,8,256]{2,1,0:T(8,128)(2,1)S(1)} %get-tuple-element.63), channel_id=1, source_target_pairs={{0,1},{1,0},{2,3},{3,2},{4,5},{5,4},{6,7},{7,6},{8,9},{9,8},{10,11... | collective-permute-start | bytes 196616 | tf_op jit(solution)/shard_map/ppermute | solution.py:612
  68.4 1.3 %collective-permute-done.33 = f16[128,256]{1,0:T(8,128)(2,1)S(1)} collective-permute-done((f16[128,256]{1,0:T(8,128)(2,1)S(1)}, f16[128,256]{1,0:T(8,128)(2,1)S(1)}, u32[]{:S(2)}, u32[]{:S(2)}) %collective-permute-start.33) | collective-permute-done | bytes 65568 | tf_op jit(solution)/shard_map/ppermute | solution.py:644
  70.4 1.2 %collective-permute-done.32 = f16[128,256]{1,0:T(8,128)(2,1)S(1)} collective-permute-done((f16[128,256]{1,0:T(8,128)(2,1)S(1)}, f16[128,256]{1,0:T(8,128)(2,1)S(1)}, u32[]{:S(2)}, u32[]{:S(2)}) %collective-permute-start.32) | collective-permute-done | bytes 65568 | tf_op jit(solution)/shard_map/ppermute | solution.py:647
  71.7 1.4 %bem_partial.5 = (f32[256,256]{1,0:T(8,128)S(1)}, f32[3,256,256]{2,1,0:T(8,128)S(1)}) custom-call(s32[9]{0:T(128)S(1)} %stack.76.refs_0_, bf16[2,512,1024]{2,1,0:T(8,128)(2,1)S(1)} %copy-done, f32[8,16,256]{2,1,0:T(8,128)S(1)} %get-tuple-element.50.refs_2_, f32[128,256]{1,0:T(8,128)S(1)} %get-tuple-element.54.refs_3_, ...), custom_call_target="tpu_custom_call" | custom-call | flops 1000 | bytes 1000 | tf_op jit(solution)/shard_map/bem_partial/pallas_call | solution.py:45
  73.2 1.2 %collective-permute-start.38 = (f16[128,256]{1,0:T(8,128)(2,1)S(1)}, f16[128,256]{1,0:T(8,128)(2,1)S(1)}, u32[]{:S(2)}, u32[]{:S(2)}) collective-permute-start(f16[128,256]{1,0:T(8,128)(2,1)S(1)} %get-tuple-element.68), channel_id=1, source_target_pairs={{0,3},{1,2},{2,1},{3,0},{4,7},{5,6},{6,5},{7,4},{8,11},{9,10},{10,... | collective-permute-start | bytes 196616 | tf_op jit(solution)/shard_map/ppermute | solution.py:596
  74.4 1.1 %collective-permute-start.36 = (f16[128,256]{1,0:T(8,128)(2,1)S(1)}, f16[128,256]{1,0:T(8,128)(2,1)S(1)}, u32[]{:S(2)}, u32[]{:S(2)}) collective-permute-start(f16[128,256]{1,0:T(8,128)(2,1)S(1)} %get-tuple-element.66), channel_id=1, source_target_pairs={{0,1},{1,0},{2,3},{3,2},{4,5},{5,4},{6,7},{7,6},{8,9},{9,8},{10,11... | collective-permute-start | bytes 196616 | tf_op jit(solution)/shard_map/ppermute | solution.py:596
  75.6 1.2 %collective-permute-start.37 = (f16[128,256]{1,0:T(8,128)(2,1)S(1)}, f16[128,256]{1,0:T(8,128)(2,1)S(1)}, u32[]{:S(2)}, u32[]{:S(2)}) collective-permute-start(f16[128,256]{1,0:T(8,128)(2,1)S(1)} %get-tuple-element.67), channel_id=1, source_target_pairs={{0,2},{1,3},{2,0},{3,1},{4,6},{5,7},{6,4},{7,5},{8,10},{9,11},{10,... | collective-permute-start | bytes 196616 | tf_op jit(solution)/shard_map/ppermute | solution.py:596
  76.8 1.2 %finish_third_kernel.1.refs_2_ = f32[5,8,128]{2,1,0:T(8,128)S(1)} custom-call(f32[16,16,8,256]{3,2,1,0:T(8,128)S(1)} %get-tuple-element.48.refs_0_, f32[8,16,256]{2,1,0:T(8,128)S(1)} %bitcast.96, f32[16,8,256]{2,1,0:T(8,128)S(1)} %get-tuple-element.94.refs_2_, f32[16,8,256]{2,1,0:T(8,128)S(1)} %get-tuple-element.93.refs_3_, ...), custom_call_target="tpu_custom_call" | custom-call | flops 1000 | bytes 1000 | tf_op jit(solution)/shard_map/finish_third_kernel/pallas_call | solution.py:45
  78.0 1.2 %collective-permute-done.36 = f16[128,256]{1,0:T(8,128)(2,1)S(1)} collective-permute-done((f16[128,256]{1,0:T(8,128)(2,1)S(1)}, f16[128,256]{1,0:T(8,128)(2,1)S(1)}, u32[]{:S(2)}, u32[]{:S(2)}) %collective-permute-start.36) | collective-permute-done | bytes 65568 | tf_op jit(solution)/shard_map/ppermute | solution.py:596
  79.2 0.9 collective-permute-done.37
  80.3 11.0 %all_to_all.10.refs_0_ = f32[32,1,1152]{2,1,0:T(1,128)S(1)} all-to-all(f32[32,1,1152]{2,1,0:T(1,128)S(1)} %local_gram.1), channel_id=1, replica_groups=mesh['sector'=8,'slab'=4] {'sector','slab'}, dimensions={0} | all-to-all | bytes 294912 | tf_op jit(solution)/shard_map/all_to_all | solution.py:787
  91.3 2.3 %final_solution.1 = (f32[16,16,8,256]{3,2,1,0:T(8,128)}, f32[8,16,256]{2,1,0:T(8,128)}) custom-call(f32[32,1,1152]{2,1,0:T(1,128)S(1)} %all_to_all.10.refs_0_, f32[16,16,8,256]{3,2,1,0:T(8,128)S(1)} %get-tuple-element.53.refs_1_, f32[16,16,8,256]{3,2,1,0:T(8,128)S(1)} %pass_after.2.refs_6_.refs_2_, f32[16,16,8,256]{3,2,1,0:T(8,128)S(1)} %pass_after.3.refs_7_.refs_3_, ...), custom_call_target="tpu_custom_call" | custom-call | flops 1000 | bytes 1000 | tf_op jit(solution)/shard_map/final_solution/pallas_call | solution.py:45
  (117 shorter events, 5.5 us)
Async XLA Ops:
  0.6 19.9 %copy-start.7 = (f32[16,16,8]{1,2,0:T(8,128)S(1)}, f32[16,16,8]{1,2,0:T(8,128)}, u32[]{:S(2)}) copy-start(f32[16,16,8]{1,2,0:T(8,128)} %param.13) | copy-start | bytes 24580
  2.4 18.6 %all-to-all-start = ((f16[16,32,256]{2,1,0:T(8,128)(2,1)}), f16[16,32,256]{2,1,0:T(8,128)(2,1)S(1)}, u32[]{:S(2)}, u32[]{:S(2)}) async-start(f16[16,32,256]{2,1,0:T(8,128)(2,1)} %bitcast.3), calls=%async_computation | async-start | bytes 524288 | tf_op jit(solution)/shard_map/all_to_all | solution.py:674
  10.7 1.6 %copy-start.1 = (f32[16,16,8,256]{3,2,1,0:T(8,128)S(1)}, f32[16,16,8,256]{3,2,1,0:T(8,128)}, u32[]{:S(2)}) copy-start(f32[16,16,8,256]{3,2,1,0:T(8,128)} %refs_0_.5) | copy-start | bytes 6291460
  12.9 8.2 %copy-start.6 = (f32[3,8,8]{2,1,0:T(8,128)S(1)}, f32[3,8,8]{2,1,0:T(8,128)}, u32[]{:S(2)}) copy-start(f32[3,8,8]{2,1,0:T(8,128)} %refs_0_.3) | copy-start | bytes 2308
  12.9 7.9 %collective-permute-start.3 = (f16[16,8,256]{2,1,0:T(8,128)(2,1)S(1)}, f16[16,8,256]{2,1,0:T(8,128)(2,1)S(1)}, u32[]{:S(2)}, u32[]{:S(2)}) collective-permute-start(f16[16,8,256]{2,1,0:T(8,128)(2,1)S(1)} %get-tuple-element.89), channel_id=1, source_target_pairs={{4,8},{8,4},{12,16},{16,12},{20,24},{24,20},{28,0},{0,28},{5,9},{9... | collective-permute-start | bytes 196616 | tf_op jit(solution)/shard_map/ppermute | solution.py:613
  15.6 5.2 %collective-permute-start.2 = (f16[16,8,256]{2,1,0:T(8,128)(2,1)S(1)}, f16[16,8,256]{2,1,0:T(8,128)(2,1)S(1)}, u32[]{:S(2)}, u32[]{:S(2)}) collective-permute-start(f16[16,8,256]{2,1,0:T(8,128)(2,1)S(1)} %get-tuple-element.90), channel_id=1, source_target_pairs={{0,4},{4,0},{8,12},{12,8},{16,20},{20,16},{24,28},{28,24},{1,5},{5... | collective-permute-start | bytes 196616 | tf_op jit(solution)/shard_map/ppermute | solution.py:612
  15.6 9.5 %collective-permute-start.5 = (f16[16,8,256]{2,1,0:T(8,128)(2,1)S(1)}, f16[16,8,256]{2,1,0:T(8,128)(2,1)S(1)}, u32[]{:S(2)}, u32[]{:S(2)}) collective-permute-start(f16[16,8,256]{2,1,0:T(8,128)(2,1)S(1)} %get-tuple-element.87), channel_id=1, source_target_pairs={{1,2},{2,1},{5,6},{6,5},{9,10},{10,9},{13,14},{14,13},{17,18},{18,... | collective-permute-start | bytes 196616 | tf_op jit(solution)/shard_map/ppermute | solution.py:613
  16.3 8.8 %collective-permute-start.4 = (f16[16,8,256]{2,1,0:T(8,128)(2,1)S(1)}, f16[16,8,256]{2,1,0:T(8,128)(2,1)S(1)}, u32[]{:S(2)}, u32[]{:S(2)}) collective-permute-start(f16[16,8,256]{2,1,0:T(8,128)(2,1)S(1)} %get-tuple-element.88), channel_id=1, source_target_pairs={{0,1},{1,0},{2,3},{3,2},{4,5},{5,4},{6,7},{7,6},{8,9},{9,8},{10,11... | collective-permute-start | bytes 196616 | tf_op jit(solution)/shard_map/ppermute | solution.py:612
  20.8 1.8 %copy-start = (bf16[2,512,1024]{2,1,0:T(8,128)(2,1)S(1)}, bf16[2,512,1024]{2,1,0:T(8,128)(2,1)}, u32[]{:S(2)}) copy-start(bf16[2,512,1024]{2,1,0:T(8,128)(2,1)} %refs_1_.7) | copy-start | bytes 6291460
  20.8 1.8 %copy-start.5 = (f32[8,16,256]{2,1,0:T(8,128)S(1)}, f32[8,16,256]{2,1,0:T(8,128)}, u32[]{:S(2)}) copy-start(f32[8,16,256]{2,1,0:T(8,128)} %refs_11_.1) | copy-start | bytes 393220
  21.0 1.5 %collective-permute-start = (f16[16,32,256]{2,1,0:T(8,128)(2,1)S(1)}, f16[16,32,256]{2,1,0:T(8,128)(2,1)S(1)}, u32[]{:S(2)}, u32[]{:S(2)}) collective-permute-start(f16[16,32,256]{2,1,0:T(8,128)(2,1)S(1)} %all-to-all-done), channel_id=1, source_target_pairs={{0,4},{4,0},{8,12},{12,8},{16,20},{20,16},{24,28},{28,24},{1,5},{5... | collective-permute-start | bytes 786440 | tf_op jit(solution)/shard_map/ppermute | solution.py:682
  24.7 4.4 %copy-start.2 = (f32[16,16,8,256]{3,2,1,0:T(8,128)S(1)}, f32[16,16,8,256]{3,2,1,0:T(8,128)}, u32[]{:S(2)}) copy-start(f32[16,16,8,256]{3,2,1,0:T(8,128)} %refs_0_.5) | copy-start | bytes 6291460
  24.8 3.9 %collective-permute-start.1 = (f16[16,128]{1,0:T(8,128)(2,1)S(1)}, f16[16,128]{1,0:T(8,128)(2,1)S(1)}, u32[]{:S(2)}, u32[]{:S(2)}) collective-permute-start(f16[16,128]{1,0:T(8,128)(2,1)S(1)} %slice.156), channel_id=1, source_target_pairs={{0,4},{4,0},{8,12},{12,8},{16,20},{20,16},{24,28},{28,24},{1,5},{5... | collective-permute-start | bytes 12296 | tf_op jit(solution)/shard_map/ppermute | solution.py:701
  25.1 9.5 %collective-permute-start.8 = (f16[256,256]{1,0:T(8,128)(2,1)S(1)}, f16[256,256]{1,0:T(8,128)(2,1)S(1)}, u32[]{:S(2)}, u32[]{:S(2)}) collective-permute-start(f16[256,256]{1,0:T(8,128)(2,1)S(1)} %get-tuple-element.74), channel_id=1, source_target_pairs={{0,3},{1,2},{2,1},{3,0},{4,7},{5,6},{6,5},{7,4},{8,11},{9,10},{10,... | collective-permute-start | bytes 393224 | tf_op jit(solution)/shard_map/ppermute | solution.py:596
  26.6 7.9 %collective-permute-start.6 = (f16[256,256]{1,0:T(8,128)(2,1)S(1)}, f16[256,256]{1,0:T(8,128)(2,1)S(1)}, u32[]{:S(2)}, u32[]{:S(2)}) collective-permute-start(f16[256,256]{1,0:T(8,128)(2,1)S(1)} %get-tuple-element.72), channel_id=1, source_target_pairs={{0,1},{1,0},{2,3},{3,2},{4,5},{5,4},{6,7},{7,6},{8,9},{9,8},{10,11... | collective-permute-start | bytes 393224 | tf_op jit(solution)/shard_map/ppermute | solution.py:596
  27.8 6.7 %collective-permute-start.7 = (f16[256,256]{1,0:T(8,128)(2,1)S(1)}, f16[256,256]{1,0:T(8,128)(2,1)S(1)}, u32[]{:S(2)}, u32[]{:S(2)}) collective-permute-start(f16[256,256]{1,0:T(8,128)(2,1)S(1)} %get-tuple-element.73), channel_id=1, source_target_pairs={{0,2},{1,3},{2,0},{3,1},{4,6},{5,7},{6,4},{7,5},{8,10},{9,11},{10,... | collective-permute-start | bytes 393224 | tf_op jit(solution)/shard_map/ppermute | solution.py:596
  29.0 1.6 %copy-start.3 = (f32[16,16,8,256]{3,2,1,0:T(8,128)S(1)}, f32[16,16,8,256]{3,2,1,0:T(8,128)}, u32[]{:S(2)}) copy-start(f32[16,16,8,256]{3,2,1,0:T(8,128)} %refs_6_.1) | copy-start | bytes 6291460
  29.1 1.6 %copy-start.4 = (f32[8,16,256]{2,1,0:T(8,128)S(1)}, f32[8,16,256]{2,1,0:T(8,128)}, u32[]{:S(2)}) copy-start(f32[8,16,256]{2,1,0:T(8,128)} %refs_4_.1) | copy-start | bytes 393220
  31.4 5.6 %collective-permute-start.10 = (f16[16,8,256]{2,1,0:T(8,128)(2,1)S(1)}, f16[16,8,256]{2,1,0:T(8,128)(2,1)S(1)}, u32[]{:S(2)}, u32[]{:S(2)}) collective-permute-start(f16[16,8,256]{2,1,0:T(8,128)(2,1)S(1)} %get-tuple-element.60), channel_id=1, source_target_pairs={{4,8},{8,4},{12,16},{16,12},{20,24},{24,20},{28,0},{0,28},{5,9},{9... | collective-permute-start | bytes 196616 | tf_op jit(solution)/shard_map/ppermute | solution.py:613
  32.6 4.4 %collective-permute-start.9 = (f16[16,8,256]{2,1,0:T(8,128)(2,1)S(1)}, f16[16,8,256]{2,1,0:T(8,128)(2,1)S(1)}, u32[]{:S(2)}, u32[]{:S(2)}) collective-permute-start(f16[16,8,256]{2,1,0:T(8,128)(2,1)S(1)} %get-tuple-element.61), channel_id=1, source_target_pairs={{0,4},{4,0},{8,12},{12,8},{16,20},{20,16},{24,28},{28,24},{1,5},{5... | collective-permute-start | bytes 196616 | tf_op jit(solution)/shard_map/ppermute | solution.py:612
  34.7 4.7 %collective-permute-start.11 = (f16[128,256]{1,0:T(8,128)(2,1)S(1)}, f16[128,256]{1,0:T(8,128)(2,1)S(1)}, u32[]{:S(2)}, u32[]{:S(2)}) collective-permute-start(f16[128,256]{1,0:T(8,128)(2,1)S(1)} %get-tuple-element.57), channel_id=1, source_target_pairs={{0,4},{4,0},{8,12},{12,8},{16,20},{20,16},{24,28},{28,24},{1,5},{5... | collective-permute-start | bytes 196616 | tf_op jit(solution)/shard_map/ppermute | solution.py:647
  37.0 9.1 %collective-permute-start.16 = (f16[128,256]{1,0:T(8,128)(2,1)S(1)}, f16[128,256]{1,0:T(8,128)(2,1)S(1)}, u32[]{:S(2)}, u32[]{:S(2)}) collective-permute-start(f16[128,256]{1,0:T(8,128)(2,1)S(1)} %get-tuple-element.57), channel_id=1, source_target_pairs={{0,16},{4,20},{8,24},{12,28},{16,0},{20,4},{24,8},{28,12},{1,17},{... | collective-permute-start | bytes 196616 | tf_op jit(solution)/shard_map/ppermute | solution.py:644
  37.1 8.4 %collective-permute-start.14 = (f16[128,256]{1,0:T(8,128)(2,1)S(1)}, f16[128,256]{1,0:T(8,128)(2,1)S(1)}, u32[]{:S(2)}, u32[]{:S(2)}) collective-permute-start(f16[128,256]{1,0:T(8,128)(2,1)S(1)} %get-tuple-element.57), channel_id=1, source_target_pairs={{0,24},{4,28},{8,0},{12,4},{16,8},{20,12},{24,16},{28,20},{1,25},{... | collective-permute-start | bytes 196616 | tf_op jit(solution)/shard_map/ppermute | solution.py:644
  39.4 6.1 %collective-permute-start.18 = (f16[128,256]{1,0:T(8,128)(2,1)S(1)}, f16[128,256]{1,0:T(8,128)(2,1)S(1)}, u32[]{:S(2)}, u32[]{:S(2)}) collective-permute-start(f16[128,256]{1,0:T(8,128)(2,1)S(1)} %get-tuple-element.57), channel_id=1, source_target_pairs={{0,8},{4,12},{8,16},{12,20},{16,24},{20,28},{24,0},{28,4},{1,9},{5... | collective-permute-start | bytes 196616 | tf_op jit(solution)/shard_map/ppermute | solution.py:644
  39.5 12.6 %collective-permute-start.13 = (f16[16,8,256]{2,1,0:T(8,128)(2,1)S(1)}, f16[16,8,256]{2,1,0:T(8,128)(2,1)S(1)}, u32[]{:S(2)}, u32[]{:S(2)}) collective-permute-start(f16[16,8,256]{2,1,0:T(8,128)(2,1)S(1)} %get-tuple-element.58), channel_id=1, source_target_pairs={{1,2},{2,1},{5,6},{6,5},{9,10},{10,9},{13,14},{14,13},{17,18},{18,... | collective-permute-start | bytes 196616 | tf_op jit(solution)/shard_map/ppermute | solution.py:613
  40.4 12.9 %collective-permute-start.12 = (f16[16,8,256]{2,1,0:T(8,128)(2,1)S(1)}, f16[16,8,256]{2,1,0:T(8,128)(2,1)S(1)}, u32[]{:S(2)}, u32[]{:S(2)}) collective-permute-start(f16[16,8,256]{2,1,0:T(8,128)(2,1)S(1)} %get-tuple-element.59), channel_id=1, source_target_pairs={{0,1},{1,0},{2,3},{3,2},{4,5},{5,4},{6,7},{7,6},{8,9},{9,8},{10,11... | collective-permute-start | bytes 196616 | tf_op jit(solution)/shard_map/ppermute | solution.py:612
  45.5 2.0 %collective-permute-start.19 = (f16[128,256]{1,0:T(8,128)(2,1)S(1)}, f16[128,256]{1,0:T(8,128)(2,1)S(1)}, u32[]{:S(2)}, u32[]{:S(2)}) collective-permute-start(f16[128,256]{1,0:T(8,128)(2,1)S(1)} %collective-permute-done.18), channel_id=1, source_target_pairs={{0,4},{4,0},{8,12},{12,8},{16,20},{20,16},{24,28},{28,24},{1,5},{5... | collective-permute-start | bytes 196616 | tf_op jit(solution)/shard_map/ppermute | solution.py:647
  45.6 1.9 %collective-permute-start.15 = (f16[128,256]{1,0:T(8,128)(2,1)S(1)}, f16[128,256]{1,0:T(8,128)(2,1)S(1)}, u32[]{:S(2)}, u32[]{:S(2)}) collective-permute-start(f16[128,256]{1,0:T(8,128)(2,1)S(1)} %collective-permute-done.14), channel_id=1, source_target_pairs={{0,4},{4,0},{8,12},{12,8},{16,20},{20,16},{24,28},{28,24},{1,5},{5... | collective-permute-start | bytes 196616 | tf_op jit(solution)/shard_map/ppermute | solution.py:647
  46.2 1.3 %collective-permute-start.17 = (f16[128,256]{1,0:T(8,128)(2,1)S(1)}, f16[128,256]{1,0:T(8,128)(2,1)S(1)}, u32[]{:S(2)}, u32[]{:S(2)}) collective-permute-start(f16[128,256]{1,0:T(8,128)(2,1)S(1)} %collective-permute-done.16), channel_id=1, source_target_pairs={{0,4},{4,0},{8,12},{12,8},{16,20},{20,16},{24,28},{28,24},{1,5},{5... | collective-permute-start | bytes 196616 | tf_op jit(solution)/shard_map/ppermute | solution.py:647
  49.7 9.3 %collective-permute-start.23 = (f16[256,256]{1,0:T(8,128)(2,1)S(1)}, f16[256,256]{1,0:T(8,128)(2,1)S(1)}, u32[]{:S(2)}, u32[]{:S(2)}) collective-permute-start(f16[256,256]{1,0:T(8,128)(2,1)S(1)} %get-tuple-element.71), channel_id=1, source_target_pairs={{0,3},{1,2},{2,1},{3,0},{4,7},{5,6},{6,5},{7,4},{8,11},{9,10},{10,... | collective-permute-start | bytes 393224 | tf_op jit(solution)/shard_map/ppermute | solution.py:596
  50.9 2.5 %collective-permute-start.20 = (f16[16,128]{1,0:T(8,128)(2,1)S(1)}, f16[16,128]{1,0:T(8,128)(2,1)S(1)}, u32[]{:S(2)}, u32[]{:S(2)}) collective-permute-start(f16[16,128]{1,0:T(8,128)(2,1)S(1)} %slice.161), channel_id=1, source_target_pairs={{0,4},{4,0},{8,12},{12,8},{16,20},{20,16},{24,28},{28,24},{1,5},{5... | collective-permute-start | bytes 12296 | tf_op jit(solution)/shard_map/ppermute | solution.py:701
  50.9 7.6 %collective-permute-start.21 = (f16[256,256]{1,0:T(8,128)(2,1)S(1)}, f16[256,256]{1,0:T(8,128)(2,1)S(1)}, u32[]{:S(2)}, u32[]{:S(2)}) collective-permute-start(f16[256,256]{1,0:T(8,128)(2,1)S(1)} %get-tuple-element.69), channel_id=1, source_target_pairs={{0,1},{1,0},{2,3},{3,2},{4,5},{5,4},{6,7},{7,6},{8,9},{9,8},{10,11... | collective-permute-start | bytes 393224 | tf_op jit(solution)/shard_map/ppermute | solution.py:596
  52.1 6.9 %collective-permute-start.22 = (f16[256,256]{1,0:T(8,128)(2,1)S(1)}, f16[256,256]{1,0:T(8,128)(2,1)S(1)}, u32[]{:S(2)}, u32[]{:S(2)}) collective-permute-start(f16[256,256]{1,0:T(8,128)(2,1)S(1)} %get-tuple-element.70), channel_id=1, source_target_pairs={{0,2},{1,3},{2,0},{3,1},{4,6},{5,7},{6,4},{7,5},{8,10},{9,11},{10,... | collective-permute-start | bytes 393224 | tf_op jit(solution)/shard_map/ppermute | solution.py:596
  56.0 5.6 %collective-permute-start.25 = (f16[16,8,256]{2,1,0:T(8,128)(2,1)S(1)}, f16[16,8,256]{2,1,0:T(8,128)(2,1)S(1)}, u32[]{:S(2)}, u32[]{:S(2)}) collective-permute-start(f16[16,8,256]{2,1,0:T(8,128)(2,1)S(1)} %get-tuple-element.64), channel_id=1, source_target_pairs={{4,8},{8,4},{12,16},{16,12},{20,24},{24,20},{28,0},{0,28},{5,9},{9... | collective-permute-start | bytes 196616 | tf_op jit(solution)/shard_map/ppermute | solution.py:613
  57.4 4.1 %collective-permute-start.24 = (f16[16,8,256]{2,1,0:T(8,128)(2,1)S(1)}, f16[16,8,256]{2,1,0:T(8,128)(2,1)S(1)}, u32[]{:S(2)}, u32[]{:S(2)}) collective-permute-start(f16[16,8,256]{2,1,0:T(8,128)(2,1)S(1)} %get-tuple-element.65), channel_id=1, source_target_pairs={{0,4},{4,0},{8,12},{12,8},{16,20},{20,16},{24,28},{28,24},{1,5},{5... | collective-permute-start | bytes 196616 | tf_op jit(solution)/shard_map/ppermute | solution.py:612
  59.2 3.1 %collective-permute-start.26 = (f16[128,256]{1,0:T(8,128)(2,1)S(1)}, f16[128,256]{1,0:T(8,128)(2,1)S(1)}, u32[]{:S(2)}, u32[]{:S(2)}) collective-permute-start(f16[128,256]{1,0:T(8,128)(2,1)S(1)} %get-tuple-element.55), channel_id=1, source_target_pairs={{0,4},{4,0},{8,12},{12,8},{16,20},{20,16},{24,28},{28,24},{1,5},{5... | collective-permute-start | bytes 196616 | tf_op jit(solution)/shard_map/ppermute | solution.py:647
  61.6 8.7 %collective-permute-start.31 = (f16[128,256]{1,0:T(8,128)(2,1)S(1)}, f16[128,256]{1,0:T(8,128)(2,1)S(1)}, u32[]{:S(2)}, u32[]{:S(2)}) collective-permute-start(f16[128,256]{1,0:T(8,128)(2,1)S(1)} %get-tuple-element.55), channel_id=1, source_target_pairs={{0,16},{4,20},{8,24},{12,28},{16,0},{20,4},{24,8},{28,12},{1,17},{... | collective-permute-start | bytes 196616 | tf_op jit(solution)/shard_map/ppermute | solution.py:644
  61.7 8.0 %collective-permute-start.29 = (f16[128,256]{1,0:T(8,128)(2,1)S(1)}, f16[128,256]{1,0:T(8,128)(2,1)S(1)}, u32[]{:S(2)}, u32[]{:S(2)}) collective-permute-start(f16[128,256]{1,0:T(8,128)(2,1)S(1)} %get-tuple-element.55), channel_id=1, source_target_pairs={{0,24},{4,28},{8,0},{12,4},{16,8},{20,12},{24,16},{28,20},{1,25},{... | collective-permute-start | bytes 196616 | tf_op jit(solution)/shard_map/ppermute | solution.py:644
  62.3 7.4 %collective-permute-start.33 = (f16[128,256]{1,0:T(8,128)(2,1)S(1)}, f16[128,256]{1,0:T(8,128)(2,1)S(1)}, u32[]{:S(2)}, u32[]{:S(2)}) collective-permute-start(f16[128,256]{1,0:T(8,128)(2,1)S(1)} %get-tuple-element.55), channel_id=1, source_target_pairs={{0,8},{4,12},{8,16},{12,20},{16,24},{20,28},{24,0},{28,4},{1,9},{5... | collective-permute-start | bytes 196616 | tf_op jit(solution)/shard_map/ppermute | solution.py:644
  64.1 11.5 %collective-permute-start.28 = (f16[16,8,256]{2,1,0:T(8,128)(2,1)S(1)}, f16[16,8,256]{2,1,0:T(8,128)(2,1)S(1)}, u32[]{:S(2)}, u32[]{:S(2)}) collective-permute-start(f16[16,8,256]{2,1,0:T(8,128)(2,1)S(1)} %get-tuple-element.62), channel_id=1, source_target_pairs={{1,2},{2,1},{5,6},{6,5},{9,10},{10,9},{13,14},{14,13},{17,18},{18,... | collective-permute-start | bytes 196616 | tf_op jit(solution)/shard_map/ppermute | solution.py:613
  64.7 12.0 %collective-permute-start.27 = (f16[16,8,256]{2,1,0:T(8,128)(2,1)S(1)}, f16[16,8,256]{2,1,0:T(8,128)(2,1)S(1)}, u32[]{:S(2)}, u32[]{:S(2)}) collective-permute-start(f16[16,8,256]{2,1,0:T(8,128)(2,1)S(1)} %get-tuple-element.63), channel_id=1, source_target_pairs={{0,1},{1,0},{2,3},{3,2},{4,5},{5,4},{6,7},{7,6},{8,9},{9,8},{10,11... | collective-permute-start | bytes 196616 | tf_op jit(solution)/shard_map/ppermute | solution.py:612
  69.7 2.0 %collective-permute-start.34 = (f16[128,256]{1,0:T(8,128)(2,1)S(1)}, f16[128,256]{1,0:T(8,128)(2,1)S(1)}, u32[]{:S(2)}, u32[]{:S(2)}) collective-permute-start(f16[128,256]{1,0:T(8,128)(2,1)S(1)} %collective-permute-done.33), channel_id=1, source_target_pairs={{0,4},{4,0},{8,12},{12,8},{16,20},{20,16},{24,28},{28,24},{1,5},{5... | collective-permute-start | bytes 196616 | tf_op jit(solution)/shard_map/ppermute | solution.py:647
  69.7 1.9 %collective-permute-start.30 = (f16[128,256]{1,0:T(8,128)(2,1)S(1)}, f16[128,256]{1,0:T(8,128)(2,1)S(1)}, u32[]{:S(2)}, u32[]{:S(2)}) collective-permute-start(f16[128,256]{1,0:T(8,128)(2,1)S(1)} %collective-permute-done.29), channel_id=1, source_target_pairs={{0,4},{4,0},{8,12},{12,8},{16,20},{20,16},{24,28},{28,24},{1,5},{5... | collective-permute-start | bytes 196616 | tf_op jit(solution)/shard_map/ppermute | solution.py:647
  70.3 1.3 %collective-permute-start.32 = (f16[128,256]{1,0:T(8,128)(2,1)S(1)}, f16[128,256]{1,0:T(8,128)(2,1)S(1)}, u32[]{:S(2)}, u32[]{:S(2)}) collective-permute-start(f16[128,256]{1,0:T(8,128)(2,1)S(1)} %collective-permute-done.31), channel_id=1, source_target_pairs={{0,4},{4,0},{8,12},{12,8},{16,20},{20,16},{24,28},{28,24},{1,5},{5... | collective-permute-start | bytes 196616 | tf_op jit(solution)/shard_map/ppermute | solution.py:647
  73.2 6.9 %collective-permute-start.38 = (f16[128,256]{1,0:T(8,128)(2,1)S(1)}, f16[128,256]{1,0:T(8,128)(2,1)S(1)}, u32[]{:S(2)}, u32[]{:S(2)}) collective-permute-start(f16[128,256]{1,0:T(8,128)(2,1)S(1)} %get-tuple-element.68), channel_id=1, source_target_pairs={{0,3},{1,2},{2,1},{3,0},{4,7},{5,6},{6,5},{7,4},{8,11},{9,10},{10,... | collective-permute-start | bytes 196616 | tf_op jit(solution)/shard_map/ppermute | solution.py:596
  74.4 2.4 %collective-permute-start.35 = (f16[16,128]{1,0:T(8,128)(2,1)S(1)}, f16[16,128]{1,0:T(8,128)(2,1)S(1)}, u32[]{:S(2)}, u32[]{:S(2)}) collective-permute-start(f16[16,128]{1,0:T(8,128)(2,1)S(1)} %slice.168), channel_id=1, source_target_pairs={{0,4},{4,0},{8,12},{12,8},{16,20},{20,16},{24,28},{28,24},{1,5},{5... | collective-permute-start | bytes 12296 | tf_op jit(solution)/shard_map/ppermute | solution.py:701
  74.4 4.8 %collective-permute-start.36 = (f16[128,256]{1,0:T(8,128)(2,1)S(1)}, f16[128,256]{1,0:T(8,128)(2,1)S(1)}, u32[]{:S(2)}, u32[]{:S(2)}) collective-permute-start(f16[128,256]{1,0:T(8,128)(2,1)S(1)} %get-tuple-element.66), channel_id=1, source_target_pairs={{0,1},{1,0},{2,3},{3,2},{4,5},{5,4},{6,7},{7,6},{8,9},{9,8},{10,11... | collective-permute-start | bytes 196616 | tf_op jit(solution)/shard_map/ppermute | solution.py:596
  75.6 4.5 %collective-permute-start.37 = (f16[128,256]{1,0:T(8,128)(2,1)S(1)}, f16[128,256]{1,0:T(8,128)(2,1)S(1)}, u32[]{:S(2)}, u32[]{:S(2)}) collective-permute-start(f16[128,256]{1,0:T(8,128)(2,1)S(1)} %get-tuple-element.67), channel_id=1, source_target_pairs={{0,2},{1,3},{2,0},{3,1},{4,6},{5,7},{6,4},{7,5},{8,10},{9,11},{10,... | collective-permute-start | bytes 196616 | tf_op jit(solution)/shard_map/ppermute | solution.py:596

commit v7 on v6

--- a/solution.py
+++ b/solution.py
@@ -659,14 +659,27 @@
     return jnp.stack([jnp.asarray(value, jnp.int32) for value in places])
 
 
+def owners_first_kernel(surface_ref, out_ref):
+    chips, slabs, turns = out_ref.shape[:3]
+    for chip in range(chips):
+        for owner in range(slabs):
+            for turn in range(turns):
+                out_ref[chip, owner, turn] = surface_ref[turn * slabs + owner]
+
+
 def first_gather(surface, scale):
     sectors, slabs = lax.axis_size("sector"), lax.axis_size("slab")
     chips = sectors // 2
     pairs, n_axial, lanes = surface.shape
     turns = pairs // slabs
-    by_owner = to_wire(surface, scale).reshape(turns, slabs, n_axial, lanes)
-    by_owner = jnp.swapaxes(by_owner, 0, 1).reshape(1, slabs, turns * n_axial, lanes)
-    messages = jnp.broadcast_to(by_owner, (chips,) + by_owner.shape[1:])
+    by_owner = call(
+        owners_first_kernel,
+        shape(chips, slabs, turns, n_axial, lanes),
+        0,
+        1,
+        name="owners_first",
+    )(surface)
+    messages = to_wire(by_owner, scale)
     groups = [
         [(2 * chip + core) * slabs + slab for chip in range(chips) for slab in range(slabs)]
         for core in range(2)

time: 94 us -> 94 us (level)
    unnamed x17 -> x19, local copies, waits for them, and re-layouts: 1.71 us -> 2.61 us
    pallas_call x15 -> x16, Pallas kernels: 16.9 us -> 17 us  [call(): return lambda *args: called(*args, *after)]
where the time goes in v7:
time: 94 us; the launch traced here: 93.7 us
  starting transfers between devices  44.9 us (48%)
  Pallas kernels  17 us (18%)
  waiting for transfers between devices  13.8 us (15%)
  blocking collectives  11 us (12%)
  local copies, waits for them, and re-layouts  3.22 us (3%)
  other arithmetic  2.39 us (3%)
  between operations  1.46 us (2%)
    pallas_call x16, Pallas kernels, call(): return lambda *args: called(*args, *after)  17 us
    ppermute x6, starting transfers between devices, neighbour_swap(): inner = lax.ppermute(jnp.where(odd, first, last), axis, within)  12 us
    all_to_all x1, blocking collectives, per_device(): lax.all_to_all(gram, ('sector', 'slab'), split_axis=0, concat_axis=0, til...  11 us
    ppermute x9, starting transfers between devices, slab_exchange(): lax.ppermute(messages[distance], 'slab', partner_perm(slabs, distance))  10.7 us
    all_to_all x1, starting transfers between devices, first_gather(): lax.all_to_all(messages.reshape(chips * slabs, turns * n_axial, lanes), (...  8.31 us
    ppermute x6, starting transfers between devices, neighbour_swap(): outer = lax.ppermute(jnp.where(odd, last, first), axis, across)  7.42 us
    ppermute x6, starting transfers between devices, sector_gather(): shares.append(lax.ppermute(own, 'sector', perm))  4.62 us
    ppermute x6, waiting for transfers between devices, neighbour_swap(): outer = lax.ppermute(jnp.where(odd, last, first), axis, across)  4.38 us
  transfers between devices with their start and end apart: 40, of which 13 were waited for; matrix products, arithmetic and copies ran while one was open for 2% of the time, Pallas kernels for 16%

profile of v7, /device:TPU:0, one launch (start us, length us, event | category | flops | bytes accessed | tf_op | source)
XLA Modules:
  0.0 93.7 jit_solution(10864268612453930755)
XLA Ops:
  0.6 0.9 copy-done.4
  1.6 0.8 multiply_convert_fusion
  2.3 8.3 %all-to-all-start = ((f16[16,32,256]{2,1,0:T(8,128)(2,1)}), f16[16,32,256]{2,1,0:T(8,128)(2,1)S(1)}, u32[]{:S(2)}, u32[]{:S(2)}) async-start(f16[16,32,256]{2,1,0:T(8,128)(2,1)} %bitcast), calls=%async_computation | async-start | bytes 524288 | tf_op jit(solution)/shard_map/all_to_all | solution.py:687
  10.7 1.6 %copy-done.1 = f32[16,16,8,256]{3,2,1,0:T(8,128)S(1)} copy-done((f32[16,16,8,256]{3,2,1,0:T(8,128)S(1)}, f32[16,16,8,256]{3,2,1,0:T(8,128)}, u32[]{:S(2)}) %copy-start.1) | copy-done | bytes 2097176
  12.3 0.6 volume_edges.1
  12.9 2.7 %collective-permute-start.3 = (f16[16,8,256]{2,1,0:T(8,128)(2,1)S(1)}, f16[16,8,256]{2,1,0:T(8,128)(2,1)S(1)}, u32[]{:S(2)}, u32[]{:S(2)}) collective-permute-start(f16[16,8,256]{2,1,0:T(8,128)(2,1)S(1)} %get-tuple-element.89), channel_id=1, source_target_pairs={{4,8},{8,4},{12,16},{16,12},{20,24},{24,20},{28,0},{0,28},{5,9},{9... | collective-permute-start | bytes 196616 | tf_op jit(solution)/shard_map/ppermute | solution.py:613
  15.6 0.7 collective-permute-start.5
  16.3 4.2 %collective-permute-start.4 = (f16[16,8,256]{2,1,0:T(8,128)(2,1)S(1)}, f16[16,8,256]{2,1,0:T(8,128)(2,1)S(1)}, u32[]{:S(2)}, u32[]{:S(2)}) collective-permute-start(f16[16,8,256]{2,1,0:T(8,128)(2,1)S(1)} %get-tuple-element.88), channel_id=1, source_target_pairs={{0,1},{1,0},{2,3},{3,2},{4,5},{5,4},{6,7},{7,6},{8,9},{9,8},{10,11... | collective-permute-start | bytes 196616 | tf_op jit(solution)/shard_map/ppermute | solution.py:612
  21.1 1.1 %volume_matrices.1 = (bf16[2,128,256]{2,1,0:T(8,128)(2,1)S(1)}, bf16[2,128,128]{2,1,0:T(8,128)(2,1)S(1)}) custom-call(f32[3,8,8]{2,1,0:T(8,128)S(1)} %copy-done.7, f32[128,256]{1,0:T(8,128)S(1)} %bitcast.88), custom_call_target="tpu_custom_call" | custom-call | flops 1000 | bytes 1000 | tf_op jit(solution)/shard_map/volume_matrices/pallas_call | solution.py:45
  22.6 2.0 %bem_partial.3 = (f32[256,256]{1,0:T(8,128)S(1)}, f32[3,256,256]{2,1,0:T(8,128)S(1)}) custom-call(s32[9]{0:T(128)S(1)} %stack.67.refs_0_, bf16[2,512,1024]{2,1,0:T(8,128)(2,1)S(1)} %copy-done, f32[8,16,256]{2,1,0:T(8,128)S(1)} %get-tuple-element.30.refs_2_, f32[128,256]{1,0:T(8,128)S(1)} %bitcast.89, f32[128,256]{1,0:T(8,128)S(1)} %bitcast.100, ...), custom_call_target="tpu_custom_call" | custom-call | flops 1000 | bytes 1000 | tf_op jit(solution)/shard_map/bem_partial/pallas_call | solution.py:45
  25.1 1.5 %collective-permute-start.8 = (f16[256,256]{1,0:T(8,128)(2,1)S(1)}, f16[256,256]{1,0:T(8,128)(2,1)S(1)}, u32[]{:S(2)}, u32[]{:S(2)}) collective-permute-start(f16[256,256]{1,0:T(8,128)(2,1)S(1)} %get-tuple-element.74), channel_id=1, source_target_pairs={{0,3},{1,2},{2,1},{3,0},{4,7},{5,6},{6,5},{7,4},{8,11},{9,10},{10,... | collective-permute-start | bytes 393224 | tf_op jit(solution)/shard_map/ppermute | solution.py:596
  26.6 1.2 %collective-permute-start.6 = (f16[256,256]{1,0:T(8,128)(2,1)S(1)}, f16[256,256]{1,0:T(8,128)(2,1)S(1)}, u32[]{:S(2)}, u32[]{:S(2)}) collective-permute-start(f16[256,256]{1,0:T(8,128)(2,1)S(1)} %get-tuple-element.72), channel_id=1, source_target_pairs={{0,1},{1,0},{2,3},{3,2},{4,5},{5,4},{6,7},{7,6},{8,9},{9,8},{10,11... | collective-permute-start | bytes 393224 | tf_op jit(solution)/shard_map/ppermute | solution.py:596
  27.8 0.8 collective-permute-start.7
  29.1 1.6 %volume_bulk.3 = (f32[16,16,8,256]{3,2,1,0:T(8,128)S(1)}, f32[256,256]{1,0:T(8,128)S(1)}, f32[16,16,8,256]{3,2,1,0:T(8,128)S(1)}) custom-call(f32[16,16,8,256]{3,2,1,0:T(8,128)S(1)} %copy-done.2, f32[16,16,8,128]{3,2,1,0:T(8,128)S(1)} %broadcast_in_dim.2.refs_1_, ...), custom_call_target="tpu_custom_call", output_to_operand_aliasing={{1}: (4, {})} | custom-call | flops 1000 | bytes 1000 | tf_op jit(solution)/shard_map/volume_bulk/pallas_call | solution.py:45
  30.7 0.7 finish_first_kernel.1
  31.4 1.2 %collective-permute-start.10 = (f16[16,8,256]{2,1,0:T(8,128)(2,1)S(1)}, f16[16,8,256]{2,1,0:T(8,128)(2,1)S(1)}, u32[]{:S(2)}, u32[]{:S(2)}) collective-permute-start(f16[16,8,256]{2,1,0:T(8,128)(2,1)S(1)} %get-tuple-element.60), channel_id=1, source_target_pairs={{4,8},{8,4},{12,16},{16,12},{20,24},{24,20},{28,0},{0,28},{5,9},{9... | collective-permute-start | bytes 196616 | tf_op jit(solution)/shard_map/ppermute | solution.py:613
  33.0 1.5 %volume_bulk.4 = (f32[16,16,8,256]{3,2,1,0:T(8,128)S(1)}, f32[256,256]{1,0:T(8,128)S(1)}) custom-call(f32[16,16,8,256]{3,2,1,0:T(8,128)S(1)} %get-tuple-element.39.refs_0_, f32[16,16,8,128]{3,2,1,0:T(8,128)S(1)} %broadcast_in_dim.2.refs_1_, bf16[2,128,256]{2,1,0:T(8,128)(2,1)S(1)} %get-tuple-element.28.refs_2_, ...), custom_call_target="tpu_custom_call", output_to_operand_aliasing={{1}: (4, {})} | custom-call | flops 1000 | bytes 1000 | tf_op jit(solution)/shard_map/volume_bulk/pallas_call | solution.py:45
  34.9 2.1 %collective-permute-done.10 = f16[16,8,256]{2,1,0:T(8,128)(2,1)S(1)} collective-permute-done((f16[16,8,256]{2,1,0:T(8,128)(2,1)S(1)}, f16[16,8,256]{2,1,0:T(8,128)(2,1)S(1)}, u32[]{:S(2)}, u32[]{:S(2)}) %collective-permute-start.10) | collective-permute-done | bytes 65568 | tf_op jit(solution)/shard_map/ppermute | solution.py:613
  37.1 2.3 %collective-permute-start.14 = (f16[128,256]{1,0:T(8,128)(2,1)S(1)}, f16[128,256]{1,0:T(8,128)(2,1)S(1)}, u32[]{:S(2)}, u32[]{:S(2)}) collective-permute-start(f16[128,256]{1,0:T(8,128)(2,1)S(1)} %get-tuple-element.57), channel_id=1, source_target_pairs={{0,24},{4,28},{8,0},{12,4},{16,8},{20,12},{24,16},{28,20},{1,25},{... | collective-permute-start | bytes 196616 | tf_op jit(solution)/shard_map/ppermute | solution.py:644
  39.5 0.8 collective-permute-start.13
  40.4 3.8 %collective-permute-start.12 = (f16[16,8,256]{2,1,0:T(8,128)(2,1)S(1)}, f16[16,8,256]{2,1,0:T(8,128)(2,1)S(1)}, u32[]{:S(2)}, u32[]{:S(2)}) collective-permute-start(f16[16,8,256]{2,1,0:T(8,128)(2,1)S(1)} %get-tuple-element.59), channel_id=1, source_target_pairs={{0,1},{1,0},{2,3},{3,2},{4,5},{5,4},{6,7},{7,6},{8,9},{9,8},{10,11... | collective-permute-start | bytes 196616 | tf_op jit(solution)/shard_map/ppermute | solution.py:612
  44.2 1.4 %collective-permute-done.18 = f16[128,256]{1,0:T(8,128)(2,1)S(1)} collective-permute-done((f16[128,256]{1,0:T(8,128)(2,1)S(1)}, f16[128,256]{1,0:T(8,128)(2,1)S(1)}, u32[]{:S(2)}, u32[]{:S(2)}) %collective-permute-start.18) | collective-permute-done | bytes 65568 | tf_op jit(solution)/shard_map/ppermute | solution.py:644
  46.3 1.2 %collective-permute-done.17 = f16[128,256]{1,0:T(8,128)(2,1)S(1)} collective-permute-done((f16[128,256]{1,0:T(8,128)(2,1)S(1)}, f16[128,256]{1,0:T(8,128)(2,1)S(1)}, u32[]{:S(2)}, u32[]{:S(2)}) %collective-permute-start.17) | collective-permute-done | bytes 65568 | tf_op jit(solution)/shard_map/ppermute | solution.py:647
  47.6 2.1 %bem_partial.4 = (f32[256,256]{1,0:T(8,128)S(1)}, f32[3,256,256]{2,1,0:T(8,128)S(1)}) custom-call(s32[9]{0:T(128)S(1)} %stack.76.refs_0_, bf16[2,512,1024]{2,1,0:T(8,128)(2,1)S(1)} %copy-done, f32[8,16,256]{2,1,0:T(8,128)S(1)} %get-tuple-element.43.refs_2_, f32[128,256]{1,0:T(8,128)S(1)} %get-tuple-element.56.refs_3_, ...), custom_call_target="tpu_custom_call" | custom-call | flops 1000 | bytes 1000 | tf_op jit(solution)/shard_map/bem_partial/pallas_call | solution.py:45
  49.7 1.1 %collective-permute-start.23 = (f16[256,256]{1,0:T(8,128)(2,1)S(1)}, f16[256,256]{1,0:T(8,128)(2,1)S(1)}, u32[]{:S(2)}, u32[]{:S(2)}) collective-permute-start(f16[256,256]{1,0:T(8,128)(2,1)S(1)} %get-tuple-element.71), channel_id=1, source_target_pairs={{0,3},{1,2},{2,1},{3,0},{4,7},{5,6},{6,5},{7,4},{8,11},{9,10},{10,... | collective-permute-start | bytes 393224 | tf_op jit(solution)/shard_map/ppermute | solution.py:596
  50.9 1.3 %collective-permute-start.21 = (f16[256,256]{1,0:T(8,128)(2,1)S(1)}, f16[256,256]{1,0:T(8,128)(2,1)S(1)}, u32[]{:S(2)}, u32[]{:S(2)}) collective-permute-start(f16[256,256]{1,0:T(8,128)(2,1)S(1)} %get-tuple-element.69), channel_id=1, source_target_pairs={{0,1},{1,0},{2,3},{3,2},{4,5},{5,4},{6,7},{7,6},{8,9},{9,8},{10,11... | collective-permute-start | bytes 393224 | tf_op jit(solution)/shard_map/ppermute | solution.py:596
  52.1 1.2 %collective-permute-start.22 = (f16[256,256]{1,0:T(8,128)(2,1)S(1)}, f16[256,256]{1,0:T(8,128)(2,1)S(1)}, u32[]{:S(2)}, u32[]{:S(2)}) collective-permute-start(f16[256,256]{1,0:T(8,128)(2,1)S(1)} %get-tuple-element.70), channel_id=1, source_target_pairs={{0,2},{1,3},{2,0},{3,1},{4,6},{5,7},{6,4},{7,5},{8,10},{9,11},{10,... | collective-permute-start | bytes 393224 | tf_op jit(solution)/shard_map/ppermute | solution.py:596
  53.4 0.9 finish_second_kernel.1
  54.5 1.5 %volume_bulk.5 = (f32[16,16,8,256]{3,2,1,0:T(8,128)S(1)}, f32[256,256]{1,0:T(8,128)S(1)}) custom-call(f32[16,16,8,256]{3,2,1,0:T(8,128)S(1)} %get-tuple-element.46.refs_0_, f32[16,16,8,128]{3,2,1,0:T(8,128)S(1)} %broadcast_in_dim.2.refs_1_, bf16[2,128,256]{2,1,0:T(8,128)(2,1)S(1)} %get-tuple-element.28.refs_2_, ...), custom_call_target="tpu_custom_call", output_to_operand_aliasing={{1}: (4, {})} | custom-call | flops 1000 | bytes 1000 | tf_op jit(solution)/shard_map/volume_bulk/pallas_call | solution.py:45
  56.0 1.4 %collective-permute-start.25 = (f16[16,8,256]{2,1,0:T(8,128)(2,1)S(1)}, f16[16,8,256]{2,1,0:T(8,128)(2,1)S(1)}, u32[]{:S(2)}, u32[]{:S(2)}) collective-permute-start(f16[16,8,256]{2,1,0:T(8,128)(2,1)S(1)} %get-tuple-element.64), channel_id=1, source_target_pairs={{4,8},{8,4},{12,16},{16,12},{20,24},{24,20},{28,0},{0,28},{5,9},{9... | collective-permute-start | bytes 196616 | tf_op jit(solution)/shard_map/ppermute | solution.py:613
  57.4 1.0 %collective-permute-done.21 = f16[256,256]{1,0:T(8,128)(2,1)S(1)} collective-permute-done((f16[256,256]{1,0:T(8,128)(2,1)S(1)}, f16[256,256]{1,0:T(8,128)(2,1)S(1)}, u32[]{:S(2)}, u32[]{:S(2)}) %collective-permute-start.21) | collective-permute-done | bytes 131104 | tf_op jit(solution)/shard_map/ppermute | solution.py:596
  58.5 0.6 collective-permute-done.22
  59.3 2.3 %collective-permute-done.25 = f16[16,8,256]{2,1,0:T(8,128)(2,1)S(1)} collective-permute-done((f16[16,8,256]{2,1,0:T(8,128)(2,1)S(1)}, f16[16,8,256]{2,1,0:T(8,128)(2,1)S(1)}, u32[]{:S(2)}, u32[]{:S(2)}) %collective-permute-start.25) | collective-permute-done | bytes 65568 | tf_op jit(solution)/shard_map/ppermute | solution.py:613
  61.7 0.6 collective-permute-start.29
  62.3 1.5 %collective-permute-start.33 = (f16[128,256]{1,0:T(8,128)(2,1)S(1)}, f16[128,256]{1,0:T(8,128)(2,1)S(1)}, u32[]{:S(2)}, u32[]{:S(2)}) collective-permute-start(f16[128,256]{1,0:T(8,128)(2,1)S(1)} %get-tuple-element.55), channel_id=1, source_target_pairs={{0,8},{4,12},{8,16},{12,20},{16,24},{20,28},{24,0},{28,4},{1,9},{5... | collective-permute-start | bytes 196616 | tf_op jit(solution)/shard_map/ppermute | solution.py:644
  64.1 0.7 collective-permute-start.28
  64.7 3.6 %collective-permute-start.27 = (f16[16,8,256]{2,1,0:T(8,128)(2,1)S(1)}, f16[16,8,256]{2,1,0:T(8,128)(2,1)S(1)}, u32[]{:S(2)}, u32[]{:S(2)}) collective-permute-start(f16[16,8,256]{2,1,0:T(8,128)(2,1)S(1)} %get-tuple-element.63), channel_id=1, source_target_pairs={{0,1},{1,0},{2,3},{3,2},{4,5},{5,4},{6,7},{7,6},{8,9},{9,8},{10,11... | collective-permute-start | bytes 196616 | tf_op jit(solution)/shard_map/ppermute | solution.py:612
  68.4 1.3 %collective-permute-done.33 = f16[128,256]{1,0:T(8,128)(2,1)S(1)} collective-permute-done((f16[128,256]{1,0:T(8,128)(2,1)S(1)}, f16[128,256]{1,0:T(8,128)(2,1)S(1)}, u32[]{:S(2)}, u32[]{:S(2)}) %collective-permute-start.33) | collective-permute-done | bytes 65568 | tf_op jit(solution)/shard_map/ppermute | solution.py:644
  70.4 1.2 %collective-permute-done.32 = f16[128,256]{1,0:T(8,128)(2,1)S(1)} collective-permute-done((f16[128,256]{1,0:T(8,128)(2,1)S(1)}, f16[128,256]{1,0:T(8,128)(2,1)S(1)}, u32[]{:S(2)}, u32[]{:S(2)}) %collective-permute-start.32) | collective-permute-done | bytes 65568 | tf_op jit(solution)/shard_map/ppermute | solution.py:647
  71.7 1.4 %bem_partial.5 = (f32[256,256]{1,0:T(8,128)S(1)}, f32[3,256,256]{2,1,0:T(8,128)S(1)}) custom-call(s32[9]{0:T(128)S(1)} %stack.76.refs_0_, bf16[2,512,1024]{2,1,0:T(8,128)(2,1)S(1)} %copy-done, f32[8,16,256]{2,1,0:T(8,128)S(1)} %get-tuple-element.50.refs_2_, f32[128,256]{1,0:T(8,128)S(1)} %get-tuple-element.54.refs_3_, ...), custom_call_target="tpu_custom_call" | custom-call | flops 1000 | bytes 1000 | tf_op jit(solution)/shard_map/bem_partial/pallas_call | solution.py:45
  73.2 1.2 %collective-permute-start.38 = (f16[128,256]{1,0:T(8,128)(2,1)S(1)}, f16[128,256]{1,0:T(8,128)(2,1)S(1)}, u32[]{:S(2)}, u32[]{:S(2)}) collective-permute-start(f16[128,256]{1,0:T(8,128)(2,1)S(1)} %get-tuple-element.68), channel_id=1, source_target_pairs={{0,3},{1,2},{2,1},{3,0},{4,7},{5,6},{6,5},{7,4},{8,11},{9,10},{10,... | collective-permute-start | bytes 196616 | tf_op jit(solution)/shard_map/ppermute | solution.py:596
  74.4 1.1 %collective-permute-start.36 = (f16[128,256]{1,0:T(8,128)(2,1)S(1)}, f16[128,256]{1,0:T(8,128)(2,1)S(1)}, u32[]{:S(2)}, u32[]{:S(2)}) collective-permute-start(f16[128,256]{1,0:T(8,128)(2,1)S(1)} %get-tuple-element.66), channel_id=1, source_target_pairs={{0,1},{1,0},{2,3},{3,2},{4,5},{5,4},{6,7},{7,6},{8,9},{9,8},{10,11... | collective-permute-start | bytes 196616 | tf_op jit(solution)/shard_map/ppermute | solution.py:596
  75.6 1.2 %collective-permute-start.37 = (f16[128,256]{1,0:T(8,128)(2,1)S(1)}, f16[128,256]{1,0:T(8,128)(2,1)S(1)}, u32[]{:S(2)}, u32[]{:S(2)}) collective-permute-start(f16[128,256]{1,0:T(8,128)(2,1)S(1)} %get-tuple-element.67), channel_id=1, source_target_pairs={{0,2},{1,3},{2,0},{3,1},{4,6},{5,7},{6,4},{7,5},{8,10},{9,11},{10,... | collective-permute-start | bytes 196616 | tf_op jit(solution)/shard_map/ppermute | solution.py:596
  76.8 1.2 %finish_third_kernel.1.refs_2_ = f32[5,8,128]{2,1,0:T(8,128)S(1)} custom-call(f32[16,16,8,256]{3,2,1,0:T(8,128)S(1)} %get-tuple-element.48.refs_0_, f32[8,16,256]{2,1,0:T(8,128)S(1)} %bitcast.92, f32[16,8,256]{2,1,0:T(8,128)S(1)} %get-tuple-element.94.refs_2_, f32[16,8,256]{2,1,0:T(8,128)S(1)} %get-tuple-element.93.refs_3_, ...), custom_call_target="tpu_custom_call" | custom-call | flops 1000 | bytes 1000 | tf_op jit(solution)/shard_map/finish_third_kernel/pallas_call | solution.py:45
  78.0 1.2 %collective-permute-done.36 = f16[128,256]{1,0:T(8,128)(2,1)S(1)} collective-permute-done((f16[128,256]{1,0:T(8,128)(2,1)S(1)}, f16[128,256]{1,0:T(8,128)(2,1)S(1)}, u32[]{:S(2)}, u32[]{:S(2)}) %collective-permute-start.36) | collective-permute-done | bytes 65568 | tf_op jit(solution)/shard_map/ppermute | solution.py:596
  79.2 0.9 collective-permute-done.37
  80.3 11.0 %all_to_all.10.refs_0_ = f32[32,1,1152]{2,1,0:T(1,128)S(1)} all-to-all(f32[32,1,1152]{2,1,0:T(1,128)S(1)} %local_gram.1), channel_id=1, replica_groups=mesh['sector'=8,'slab'=4] {'sector','slab'}, dimensions={0} | all-to-all | bytes 294912 | tf_op jit(solution)/shard_map/all_to_all | solution.py:800
  91.3 2.3 %final_solution.1 = (f32[16,16,8,256]{3,2,1,0:T(8,128)}, f32[8,16,256]{2,1,0:T(8,128)}) custom-call(f32[32,1,1152]{2,1,0:T(1,128)S(1)} %all_to_all.10.refs_0_, f32[16,16,8,256]{3,2,1,0:T(8,128)S(1)} %get-tuple-element.53.refs_1_, f32[16,16,8,256]{3,2,1,0:T(8,128)S(1)} %pass_after.2.refs_6_.refs_2_, f32[16,16,8,256]{3,2,1,0:T(8,128)S(1)} %pass_after.3.refs_7_.refs_3_, ...), custom_call_target="tpu_custom_call" | custom-call | flops 1000 | bytes 1000 | tf_op jit(solution)/shard_map/final_solution/pallas_call | solution.py:45
  (118 shorter events, 5.5 us)
Async XLA Ops:
  1.6 19.0 %copy-start.8 = (f32[16,16,8]{1,2,0:T(8,128)S(1)}, f32[16,16,8]{1,2,0:T(8,128)}, u32[]{:S(2)}) copy-start(f32[16,16,8]{1,2,0:T(8,128)} %param.13) | copy-start | bytes 24580
  2.3 18.6 %all-to-all-start = ((f16[16,32,256]{2,1,0:T(8,128)(2,1)}), f16[16,32,256]{2,1,0:T(8,128)(2,1)S(1)}, u32[]{:S(2)}, u32[]{:S(2)}) async-start(f16[16,32,256]{2,1,0:T(8,128)(2,1)} %bitcast), calls=%async_computation | async-start | bytes 524288 | tf_op jit(solution)/shard_map/all_to_all | solution.py:687
  10.7 1.6 %copy-start.1 = (f32[16,16,8,256]{3,2,1,0:T(8,128)S(1)}, f32[16,16,8,256]{3,2,1,0:T(8,128)}, u32[]{:S(2)}) copy-start(f32[16,16,8,256]{3,2,1,0:T(8,128)} %refs_0_.7) | copy-start | bytes 6291460
  12.9 8.2 %copy-start.7 = (f32[3,8,8]{2,1,0:T(8,128)S(1)}, f32[3,8,8]{2,1,0:T(8,128)}, u32[]{:S(2)}) copy-start(f32[3,8,8]{2,1,0:T(8,128)} %refs_0_.5) | copy-start | bytes 2308
  12.9 7.9 %collective-permute-start.3 = (f16[16,8,256]{2,1,0:T(8,128)(2,1)S(1)}, f16[16,8,256]{2,1,0:T(8,128)(2,1)S(1)}, u32[]{:S(2)}, u32[]{:S(2)}) collective-permute-start(f16[16,8,256]{2,1,0:T(8,128)(2,1)S(1)} %get-tuple-element.89), channel_id=1, source_target_pairs={{4,8},{8,4},{12,16},{16,12},{20,24},{24,20},{28,0},{0,28},{5,9},{9... | collective-permute-start | bytes 196616 | tf_op jit(solution)/shard_map/ppermute | solution.py:613
  15.6 5.2 %collective-permute-start.2 = (f16[16,8,256]{2,1,0:T(8,128)(2,1)S(1)}, f16[16,8,256]{2,1,0:T(8,128)(2,1)S(1)}, u32[]{:S(2)}, u32[]{:S(2)}) collective-permute-start(f16[16,8,256]{2,1,0:T(8,128)(2,1)S(1)} %get-tuple-element.90), channel_id=1, source_target_pairs={{0,4},{4,0},{8,12},{12,8},{16,20},{20,16},{24,28},{28,24},{1,5},{5... | collective-permute-start | bytes 196616 | tf_op jit(solution)/shard_map/ppermute | solution.py:612
  15.6 9.5 %collective-permute-start.5 = (f16[16,8,256]{2,1,0:T(8,128)(2,1)S(1)}, f16[16,8,256]{2,1,0:T(8,128)(2,1)S(1)}, u32[]{:S(2)}, u32[]{:S(2)}) collective-permute-start(f16[16,8,256]{2,1,0:T(8,128)(2,1)S(1)} %get-tuple-element.87), channel_id=1, source_target_pairs={{1,2},{2,1},{5,6},{6,5},{9,10},{10,9},{13,14},{14,13},{17,18},{18,... | collective-permute-start | bytes 196616 | tf_op jit(solution)/shard_map/ppermute | solution.py:613
  16.3 8.8 %collective-permute-start.4 = (f16[16,8,256]{2,1,0:T(8,128)(2,1)S(1)}, f16[16,8,256]{2,1,0:T(8,128)(2,1)S(1)}, u32[]{:S(2)}, u32[]{:S(2)}) collective-permute-start(f16[16,8,256]{2,1,0:T(8,128)(2,1)S(1)} %get-tuple-element.88), channel_id=1, source_target_pairs={{0,1},{1,0},{2,3},{3,2},{4,5},{5,4},{6,7},{7,6},{8,9},{9,8},{10,11... | collective-permute-start | bytes 196616 | tf_op jit(solution)/shard_map/ppermute | solution.py:612
  20.8 1.8 %copy-start = (bf16[2,512,1024]{2,1,0:T(8,128)(2,1)S(1)}, bf16[2,512,1024]{2,1,0:T(8,128)(2,1)}, u32[]{:S(2)}) copy-start(bf16[2,512,1024]{2,1,0:T(8,128)(2,1)} %refs_1_.7) | copy-start | bytes 6291460
  20.8 1.8 %copy-start.6 = (f32[8,16,256]{2,1,0:T(8,128)S(1)}, f32[8,16,256]{2,1,0:T(8,128)}, u32[]{:S(2)}) copy-start(f32[8,16,256]{2,1,0:T(8,128)} %refs_11_.1) | copy-start | bytes 393220
  21.0 1.5 %collective-permute-start = (f16[16,32,256]{2,1,0:T(8,128)(2,1)S(1)}, f16[16,32,256]{2,1,0:T(8,128)(2,1)S(1)}, u32[]{:S(2)}, u32[]{:S(2)}) collective-permute-start(f16[16,32,256]{2,1,0:T(8,128)(2,1)S(1)} %all-to-all-done), channel_id=1, source_target_pairs={{0,4},{4,0},{8,12},{12,8},{16,20},{20,16},{24,28},{28,24},{1,5},{5... | collective-permute-start | bytes 786440 | tf_op jit(solution)/shard_map/ppermute | solution.py:695
  24.7 4.4 %copy-start.2 = (f32[16,16,8,256]{3,2,1,0:T(8,128)S(1)}, f32[16,16,8,256]{3,2,1,0:T(8,128)}, u32[]{:S(2)}) copy-start(f32[16,16,8,256]{3,2,1,0:T(8,128)} %refs_0_.7) | copy-start | bytes 6291460
  24.8 3.9 %collective-permute-start.1 = (f16[16,128]{1,0:T(8,128)(2,1)S(1)}, f16[16,128]{1,0:T(8,128)(2,1)S(1)}, u32[]{:S(2)}, u32[]{:S(2)}) collective-permute-start(f16[16,128]{1,0:T(8,128)(2,1)S(1)} %slice.156), channel_id=1, source_target_pairs={{0,4},{4,0},{8,12},{12,8},{16,20},{20,16},{24,28},{28,24},{1,5},{5... | collective-permute-start | bytes 12296 | tf_op jit(solution)/shard_map/ppermute | solution.py:714
  25.1 9.5 %collective-permute-start.8 = (f16[256,256]{1,0:T(8,128)(2,1)S(1)}, f16[256,256]{1,0:T(8,128)(2,1)S(1)}, u32[]{:S(2)}, u32[]{:S(2)}) collective-permute-start(f16[256,256]{1,0:T(8,128)(2,1)S(1)} %get-tuple-element.74), channel_id=1, source_target_pairs={{0,3},{1,2},{2,1},{3,0},{4,7},{5,6},{6,5},{7,4},{8,11},{9,10},{10,... | collective-permute-start | bytes 393224 | tf_op jit(solution)/shard_map/ppermute | solution.py:596
  26.6 7.9 %collective-permute-start.6 = (f16[256,256]{1,0:T(8,128)(2,1)S(1)}, f16[256,256]{1,0:T(8,128)(2,1)S(1)}, u32[]{:S(2)}, u32[]{:S(2)}) collective-permute-start(f16[256,256]{1,0:T(8,128)(2,1)S(1)} %get-tuple-element.72), channel_id=1, source_target_pairs={{0,1},{1,0},{2,3},{3,2},{4,5},{5,4},{6,7},{7,6},{8,9},{9,8},{10,11... | collective-permute-start | bytes 393224 | tf_op jit(solution)/shard_map/ppermute | solution.py:596
  27.8 6.7 %collective-permute-start.7 = (f16[256,256]{1,0:T(8,128)(2,1)S(1)}, f16[256,256]{1,0:T(8,128)(2,1)S(1)}, u32[]{:S(2)}, u32[]{:S(2)}) collective-permute-start(f16[256,256]{1,0:T(8,128)(2,1)S(1)} %get-tuple-element.73), channel_id=1, source_target_pairs={{0,2},{1,3},{2,0},{3,1},{4,6},{5,7},{6,4},{7,5},{8,10},{9,11},{10,... | collective-permute-start | bytes 393224 | tf_op jit(solution)/shard_map/ppermute | solution.py:596
  29.0 1.6 %copy-start.3 = (f32[16,16,8,256]{3,2,1,0:T(8,128)S(1)}, f32[16,16,8,256]{3,2,1,0:T(8,128)}, u32[]{:S(2)}) copy-start(f32[16,16,8,256]{3,2,1,0:T(8,128)} %refs_6_.1) | copy-start | bytes 6291460
  29.0 1.6 %copy-start.5 = (f32[8,16,256]{2,1,0:T(8,128)S(1)}, f32[8,16,256]{2,1,0:T(8,128)}, u32[]{:S(2)}) copy-start(f32[8,16,256]{2,1,0:T(8,128)} %refs_4_.1) | copy-start | bytes 393220
  31.4 5.6 %collective-permute-start.10 = (f16[16,8,256]{2,1,0:T(8,128)(2,1)S(1)}, f16[16,8,256]{2,1,0:T(8,128)(2,1)S(1)}, u32[]{:S(2)}, u32[]{:S(2)}) collective-permute-start(f16[16,8,256]{2,1,0:T(8,128)(2,1)S(1)} %get-tuple-element.60), channel_id=1, source_target_pairs={{4,8},{8,4},{12,16},{16,12},{20,24},{24,20},{28,0},{0,28},{5,9},{9... | collective-permute-start | bytes 196616 | tf_op jit(solution)/shard_map/ppermute | solution.py:613
  32.6 4.4 %collective-permute-start.9 = (f16[16,8,256]{2,1,0:T(8,128)(2,1)S(1)}, f16[16,8,256]{2,1,0:T(8,128)(2,1)S(1)}, u32[]{:S(2)}, u32[]{:S(2)}) collective-permute-start(f16[16,8,256]{2,1,0:T(8,128)(2,1)S(1)} %get-tuple-element.61), channel_id=1, source_target_pairs={{0,4},{4,0},{8,12},{12,8},{16,20},{20,16},{24,28},{28,24},{1,5},{5... | collective-permute-start | bytes 196616 | tf_op jit(solution)/shard_map/ppermute | solution.py:612
  34.7 4.7 %collective-permute-start.11 = (f16[128,256]{1,0:T(8,128)(2,1)S(1)}, f16[128,256]{1,0:T(8,128)(2,1)S(1)}, u32[]{:S(2)}, u32[]{:S(2)}) collective-permute-start(f16[128,256]{1,0:T(8,128)(2,1)S(1)} %get-tuple-element.57), channel_id=1, source_target_pairs={{0,4},{4,0},{8,12},{12,8},{16,20},{20,16},{24,28},{28,24},{1,5},{5... | collective-permute-start | bytes 196616 | tf_op jit(solution)/shard_map/ppermute | solution.py:647
  37.0 9.1 %collective-permute-start.16 = (f16[128,256]{1,0:T(8,128)(2,1)S(1)}, f16[128,256]{1,0:T(8,128)(2,1)S(1)}, u32[]{:S(2)}, u32[]{:S(2)}) collective-permute-start(f16[128,256]{1,0:T(8,128)(2,1)S(1)} %get-tuple-element.57), channel_id=1, source_target_pairs={{0,16},{4,20},{8,24},{12,28},{16,0},{20,4},{24,8},{28,12},{1,17},{... | collective-permute-start | bytes 196616 | tf_op jit(solution)/shard_map/ppermute | solution.py:644
  37.1 8.4 %collective-permute-start.14 = (f16[128,256]{1,0:T(8,128)(2,1)S(1)}, f16[128,256]{1,0:T(8,128)(2,1)S(1)}, u32[]{:S(2)}, u32[]{:S(2)}) collective-permute-start(f16[128,256]{1,0:T(8,128)(2,1)S(1)} %get-tuple-element.57), channel_id=1, source_target_pairs={{0,24},{4,28},{8,0},{12,4},{16,8},{20,12},{24,16},{28,20},{1,25},{... | collective-permute-start | bytes 196616 | tf_op jit(solution)/shard_map/ppermute | solution.py:644
  39.4 6.1 %collective-permute-start.18 = (f16[128,256]{1,0:T(8,128)(2,1)S(1)}, f16[128,256]{1,0:T(8,128)(2,1)S(1)}, u32[]{:S(2)}, u32[]{:S(2)}) collective-permute-start(f16[128,256]{1,0:T(8,128)(2,1)S(1)} %get-tuple-element.57), channel_id=1, source_target_pairs={{0,8},{4,12},{8,16},{12,20},{16,24},{20,28},{24,0},{28,4},{1,9},{5... | collective-permute-start | bytes 196616 | tf_op jit(solution)/shard_map/ppermute | solution.py:644
  39.5 12.6 %collective-permute-start.13 = (f16[16,8,256]{2,1,0:T(8,128)(2,1)S(1)}, f16[16,8,256]{2,1,0:T(8,128)(2,1)S(1)}, u32[]{:S(2)}, u32[]{:S(2)}) collective-permute-start(f16[16,8,256]{2,1,0:T(8,128)(2,1)S(1)} %get-tuple-element.58), channel_id=1, source_target_pairs={{1,2},{2,1},{5,6},{6,5},{9,10},{10,9},{13,14},{14,13},{17,18},{18,... | collective-permute-start | bytes 196616 | tf_op jit(solution)/shard_map/ppermute | solution.py:613
  40.4 12.9 %collective-permute-start.12 = (f16[16,8,256]{2,1,0:T(8,128)(2,1)S(1)}, f16[16,8,256]{2,1,0:T(8,128)(2,1)S(1)}, u32[]{:S(2)}, u32[]{:S(2)}) collective-permute-start(f16[16,8,256]{2,1,0:T(8,128)(2,1)S(1)} %get-tuple-element.59), channel_id=1, source_target_pairs={{0,1},{1,0},{2,3},{3,2},{4,5},{5,4},{6,7},{7,6},{8,9},{9,8},{10,11... | collective-permute-start | bytes 196616 | tf_op jit(solution)/shard_map/ppermute | solution.py:612
  45.5 2.0 %collective-permute-start.19 = (f16[128,256]{1,0:T(8,128)(2,1)S(1)}, f16[128,256]{1,0:T(8,128)(2,1)S(1)}, u32[]{:S(2)}, u32[]{:S(2)}) collective-permute-start(f16[128,256]{1,0:T(8,128)(2,1)S(1)} %collective-permute-done.18), channel_id=1, source_target_pairs={{0,4},{4,0},{8,12},{12,8},{16,20},{20,16},{24,28},{28,24},{1,5},{5... | collective-permute-start | bytes 196616 | tf_op jit(solution)/shard_map/ppermute | solution.py:647
  45.6 1.9 %collective-permute-start.15 = (f16[128,256]{1,0:T(8,128)(2,1)S(1)}, f16[128,256]{1,0:T(8,128)(2,1)S(1)}, u32[]{:S(2)}, u32[]{:S(2)}) collective-permute-start(f16[128,256]{1,0:T(8,128)(2,1)S(1)} %collective-permute-done.14), channel_id=1, source_target_pairs={{0,4},{4,0},{8,12},{12,8},{16,20},{20,16},{24,28},{28,24},{1,5},{5... | collective-permute-start | bytes 196616 | tf_op jit(solution)/shard_map/ppermute | solution.py:647
  46.2 1.3 %collective-permute-start.17 = (f16[128,256]{1,0:T(8,128)(2,1)S(1)}, f16[128,256]{1,0:T(8,128)(2,1)S(1)}, u32[]{:S(2)}, u32[]{:S(2)}) collective-permute-start(f16[128,256]{1,0:T(8,128)(2,1)S(1)} %collective-permute-done.16), channel_id=1, source_target_pairs={{0,4},{4,0},{8,12},{12,8},{16,20},{20,16},{24,28},{28,24},{1,5},{5... | collective-permute-start | bytes 196616 | tf_op jit(solution)/shard_map/ppermute | solution.py:647
  49.7 9.3 %collective-permute-start.23 = (f16[256,256]{1,0:T(8,128)(2,1)S(1)}, f16[256,256]{1,0:T(8,128)(2,1)S(1)}, u32[]{:S(2)}, u32[]{:S(2)}) collective-permute-start(f16[256,256]{1,0:T(8,128)(2,1)S(1)} %get-tuple-element.71), channel_id=1, source_target_pairs={{0,3},{1,2},{2,1},{3,0},{4,7},{5,6},{6,5},{7,4},{8,11},{9,10},{10,... | collective-permute-start | bytes 393224 | tf_op jit(solution)/shard_map/ppermute | solution.py:596
  50.8 2.5 %collective-permute-start.20 = (f16[16,128]{1,0:T(8,128)(2,1)S(1)}, f16[16,128]{1,0:T(8,128)(2,1)S(1)}, u32[]{:S(2)}, u32[]{:S(2)}) collective-permute-start(f16[16,128]{1,0:T(8,128)(2,1)S(1)} %slice.161), channel_id=1, source_target_pairs={{0,4},{4,0},{8,12},{12,8},{16,20},{20,16},{24,28},{28,24},{1,5},{5... | collective-permute-start | bytes 12296 | tf_op jit(solution)/shard_map/ppermute | solution.py:714
  50.9 7.6 %collective-permute-start.21 = (f16[256,256]{1,0:T(8,128)(2,1)S(1)}, f16[256,256]{1,0:T(8,128)(2,1)S(1)}, u32[]{:S(2)}, u32[]{:S(2)}) collective-permute-start(f16[256,256]{1,0:T(8,128)(2,1)S(1)} %get-tuple-element.69), channel_id=1, source_target_pairs={{0,1},{1,0},{2,3},{3,2},{4,5},{5,4},{6,7},{7,6},{8,9},{9,8},{10,11... | collective-permute-start | bytes 393224 | tf_op jit(solution)/shard_map/ppermute | solution.py:596
  52.1 7.0 %collective-permute-start.22 = (f16[256,256]{1,0:T(8,128)(2,1)S(1)}, f16[256,256]{1,0:T(8,128)(2,1)S(1)}, u32[]{:S(2)}, u32[]{:S(2)}) collective-permute-start(f16[256,256]{1,0:T(8,128)(2,1)S(1)} %get-tuple-element.70), channel_id=1, source_target_pairs={{0,2},{1,3},{2,0},{3,1},{4,6},{5,7},{6,4},{7,5},{8,10},{9,11},{10,... | collective-permute-start | bytes 393224 | tf_op jit(solution)/shard_map/ppermute | solution.py:596
  56.0 5.6 %collective-permute-start.25 = (f16[16,8,256]{2,1,0:T(8,128)(2,1)S(1)}, f16[16,8,256]{2,1,0:T(8,128)(2,1)S(1)}, u32[]{:S(2)}, u32[]{:S(2)}) collective-permute-start(f16[16,8,256]{2,1,0:T(8,128)(2,1)S(1)} %get-tuple-element.64), channel_id=1, source_target_pairs={{4,8},{8,4},{12,16},{16,12},{20,24},{24,20},{28,0},{0,28},{5,9},{9... | collective-permute-start | bytes 196616 | tf_op jit(solution)/shard_map/ppermute | solution.py:613
  57.4 4.1 %collective-permute-start.24 = (f16[16,8,256]{2,1,0:T(8,128)(2,1)S(1)}, f16[16,8,256]{2,1,0:T(8,128)(2,1)S(1)}, u32[]{:S(2)}, u32[]{:S(2)}) collective-permute-start(f16[16,8,256]{2,1,0:T(8,128)(2,1)S(1)} %get-tuple-element.65), channel_id=1, source_target_pairs={{0,4},{4,0},{8,12},{12,8},{16,20},{20,16},{24,28},{28,24},{1,5},{5... | collective-permute-start | bytes 196616 | tf_op jit(solution)/shard_map/ppermute | solution.py:612
  59.2 3.0 %collective-permute-start.26 = (f16[128,256]{1,0:T(8,128)(2,1)S(1)}, f16[128,256]{1,0:T(8,128)(2,1)S(1)}, u32[]{:S(2)}, u32[]{:S(2)}) collective-permute-start(f16[128,256]{1,0:T(8,128)(2,1)S(1)} %get-tuple-element.55), channel_id=1, source_target_pairs={{0,4},{4,0},{8,12},{12,8},{16,20},{20,16},{24,28},{28,24},{1,5},{5... | collective-permute-start | bytes 196616 | tf_op jit(solution)/shard_map/ppermute | solution.py:647
  61.6 8.7 %collective-permute-start.31 = (f16[128,256]{1,0:T(8,128)(2,1)S(1)}, f16[128,256]{1,0:T(8,128)(2,1)S(1)}, u32[]{:S(2)}, u32[]{:S(2)}) collective-permute-start(f16[128,256]{1,0:T(8,128)(2,1)S(1)} %get-tuple-element.55), channel_id=1, source_target_pairs={{0,16},{4,20},{8,24},{12,28},{16,0},{20,4},{24,8},{28,12},{1,17},{... | collective-permute-start | bytes 196616 | tf_op jit(solution)/shard_map/ppermute | solution.py:644
  61.7 8.0 %collective-permute-start.29 = (f16[128,256]{1,0:T(8,128)(2,1)S(1)}, f16[128,256]{1,0:T(8,128)(2,1)S(1)}, u32[]{:S(2)}, u32[]{:S(2)}) collective-permute-start(f16[128,256]{1,0:T(8,128)(2,1)S(1)} %get-tuple-element.55), channel_id=1, source_target_pairs={{0,24},{4,28},{8,0},{12,4},{16,8},{20,12},{24,16},{28,20},{1,25},{... | collective-permute-start | bytes 196616 | tf_op jit(solution)/shard_map/ppermute | solution.py:644
  62.3 7.4 %collective-permute-start.33 = (f16[128,256]{1,0:T(8,128)(2,1)S(1)}, f16[128,256]{1,0:T(8,128)(2,1)S(1)}, u32[]{:S(2)}, u32[]{:S(2)}) collective-permute-start(f16[128,256]{1,0:T(8,128)(2,1)S(1)} %get-tuple-element.55), channel_id=1, source_target_pairs={{0,8},{4,12},{8,16},{12,20},{16,24},{20,28},{24,0},{28,4},{1,9},{5... | collective-permute-start | bytes 196616 | tf_op jit(solution)/shard_map/ppermute | solution.py:644
  64.1 11.5 %collective-permute-start.28 = (f16[16,8,256]{2,1,0:T(8,128)(2,1)S(1)}, f16[16,8,256]{2,1,0:T(8,128)(2,1)S(1)}, u32[]{:S(2)}, u32[]{:S(2)}) collective-permute-start(f16[16,8,256]{2,1,0:T(8,128)(2,1)S(1)} %get-tuple-element.62), channel_id=1, source_target_pairs={{1,2},{2,1},{5,6},{6,5},{9,10},{10,9},{13,14},{14,13},{17,18},{18,... | collective-permute-start | bytes 196616 | tf_op jit(solution)/shard_map/ppermute | solution.py:613
  64.7 12.0 %collective-permute-start.27 = (f16[16,8,256]{2,1,0:T(8,128)(2,1)S(1)}, f16[16,8,256]{2,1,0:T(8,128)(2,1)S(1)}, u32[]{:S(2)}, u32[]{:S(2)}) collective-permute-start(f16[16,8,256]{2,1,0:T(8,128)(2,1)S(1)} %get-tuple-element.63), channel_id=1, source_target_pairs={{0,1},{1,0},{2,3},{3,2},{4,5},{5,4},{6,7},{7,6},{8,9},{9,8},{10,11... | collective-permute-start | bytes 196616 | tf_op jit(solution)/shard_map/ppermute | solution.py:612
  69.7 2.0 %collective-permute-start.34 = (f16[128,256]{1,0:T(8,128)(2,1)S(1)}, f16[128,256]{1,0:T(8,128)(2,1)S(1)}, u32[]{:S(2)}, u32[]{:S(2)}) collective-permute-start(f16[128,256]{1,0:T(8,128)(2,1)S(1)} %collective-permute-done.33), channel_id=1, source_target_pairs={{0,4},{4,0},{8,12},{12,8},{16,20},{20,16},{24,28},{28,24},{1,5},{5... | collective-permute-start | bytes 196616 | tf_op jit(solution)/shard_map/ppermute | solution.py:647
  69.7 1.9 %collective-permute-start.30 = (f16[128,256]{1,0:T(8,128)(2,1)S(1)}, f16[128,256]{1,0:T(8,128)(2,1)S(1)}, u32[]{:S(2)}, u32[]{:S(2)}) collective-permute-start(f16[128,256]{1,0:T(8,128)(2,1)S(1)} %collective-permute-done.29), channel_id=1, source_target_pairs={{0,4},{4,0},{8,12},{12,8},{16,20},{20,16},{24,28},{28,24},{1,5},{5... | collective-permute-start | bytes 196616 | tf_op jit(solution)/shard_map/ppermute | solution.py:647
  70.3 1.3 %collective-permute-start.32 = (f16[128,256]{1,0:T(8,128)(2,1)S(1)}, f16[128,256]{1,0:T(8,128)(2,1)S(1)}, u32[]{:S(2)}, u32[]{:S(2)}) collective-permute-start(f16[128,256]{1,0:T(8,128)(2,1)S(1)} %collective-permute-done.31), channel_id=1, source_target_pairs={{0,4},{4,0},{8,12},{12,8},{16,20},{20,16},{24,28},{28,24},{1,5},{5... | collective-permute-start | bytes 196616 | tf_op jit(solution)/shard_map/ppermute | solution.py:647
  73.2 6.9 %collective-permute-start.38 = (f16[128,256]{1,0:T(8,128)(2,1)S(1)}, f16[128,256]{1,0:T(8,128)(2,1)S(1)}, u32[]{:S(2)}, u32[]{:S(2)}) collective-permute-start(f16[128,256]{1,0:T(8,128)(2,1)S(1)} %get-tuple-element.68), channel_id=1, source_target_pairs={{0,3},{1,2},{2,1},{3,0},{4,7},{5,6},{6,5},{7,4},{8,11},{9,10},{10,... | collective-permute-start | bytes 196616 | tf_op jit(solution)/shard_map/ppermute | solution.py:596
  74.4 2.4 %collective-permute-start.35 = (f16[16,128]{1,0:T(8,128)(2,1)S(1)}, f16[16,128]{1,0:T(8,128)(2,1)S(1)}, u32[]{:S(2)}, u32[]{:S(2)}) collective-permute-start(f16[16,128]{1,0:T(8,128)(2,1)S(1)} %slice.168), channel_id=1, source_target_pairs={{0,4},{4,0},{8,12},{12,8},{16,20},{20,16},{24,28},{28,24},{1,5},{5... | collective-permute-start | bytes 12296 | tf_op jit(solution)/shard_map/ppermute | solution.py:714
  74.4 4.8 %collective-permute-start.36 = (f16[128,256]{1,0:T(8,128)(2,1)S(1)}, f16[128,256]{1,0:T(8,128)(2,1)S(1)}, u32[]{:S(2)}, u32[]{:S(2)}) collective-permute-start(f16[128,256]{1,0:T(8,128)(2,1)S(1)} %get-tuple-element.66), channel_id=1, source_target_pairs={{0,1},{1,0},{2,3},{3,2},{4,5},{5,4},{6,7},{7,6},{8,9},{9,8},{10,11... | collective-permute-start | bytes 196616 | tf_op jit(solution)/shard_map/ppermute | solution.py:596
  75.6 4.5 %collective-permute-start.37 = (f16[128,256]{1,0:T(8,128)(2,1)S(1)}, f16[128,256]{1,0:T(8,128)(2,1)S(1)}, u32[]{:S(2)}, u32[]{:S(2)}) collective-permute-start(f16[128,256]{1,0:T(8,128)(2,1)S(1)} %get-tuple-element.67), channel_id=1, source_target_pairs={{0,2},{1,3},{2,0},{3,1},{4,6},{5,7},{6,4},{7,5},{8,10},{9,11},{10,... | collective-permute-start | bytes 196616 | tf_op jit(solution)/shard_map/ppermute | solution.py:596
  (1 other events, 0.9 us)
